TPU v7x, 256 devices: a whole 4x4x8 slice. The times are simulated.
256 devices in a mesh: dp: 16 (over y_hi, z), layer: 4 (over x), query: 4 (over y_lo, core).
Axes of the slice: x: 4, y: 4 (y_hi: 2, y_lo: 2; y = y_hi * 2 + y_lo), z: 8, core: 2. Of those that a mesh axis runs over, the one named last changes fastest.
Arguments:
- mantissas: bfloat16 [4096, 4, 4096], P('dp', 'layer'), may hold values from -6 to 6
- exponents: int32 [4096, 4, 32], P('dp', 'layer'), may hold values from -2 to 1
- queries: bfloat16 [1024, 4, 4096], P('query', 'layer'), may hold values from -0.046875 to 0.046875
- doc_ids: int32 [4096], P('dp'), may hold values from 0 to 1023, never falling along the last dimension, each value on 1 to 32 neighbouring positions
- owners: int32 [1024], replicated, may hold values from 0 to 1023, each once
Outputs:
- fisher: float32 [4, 4096, 4096], P('layer', 'dp', 'query')
- doc_scores: float32 [1024, 1024], P('dp', 'query')
Inputs may be any that keep to these rules, and one draw needn't show every extreme that they name: `doc_ids`: never falling along the rows; every document has 1 to 32 rows, one exactly 32. `owners`: each slot is taken by exactly one document.
All inputs are finite; a program needn't handle non-finite values.
Results may differ from a plain program's by a relative error of at most 0.0003.
Values may be sent and summed in bfloat16 or wider, within the bound.
No kernel may reach another device: no remote copies, remote signals or barrier semaphores. Data moves between devices by JAX's collectives and lax.ppermute only.
A program may use at most 64 MiB of HBM per device.

v0:
```python
import jax
import jax.numpy as jnp
from jax import lax
from jax.sharding import PartitionSpec as P


def dequant(mantissas, exponents):
    scale = jnp.exp2(exponents.astype(jnp.float32)).astype(jnp.bfloat16)
    rows, layers, width = mantissas.shape
    blocks = mantissas.reshape(rows, layers, width // 128, 128) * scale[..., None]
    return blocks.reshape(rows, layers, width)


def local_sums(values, doc_ids, owners):
    row_count = values.shape[0]
    doc_total = owners.shape[0]
    first_doc = doc_ids[0]
    local_ids = doc_ids - first_doc
    positions = jnp.arange(row_count, dtype=jnp.int32)
    member = (local_ids[:, None] == positions[None, :]).astype(jnp.float32)
    summed = lax.dot_general(
        member,
        values,
        (((0,), (0,)), ((), ())),
        precision=lax.Precision.HIGHEST,
        preferred_element_type=jnp.float32,
    )
    doc_index = jnp.minimum(first_doc + positions, doc_total - 1)
    slot_ids = owners[doc_index]
    placed = jnp.zeros((doc_total, values.shape[1]), jnp.float32)
    return placed.at[slot_ids].add(summed)


def per_device(mantissas, exponents, queries, doc_ids, owners):
    grads = dequant(mantissas, exponents)
    rows, layers, width = grads.shape
    col_width = width // lax.axis_size("query")
    col_start = lax.axis_index("query") * col_width
    own_width = width // lax.axis_size("dp")
    total_rows = rows * lax.axis_size("dp")
    slab = grads[:, 0, :]
    columns = lax.dynamic_slice_in_dim(slab, col_start, col_width, 1)

    def gram_term(start, count, slab=slab, columns=columns):
        return lax.dot_general(
            slab, columns, (((0,), (0,)), ((), ())), preferred_element_type=jnp.float32
        )

    block = lax.psum_scatter(
        gram_term(jnp.int32(0), own_width * lax.axis_size("dp")),
        "dp",
        scatter_dimension=0,
        tiled=True,
    )
    blocks_out = [block * (1.0 / total_rows)]
    fisher = jnp.stack(blocks_out, 0)
    flat_grads = grads.reshape(rows, layers * width)
    flat_queries = queries.reshape(queries.shape[0], layers * width)
    scores = lax.dot_general(
        flat_grads, flat_queries, (((1,), (1,)), ((), ())), preferred_element_type=jnp.float32
    )
    summed = lax.psum(scores, "layer")
    doc_terms = local_sums(summed, doc_ids, owners)
    doc_scores = lax.psum_scatter(doc_terms, "dp", scatter_dimension=0, tiled=True)
    return (fisher, doc_scores)


def solution(mesh):
    in_specs = (
        P("dp", "layer", None),
        P("dp", "layer", None),
        P("query", "layer", None),
        P("dp"),
        P(),
    )
    out_specs = (P("layer", "dp", "query"), P("dp", "query"))
    return jax.shard_map(
        per_device, mesh=mesh, in_specs=in_specs, out_specs=out_specs, check_vma=False
    )
```

profile of v0, /device:TPU:2, one launch (start us, length us, event | category | flops | bytes accessed | tf_op | source)
XLA Modules:
  0.0 530.6 jit_solution(15688911684187519245)
XLA Ops:
  8.0 0.0 copy-start
  8.0 0.0 all-reduce.2.cloned.1.call-start
  8.1 0.9 fusion.10
  9.0 0.1 copy.8
  9.1 2.3 mul.32
  11.4 4.2 mul.38
  15.5 0.0 copy-done
  15.5 3.7 fusion
  19.2 0.0 all-reduce.2.cloned.1.call-update
  19.2 0.0 reduce-scatter.3.cloned.1.call-start
  19.3 4.3 bitcast_multiply_fusion
  23.6 9.8 %fusion.6 = f32[4096,1024]{1,0:T(8,128)} fusion(bf16[256,4096]{1,0:T(8,128)(2,1)} %bitcast_multiply_fusion, s32[]{:T(128)S(6)} %select_n.23), kind=kOutput, calls=%fused_computation.10 | convolution fusion | flops 2147483648 | bytes 19398660 | tf_op jit(solution)/shard_map/dot_general | solution.py:45
  33.3 0.0 copy-start.2
  33.3 0.0 copy-start.1
  33.3 0.0 reduce-scatter.3.cloned.1.call-update
  33.4 0.0 reduce-scatter.5.cloned.1.call-start
  33.4 0.6 copy-done.2
  34.0 0.5 slice.3
  34.5 0.7 compare_select_fusion.1
  35.2 0.0 copy-done.1
  35.2 1.4 gather_fusion
  36.6 0.7 broadcast_subtract_fusion
  37.2 30.8 %all-reduce.2.cloned.1.call-done = f32[256,256]{1,0:T(8,128)} async-done(((f32[256,256]{1,0:T(8,128)}), f32[256,256]{1,0:T(8,128)}) %all-reduce.2.cloned.1.call-update) | async-done | bytes 262160 | tf_op jit(solution)/shard_map/psum | solution.py:62
  68.1 1.4 fusion.8
  69.5 3.0 scatter_custom_fusion
  72.5 0.0 reduce-scatter.5.cloned.1.call-update
  72.5 249.3 %reduce-scatter.3.cloned.1.call-done = f32[256,1024]{1,0:T(8,128)} async-done(((f32[4096,1024]{1,0:T(8,128)}), f32[256,1024]{1,0:T(8,128)}) %reduce-scatter.3.cloned.1.call-update) | async-done | bytes 1048592 | tf_op jit(solution)/shard_map/reduce_scatter | solution.py:49
  321.8 2.3 multiply_bitcast_fusion
  324.1 199.0 %reduce-scatter.5.cloned.1.call-done = f32[64,256]{1,0:T(8,128)} async-done(((f32[1024,256]{1,0:T(8,128)}), f32[64,256]{1,0:T(8,128)}) %reduce-scatter.5.cloned.1.call-update) | async-done | bytes 65552 | tf_op jit(solution)/shard_map/reduce_scatter | solution.py:64
  (2 shorter events, 0.0 us)
Async XLA Ops:
  8.0 7.5 %copy-start = (bf16[256,1,4096]{2,0,1:T(8,128)(2,1)S(1)}, bf16[256,1,4096]{2,0,1:T(8,128)(2,1)}, u32[]{:S(2)}) copy-start(bf16[256,1,4096]{2,0,1:T(8,128)(2,1)} %param.7) | copy-start | bytes 6291460
  8.0 60.1 %all-reduce.2.cloned.1.call-start = ((), (), s32[]{:S(2)}) async-start(), calls=%async_computation.3 | async-start | bytes 524288 | tf_op jit(solution)/shard_map/psum | solution.py:62
  19.2 302.5 %reduce-scatter.3.cloned.1.call-start = ((), (), s32[]{:S(2)}) async-start(), calls=%async_computation.2 | async-start | bytes 17825792 | tf_op jit(solution)/shard_map/reduce_scatter | solution.py:49
  33.3 0.7 copy-start.2
  33.3 1.9 copy-start.1
  33.4 489.8 %reduce-scatter.5.cloned.1.call-start = ((), (), s32[]{:S(2)}) async-start(), calls=%async_computation.4 | async-start | bytes 1114112 | tf_op jit(solution)/shard_map/reduce_scatter | solution.py:64
Sparse Core Ops, SparseCore 0:
  19.4 48.6 all-reduce.1
Sparse Core Ops, SparseCore 1:
  33.4 288.3 reduce-scatter.2
  326.5 196.5 reduce-scatter.4
where the time goes:
time: 531 us
  waiting for transfers between devices  479 us (90%)
  between operations  15.6 us (3%)
  matrix products  14.9 us (3%)
  other arithmetic  11.8 us (2%)
  local copies, waits for them, and re-layouts  9.05 us (2%)
    reduce_scatter x1, waiting for transfers between devices, per_device(): lax.psum_scatter(gram_term(jnp.int32(0), own_width * lax.axis_size('dp'))...  249 us
    reduce_scatter x1, waiting for transfers between devices, per_device(): lax.psum_scatter(doc_terms, 'dp', scatter_dimension=0, tiled=True)  199 us
    psum x1, waiting for transfers between devices, per_device(): summed = lax.psum(scores, 'layer')  30.8 us
  transfers between devices with their start and end apart: 3, of which 3 were waited for; matrix products, arithmetic and copies ran while one was open for 5% of the time, Pallas kernels for 0%

commit v1 on v0

v1 whole, which is shorter than its diff:
```python
import jax
import jax.numpy as jnp
from jax import lax
from jax.sharding import Mesh, PartitionSpec as P

YH, Z, X, YL, CORE = 2, 8, 4, 2, 2
ROW_AXES = ("yh", "z")
COL_AXES = ("yl", "core")


def powers(exponents):
    return jnp.exp2(exponents.astype(jnp.float32)).astype(jnp.bfloat16)


def spread(scale):
    blocks = scale.shape[1]
    lane_block = jnp.arange(blocks * 128, dtype=jnp.int32) // 128
    pick = (lane_block[None, :] == jnp.arange(blocks, dtype=jnp.int32)[:, None]).astype(jnp.bfloat16)
    wide = lax.dot_general(scale, pick, (((1,), (0,)), ((), ())), preferred_element_type=jnp.float32)
    return wide.astype(jnp.bfloat16)


def ring_gather(block, forward_steps, backward_steps):
    ahead = [(i, (i + 1) % Z) for i in range(Z)]
    behind = [(i, (i - 1) % Z) for i in range(Z)]
    shards = {0: block}
    now = block
    for step in range(1, forward_steps + 1):
        now = lax.ppermute(now, "z", ahead)
        shards[(-step) % Z] = now
    now = block
    for step in range(1, backward_steps + 1):
        now = lax.ppermute(now, "z", behind)
        shards[step % Z] = now
    return [shards[i] for i in range(Z)]


def fisher_block(mantissas, scale, total_rows):
    yh, z = lax.axis_index("yh"), lax.axis_index("z")
    yl, core = lax.axis_index("yl"), lax.axis_index("core")
    rows, width = mantissas.shape
    col_width = width // (YL * CORE)
    col_index = yl * CORE + core
    own = lax.dynamic_slice_in_dim(mantissas, col_index * col_width, col_width, 1)
    own = own * spread(lax.dynamic_slice_in_dim(scale, col_index * (col_width // 128), col_width // 128, 1))
    low = jnp.concatenate([own[:, i : i + 128] for i in range(0, col_width, 256)], 1)
    high = jnp.concatenate([own[:, i : i + 128] for i in range(128, col_width, 256)], 1)
    lows = jnp.concatenate(ring_gather(low, 4, 3), 0)
    highs = jnp.concatenate(ring_gather(high, 3, 4), 0)

    start = lax.rem(z, 4) * 128
    here = jnp.concatenate(
        [lax.dynamic_slice_in_dim(lows, start, 128, 1), lax.dynamic_slice_in_dim(highs, start, 128, 1)], 1
    )
    holder = z // 4
    sent = lax.ppermute(
        here, ("z", "core"), [(i * CORE + i // 4, i * CORE + 1 - i // 4) for i in range(Z)]
    )
    mine = jnp.where(core == holder, here, sent)
    swap = [(0, 1), (1, 0)]
    half = mine.shape[0] // 2
    piece = lax.ppermute(lax.dynamic_slice_in_dim(mine, core * half, half, 0), "yl", swap)
    other_piece = lax.ppermute(piece, "core", swap)
    theirs = jnp.where(
        core == 0,
        jnp.concatenate([piece, other_piece], 0),
        jnp.concatenate([other_piece, piece], 0),
    )
    kept = jnp.where(yl == yh, mine, theirs)
    given = jnp.where(yl == yh, theirs, mine)

    def term(left, right):
        return lax.dot_general(left, right, (((0,), (0,)), ((), ())), preferred_element_type=jnp.float32)

    halves = []
    for right in (lows, highs):
        got = lax.ppermute(term(given, right), "yh", swap)
        halves.append((term(kept, right) + got) * (1.0 / total_rows))
    return jnp.concatenate(
        [h[:, i : i + 128] for i in range(0, col_width // 2, 128) for h in halves], 1
    )


def score_block(mantissas, scale, queries, doc_ids, owners):
    yh = lax.axis_index("yh")
    docs = owners.shape[0]
    grads = mantissas * spread(scale)
    scores = lax.dot_general(queries, grads, (((1,), (1,)), ((), ())), preferred_element_type=jnp.float32)
    count, rows = scores.shape
    share = count // X
    summed = lax.all_to_all(scores.reshape(X, share, rows), "x", 0, 0, tiled=True).sum(0)
    slots = owners[doc_ids]
    own_docs = docs // (YH * Z)
    half = own_docs // 2
    place = jnp.arange(YH * Z, dtype=jnp.int32)[:, None] * own_docs + jnp.arange(half, dtype=jnp.int32)[None, :]
    place = place.reshape(-1, 1)
    member = jnp.concatenate([place == slots[None, :], place + half == slots[None, :]], 1).astype(jnp.float32)
    zero = jnp.zeros_like(summed)
    spaced = jnp.concatenate(
        [jnp.concatenate([summed, zero], 1), jnp.concatenate([zero, summed], 1)], 0
    )
    placed = lax.dot_general(
        member, spaced, (((1,), (1,)), ((), ())),
        precision=lax.Precision.HIGHEST, preferred_element_type=jnp.float32,
    )
    placed = placed.reshape(YH, Z, half, 2 * share)
    kept = lax.dynamic_index_in_dim(placed, yh, 0, keepdims=False)
    given = lax.dynamic_index_in_dim(placed, 1 - yh, 0, keepdims=False)
    placed = kept + lax.ppermute(given, "yh", [(0, 1), (1, 0)])
    mine = lax.all_to_all(placed, "z", 0, 0, tiled=True).sum(0)
    every = lax.all_gather(mine, "x")
    return every.reshape(X, half, 2, share).transpose(2, 1, 0, 3).reshape(own_docs, count)


def per_device(mantissas, exponents, queries, doc_ids, owners):
    mantissas = mantissas[:, 0, :]
    scale = powers(exponents[:, 0, :])
    total_rows = mantissas.shape[0] * YH * Z
    fisher = fisher_block(mantissas, scale, total_rows)
    doc_scores = score_block(mantissas, scale, queries[:, 0, :], doc_ids, owners)
    return fisher[None], doc_scores


def solution(mesh):
    fine = Mesh(mesh.devices.reshape(YH, Z, X, YL, CORE), ("yh", "z", "x", "yl", "core"))
    in_specs = (
        P(ROW_AXES, "x", None),
        P(ROW_AXES, "x", None),
        P(COL_AXES, "x", None),
        P(ROW_AXES),
        P(),
    )
    out_specs = (P("x", ROW_AXES, COL_AXES), P(ROW_AXES, COL_AXES))
    return jax.shard_map(per_device, mesh=fine, in_specs=in_specs, out_specs=out_specs, check_vma=False)
```

time: 531 us -> 145 us (0.27)
  waiting for transfers between devices: 479 us -> 32.6 us
  starting transfers between devices: 0.13 us -> 53.2 us
  between operations: 15.6 us -> 0.94 us
  local copies, waits for them, and re-layouts: 9.05 us -> 21.4 us
  blocking collectives: 0 us -> 11.9 us
  other arithmetic: 11.8 us -> 6.04 us
    reduce_scatter x2 -> x0, waiting for transfers between devices: 448 us -> none  [the longest x1 249 us: per_device(): lax.psum_scatter(gram_term(jnp.int32(0), own_width * lax.axis_size('dp'))...]
    ppermute x0 -> x20, starting transfers between devices: none -> 40.8 us  [the longest x7 27.2 us: ring_gather(): now = lax.ppermute(now, 'z', behind)]
    psum x1 -> x0, waiting for transfers between devices: 30.8 us -> none  [per_device(): summed = lax.psum(scores, 'layer')]
    ppermute x0 -> x20, waiting for transfers between devices: none -> 30.5 us  [the longest x7 8.34 us: ring_gather(): now = lax.ppermute(now, 'z', behind)]
    unnamed x6 -> x35, local copies, waits for them, and re-layouts: 0.61 us -> 13.7 us
    all_to_all x0 -> x2, starting transfers between devices: none -> 12.4 us  [the longest x1 7.58 us: score_block(): mine = lax.all_to_all(placed, 'z', 0, 0, tiled=True).sum(0)]
    all_gather x0 -> x1, blocking collectives: none -> 11.9 us  [score_block(): every = lax.all_gather(mine, 'x')]
    mul x3 -> x0, local copies, waits for them, and re-layouts: 6.56 us -> none  [dequant(): mantissas.reshape(rows, layers, width // 128, 128) * scale[..., None]]
  transfers between devices with their start and end apart: 3 -> 22, of which waited for: 3 -> 11; matrix products, arithmetic and copies ran while one was open for 5% -> 23% of each run, Pallas kernels for 0% -> 0%
where the time goes in v1:
time: 145 us; the launch traced here: 144 us
  starting transfers between devices  53.2 us (37%)
  waiting for transfers between devices  32.6 us (22%)
  local copies, waits for them, and re-layouts  21.4 us (15%)
  matrix products  18.4 us (13%)
  blocking collectives  11.9 us (8%)
  other arithmetic  6.04 us (4%)
    ppermute x7, starting transfers between devices, ring_gather(): now = lax.ppermute(now, 'z', behind)  27.2 us
    unnamed x35, local copies, waits for them, and re-layouts  13.7 us
    all_gather x1, blocking collectives, score_block(): every = lax.all_gather(mine, 'x')  11.9 us
    dot_general x4, matrix products, term(): lax.dot_general(left, right, (((0,), (0,)), ((), ())), preferred_element_...  11.7 us
    ppermute x7, waiting for transfers between devices, ring_gather(): now = lax.ppermute(now, 'z', behind)  8.34 us
    all_to_all x1, starting transfers between devices, score_block(): mine = lax.all_to_all(placed, 'z', 0, 0, tiled=True).sum(0)  7.58 us
    ppermute x2, starting transfers between devices, fisher_block(): got = lax.ppermute(term(given, right), 'yh', swap)  6.48 us
    ppermute x2, waiting for transfers between devices, fisher_block(): got = lax.ppermute(term(given, right), 'yh', swap)  6.09 us
  transfers between devices with their start and end apart: 22, of which 11 were waited for; matrix products, arithmetic and copies ran while one was open for 23% of the time, Pallas kernels for 0%

profile of v1, /device:TPU:2, one launch (start us, length us, event | category | flops | bytes accessed | tf_op | source)
XLA Modules:
  0.0 144.4 jit_solution(5418499924656857109)
XLA Ops:
  0.7 0.9 exponential_convert_fusion
  1.6 1.4 fusion.5
  3.1 0.7 pad_maximum_fusion.2
  3.8 5.9 %collective-permute-start.7 = (bf16[256,512]{1,0:T(8,128)(2,1)S(1)}, bf16[256,512]{1,0:T(8,128)(2,1)S(1)}, u32[]{:S(2)}, u32[]{:S(2)}) collective-permute-start(bf16[256,512]{1,0:T(8,128)(2,1)S(1)} %get-tuple-element.10), channel_id=1, source_target_pairs={{0,112},{16,0},{32,16},{48,32},{64,48},{80,64},{96,80},{112,96},{1... | collective-permute-start | bytes 786440 | tf_op jit(solution)/shard_map/ppermute | solution.py:33
  9.7 0.7 pad_maximum_fusion.1
  10.4 3.2 %collective-permute-start = (bf16[256,512]{1,0:T(8,128)(2,1)S(1)}, bf16[256,512]{1,0:T(8,128)(2,1)}, u32[]{:S(2)}, u32[]{:S(2)}) collective-permute-start(bf16[256,512]{1,0:T(8,128)(2,1)S(1)} %get-tuple-element.12), channel_id=1, source_target_pairs={{0,112},{16,0},{32,16},{48,32},{64,48},{80,64},{96,80},{112,96},{1... | collective-permute-start | bytes 786440 | tf_op jit(solution)/shard_map/ppermute | solution.py:33
  13.7 2.7 %collective-permute-done.7 = bf16[256,512]{1,0:T(8,128)(2,1)S(1)} collective-permute-done((bf16[256,512]{1,0:T(8,128)(2,1)S(1)}, bf16[256,512]{1,0:T(8,128)(2,1)S(1)}, u32[]{:S(2)}, u32[]{:S(2)}) %collective-permute-start.7) | collective-permute-done | bytes 262176 | tf_op jit(solution)/shard_map/ppermute | solution.py:33
  16.4 3.7 %collective-permute-start.8 = (bf16[256,512]{1,0:T(8,128)(2,1)S(1)}, bf16[256,512]{1,0:T(8,128)(2,1)}, u32[]{:S(2)}, u32[]{:S(2)}) collective-permute-start(bf16[256,512]{1,0:T(8,128)(2,1)S(1)} %collective-permute-done.7), channel_id=1, source_target_pairs={{0,112},{16,0},{32,16},{48,32},{64,48},{80,64},{96,80},{112,96},{1... | collective-permute-start | bytes 786440 | tf_op jit(solution)/shard_map/ppermute | solution.py:33
  20.1 1.9 %collective-permute-done = bf16[256,512]{1,0:T(8,128)(2,1)} collective-permute-done((bf16[256,512]{1,0:T(8,128)(2,1)S(1)}, bf16[256,512]{1,0:T(8,128)(2,1)}, u32[]{:S(2)}, u32[]{:S(2)}) %collective-permute-start) | collective-permute-done | bytes 262176 | tf_op jit(solution)/shard_map/ppermute | solution.py:33
  22.0 3.8 %collective-permute-start.1 = (bf16[256,512]{1,0:T(8,128)(2,1)}, bf16[256,512]{1,0:T(8,128)(2,1)}, u32[]{:S(2)}, u32[]{:S(2)}) collective-permute-start(bf16[256,512]{1,0:T(8,128)(2,1)} %collective-permute-done), channel_id=1, source_target_pairs={{0,112},{16,0},{32,16},{48,32},{64,48},{80,64},{96,80},{112,96},{1... | collective-permute-start | bytes 786440 | tf_op jit(solution)/shard_map/ppermute | solution.py:33
  25.8 1.8 %collective-permute-done.8 = bf16[256,512]{1,0:T(8,128)(2,1)} collective-permute-done((bf16[256,512]{1,0:T(8,128)(2,1)S(1)}, bf16[256,512]{1,0:T(8,128)(2,1)}, u32[]{:S(2)}, u32[]{:S(2)}) %collective-permute-start.8) | collective-permute-done | bytes 262176 | tf_op jit(solution)/shard_map/ppermute | solution.py:33
  27.6 3.8 %collective-permute-start.9 = (bf16[256,512]{1,0:T(8,128)(2,1)}, bf16[256,512]{1,0:T(8,128)(2,1)S(1)}, u32[]{:S(2)}, u32[]{:S(2)}) collective-permute-start(bf16[256,512]{1,0:T(8,128)(2,1)} %collective-permute-done.8), channel_id=1, source_target_pairs={{0,112},{16,0},{32,16},{48,32},{64,48},{80,64},{96,80},{112,96},{1... | collective-permute-start | bytes 786440 | tf_op jit(solution)/shard_map/ppermute | solution.py:33
  31.4 1.7 %constant_dynamic-update-slice_fusion.6 = bf16[2048,512]{1,0:T(8,128)(2,1)} fusion(bf16[2048,512]{1,0:T(8,128)(2,1)} %get-tuple-element.13, bf16[256,512]{1,0:T(8,128)(2,1)} %collective-permute-done), kind=kLoop, calls=%fused_computation.52 | loop fusion | bytes 524288
  34.0 3.2 %collective-permute-start.2 = (bf16[256,512]{1,0:T(8,128)(2,1)}, bf16[256,512]{1,0:T(8,128)(2,1)S(1)}, u32[]{:S(2)}, u32[]{:S(2)}) collective-permute-start(bf16[256,512]{1,0:T(8,128)(2,1)} %collective-permute-done.1), channel_id=1, source_target_pairs={{0,112},{16,0},{32,16},{48,32},{64,48},{80,64},{96,80},{112,96},{1... | collective-permute-start | bytes 786440 | tf_op jit(solution)/shard_map/ppermute | solution.py:33
  37.2 1.7 %constant_dynamic-update-slice_fusion.5 = bf16[2048,512]{1,0:T(8,128)(2,1)} fusion(bf16[2048,512]{1,0:T(8,128)(2,1)} %constant_dynamic-update-slice_fusion.6, bf16[256,512]{1,0:T(8,128)(2,1)} %collective-permute-done.1), kind=kLoop, calls=%fused_computation.51 | loop fusion | bytes 524288
  39.0 3.6 %collective-permute-start.10 = (bf16[256,512]{1,0:T(8,128)(2,1)S(1)}, bf16[256,512]{1,0:T(8,128)(2,1)S(1)}, u32[]{:S(2)}, u32[]{:S(2)}) collective-permute-start(bf16[256,512]{1,0:T(8,128)(2,1)S(1)} %collective-permute-done.9), channel_id=1, source_target_pairs={{0,112},{16,0},{32,16},{48,32},{64,48},{80,64},{96,80},{112,96},{1... | collective-permute-start | bytes 786440 | tf_op jit(solution)/shard_map/ppermute | solution.py:33
  42.6 1.7 %constant_dynamic-update-slice_fusion.13 = bf16[2048,512]{1,0:T(8,128)(2,1)} fusion(bf16[2048,512]{1,0:T(8,128)(2,1)} %constant_dynamic-update-slice_fusion.14, bf16[256,512]{1,0:T(8,128)(2,1)} %collective-permute-done.8), kind=kLoop, calls=%fused_computation.59 | loop fusion | bytes 524288
  44.3 1.4 %collective-permute-done.5 = bf16[256,512]{1,0:T(8,128)(2,1)S(1)} collective-permute-done((bf16[256,512]{1,0:T(8,128)(2,1)S(1)}, bf16[256,512]{1,0:T(8,128)(2,1)S(1)}, u32[]{:S(2)}, u32[]{:S(2)}) %collective-permute-start.5) | collective-permute-done | bytes 262176 | tf_op jit(solution)/shard_map/ppermute | solution.py:29
  47.2 1.8 %collective-permute-done.10 = bf16[256,512]{1,0:T(8,128)(2,1)S(1)} collective-permute-done((bf16[256,512]{1,0:T(8,128)(2,1)S(1)}, bf16[256,512]{1,0:T(8,128)(2,1)S(1)}, u32[]{:S(2)}, u32[]{:S(2)}) %collective-permute-start.10) | collective-permute-done | bytes 262176 | tf_op jit(solution)/shard_map/ppermute | solution.py:33
  49.7 4.4 %collective-permute-done.13 = bf16[256,512]{1,0:T(8,128)(2,1)S(1)} collective-permute-done((bf16[256,512]{1,0:T(8,128)(2,1)S(1)}, bf16[256,512]{1,0:T(8,128)(2,1)S(1)}, u32[]{:S(2)}, u32[]{:S(2)}) %collective-permute-start.13) | collective-permute-done | bytes 262176 | tf_op jit(solution)/shard_map/ppermute | solution.py:29
  56.3 1.1 constant_dynamic-slice_fusion.1
  58.1 0.8 constant_dynamic-update-slice_fusion.2
  60.3 1.1 constant_dynamic-slice_fusion.2
  61.4 1.1 pad_maximum_fusion
  62.5 2.3 %collective-permute-start.14 = (bf16[2048,256]{1,0:T(8,128)(2,1)}, bf16[2048,256]{1,0:T(8,128)(2,1)}, u32[]{:S(2)}, u32[]{:S(2)}) collective-permute-start(bf16[2048,256]{1,0:T(8,128)(2,1)} %pad_maximum_fusion), channel_id=1, source_target_pairs={{0,1},{16,17},{32,33},{48,49},{65,64},{81,80},{97,96},{113,112},{2... | collective-permute-start | bytes 3145736 | tf_op jit(solution)/shard_map/ppermute | solution.py:56
  64.8 3.8 %fusion.1 = f32[256,256]{0,1:T(8,128)} fusion(bf16[256,1,4096]{2,0,1:T(8,128)(2,1)S(1)} %copy-done, bf16[256,1,4096]{2,0,1:T(8,128)(2,1)} %param.5, s32[4096]{0:T(1024)S(1)} %add_select_fusion, bf16[256,1,32]{0,2,1:T(8,128)(2,1)S(1)} %exponential_convert_fusion), kind=kOutput, calls=%fused_computation.3 | convolution fusion | flops 606208000 | bytes 4489216 | tf_op jit(solution)/shard_map/dot_general | solution.py:88
  68.6 4.8 %all-to-all-start = ((f32[4,64,256]{2,1,0:T(8,128)}), f32[4,64,256]{2,1,0:T(8,128)S(1)}, u32[]{:S(2)}, u32[]{:S(2)}) async-start(f32[4,64,256]{2,1,0:T(8,128)} %bitcast.31), calls=%async_computation | async-start | bytes 524288 | tf_op jit(solution)/shard_map/all_to_all | solution.py:91
  73.9 1.0 copy-done.2
  74.8 0.9 constant_dynamic-slice_fusion
  75.7 1.6 %collective-permute-start.15 = (bf16[1024,256]{1,0:T(8,128)(2,1)}, bf16[1024,256]{1,0:T(8,128)(2,1)}, u32[]{:S(2)}, u32[]{:S(2)}) collective-permute-start(bf16[1024,256]{1,0:T(8,128)(2,1)} %constant_dynamic-slice_fusion), channel_id=1, source_target_pairs={{0,2},{2,0},{1,3},{3,1},{4,6},{6,4},{5,7},{7,5},{8,10},{10,8},{9,1... | collective-permute-start | bytes 1572872 | tf_op jit(solution)/shard_map/ppermute | solution.py:62
  77.3 1.4 gather_fusion
  78.7 0.9 broadcast_compare_fusion.1
  80.2 5.7 %collective-permute-done.15 = bf16[1024,256]{1,0:T(8,128)(2,1)} collective-permute-done((bf16[1024,256]{1,0:T(8,128)(2,1)}, bf16[1024,256]{1,0:T(8,128)(2,1)}, u32[]{:S(2)}, u32[]{:S(2)}) %collective-permute-start.15) | collective-permute-done | bytes 524320 | tf_op jit(solution)/shard_map/ppermute | solution.py:62
  85.9 1.5 %fusion.6 = f32[512,128]{1,0:T(8,128)S(1)} fusion(pred[512,256]{1,0:T(32,128)(4,1)} %get-tuple-element.15, pred[512,256]{1,0:T(32,128)(4,1)S(1)} %get-tuple-element.14, f32[64,256]{1,0:T(8,128)} %reduce_sum.18), kind=kOutput, calls=%fused_computation.13 | convolution fusion | flops 403243008 | bytes 589824 | tf_op jit(solution)/shard_map/dot_general | solution.py:102
  88.1 3.2 %collective-permute-start.19 = (f32[8,32,128]{2,1,0:T(8,128)}, f32[8,32,128]{2,1,0:T(8,128)S(1)}, u32[]{:S(2)}, u32[]{:S(2)}) collective-permute-start(f32[8,32,128]{2,1,0:T(8,128)} %dynamic-slice_bitcast_fusion), channel_id=1, source_target_pairs={{0,128},{128,0},{1,129},{129,1},{2,130},{130,2},{3,131},{131,3},{4... | collective-permute-start | bytes 393224 | tf_op jit(solution)/shard_map/ppermute | solution.py:109
  91.3 4.4 %collective-permute-done.19 = f32[8,32,128]{2,1,0:T(8,128)S(1)} collective-permute-done((f32[8,32,128]{2,1,0:T(8,128)}, f32[8,32,128]{2,1,0:T(8,128)S(1)}, u32[]{:S(2)}, u32[]{:S(2)}) %collective-permute-start.19) | collective-permute-done | bytes 131104 | tf_op jit(solution)/shard_map/ppermute | solution.py:109
  96.4 7.6 %all-to-all-start.1 = ((f32[8,32,128]{2,1,0:T(8,128)}), f32[8,32,128]{2,1,0:T(8,128)S(1)}, u32[]{:S(2)}, u32[]{:S(2)}) async-start(f32[8,32,128]{2,1,0:T(8,128)} %bitcast_add_fusion), calls=%async_computation.1 | async-start | bytes 262144 | tf_op jit(solution)/shard_map/all_to_all | solution.py:110
  104.0 3.8 %fusion.11 = f32[256,512]{1,0:T(8,128)} fusion(bf16[2048,512]{1,0:T(8,128)(2,1)} %constant_dynamic-update-slice_fusion, bf16[2048,256]{1,0:T(8,128)(2,1)S(1)} %copy-done.3, pred[]{:T(512)S(6)} %eq.28, bf16[1024,256]{1,0:T(8,128)(2,1)} %collective-permute-done.16, bf16[1024,256]{1,0:T(8,128)(2,1)} %collective-permute-done.15, pred[]{:T(512)S(6)} %eq.65), kind=kOutput, calls=%fused_computation.22 | convolution fusion | flops 542113792 | bytes 4718594 | tf_op jit(solution)/shard_map/dot_general | solution.py:73
  107.8 3.2 %collective-permute-start.17 = (f32[256,512]{1,0:T(8,128)}, f32[256,512]{1,0:T(8,128)}, u32[]{:S(2)}, u32[]{:S(2)}) collective-permute-start(f32[256,512]{1,0:T(8,128)} %fusion.11), channel_id=1, source_target_pairs={{0,128},{128,0},{1,129},{129,1},{2,130},{130,2},{3,131},{131,3},{4... | collective-permute-start | bytes 1572872 | tf_op jit(solution)/shard_map/ppermute | solution.py:77
  111.0 2.1 %all-to-all-done.1 = f32[8,32,128]{2,1,0:T(8,128)S(1)} async-done(((f32[8,32,128]{2,1,0:T(8,128)}), f32[8,32,128]{2,1,0:T(8,128)S(1)}, u32[]{:S(2)}, u32[]{:S(2)}) %all-to-all-start.1) | async-done | bytes 131104 | tf_op jit(solution)/shard_map/all_to_all | solution.py:110
  113.1 11.9 %all-gather = f32[128,128]{1,0:T(8,128)S(1)} all-gather(f32[32,128]{1,0:T(8,128)S(1)} %reduce_sum.19), channel_id=2, replica_groups=mesh['yh'=2,'z'=8,'x'=4,'yl'=2,'core'=2] {'x'}, dimensions={0}, use_global_device_ids=true | all-gather | bytes 81920 | tf_op jit(solution)/shard_map/all_gather | solution.py:111
  125.2 0.8 reshape.84
  125.9 3.1 %fusion.10 = f32[256,512]{1,0:T(8,128)S(1)} fusion(bf16[2048,512]{1,0:T(8,128)(2,1)} %constant_dynamic-update-slice_fusion.8, bf16[2048,256]{1,0:T(8,128)(2,1)S(1)} %copy-done.3, pred[]{:T(512)S(6)} %eq.28, bf16[1024,256]{1,0:T(8,128)(2,1)} %collective-permute-done.16, bf16[1024,256]{1,0:T(8,128)(2,1)} %collective-permute-done.15, pred[]{:T(512)S(6)} %eq.65), kind=kOutput, calls=%fused_computation.21 | convolution fusion | flops 542113792 | bytes 4718594 | tf_op jit(solution)/shard_map/dot_general | solution.py:73
  129.1 3.3 %collective-permute-start.18 = (f32[256,512]{1,0:T(8,128)S(1)}, f32[256,512]{1,0:T(8,128)S(1)}, u32[]{:S(2)}, u32[]{:S(2)}) collective-permute-start(f32[256,512]{1,0:T(8,128)S(1)} %fusion.10), channel_id=1, source_target_pairs={{0,128},{128,0},{1,129},{129,1},{2,130},{130,2},{3,131},{131,3},{4... | collective-permute-start | bytes 1572872 | tf_op jit(solution)/shard_map/ppermute | solution.py:77
  132.4 2.5 %fusion.4 = f32[256,512]{1,0:T(8,128)S(1)} fusion(f32[256,512]{1,0:T(8,128)} %collective-permute-done.17, bf16[2048,512]{1,0:T(8,128)(2,1)S(1)} %copy-done.5, bf16[2048,256]{1,0:T(8,128)(2,1)S(1)} %copy-done.3, pred[]{:T(512)S(6)} %eq.28, bf16[1024,256]{1,0:T(8,128)(2,1)} %collective-permute-done.16, bf16[1024,256]{1,0:T(8,128)(2,1)} %collective-permute-done.15, ...), kind=kOutput, calls=%fused_computation.9 | convolution fusion | flops 542375936 | bytes 5242882 | tf_op jit(solution)/shard_map/dot_general | solution.py:73
  134.9 6.1 %collective-permute-done.18 = f32[256,512]{1,0:T(8,128)S(1)} collective-permute-done((f32[256,512]{1,0:T(8,128)S(1)}, f32[256,512]{1,0:T(8,128)S(1)}, u32[]{:S(2)}, u32[]{:S(2)}) %collective-permute-start.18) | collective-permute-done | bytes 524320 | tf_op jit(solution)/shard_map/ppermute | solution.py:77
  140.9 2.3 %fusion.3 = f32[256,512]{1,0:T(8,128)S(1)} fusion(f32[256,512]{1,0:T(8,128)S(1)} %collective-permute-done.18, bf16[2048,512]{1,0:T(8,128)(2,1)S(1)} %copy-done.4, bf16[2048,256]{1,0:T(8,128)(2,1)S(1)} %copy-done.3, pred[]{:T(512)S(6)} %eq.28, bf16[1024,256]{1,0:T(8,128)(2,1)} %collective-permute-done.16, bf16[1024,256]{1,0:T(8,128)(2,1)} %collective-permute-done.15, ...), kind=kOutput, calls=%fused_computation.7 | convolution fusion | flops 542375936 | bytes 5242882 | tf_op jit(solution)/shard_map/dot_general | solution.py:73
  143.5 1.0 copy-done.6
  (68 shorter events, 10.5 us)
Async XLA Ops:
  0.6 64.2 %copy-start = (bf16[256,1,4096]{2,0,1:T(8,128)(2,1)S(1)}, bf16[256,1,4096]{2,0,1:T(8,128)(2,1)}, u32[]{:S(2)}) copy-start(bf16[256,1,4096]{2,0,1:T(8,128)(2,1)} %param.7) | copy-start | bytes 6291460
  3.8 12.6 %collective-permute-start.7 = (bf16[256,512]{1,0:T(8,128)(2,1)S(1)}, bf16[256,512]{1,0:T(8,128)(2,1)S(1)}, u32[]{:S(2)}, u32[]{:S(2)}) collective-permute-start(bf16[256,512]{1,0:T(8,128)(2,1)S(1)} %get-tuple-element.10), channel_id=1, source_target_pairs={{0,112},{16,0},{32,16},{48,32},{64,48},{80,64},{96,80},{112,96},{1... | collective-permute-start | bytes 786440 | tf_op jit(solution)/shard_map/ppermute | solution.py:33
  10.4 9.7 %collective-permute-start.3 = (bf16[256,512]{1,0:T(8,128)(2,1)S(1)}, bf16[256,512]{1,0:T(8,128)(2,1)S(1)}, u32[]{:S(2)}, u32[]{:S(2)}) collective-permute-start(bf16[256,512]{1,0:T(8,128)(2,1)S(1)} %get-tuple-element.12), channel_id=1, source_target_pairs={{0,16},{16,32},{32,48},{48,64},{64,80},{80,96},{96,112},{112,0},{1... | collective-permute-start | bytes 786440 | tf_op jit(solution)/shard_map/ppermute | solution.py:29
  10.4 11.6 %collective-permute-start = (bf16[256,512]{1,0:T(8,128)(2,1)S(1)}, bf16[256,512]{1,0:T(8,128)(2,1)}, u32[]{:S(2)}, u32[]{:S(2)}) collective-permute-start(bf16[256,512]{1,0:T(8,128)(2,1)S(1)} %get-tuple-element.12), channel_id=1, source_target_pairs={{0,112},{16,0},{32,16},{48,32},{64,48},{80,64},{96,80},{112,96},{1... | collective-permute-start | bytes 786440 | tf_op jit(solution)/shard_map/ppermute | solution.py:33
  16.4 11.2 %collective-permute-start.8 = (bf16[256,512]{1,0:T(8,128)(2,1)S(1)}, bf16[256,512]{1,0:T(8,128)(2,1)}, u32[]{:S(2)}, u32[]{:S(2)}) collective-permute-start(bf16[256,512]{1,0:T(8,128)(2,1)S(1)} %collective-permute-done.7), channel_id=1, source_target_pairs={{0,112},{16,0},{32,16},{48,32},{64,48},{80,64},{96,80},{112,96},{1... | collective-permute-start | bytes 786440 | tf_op jit(solution)/shard_map/ppermute | solution.py:33
  20.1 13.0 %collective-permute-start.11 = (bf16[256,512]{1,0:T(8,128)(2,1)S(1)}, bf16[256,512]{1,0:T(8,128)(2,1)S(1)}, u32[]{:S(2)}, u32[]{:S(2)}) collective-permute-start(bf16[256,512]{1,0:T(8,128)(2,1)S(1)} %get-tuple-element.10), channel_id=1, source_target_pairs={{0,16},{16,32},{32,48},{48,64},{64,80},{80,96},{96,112},{112,0},{1... | collective-permute-start | bytes 786440 | tf_op jit(solution)/shard_map/ppermute | solution.py:29
  20.1 13.0 %collective-permute-start.4 = (bf16[256,512]{1,0:T(8,128)(2,1)S(1)}, bf16[256,512]{1,0:T(8,128)(2,1)S(1)}, u32[]{:S(2)}, u32[]{:S(2)}) collective-permute-start(bf16[256,512]{1,0:T(8,128)(2,1)S(1)} %collective-permute-done.3), channel_id=1, source_target_pairs={{0,16},{16,32},{32,48},{48,64},{64,80},{80,96},{96,112},{112,0},{1... | collective-permute-start | bytes 786440 | tf_op jit(solution)/shard_map/ppermute | solution.py:29
  22.0 11.9 %collective-permute-start.1 = (bf16[256,512]{1,0:T(8,128)(2,1)}, bf16[256,512]{1,0:T(8,128)(2,1)}, u32[]{:S(2)}, u32[]{:S(2)}) collective-permute-start(bf16[256,512]{1,0:T(8,128)(2,1)} %collective-permute-done), channel_id=1, source_target_pairs={{0,112},{16,0},{32,16},{48,32},{64,48},{80,64},{96,80},{112,96},{1... | collective-permute-start | bytes 786440 | tf_op jit(solution)/shard_map/ppermute | solution.py:33
  27.6 11.3 %collective-permute-start.9 = (bf16[256,512]{1,0:T(8,128)(2,1)}, bf16[256,512]{1,0:T(8,128)(2,1)S(1)}, u32[]{:S(2)}, u32[]{:S(2)}) collective-permute-start(bf16[256,512]{1,0:T(8,128)(2,1)} %collective-permute-done.8), channel_id=1, source_target_pairs={{0,112},{16,0},{32,16},{48,32},{64,48},{80,64},{96,80},{112,96},{1... | collective-permute-start | bytes 786440 | tf_op jit(solution)/shard_map/ppermute | solution.py:33
  33.1 11.1 %collective-permute-start.12 = (bf16[256,512]{1,0:T(8,128)(2,1)S(1)}, bf16[256,512]{1,0:T(8,128)(2,1)S(1)}, u32[]{:S(2)}, u32[]{:S(2)}) collective-permute-start(bf16[256,512]{1,0:T(8,128)(2,1)S(1)} %collective-permute-done.11), channel_id=1, source_target_pairs={{0,16},{16,32},{32,48},{48,64},{64,80},{80,96},{96,112},{112,0},{1... | collective-permute-start | bytes 786440 | tf_op jit(solution)/shard_map/ppermute | solution.py:29
  33.1 12.6 %collective-permute-start.5 = (bf16[256,512]{1,0:T(8,128)(2,1)S(1)}, bf16[256,512]{1,0:T(8,128)(2,1)S(1)}, u32[]{:S(2)}, u32[]{:S(2)}) collective-permute-start(bf16[256,512]{1,0:T(8,128)(2,1)S(1)} %collective-permute-done.4), channel_id=1, source_target_pairs={{0,16},{16,32},{32,48},{48,64},{64,80},{80,96},{96,112},{112,0},{1... | collective-permute-start | bytes 786440 | tf_op jit(solution)/shard_map/ppermute | solution.py:29
  34.0 12.5 %collective-permute-start.2 = (bf16[256,512]{1,0:T(8,128)(2,1)}, bf16[256,512]{1,0:T(8,128)(2,1)S(1)}, u32[]{:S(2)}, u32[]{:S(2)}) collective-permute-start(bf16[256,512]{1,0:T(8,128)(2,1)} %collective-permute-done.1), channel_id=1, source_target_pairs={{0,112},{16,0},{32,16},{48,32},{64,48},{80,64},{96,80},{112,96},{1... | collective-permute-start | bytes 786440 | tf_op jit(solution)/shard_map/ppermute | solution.py:33
  39.0 10.0 %collective-permute-start.10 = (bf16[256,512]{1,0:T(8,128)(2,1)S(1)}, bf16[256,512]{1,0:T(8,128)(2,1)S(1)}, u32[]{:S(2)}, u32[]{:S(2)}) collective-permute-start(bf16[256,512]{1,0:T(8,128)(2,1)S(1)} %collective-permute-done.9), channel_id=1, source_target_pairs={{0,112},{16,0},{32,16},{48,32},{64,48},{80,64},{96,80},{112,96},{1... | collective-permute-start | bytes 786440 | tf_op jit(solution)/shard_map/ppermute | solution.py:33
  44.3 9.9 %collective-permute-start.13 = (bf16[256,512]{1,0:T(8,128)(2,1)S(1)}, bf16[256,512]{1,0:T(8,128)(2,1)S(1)}, u32[]{:S(2)}, u32[]{:S(2)}) collective-permute-start(bf16[256,512]{1,0:T(8,128)(2,1)S(1)} %collective-permute-done.12), channel_id=1, source_target_pairs={{0,16},{16,32},{32,48},{48,64},{64,80},{80,96},{96,112},{112,0},{1... | collective-permute-start | bytes 786440 | tf_op jit(solution)/shard_map/ppermute | solution.py:29
  45.7 11.7 %collective-permute-start.6 = (bf16[256,512]{1,0:T(8,128)(2,1)S(1)}, bf16[256,512]{1,0:T(8,128)(2,1)S(1)}, u32[]{:S(2)}, u32[]{:S(2)}) collective-permute-start(bf16[256,512]{1,0:T(8,128)(2,1)S(1)} %collective-permute-done.5), channel_id=1, source_target_pairs={{0,16},{16,32},{32,48},{48,64},{64,80},{80,96},{96,112},{112,0},{1... | collective-permute-start | bytes 786440 | tf_op jit(solution)/shard_map/ppermute | solution.py:29
  62.5 11.1 %collective-permute-start.14 = (bf16[2048,256]{1,0:T(8,128)(2,1)}, bf16[2048,256]{1,0:T(8,128)(2,1)}, u32[]{:S(2)}, u32[]{:S(2)}) collective-permute-start(bf16[2048,256]{1,0:T(8,128)(2,1)} %pad_maximum_fusion), channel_id=1, source_target_pairs={{0,1},{16,17},{32,33},{48,49},{65,64},{81,80},{97,96},{113,112},{2... | collective-permute-start | bytes 3145736 | tf_op jit(solution)/shard_map/ppermute | solution.py:56
  64.8 8.8 %copy-start.7 = (s32[256]{0:T(256)S(1)}, s32[256]{0:T(256)}, u32[]{:S(2)}) copy-start(s32[256]{0:T(256)} %param.8) | copy-start | bytes 3076
  68.6 11.0 %all-to-all-start = ((f32[4,64,256]{2,1,0:T(8,128)}), f32[4,64,256]{2,1,0:T(8,128)S(1)}, u32[]{:S(2)}, u32[]{:S(2)}) async-start(f32[4,64,256]{2,1,0:T(8,128)} %bitcast.31), calls=%async_computation | async-start | bytes 524288 | tf_op jit(solution)/shard_map/all_to_all | solution.py:91
  73.6 3.7 %copy-start.1 = (s32[1024]{0:T(1024)S(1)}, s32[1024]{0:T(1024)}, u32[]{:S(2)}) copy-start(s32[1024]{0:T(1024)} %param.9) | copy-start | bytes 12292
  73.9 1.0 copy-start.2
  75.7 28.3 %copy-start.3 = (bf16[2048,256]{1,0:T(8,128)(2,1)S(1)}, bf16[2048,256]{1,0:T(8,128)(2,1)}, u32[]{:S(2)}) copy-start(bf16[2048,256]{1,0:T(8,128)(2,1)} %copy-done.2) | copy-start | bytes 3145732
  75.7 10.2 %collective-permute-start.15 = (bf16[1024,256]{1,0:T(8,128)(2,1)}, bf16[1024,256]{1,0:T(8,128)(2,1)}, u32[]{:S(2)}, u32[]{:S(2)}) collective-permute-start(bf16[1024,256]{1,0:T(8,128)(2,1)} %constant_dynamic-slice_fusion), channel_id=1, source_target_pairs={{0,2},{2,0},{1,3},{3,1},{4,6},{6,4},{5,7},{7,5},{8,10},{10,8},{9,1... | collective-permute-start | bytes 1572872 | tf_op jit(solution)/shard_map/ppermute | solution.py:62
  85.9 18.1 %collective-permute-start.16 = (bf16[1024,256]{1,0:T(8,128)(2,1)}, bf16[1024,256]{1,0:T(8,128)(2,1)}, u32[]{:S(2)}, u32[]{:S(2)}) collective-permute-start(bf16[1024,256]{1,0:T(8,128)(2,1)} %collective-permute-done.15), channel_id=1, source_target_pairs={{0,1},{1,0},{2,3},{3,2},{4,5},{5,4},{6,7},{7,6},{8,9},{9,8},{10,11... | collective-permute-start | bytes 1572872 | tf_op jit(solution)/shard_map/ppermute | solution.py:63
  88.1 7.6 %collective-permute-start.19 = (f32[8,32,128]{2,1,0:T(8,128)}, f32[8,32,128]{2,1,0:T(8,128)S(1)}, u32[]{:S(2)}, u32[]{:S(2)}) collective-permute-start(f32[8,32,128]{2,1,0:T(8,128)} %dynamic-slice_bitcast_fusion), channel_id=1, source_target_pairs={{0,128},{128,0},{1,129},{129,1},{2,130},{130,2},{3,131},{131,3},{4... | collective-permute-start | bytes 393224 | tf_op jit(solution)/shard_map/ppermute | solution.py:109
  96.4 16.7 %all-to-all-start.1 = ((f32[8,32,128]{2,1,0:T(8,128)}), f32[8,32,128]{2,1,0:T(8,128)S(1)}, u32[]{:S(2)}, u32[]{:S(2)}) async-start(f32[8,32,128]{2,1,0:T(8,128)} %bitcast_add_fusion), calls=%async_computation.1 | async-start | bytes 262144 | tf_op jit(solution)/shard_map/all_to_all | solution.py:110
  107.8 24.6 %collective-permute-start.17 = (f32[256,512]{1,0:T(8,128)}, f32[256,512]{1,0:T(8,128)}, u32[]{:S(2)}, u32[]{:S(2)}) collective-permute-start(f32[256,512]{1,0:T(8,128)} %fusion.11), channel_id=1, source_target_pairs={{0,128},{128,0},{1,129},{129,1},{2,130},{130,2},{3,131},{131,3},{4... | collective-permute-start | bytes 1572872 | tf_op jit(solution)/shard_map/ppermute | solution.py:77
  125.9 6.4 %copy-start.5 = (bf16[2048,512]{1,0:T(8,128)(2,1)S(1)}, bf16[2048,512]{1,0:T(8,128)(2,1)}, u32[]{:S(2)}) copy-start(bf16[2048,512]{1,0:T(8,128)(2,1)} %constant_dynamic-update-slice_fusion) | copy-start | bytes 6291460
  129.1 11.9 %copy-start.4 = (bf16[2048,512]{1,0:T(8,128)(2,1)S(1)}, bf16[2048,512]{1,0:T(8,128)(2,1)}, u32[]{:S(2)}) copy-start(bf16[2048,512]{1,0:T(8,128)(2,1)} %constant_dynamic-update-slice_fusion.8) | copy-start | bytes 6291460
  129.1 11.9 %collective-permute-start.18 = (f32[256,512]{1,0:T(8,128)S(1)}, f32[256,512]{1,0:T(8,128)S(1)}, u32[]{:S(2)}, u32[]{:S(2)}) collective-permute-start(f32[256,512]{1,0:T(8,128)S(1)} %fusion.10), channel_id=1, source_target_pairs={{0,128},{128,0},{1,129},{129,1},{2,130},{130,2},{3,131},{131,3},{4... | collective-permute-start | bytes 1572872 | tf_op jit(solution)/shard_map/ppermute | solution.py:77
  143.5 1.0 copy-start.6

commit v2 on v1

v2 whole, which is shorter than its diff:
```python
import functools

import jax
import jax.numpy as jnp
from jax import lax
from jax.experimental import pallas as pl
from jax.experimental.pallas import tpu as pltpu
from jax.sharding import Mesh, PartitionSpec as P

YH, Z, X, YL, CORE = 2, 8, 4, 2, 2
ROW_AXES = ("yh", "z")
COL_AXES = ("yl", "core")
SWAP = [(0, 1), (1, 0)]
RING = [(2 * i, 2 * ((i + 1) % Z)) for i in range(Z)] + [(2 * i + 1, 2 * ((i - 1) % Z) + 1) for i in range(Z)]
TURNED = (((0,), (0,)), ((), ()))


def powers(exponents):
    return jnp.exp2(exponents.astype(jnp.float32)).astype(jnp.bfloat16)


def params():
    return pltpu.CompilerParams(vmem_limit_bytes=24 << 20)


def cost(flops, moved):
    return pl.CostEstimate(flops=flops, bytes_accessed=moved, transcendentals=0)


AT_Z, AT_CORE, AT_YL, AT_FAR = 0, 1, 2, 3


def wide_scale(turned, first_block, columns):
    blocks = turned.shape[0]
    lane_block = lax.broadcasted_iota(jnp.int32, (blocks, columns), 1) // 128 + first_block
    pick = (lane_block == lax.broadcasted_iota(jnp.int32, (blocks, columns), 0)).astype(jnp.bfloat16)
    return lax.dot_general(turned, pick, TURNED, preferred_element_type=jnp.float32)


def dequant_kernel(at, exps, values, far_values, low, high, far):
    step = pl.program_id(0)
    turned = powers(exps[...])
    grads = values[...].astype(jnp.float32) * wide_scale(turned, at[AT_YL] * 16 + step * 4, 512)
    grads = grads.astype(jnp.bfloat16)
    low[...] = jnp.concatenate([grads[:, 0:128], grads[:, 256:384]], 1)
    high[...] = jnp.concatenate([grads[:, 128:256], grads[:, 384:512]], 1)

    @pl.when(step == 0)
    def _():
        half = far.shape[0]
        scale = wide_scale(turned, at[AT_FAR] * 2, 256)
        scale = jnp.where(at[AT_CORE] == 0, scale[:half], scale[half:])
        far[...] = (far_values[...].astype(jnp.float32) * scale).astype(jnp.bfloat16)


def dequant(at, exps, mantissas):
    rows, width = mantissas.shape
    side = jax.ShapeDtypeStruct((rows, width // 4), jnp.bfloat16)
    return pl.pallas_call(
        dequant_kernel,
        grid_spec=pltpu.PrefetchScalarGridSpec(
            num_scalar_prefetch=1,
            grid=(4,),
            in_specs=[
                pl.BlockSpec(exps.shape, lambda g, at: (0, 0)),
                pl.BlockSpec((rows, 512), lambda g, at: (0, at[AT_YL] * 4 + g)),
                pl.BlockSpec((rows // 2, 256), lambda g, at: (at[AT_CORE], at[AT_FAR])),
            ],
            out_specs=[
                pl.BlockSpec((rows, 256), lambda g, at: (0, g)),
                pl.BlockSpec((rows, 256), lambda g, at: (0, g)),
                pl.BlockSpec((rows // 2, 256), lambda g, at: (0, 0)),
            ],
        ),
        out_shape=[side, side, jax.ShapeDtypeStruct((rows // 2, 256), jnp.bfloat16)],
        compiler_params=params(),
        cost_estimate=cost(1 << 25, 2 << 20),
        name="dequant",
    )(at, exps, mantissas, mantissas)


def pick_kernel(count, at, *refs):
    sides, out = refs[:-1], refs[-1]
    row = 0
    for i in range(count):
        rows = sides[2 * i].shape[0]
        out[row : row + rows] = jnp.concatenate([sides[2 * i][...], sides[2 * i + 1][...]], 1)
        row += rows


def lanes_at_z(rows, by_core):
    if by_core:
        return pl.BlockSpec((rows, 128), lambda g, at: (at[AT_CORE], at[AT_Z]))
    return pl.BlockSpec((rows, 128), lambda g, at: (0, at[AT_Z]))


def pick(at, pieces):
    rows = sum(n for n, _, _, _ in pieces)
    specs = [lanes_at_z(n, by_core) for n, by_core, _, _ in pieces for _ in range(2)]
    return pl.pallas_call(
        functools.partial(pick_kernel, len(pieces)),
        grid_spec=pltpu.PrefetchScalarGridSpec(
            num_scalar_prefetch=1, grid=(1,), in_specs=specs,
            out_specs=pl.BlockSpec((rows, 256), lambda g, at: (0, 0)),
        ),
        out_shape=jax.ShapeDtypeStruct((rows, 256), jnp.bfloat16),
        compiler_params=params(),
        cost_estimate=cost(0, rows * 1024),
        name="pick",
    )(at, *[side for _, _, low, high in pieces for side in (low, high)])


def gram_kernel(sizes, kept, added, at, *refs):
    count = len(sizes)
    lows, highs, rights = refs[:count], refs[count : 2 * count], refs[2 * count : 3 * count]
    near, third, far = refs[3 * count : 3 * count + 3]
    out = refs[-1]
    mine_first = at[AT_YL] == at[4]
    use_mine = mine_first if kept else jnp.logical_not(mine_first)
    total, row = None, 0
    for i, rows in enumerate(sizes):
        mine = jnp.concatenate([lows[i][...], highs[i][...]], 1)
        if i < count - 2:
            theirs = near[row : row + rows]
            row += rows
        else:
            theirs = third[...] if i == count - 2 else far[...]
        left = jnp.where(use_mine, mine, theirs)
        term = lax.dot_general(left, rights[i][...], TURNED, preferred_element_type=jnp.float32)
        total = term if total is None else total + term
    if added:
        total = total + refs[3 * count + 3][...]
    out[...] = total


def gram(at, pieces, side, received, kept, own, addend=None):
    sizes = tuple(n for n, _, _, _ in pieces)
    specs = [lanes_at_z(n, by_core) for n, by_core, _, _ in pieces] * 2
    for n, by_core, _, _ in pieces:
        specs.append(
            pl.BlockSpec(
                (n, 512),
                lambda g, at, by_core=by_core: (
                    at[AT_CORE] if by_core else 0,
                    at[AT_CORE] if own else 1 - at[AT_CORE],
                ),
            )
        )
    specs += [pl.BlockSpec(r.shape, lambda g, at: (0, 0)) for r in received]
    operands = [p[2] for p in pieces] + [p[3] for p in pieces] + [p[2 + side] for p in pieces] + list(received)
    if addend is not None:
        specs.append(pl.BlockSpec(addend.shape, lambda g, at: (0, 0)))
        operands.append(addend)
    return pl.pallas_call(
        functools.partial(gram_kernel, sizes, kept, addend is not None),
        grid_spec=pltpu.PrefetchScalarGridSpec(
            num_scalar_prefetch=1, grid=(1,), in_specs=specs,
            out_specs=pl.BlockSpec((256, 512), lambda g, at: (0, 0)),
        ),
        out_shape=jax.ShapeDtypeStruct((256, 512), jnp.float32),
        compiler_params=params(),
        cost_estimate=cost(2 * sum(sizes) * 256 * 512, 3 << 20),
        name="gram",
    )(at, *operands)


def finish_kernel(factor, low, high, low_got, high_got, out):
    for i in range(4):
        lanes = slice(i * 128, i * 128 + 128)
        out[:, i * 256 : i * 256 + 128] = (low[:, lanes] + low_got[:, lanes]) * factor
        out[:, i * 256 + 128 : i * 256 + 256] = (high[:, lanes] + high_got[:, lanes]) * factor


def finish(factor, terms):
    rows, columns = terms[0].shape
    return pl.pallas_call(
        functools.partial(finish_kernel, factor),
        grid=(2,),
        in_specs=[pl.BlockSpec((rows // 2, columns), lambda g: (g, 0))] * 4,
        out_specs=pl.BlockSpec((rows // 2, 2 * columns), lambda g: (g, 0)),
        out_shape=jax.ShapeDtypeStruct((rows, 2 * columns), jnp.float32),
        compiler_params=params(),
        cost_estimate=cost(1 << 19, 3 << 20),
        name="finish",
    )(*terms)


def fisher_block(mantissas, exps, total_rows):
    yh, z = lax.axis_index("yh"), lax.axis_index("z")
    yl, core = lax.axis_index("yl"), lax.axis_index("core")
    rows = mantissas.shape[0]
    far_block = (1 - yl) * Z + lax.rem(z + Z // 2, Z)
    at = jnp.stack([z, core, yl, far_block, yh]).astype(jnp.int32)
    low, high, far = dequant(at, exps, mantissas)
    far = lax.ppermute(far, "z", [(i, (i + Z // 2) % Z) for i in range(Z)])

    half = rows // 2
    pieces = [(half, True, low, high)]
    for step in range(1, Z // 2 + 1):
        if step == Z // 2:
            low = lax.dynamic_slice_in_dim(low, core * half, half, 0)
            high = lax.dynamic_slice_in_dim(high, core * half, half, 0)
        low = lax.ppermute(low, ("z", "core"), RING)
        high = lax.ppermute(high, ("z", "core"), RING)
        pieces.append((low.shape[0], False, low, high))
    near = lax.ppermute(pick(at, pieces[:3]), "yl", SWAP)
    third = lax.ppermute(pick(at, pieces[3:4]), "yl", SWAP)
    received = (near, third, far)

    given = [lax.ppermute(gram(at, pieces, s, received, False, False), "core", SWAP) for s in range(2)]
    given = [lax.ppermute(gram(at, pieces, s, received, False, True, given[s]), "yh", SWAP) for s in range(2)]
    kept = [lax.ppermute(gram(at, pieces, s, received, True, False), "core", SWAP) for s in range(2)]
    kept = [gram(at, pieces, s, received, True, True, kept[s]) for s in range(2)]
    return finish(1.0 / total_rows, kept + given)


def spread(scale):
    blocks = scale.shape[1]
    lane_block = jnp.arange(blocks * 128, dtype=jnp.int32) // 128
    pick = (lane_block[None, :] == jnp.arange(blocks, dtype=jnp.int32)[:, None]).astype(jnp.bfloat16)
    wide = lax.dot_general(scale, pick, (((1,), (0,)), ((), ())), preferred_element_type=jnp.float32)
    return wide.astype(jnp.bfloat16)


def score_block(mantissas, scale, queries, doc_ids, owners):
    docs = owners.shape[0]
    grads = mantissas * spread(scale)
    scores = lax.dot_general(queries, grads, (((1,), (1,)), ((), ())), preferred_element_type=jnp.float32)
    count, rows = scores.shape
    share = count // X
    summed = lax.all_to_all(scores.reshape(X, share, rows), "x", 0, 0, tiled=True).sum(0)
    slots = owners[doc_ids]
    own_docs = docs // (YH * Z)
    half = own_docs // 2
    place = jnp.arange(YH * Z, dtype=jnp.int32)[:, None] * own_docs + jnp.arange(half, dtype=jnp.int32)[None, :]
    place = place.reshape(-1, 1)
    member = jnp.concatenate([place == slots[None, :], place + half == slots[None, :]], 1).astype(jnp.float32)
    zero = jnp.zeros_like(summed)
    spaced = jnp.concatenate(
        [jnp.concatenate([summed, zero], 1), jnp.concatenate([zero, summed], 1)], 0
    )
    placed = lax.dot_general(
        member, spaced, (((1,), (1,)), ((), ())),
        precision=lax.Precision.HIGHEST, preferred_element_type=jnp.float32,
    )
    placed = placed.reshape(YH * Z, half, 2 * share)
    mine = lax.all_to_all(placed, ("yh", "z"), 0, 0, tiled=True).sum(0)
    every = lax.all_to_all(jnp.broadcast_to(mine[None], (X, half, 2 * share)), "x", 0, 0, tiled=True)
    return every.reshape(X, half, 2, share).transpose(2, 1, 0, 3).reshape(own_docs, count)


def per_device(mantissas, exponents, queries, doc_ids, owners):
    mantissas = mantissas[:, 0, :]
    exponents = exponents[:, 0, :]
    total_rows = mantissas.shape[0] * YH * Z
    fisher = fisher_block(mantissas, exponents.T, total_rows)
    doc_scores = score_block(mantissas, powers(exponents), queries[:, 0, :], doc_ids, owners)
    return fisher[None], doc_scores


def solution(mesh):
    fine = Mesh(mesh.devices.reshape(YH, Z, X, YL, CORE), ("yh", "z", "x", "yl", "core"))
    in_specs = (
        P(ROW_AXES, "x", None),
        P(ROW_AXES, "x", None),
        P(COL_AXES, "x", None),
        P(ROW_AXES),
        P(),
    )
    out_specs = (P("x", ROW_AXES, COL_AXES), P(ROW_AXES, COL_AXES))
    return jax.shard_map(per_device, mesh=fine, in_specs=in_specs, out_specs=out_specs, check_vma=False)
```

time: 145 us -> 143 us (0.986); the launches traced: 144 us -> 140 us
  Pallas kernels: 0 us -> 30 us
  starting transfers between devices: 53.2 us -> 33 us
  matrix products: 18.4 us -> 6.07 us
  local copies, waits for them, and re-layouts: 21.4 us -> 29.9 us
  waiting for transfers between devices: 32.6 us -> 25.8 us
  blocking collectives: 11.9 us -> 8.85 us
    pallas_call x0 -> x12, Pallas kernels: none -> 30 us  [the longest x8 23.1 us: gram(): pl.pallas_call(functools.partial(gram_kernel, sizes, kept, addend is not...]
    ppermute x20 -> x17, starting transfers between devices: 40.8 us -> 19.2 us  [the longest x4 5.16 us: fisher_block(): low = lax.ppermute(low, ('z', 'core'), RING)]
    dot_general x5 -> x0, matrix products: 13.1 us -> none  [the longest x4 11.7 us: term(): lax.dot_general(left, right, (((0,), (0,)), ((), ())), preferred_element_...]
    all_gather x1 -> x0, blocking collectives: 11.9 us -> none  [score_block(): every = lax.all_gather(mine, 'x')]
    all_to_all x0 -> x1, blocking collectives: none -> 8.85 us  [score_block(): lax.all_to_all(jnp.broadcast_to(mine[None], (X, half, 2 * share)), 'x', 0...]
    unnamed x35 -> x58, local copies, waits for them, and re-layouts: 13.7 us -> 22 us
    ppermute x20 -> x17, waiting for transfers between devices: 30.5 us -> 25.8 us  [the longest x4 11.1 us: fisher_block(): high = lax.ppermute(high, ('z', 'core'), RING)]
    dynamic_slice x3 -> x2, local copies, waits for them, and re-layouts: 3 us -> 0.04 us  [the longest x1 0.02 us: fisher_block(): low = lax.dynamic_slice_in_dim(low, core * half, half, 0)]
  transfers between devices with their start and end apart: 22 -> 19, of which waited for: 11 -> 6; matrix products, arithmetic and copies ran while one was open for 23% -> 14% of each run, Pallas kernels for 0% -> 18%
where the time goes in v2:
time: 143 us; the launch traced here: 140 us
  starting transfers between devices  33 us (23%)
  Pallas kernels  30 us (21%)
  local copies, waits for them, and re-layouts  29.9 us (21%)
  waiting for transfers between devices  25.8 us (18%)
  blocking collectives  8.85 us (6%)
  matrix products  6.07 us (4%)
  other arithmetic  5.39 us (4%)
    pallas_call x8, Pallas kernels, gram(): pl.pallas_call(functools.partial(gram_kernel, sizes, kept, addend is not...  23.1 us
    unnamed x58, local copies, waits for them, and re-layouts  22 us
    ppermute x4, waiting for transfers between devices, fisher_block(): high = lax.ppermute(high, ('z', 'core'), RING)  11.1 us
    all_to_all x1, starting transfers between devices, score_block(): mine = lax.all_to_all(placed, ('yh', 'z'), 0, 0, tiled=True).sum(0)  9.02 us
    all_to_all x1, blocking collectives, score_block(): lax.all_to_all(jnp.broadcast_to(mine[None], (X, half, 2 * share)), 'x', 0...  8.85 us
    ppermute x4, waiting for transfers between devices, fisher_block(): low = lax.ppermute(low, ('z', 'core'), RING)  8.64 us
    ppermute x4, starting transfers between devices, fisher_block(): low = lax.ppermute(low, ('z', 'core'), RING)  5.16 us
    all_to_all x1, starting transfers between devices, score_block(): lax.all_to_all(scores.reshape(X, share, rows), 'x', 0, 0, tiled=True).sum(0)  4.82 us
  transfers between devices with their start and end apart: 19, of which 6 were waited for; matrix products, arithmetic and copies ran while one was open for 14% of the time, Pallas kernels for 18%

profile of v2, /device:TPU:2, one launch (start us, length us, event | category | flops | bytes accessed | tf_op | source)
XLA Modules:
  0.0 139.9 jit_solution(17244007381650269414)
XLA Ops:
  0.7 1.7 %copy-done.24 = bf16[256,1,4096]{2,0,1:T(8,128)(2,1)S(1)} copy-done((bf16[256,1,4096]{2,0,1:T(8,128)(2,1)S(1)}, bf16[256,1,4096]{2,0,1:T(8,128)(2,1)}, u32[]{:S(2)}) %copy-start.24) | copy-done | bytes 2097176
  3.2 2.7 %dequant.1 = (bf16[256,1024]{1,0:T(8,128)(2,1)S(1)}, bf16[256,1024]{1,0:T(8,128)(2,1)S(1)}, bf16[128,256]{1,0:T(8,128)(2,1)}) custom-call(s32[5]{0:T(128)S(1)} %stack.23.at, s32[32,256]{1,0:T(8,128)S(1)} %bitcast.33, bf16[256,4096]{1,0:T(8,128)(2,1)S(1)} %bitcast.31, bf16[256,4096]{1,0:T(8,128)(2,1)S(1)} %bitcast.32), custom_call_target="tpu_custom_call" | custom-call | flops 33554432 | bytes 2097152 | tf_op jit(solution)/shard_map/dequant/pallas_call | solution.py:59
  5.9 1.9 %collective-permute-start = (bf16[256,1024]{1,0:T(8,128)(2,1)S(1)}, bf16[256,1024]{1,0:T(8,128)(2,1)S(1)}, u32[]{:S(2)}, u32[]{:S(2)}) collective-permute-start(bf16[256,1024]{1,0:T(8,128)(2,1)S(1)} %get-tuple-element.5.refs_0_.refs_10_), channel_id=1, source_target_pairs={{0,16},{16,32},{32,48},{48,64},{64,80},{80,96},{96,112},{112,0},{1... | collective-permute-start | bytes 1572872 | tf_op jit(solution)/shard_map/ppermute | solution.py:203
  8.6 1.9 %collective-permute-start.4 = (bf16[256,1024]{1,0:T(8,128)(2,1)S(1)}, bf16[256,1024]{1,0:T(8,128)(2,1)S(1)}, u32[]{:S(2)}, u32[]{:S(2)}) collective-permute-start(bf16[256,1024]{1,0:T(8,128)(2,1)S(1)} %get-tuple-element.6.refs_1_.refs_5_.refs_10_), channel_id=1, source_target_pairs={{0,16},{16,32},{32,48},{48,64},{64,80},{80,96},{96,112},{112,0},{1... | collective-permute-start | bytes 1572872 | tf_op jit(solution)/shard_map/ppermute | solution.py:204
  11.3 7.6 %collective-permute-done.refs_2_.refs_1_.refs_11_ = bf16[256,1024]{1,0:T(8,128)(2,1)S(1)} collective-permute-done((bf16[256,1024]{1,0:T(8,128)(2,1)S(1)}, bf16[256,1024]{1,0:T(8,128)(2,1)S(1)}, u32[]{:S(2)}, u32[]{:S(2)}) %collective-permute-start) | collective-permute-done | bytes 524320 | tf_op jit(solution)/shard_map/ppermute | solution.py:203
  19.7 4.8 %collective-permute-done.4.refs_3_.refs_6_.refs_11_ = bf16[256,1024]{1,0:T(8,128)(2,1)S(1)} collective-permute-done((bf16[256,1024]{1,0:T(8,128)(2,1)S(1)}, bf16[256,1024]{1,0:T(8,128)(2,1)S(1)}, u32[]{:S(2)}, u32[]{:S(2)}) %collective-permute-start.4) | collective-permute-done | bytes 524320 | tf_op jit(solution)/shard_map/ppermute | solution.py:204
  25.3 4.6 %collective-permute-start.10 = (bf16[128,256]{1,0:T(8,128)(2,1)}, bf16[128,256]{1,0:T(8,128)(2,1)}, u32[]{:S(2)}, u32[]{:S(2)}) collective-permute-start(bf16[128,256]{1,0:T(8,128)(2,1)} %get-tuple-element.7), channel_id=1, source_target_pairs={{0,64},{16,80},{32,96},{48,112},{64,0},{80,16},{96,32},{112,48},{1... | collective-permute-start | bytes 196616 | tf_op jit(solution)/shard_map/ppermute | solution.py:195
  29.9 1.0 collective-permute-done.1.refs_4_.refs_2_.refs_12_
  31.0 6.3 %collective-permute-done.5.refs_5_.refs_7_.refs_12_ = bf16[256,1024]{1,0:T(8,128)(2,1)} collective-permute-done((bf16[256,1024]{1,0:T(8,128)(2,1)S(1)}, bf16[256,1024]{1,0:T(8,128)(2,1)}, u32[]{:S(2)}, u32[]{:S(2)}) %collective-permute-start.5) | collective-permute-done | bytes 524320 | tf_op jit(solution)/shard_map/ppermute | solution.py:204
  37.3 3.8 %fusion.1 = f32[256,256]{0,1:T(8,128)} fusion(bf16[256,1,4096]{2,0,1:T(8,128)(2,1)S(1)} %copy-done, s32[4096]{0:T(1024)S(1)} %add_select_fusion, s32[256,1,32]{0,2,1:T(8,128)S(1)} %copy-done.26, bf16[256,1,4096]{2,0,1:T(8,128)(2,1)} %param.5), kind=kOutput, calls=%fused_computation.3 | convolution fusion | flops 606232576 | bytes 4505600 | tf_op jit(solution)/shard_map/dot_general | solution.py:228
  41.1 4.8 %all-to-all-start = ((f32[4,64,256]{2,1,0:T(8,128)}), f32[4,64,256]{2,1,0:T(8,128)}, u32[]{:S(2)}, u32[]{:S(2)}) async-start(f32[4,64,256]{2,1,0:T(8,128)} %bitcast.11), calls=%async_computation | async-start | bytes 524288 | tf_op jit(solution)/shard_map/all_to_all | solution.py:231
  46.0 1.0 copy-done.2
  47.1 1.0 copy-done.6
  48.1 1.0 copy-done.10
  49.2 1.0 copy-done.15
  50.2 1.5 %pick.2 = bf16[640,256]{1,0:T(8,128)(2,1)S(1)} custom-call(s32[5]{0:T(128)S(1)} %stack.23.at, bf16[256,1024]{1,0:T(8,128)(2,1)S(1)} %copy-done.2, bf16[256,1024]{1,0:T(8,128)(2,1)S(1)} %copy-done.6, bf16[256,1024]{1,0:T(8,128)(2,1)S(1)} %copy-done.10, bf16[256,1024]{1,0:T(8,128)(2,1)S(1)} %copy-done.15, ...), custom_call_target="tpu_custom_call" | custom-call | bytes 655360 | tf_op jit(solution)/shard_map/pick/pallas_call | solution.py:100
  51.7 1.7 %collective-permute-start.8 = (bf16[640,256]{1,0:T(8,128)(2,1)S(1)}, bf16[640,256]{1,0:T(8,128)(2,1)S(1)}, u32[]{:S(2)}, u32[]{:S(2)}) collective-permute-start(bf16[640,256]{1,0:T(8,128)(2,1)S(1)} %pick.2), channel_id=1, source_target_pairs={{0,2},{2,0},{1,3},{3,1},{4,6},{6,4},{5,7},{7,5},{8,10},{10,8},{9,1... | collective-permute-start | bytes 983048 | tf_op jit(solution)/shard_map/ppermute | solution.py:206
  54.2 3.2 %collective-permute-start.3 = (bf16[128,1024]{1,0:T(8,128)(2,1)S(1)}, bf16[128,1024]{1,0:T(8,128)(2,1)S(1)}, u32[]{:S(2)}, u32[]{:S(2)}) collective-permute-start(bf16[128,1024]{1,0:T(8,128)(2,1)S(1)} %constant_dynamic-slice_fusion.1), channel_id=1, source_target_pairs={{0,16},{16,32},{32,48},{48,64},{64,80},{80,96},{96,112},{112,0},{1... | collective-permute-start | bytes 786440 | tf_op jit(solution)/shard_map/ppermute | solution.py:203
  58.6 2.2 %collective-permute-done.8.refs_15_ = bf16[640,256]{1,0:T(8,128)(2,1)S(1)} collective-permute-done((bf16[640,256]{1,0:T(8,128)(2,1)S(1)}, bf16[640,256]{1,0:T(8,128)(2,1)S(1)}, u32[]{:S(2)}, u32[]{:S(2)}) %collective-permute-start.8) | collective-permute-done | bytes 327712 | tf_op jit(solution)/shard_map/ppermute | solution.py:206
  60.8 3.8 %collective-permute-done.9.refs_16_ = bf16[256,256]{1,0:T(8,128)(2,1)S(1)} collective-permute-done((bf16[256,256]{1,0:T(8,128)(2,1)S(1)}, bf16[256,256]{1,0:T(8,128)(2,1)S(1)}, u32[]{:S(2)}, u32[]{:S(2)}) %collective-permute-start.9) | collective-permute-done | bytes 131104 | tf_op jit(solution)/shard_map/ppermute | solution.py:207
  64.6 3.0 %gram.14 = f32[256,512]{1,0:T(8,128)} custom-call(s32[5]{0:T(128)S(1)} %stack.23.at, bf16[256,1024]{1,0:T(8,128)(2,1)S(1)} %copy-done.2, bf16[256,1024]{1,0:T(8,128)(2,1)S(1)} %copy-done.11, bf16[256,1024]{1,0:T(8,128)(2,1)} %collective-permute-done.1.refs_4_.refs_2_.refs_12_, bf16[256,1024]{1,0:T(8,128)(2,1)S(1)} %collective-permute-done.2.refs_0_.refs_3_.refs_13_, ...), custom_call_target="tpu_custom_call" | custom-call | flops 268435456 | bytes 3145728 | tf_op jit(solution)/shard_map/gram/pallas_call | solution.py:154
  68.1 3.0 %gram.12 = f32[256,512]{1,0:T(8,128)} custom-call(s32[5]{0:T(128)S(1)} %stack.23.at, bf16[256,1024]{1,0:T(8,128)(2,1)S(1)} %copy-done.2, bf16[256,1024]{1,0:T(8,128)(2,1)S(1)} %copy-done.11, bf16[256,1024]{1,0:T(8,128)(2,1)} %collective-permute-done.1.refs_4_.refs_2_.refs_12_, bf16[256,1024]{1,0:T(8,128)(2,1)S(1)} %collective-permute-done.2.refs_0_.refs_3_.refs_13_, ...), custom_call_target="tpu_custom_call" | custom-call | flops 268435456 | bytes 3145728 | tf_op jit(solution)/shard_map/gram/pallas_call | solution.py:154
  71.7 2.0 %gather_fusion = s32[256]{0:T(256)} fusion(s32[1024]{0:T(1024)S(1)} %copy-done.27, s32[1024]{0:T(1024)} %pad_clamp_fusion), kind=kCustom, calls=%fused_computation | custom fusion | bytes 3072 | tf_op jit(solution)/shard_map/gather | solution.py:232
  73.8 1.5 %broadcast_compare_fusion.1 = (pred[512,256]{1,0:T(32,128)(4,1)}, pred[512,256]{1,0:T(32,128)(4,1)}) fusion(s32[256]{0:T(256)} %gather_fusion, s32[512]{0:T(512)S(1)} %add.74, s32[512]{0:T(512)S(1)} %broadcast_add_fusion), kind=kLoop, calls=%fused_computation.18 | loop fusion | flops 262144 | bytes 267264 | tf_op jit(solution)/shard_map/eq | solution.py:237
  75.3 1.6 %reduce_sum.18 = f32[64,256]{1,0:T(8,128)} reduce(f32[4,64,256]{2,1,0:T(8,128)} %all-to-all-done, f32[]{:T(128)} %constant.55.clone.1), dimensions={0}, to_apply=%region_0.1 | reduce | flops 49152 | bytes 327684 | tf_op jit(solution)/shard_map/reduce_sum | solution.py:231
  76.9 2.3 %fusion.3 = f32[512,128]{1,0:T(8,128)} fusion(pred[512,256]{1,0:T(32,128)(4,1)} %get-tuple-element.9, pred[512,256]{1,0:T(32,128)(4,1)} %get-tuple-element.8, f32[64,256]{1,0:T(8,128)} %reduce_sum.18), kind=kOutput, calls=%fused_computation.5 | convolution fusion | flops 403243008 | bytes 589824 | tf_op jit(solution)/shard_map/dot_general | solution.py:242
  79.2 9.0 %all-to-all-start.1 = ((f32[16,32,128]{2,1,0:T(8,128)}), f32[16,32,128]{2,1,0:T(8,128)}, u32[]{:S(2)}, u32[]{:S(2)}) async-start(f32[16,32,128]{2,1,0:T(8,128)} %bitcast.36), calls=%async_computation.1 | async-start | bytes 524288 | tf_op jit(solution)/shard_map/all_to_all | solution.py:247
  88.2 1.0 copy-done.3
  89.3 1.0 copy-done.7
  90.3 1.0 copy-done.12
  91.4 1.0 copy-done.16
  94.3 3.0 %gram.10 = f32[256,512]{1,0:T(8,128)} custom-call(s32[5]{0:T(128)S(1)} %stack.23.at, bf16[256,1024]{1,0:T(8,128)(2,1)S(1)} %copy-done.3, bf16[256,1024]{1,0:T(8,128)(2,1)S(1)} %copy-done.12, bf16[256,1024]{1,0:T(8,128)(2,1)} %collective-permute-done.1.refs_4_.refs_2_.refs_12_, bf16[256,1024]{1,0:T(8,128)(2,1)S(1)} %collective-permute-done.2.refs_0_.refs_3_.refs_13_, ...), custom_call_target="tpu_custom_call" | custom-call | flops 268435456 | bytes 3145728 | tf_op jit(solution)/shard_map/gram/pallas_call | solution.py:154
  97.3 3.0 %gram.8 = f32[256,512]{1,0:T(8,128)} custom-call(s32[5]{0:T(128)S(1)} %stack.23.at, bf16[256,1024]{1,0:T(8,128)(2,1)S(1)} %copy-done.3, bf16[256,1024]{1,0:T(8,128)(2,1)S(1)} %copy-done.12, bf16[256,1024]{1,0:T(8,128)(2,1)} %collective-permute-done.1.refs_4_.refs_2_.refs_12_, bf16[256,1024]{1,0:T(8,128)(2,1)S(1)} %collective-permute-done.2.refs_0_.refs_3_.refs_13_, ...), custom_call_target="tpu_custom_call" | custom-call | flops 268435456 | bytes 3145728 | tf_op jit(solution)/shard_map/gram/pallas_call | solution.py:154
  100.8 3.2 %gram.15 = f32[256,512]{1,0:T(8,128)} custom-call(s32[5]{0:T(128)S(1)} %stack.23.at, bf16[256,1024]{1,0:T(8,128)(2,1)S(1)} %copy-done.3, bf16[256,1024]{1,0:T(8,128)(2,1)S(1)} %copy-done.12, bf16[256,1024]{1,0:T(8,128)(2,1)} %collective-permute-done.1.refs_4_.refs_2_.refs_12_, bf16[256,1024]{1,0:T(8,128)(2,1)S(1)} %collective-permute-done.2.refs_0_.refs_3_.refs_13_, ...), custom_call_target="tpu_custom_call" | custom-call | flops 268435456 | bytes 3145728 | tf_op jit(solution)/shard_map/gram/pallas_call | solution.py:154
  104.0 3.4 %collective-permute-start.16 = (f32[256,512]{1,0:T(8,128)}, f32[256,512]{1,0:T(8,128)}, u32[]{:S(2)}, u32[]{:S(2)}) collective-permute-start(f32[256,512]{1,0:T(8,128)} %gram.15), channel_id=1, source_target_pairs={{0,128},{128,0},{1,129},{129,1},{2,130},{130,2},{3,131},{131,3},{4... | collective-permute-start | bytes 1572872 | tf_op jit(solution)/shard_map/ppermute | solution.py:211
  107.3 3.2 %gram.13 = f32[256,512]{1,0:T(8,128)} custom-call(s32[5]{0:T(128)S(1)} %stack.23.at, bf16[256,1024]{1,0:T(8,128)(2,1)S(1)} %copy-done.3, bf16[256,1024]{1,0:T(8,128)(2,1)S(1)} %copy-done.12, bf16[256,1024]{1,0:T(8,128)(2,1)} %collective-permute-done.1.refs_4_.refs_2_.refs_12_, bf16[256,1024]{1,0:T(8,128)(2,1)S(1)} %collective-permute-done.2.refs_0_.refs_3_.refs_13_, ...), custom_call_target="tpu_custom_call" | custom-call | flops 268435456 | bytes 3145728 | tf_op jit(solution)/shard_map/gram/pallas_call | solution.py:154
  110.7 1.6 %reduce_sum.19 = f32[32,128]{1,0:T(8,128)} reduce(f32[16,32,128]{2,1,0:T(8,128)} %all-to-all-done.1, f32[]{:T(128)} %constant.55.clone.1), dimensions={0}, to_apply=%region_1.2 | reduce | flops 61440 | bytes 278532 | tf_op jit(solution)/shard_map/reduce_sum | solution.py:247
  113.0 8.9 %all_to_all.15 = f32[4,32,128]{2,1,0:T(8,128)} all-to-all(f32[4,32,128]{2,1,0:T(8,128)S(1)} %broadcast_in_dim.8), channel_id=1, replica_groups=mesh['yh'=2,'z'=8,'x'=4,'yl'=2,'core'=2] {'x'}, dimensions={0} | all-to-all | bytes 131072 | tf_op jit(solution)/shard_map/all_to_all | solution.py:248
  121.9 1.6 %reshape.64 = f32[4,32,2,64]{3,2,1,0:T(2,128)} reshape(f32[4,32,128]{2,1,0:T(8,128)} %all_to_all.15) | data formatting | bytes 131072 | tf_op jit(solution)/shard_map/reshape | solution.py:249
  123.5 1.7 %copy.7 = f32[2,32,4,64]{3,2,1,0:T(4,128)} copy(f32[2,32,4,64]{3,0,1,2:T(2,128)} %bitcast.35) | data formatting | bytes 131072 | tf_op jit(solution)/shard_map/transpose | solution.py:249
  125.2 1.7 %reshape.65 = f32[64,256]{1,0:T(8,128)} reshape(f32[2,32,4,64]{3,2,1,0:T(4,128)} %copy.7) | data formatting | bytes 131072 | tf_op jit(solution)/shard_map/reshape | solution.py:249
  126.8 1.0 copy-done.4
  127.9 1.0 copy-done.8
  128.9 1.0 copy-done.13
  130.0 1.0 copy-done.17
  132.9 2.4 %gram.11.high = f32[256,512]{1,0:T(8,128)S(1)} custom-call(s32[5]{0:T(128)S(1)} %stack.23.at, bf16[256,1024]{1,0:T(8,128)(2,1)S(1)} %copy-done.4, bf16[256,1024]{1,0:T(8,128)(2,1)S(1)} %copy-done.13, bf16[256,1024]{1,0:T(8,128)(2,1)} %collective-permute-done.1.refs_4_.refs_2_.refs_12_, bf16[256,1024]{1,0:T(8,128)(2,1)S(1)} %collective-permute-done.2.refs_0_.refs_3_.refs_13_, ...), custom_call_target="tpu_custom_call" | custom-call | flops 268435456 | bytes 3145728 | tf_op jit(solution)/shard_map/gram/pallas_call | solution.py:154
  135.3 2.4 %gram.9.low = f32[256,512]{1,0:T(8,128)S(1)} custom-call(s32[5]{0:T(128)S(1)} %stack.23.at, bf16[256,1024]{1,0:T(8,128)(2,1)S(1)} %copy-done.4, bf16[256,1024]{1,0:T(8,128)(2,1)S(1)} %copy-done.13, bf16[256,1024]{1,0:T(8,128)(2,1)} %collective-permute-done.1.refs_4_.refs_2_.refs_12_, bf16[256,1024]{1,0:T(8,128)(2,1)S(1)} %collective-permute-done.2.refs_0_.refs_3_.refs_13_, ...), custom_call_target="tpu_custom_call" | custom-call | flops 268435456 | bytes 3145728 | tf_op jit(solution)/shard_map/gram/pallas_call | solution.py:154
  137.8 2.1 %finish.1 = f32[256,1024]{1,0:T(8,128)} custom-call(f32[256,512]{1,0:T(8,128)S(1)} %gram.9.low, f32[256,512]{1,0:T(8,128)S(1)} %gram.11.high, f32[256,512]{1,0:T(8,128)} %collective-permute-done.14.low_got, f32[256,512]{1,0:T(8,128)} %collective-permute-done.16.high_got), custom_call_target="tpu_custom_call" | custom-call | flops 524288 | bytes 3145728 | tf_op jit(solution)/shard_map/finish/pallas_call | solution.py:176
  (81 shorter events, 12.6 us)
Async XLA Ops:
  0.6 36.7 %copy-start = (bf16[256,1,4096]{2,0,1:T(8,128)(2,1)S(1)}, bf16[256,1,4096]{2,0,1:T(8,128)(2,1)}, u32[]{:S(2)}) copy-start(bf16[256,1,4096]{2,0,1:T(8,128)(2,1)} %param.7) | copy-start | bytes 6291460
  0.7 1.7 %copy-start.24 = (bf16[256,1,4096]{2,0,1:T(8,128)(2,1)S(1)}, bf16[256,1,4096]{2,0,1:T(8,128)(2,1)}, u32[]{:S(2)}) copy-start(bf16[256,1,4096]{2,0,1:T(8,128)(2,1)} %param.5) | copy-start | bytes 6291460
  2.5 0.8 copy-start.25
  3.2 34.1 %copy-start.26 = (s32[256,1,32]{0,2,1:T(8,128)S(1)}, s32[256,1,32]{0,2,1:T(8,128)}, u32[]{:S(2)}) copy-start(s32[256,1,32]{0,2,1:T(8,128)} %param.6) | copy-start | bytes 98308
  5.9 13.0 %collective-permute-start = (bf16[256,1024]{1,0:T(8,128)(2,1)S(1)}, bf16[256,1024]{1,0:T(8,128)(2,1)S(1)}, u32[]{:S(2)}, u32[]{:S(2)}) collective-permute-start(bf16[256,1024]{1,0:T(8,128)(2,1)S(1)} %get-tuple-element.5.refs_0_.refs_10_), channel_id=1, source_target_pairs={{0,16},{16,32},{32,48},{48,64},{64,80},{80,96},{96,112},{112,0},{1... | collective-permute-start | bytes 1572872 | tf_op jit(solution)/shard_map/ppermute | solution.py:203
  7.8 0.8 copy-start.1
  8.6 15.9 %collective-permute-start.4 = (bf16[256,1024]{1,0:T(8,128)(2,1)S(1)}, bf16[256,1024]{1,0:T(8,128)(2,1)S(1)}, u32[]{:S(2)}, u32[]{:S(2)}) collective-permute-start(bf16[256,1024]{1,0:T(8,128)(2,1)S(1)} %get-tuple-element.6.refs_1_.refs_5_.refs_10_), channel_id=1, source_target_pairs={{0,16},{16,32},{32,48},{48,64},{64,80},{80,96},{96,112},{112,0},{1... | collective-permute-start | bytes 1572872 | tf_op jit(solution)/shard_map/ppermute | solution.py:204
  10.5 0.8 copy-start.5
  18.9 12.0 %collective-permute-start.1 = (bf16[256,1024]{1,0:T(8,128)(2,1)S(1)}, bf16[256,1024]{1,0:T(8,128)(2,1)}, u32[]{:S(2)}, u32[]{:S(2)}) collective-permute-start(bf16[256,1024]{1,0:T(8,128)(2,1)S(1)} %collective-permute-done.refs_2_.refs_1_.refs_11_), channel_id=1, source_target_pairs={{0,16},{16,32},{32,48},{48,64},{64,80},{80,96},{96,112},{112,0},{1... | collective-permute-start | bytes 1572872 | tf_op jit(solution)/shard_map/ppermute | solution.py:203
  18.9 0.8 copy-start.9
  24.5 12.7 %collective-permute-start.5 = (bf16[256,1024]{1,0:T(8,128)(2,1)S(1)}, bf16[256,1024]{1,0:T(8,128)(2,1)}, u32[]{:S(2)}, u32[]{:S(2)}) collective-permute-start(bf16[256,1024]{1,0:T(8,128)(2,1)S(1)} %collective-permute-done.4.refs_3_.refs_6_.refs_11_), channel_id=1, source_target_pairs={{0,16},{16,32},{32,48},{48,64},{64,80},{80,96},{96,112},{112,0},{1... | collective-permute-start | bytes 1572872 | tf_op jit(solution)/shard_map/ppermute | solution.py:204
  24.5 0.8 copy-start.14
  25.3 33.3 %collective-permute-start.10 = (bf16[128,256]{1,0:T(8,128)(2,1)}, bf16[128,256]{1,0:T(8,128)(2,1)}, u32[]{:S(2)}, u32[]{:S(2)}) collective-permute-start(bf16[128,256]{1,0:T(8,128)(2,1)} %get-tuple-element.7), channel_id=1, source_target_pairs={{0,64},{16,80},{32,96},{48,112},{64,0},{80,16},{96,32},{112,48},{1... | collective-permute-start | bytes 196616 | tf_op jit(solution)/shard_map/ppermute | solution.py:195
  31.0 23.2 %collective-permute-start.2 = (bf16[256,1024]{1,0:T(8,128)(2,1)}, bf16[256,1024]{1,0:T(8,128)(2,1)S(1)}, u32[]{:S(2)}, u32[]{:S(2)}) collective-permute-start(bf16[256,1024]{1,0:T(8,128)(2,1)} %collective-permute-done.1.refs_4_.refs_2_.refs_12_), channel_id=1, source_target_pairs={{0,16},{16,32},{32,48},{48,64},{64,80},{80,96},{96,112},{112,0},{1... | collective-permute-start | bytes 1572872 | tf_op jit(solution)/shard_map/ppermute | solution.py:203
  37.3 16.1 %collective-permute-start.6 = (bf16[256,1024]{1,0:T(8,128)(2,1)}, bf16[256,1024]{1,0:T(8,128)(2,1)S(1)}, u32[]{:S(2)}, u32[]{:S(2)}) collective-permute-start(bf16[256,1024]{1,0:T(8,128)(2,1)} %collective-permute-done.5.refs_5_.refs_7_.refs_12_), channel_id=1, source_target_pairs={{0,16},{16,32},{32,48},{48,64},{64,80},{80,96},{96,112},{112,0},{1... | collective-permute-start | bytes 1572872 | tf_op jit(solution)/shard_map/ppermute | solution.py:204
  41.1 34.2 %all-to-all-start = ((f32[4,64,256]{2,1,0:T(8,128)}), f32[4,64,256]{2,1,0:T(8,128)}, u32[]{:S(2)}, u32[]{:S(2)}) async-start(f32[4,64,256]{2,1,0:T(8,128)} %bitcast.11), calls=%async_computation | async-start | bytes 524288 | tf_op jit(solution)/shard_map/all_to_all | solution.py:231
  46.0 1.0 copy-start.2
  47.1 1.0 copy-start.6
  48.1 1.0 copy-start.10
  49.2 1.0 copy-start.15
  50.2 8.4 %copy-start.28 = (s32[256]{0:T(256)S(1)}, s32[256]{0:T(256)}, u32[]{:S(2)}) copy-start(s32[256]{0:T(256)} %param.8) | copy-start | bytes 3076
  50.2 14.4 %copy-start.11 = (bf16[256,1024]{1,0:T(8,128)(2,1)S(1)}, bf16[256,1024]{1,0:T(8,128)(2,1)}, u32[]{:S(2)}) copy-start(bf16[256,1024]{1,0:T(8,128)(2,1)} %copy-done.9) | copy-start | bytes 1572868
  51.7 9.1 %collective-permute-start.8 = (bf16[640,256]{1,0:T(8,128)(2,1)S(1)}, bf16[640,256]{1,0:T(8,128)(2,1)S(1)}, u32[]{:S(2)}, u32[]{:S(2)}) collective-permute-start(bf16[640,256]{1,0:T(8,128)(2,1)S(1)} %pick.2), channel_id=1, source_target_pairs={{0,2},{2,0},{1,3},{3,1},{4,6},{6,4},{5,7},{7,5},{8,10},{10,8},{9,1... | collective-permute-start | bytes 983048 | tf_op jit(solution)/shard_map/ppermute | solution.py:206
  53.4 11.2 %collective-permute-start.7 = (bf16[128,1024]{1,0:T(8,128)(2,1)S(1)}, bf16[128,1024]{1,0:T(8,128)(2,1)S(1)}, u32[]{:S(2)}, u32[]{:S(2)}) collective-permute-start(bf16[128,1024]{1,0:T(8,128)(2,1)S(1)} %constant_dynamic-slice_fusion), channel_id=1, source_target_pairs={{0,16},{16,32},{32,48},{48,64},{64,80},{80,96},{96,112},{112,0},{1... | collective-permute-start | bytes 786440 | tf_op jit(solution)/shard_map/ppermute | solution.py:204
  54.2 10.4 %collective-permute-start.3 = (bf16[128,1024]{1,0:T(8,128)(2,1)S(1)}, bf16[128,1024]{1,0:T(8,128)(2,1)S(1)}, u32[]{:S(2)}, u32[]{:S(2)}) collective-permute-start(bf16[128,1024]{1,0:T(8,128)(2,1)S(1)} %constant_dynamic-slice_fusion.1), channel_id=1, source_target_pairs={{0,16},{16,32},{32,48},{48,64},{64,80},{80,96},{96,112},{112,0},{1... | collective-permute-start | bytes 786440 | tf_op jit(solution)/shard_map/ppermute | solution.py:203
  58.1 6.5 %collective-permute-start.9 = (bf16[256,256]{1,0:T(8,128)(2,1)S(1)}, bf16[256,256]{1,0:T(8,128)(2,1)S(1)}, u32[]{:S(2)}, u32[]{:S(2)}) collective-permute-start(bf16[256,256]{1,0:T(8,128)(2,1)S(1)} %pick.3), channel_id=1, source_target_pairs={{0,2},{2,0},{1,3},{3,1},{4,6},{6,4},{5,7},{7,5},{8,10},{10,8},{9,1... | collective-permute-start | bytes 393224 | tf_op jit(solution)/shard_map/ppermute | solution.py:207
  60.8 7.2 %copy-start.21 = (bf16[640,256]{1,0:T(8,128)(2,1)}, bf16[640,256]{1,0:T(8,128)(2,1)S(1)}, u32[]{:S(2)}) copy-start(bf16[640,256]{1,0:T(8,128)(2,1)S(1)} %collective-permute-done.8.refs_15_) | copy-start | bytes 983044
  64.6 3.5 %copy-start.18 = (bf16[128,1024]{1,0:T(8,128)(2,1)}, bf16[128,1024]{1,0:T(8,128)(2,1)S(1)}, u32[]{:S(2)}) copy-start(bf16[128,1024]{1,0:T(8,128)(2,1)S(1)} %collective-permute-done.3.refs_4_.refs_14_) | copy-start | bytes 786436
  67.6 4.1 %copy-start.27 = (s32[1024]{0:T(1024)S(1)}, s32[1024]{0:T(1024)}, u32[]{:S(2)}) copy-start(s32[1024]{0:T(1024)} %param.9) | copy-start | bytes 12292
  67.6 33.2 %collective-permute-start.15 = (f32[256,512]{1,0:T(8,128)}, f32[256,512]{1,0:T(8,128)}, u32[]{:S(2)}, u32[]{:S(2)}) collective-permute-start(f32[256,512]{1,0:T(8,128)} %gram.14), channel_id=1, source_target_pairs={{0,1},{1,0},{2,3},{3,2},{4,5},{5,4},{6,7},{7,6},{8,9},{9,8},{10,11... | collective-permute-start | bytes 1572872 | tf_op jit(solution)/shard_map/ppermute | solution.py:210
  71.1 36.3 %collective-permute-start.13 = (f32[256,512]{1,0:T(8,128)}, f32[256,512]{1,0:T(8,128)}, u32[]{:S(2)}, u32[]{:S(2)}) collective-permute-start(f32[256,512]{1,0:T(8,128)} %gram.12), channel_id=1, source_target_pairs={{0,1},{1,0},{2,3},{3,2},{4,5},{5,4},{6,7},{7,6},{8,9},{9,8},{10,11... | collective-permute-start | bytes 1572872 | tf_op jit(solution)/shard_map/ppermute | solution.py:210
  79.2 31.5 %all-to-all-start.1 = ((f32[16,32,128]{2,1,0:T(8,128)}), f32[16,32,128]{2,1,0:T(8,128)}, u32[]{:S(2)}, u32[]{:S(2)}) async-start(f32[16,32,128]{2,1,0:T(8,128)} %bitcast.36), calls=%async_computation.1 | async-start | bytes 524288 | tf_op jit(solution)/shard_map/all_to_all | solution.py:247
  88.2 1.0 copy-start.3
  89.3 1.0 copy-start.7
  90.3 1.0 copy-start.12
  91.4 1.0 copy-start.16
  92.4 0.9 copy-start.19
  93.3 1.0 copy-start.22
  97.3 29.5 %collective-permute-start.12 = (f32[256,512]{1,0:T(8,128)}, f32[256,512]{1,0:T(8,128)}, u32[]{:S(2)}, u32[]{:S(2)}) collective-permute-start(f32[256,512]{1,0:T(8,128)} %gram.10), channel_id=1, source_target_pairs={{0,1},{1,0},{2,3},{3,2},{4,5},{5,4},{6,7},{7,6},{8,9},{9,8},{10,11... | collective-permute-start | bytes 1572872 | tf_op jit(solution)/shard_map/ppermute | solution.py:212
  100.3 35.0 %collective-permute-start.11 = (f32[256,512]{1,0:T(8,128)}, f32[256,512]{1,0:T(8,128)}, u32[]{:S(2)}, u32[]{:S(2)}) collective-permute-start(f32[256,512]{1,0:T(8,128)} %gram.8), channel_id=1, source_target_pairs={{0,1},{1,0},{2,3},{3,2},{4,5},{5,4},{6,7},{7,6},{8,9},{9,8},{10,11... | collective-permute-start | bytes 1572872 | tf_op jit(solution)/shard_map/ppermute | solution.py:212
  104.0 33.8 %collective-permute-start.16 = (f32[256,512]{1,0:T(8,128)}, f32[256,512]{1,0:T(8,128)}, u32[]{:S(2)}, u32[]{:S(2)}) collective-permute-start(f32[256,512]{1,0:T(8,128)} %gram.15), channel_id=1, source_target_pairs={{0,128},{128,0},{1,129},{129,1},{2,130},{130,2},{3,131},{131,3},{4... | collective-permute-start | bytes 1572872 | tf_op jit(solution)/shard_map/ppermute | solution.py:211
  110.6 27.2 %collective-permute-start.14 = (f32[256,512]{1,0:T(8,128)}, f32[256,512]{1,0:T(8,128)}, u32[]{:S(2)}, u32[]{:S(2)}) collective-permute-start(f32[256,512]{1,0:T(8,128)} %gram.13), channel_id=1, source_target_pairs={{0,128},{128,0},{1,129},{129,1},{2,130},{130,2},{3,131},{131,3},{4... | collective-permute-start | bytes 1572872 | tf_op jit(solution)/shard_map/ppermute | solution.py:211
  126.8 1.0 copy-start.4
  127.9 1.0 copy-start.8
  128.9 1.0 copy-start.13
  130.0 1.0 copy-start.17
  131.0 0.9 copy-start.20
  131.9 1.0 copy-start.23

commit v3 on v2

v3 whole, which is shorter than its diff:
```python
import functools

import jax
import jax.numpy as jnp
from jax import lax
from jax.experimental import pallas as pl
from jax.experimental.pallas import tpu as pltpu
from jax.sharding import Mesh, PartitionSpec as P

YH, Z, X, YL, CORE = 2, 8, 4, 2, 2
ROW_AXES = ("yh", "z")
COL_AXES = ("yl", "core")
SWAP = [(0, 1), (1, 0)]
RING = [(2 * i, 2 * ((i + 1) % Z)) for i in range(Z)] + [(2 * i + 1, 2 * ((i - 1) % Z) + 1) for i in range(Z)]
TURNED = (((0,), (0,)), ((), ()))


def powers(exponents):
    return jnp.exp2(exponents.astype(jnp.float32)).astype(jnp.bfloat16)


def params(mebibytes):
    return pltpu.CompilerParams(vmem_limit_bytes=mebibytes << 20)


def cost(flops, moved):
    return pl.CostEstimate(flops=flops, bytes_accessed=moved, transcendentals=0)


AT_Z, AT_CORE, AT_YL, AT_FAR, AT_YH, AT_X = 0, 1, 2, 3, 4, 5


def wide_scale(turned, first_block, columns):
    blocks = turned.shape[0]
    lane_block = lax.broadcasted_iota(jnp.int32, (blocks, columns), 1) // 128 + first_block
    pick = (lane_block == lax.broadcasted_iota(jnp.int32, (blocks, columns), 0)).astype(jnp.bfloat16)
    return lax.dot_general(turned, pick, TURNED, preferred_element_type=jnp.float32)


def dequant_kernel(at, exps, values, far_values, low, high, far):
    step = pl.program_id(0)
    turned = powers(exps[...])
    grads = values[...].astype(jnp.float32) * wide_scale(turned, at[AT_YL] * 16 + step * 4, 512)
    grads = grads.astype(jnp.bfloat16)
    low[...] = jnp.concatenate([grads[:, 0:128], grads[:, 256:384]], 1)
    high[...] = jnp.concatenate([grads[:, 128:256], grads[:, 384:512]], 1)

    @pl.when(step == 0)
    def _():
        half = far.shape[0]
        scale = wide_scale(turned, at[AT_FAR] * 2, 256)
        scale = jnp.where(at[AT_CORE] == 0, scale[:half], scale[half:])
        far[...] = (far_values[...].astype(jnp.float32) * scale).astype(jnp.bfloat16)


def dequant(at, exps, mantissas):
    rows, width = mantissas.shape
    side = jax.ShapeDtypeStruct((rows, width // 4), jnp.bfloat16)
    return pl.pallas_call(
        dequant_kernel,
        grid_spec=pltpu.PrefetchScalarGridSpec(
            num_scalar_prefetch=1,
            grid=(4,),
            in_specs=[
                pl.BlockSpec(exps.shape, lambda g, at: (0, 0)),
                pl.BlockSpec((rows, 512), lambda g, at: (0, at[AT_YL] * 4 + g)),
                pl.BlockSpec((rows // 2, 256), lambda g, at: (at[AT_CORE], at[AT_FAR])),
            ],
            out_specs=[
                pl.BlockSpec((rows, 256), lambda g, at: (0, g)),
                pl.BlockSpec((rows, 256), lambda g, at: (0, g)),
                pl.BlockSpec((rows // 2, 256), lambda g, at: (0, 0)),
            ],
        ),
        out_shape=[side, side, jax.ShapeDtypeStruct((rows // 2, 256), jnp.bfloat16)],
        compiler_params=params(58),
        cost_estimate=cost(1 << 25, 2 << 20),
        name="dequant",
    )(at, exps, mantissas, mantissas)


def pick_kernel(count, at, *refs):
    sides, out = refs[:-1], refs[-1]
    row = 0
    for i in range(count):
        rows = sides[2 * i].shape[0]
        out[row : row + rows] = jnp.concatenate([sides[2 * i][...], sides[2 * i + 1][...]], 1)
        row += rows


def lanes_at_z(rows, by_core):
    if by_core:
        return pl.BlockSpec((rows, 128), lambda g, at: (at[AT_CORE], at[AT_Z]))
    return pl.BlockSpec((rows, 128), lambda g, at: (0, at[AT_Z]))


def pick(at, pieces):
    rows = sum(n for n, _, _, _ in pieces)
    specs = [lanes_at_z(n, by_core) for n, by_core, _, _ in pieces for _ in range(2)]
    return pl.pallas_call(
        functools.partial(pick_kernel, len(pieces)),
        grid_spec=pltpu.PrefetchScalarGridSpec(
            num_scalar_prefetch=1, grid=(1,), in_specs=specs,
            out_specs=pl.BlockSpec((rows, 256), lambda g, at: (0, 0)),
        ),
        out_shape=jax.ShapeDtypeStruct((rows, 256), jnp.bfloat16),
        compiler_params=params(6),
        cost_estimate=cost(0, rows * 1024),
        name="pick",
    )(at, *[side for _, _, low, high in pieces for side in (low, high)])


def gram_kernel(sizes, kept, at, *refs):
    count = len(sizes)
    lows, highs = refs[:count], refs[count : 2 * count]
    low_rights, high_rights = refs[2 * count : 3 * count], refs[3 * count : 4 * count]
    near, third, far = refs[4 * count : 4 * count + 3]
    low_other, high_other, low_own, high_own = refs[4 * count + 3 : 4 * count + 7]
    left = refs[-1]
    step = pl.program_id(0)

    @pl.when(step == 0)
    def _():
        mine_first = at[AT_YL] == at[AT_YH]
        use_mine = mine_first if kept else jnp.logical_not(mine_first)
        row, start = 0, 0
        for i, rows in enumerate(sizes):
            mine = jnp.concatenate([lows[i][...], highs[i][...]], 1)
            if i < count - 2:
                theirs = near[row : row + rows]
                row += rows
            else:
                theirs = third[...] if i == count - 2 else far[...]
            left[start : start + rows] = jnp.where(use_mine, mine, theirs)
            start += rows

    def terms(rights):
        total, start = None, 0
        for i, rows in enumerate(sizes):
            term = lax.dot_general(
                left[start : start + rows], rights[i][...], TURNED, preferred_element_type=jnp.float32
            )
            total = term if total is None else total + term
            start += rows
        return total

    @pl.when(step == 0)
    def _():
        low_other[...] = terms(low_rights)
        high_other[...] = terms(high_rights)

    @pl.when(step == 1)
    def _():
        low_own[...] = terms(low_rights)
        high_own[...] = terms(high_rights)


def gram(at, pieces, received, kept):
    sizes = tuple(n for n, _, _, _ in pieces)
    specs = [lanes_at_z(n, by_core) for n, by_core, _, _ in pieces] * 2
    for n, by_core, _, _ in pieces:
        specs.append(
            pl.BlockSpec(
                (n, 512),
                lambda g, at, by_core=by_core: (
                    at[AT_CORE] if by_core else 0,
                    (1 - g) * (1 - at[AT_CORE]) + g * at[AT_CORE],
                ),
            )
        )
    specs += specs[-len(pieces) :]
    specs += [pl.BlockSpec(r.shape, lambda g, at: (0, 0)) for r in received]
    sides = [p[2] for p in pieces], [p[3] for p in pieces]
    return pl.pallas_call(
        functools.partial(gram_kernel, sizes, kept),
        grid_spec=pltpu.PrefetchScalarGridSpec(
            num_scalar_prefetch=1, grid=(2,), in_specs=specs,
            out_specs=[pl.BlockSpec((256, 512), lambda g, at: (0, 0))] * 4,
            scratch_shapes=[pltpu.VMEM((sum(sizes), 256), jnp.bfloat16)],
        ),
        out_shape=[jax.ShapeDtypeStruct((256, 512), jnp.float32)] * 4,
        compiler_params=params(20),
        cost_estimate=cost(2 * sum(sizes) * 256 * 2048, 7 << 20),
        name="gram",
    )(at, *sides[0], *sides[1], *sides[0], *sides[1], *received)


def add_kernel(left, right, out):
    out[...] = left[...] + right[...]


def add(left, right):
    rows, columns = left.shape
    spec = pl.BlockSpec((rows // 2, columns), lambda g: (g, 0))
    return pl.pallas_call(
        add_kernel,
        grid=(2,),
        in_specs=[spec, spec],
        out_specs=spec,
        out_shape=jax.ShapeDtypeStruct(left.shape, left.dtype),
        compiler_params=params(6),
        cost_estimate=cost(1 << 18, 3 << 19),
        name="add",
    )(left, right)


def finish_kernel(factor, low, high, low_core, high_core, low_got, high_got, out):
    for i in range(4):
        lanes = slice(i * 128, i * 128 + 128)
        first = (low[:, lanes] + low_core[:, lanes]) + low_got[:, lanes]
        second = (high[:, lanes] + high_core[:, lanes]) + high_got[:, lanes]
        out[:, i * 256 : i * 256 + 128] = first * factor
        out[:, i * 256 + 128 : i * 256 + 256] = second * factor


def finish(factor, terms):
    rows, columns = terms[0].shape
    return pl.pallas_call(
        functools.partial(finish_kernel, factor),
        grid=(4,),
        in_specs=[pl.BlockSpec((rows // 4, columns), lambda g: (g, 0))] * 6,
        out_specs=pl.BlockSpec((rows // 4, 2 * columns), lambda g: (g, 0)),
        out_shape=jax.ShapeDtypeStruct((rows, 2 * columns), jnp.float32),
        compiler_params=params(8),
        cost_estimate=cost(1 << 20, 4 << 20),
        name="finish",
    )(*terms)


def tie_kernel(*refs):
    del refs


def tie(value, *earlier):
    return pl.pallas_call(
        tie_kernel,
        in_specs=[pl.BlockSpec(memory_space=pl.ANY)] * (1 + len(earlier)),
        out_specs=pl.BlockSpec(memory_space=pl.ANY),
        out_shape=jax.ShapeDtypeStruct(value.shape, value.dtype),
        input_output_aliases={0: 0},
        compiler_params=params(1),
        cost_estimate=cost(0, 0),
        name="tie",
    )(value, *earlier)


def fisher_block(at, mantissas, exps, total_rows, stages):
    core = lax.axis_index("core")
    rows = mantissas.shape[0]
    low, high, far = dequant(at, exps, mantissas)

    half = rows // 2
    pieces = [(half, True, low, high)]
    for step in range(1, Z // 2 + 1):
        if step == Z // 2:
            low = lax.dynamic_slice_in_dim(low, core * half, half, 0)
            high = lax.dynamic_slice_in_dim(high, core * half, half, 0)
        low = lax.ppermute(low, ("z", "core"), RING)
        high = lax.ppermute(high, ("z", "core"), RING)
        if step == 1:
            far = lax.ppermute(far, "z", [(i, (i + Z // 2) % Z) for i in range(Z)])
        if step < Z // 2:
            low = tie(low, stages[step - 1])
        pieces.append((low.shape[0], False, low, high))
    near = lax.ppermute(pick(at, pieces[:3]), "yl", SWAP)
    third = lax.ppermute(pick(at, pieces[3:4]), "yl", SWAP)
    received = (near, third, far)

    *given_other, low_given, high_given = gram(at, pieces, received, False)
    swapped = [lax.ppermute(g, "core", SWAP) for g in given_other]
    given = [lax.ppermute(add(g, s), "yh", SWAP) for g, s in zip((low_given, high_given), swapped)]
    *kept_other, low_kept, high_kept = gram(at, pieces, received, True)
    kept = [lax.ppermute(k, "core", SWAP) for k in kept_other]
    return finish(1.0 / total_rows, [low_kept, high_kept, *kept, *given])


def spread(scale):
    blocks = scale.shape[1]
    lane_block = jnp.arange(blocks * 128, dtype=jnp.int32) // 128
    pick = (lane_block[None, :] == jnp.arange(blocks, dtype=jnp.int32)[:, None]).astype(jnp.bfloat16)
    wide = lax.dot_general(scale, pick, (((1,), (0,)), ((), ())), preferred_element_type=jnp.float32)
    return wide.astype(jnp.bfloat16)


def place_kernel(parts, ids, owners, out):
    docs, rows = owners.shape[1], ids.shape[1]
    summed = (parts[0] + parts[1]) + (parts[2] + parts[3])
    owner = jnp.broadcast_to(owners[...], (8, docs))
    digit = jnp.where(lax.broadcasted_iota(jnp.int32, (8, docs), 0) == 0, owner >> 5, owner & 31)
    doc = (lax.broadcasted_iota(jnp.int32, (docs, rows), 0) == ids[...]).astype(jnp.bfloat16)
    digits = lax.dot_general(
        digit.astype(jnp.float32).astype(jnp.bfloat16), doc, (((1,), (0,)), ((), ())),
        preferred_element_type=jnp.float32,
    )
    slots = (digits[0:1] * 32.0 + digits[1:2]).astype(jnp.int32)
    count = out.shape[0]
    own_docs = docs // (YH * Z)
    half = own_docs // 2
    place = lax.broadcasted_iota(jnp.int32, (count, rows), 0)
    place = (place // half) * own_docs + place % half
    member = jnp.concatenate([place == slots, place + half == slots], 1)
    member = jnp.where(member, 1.0, 0.0).astype(jnp.bfloat16)
    zero = jnp.zeros_like(summed)
    rest = jnp.concatenate(
        [jnp.concatenate([summed, zero], 1), jnp.concatenate([zero, summed], 1)], 0
    )
    total = None
    for _ in range(3):
        part = rest.astype(jnp.bfloat16)
        rest = rest - part.astype(jnp.float32)
        term = lax.dot_general(member, part, (((1,), (1,)), ((), ())), preferred_element_type=jnp.float32)
        total = term if total is None else total + term
    out[...] = total


def sum_kernel(parts, out):
    total = parts[0]
    for i in range(1, parts.shape[0]):
        total = total + parts[i]
    out[...] = total


def assemble_kernel(at, *refs):
    parts, out = refs[:-1], refs[-1]
    half, double = parts[0].shape
    share = double // 2
    values = []
    for source in range(X):
        value = parts[0][...]
        for shift in range(1, X):
            value = jnp.where(lax.rem(source + shift, X) == at[AT_X], parts[shift][...], value)
        values.append(value)
    out[0:half] = jnp.concatenate([v[:, :share] for v in values], 1)
    out[half:] = jnp.concatenate([v[:, share:] for v in values], 1)


def score_stages(mantissas, scale, queries, doc_ids, owners):
    docs = owners.shape[0]
    grads = mantissas * spread(scale)
    scores = lax.dot_general(queries, grads, (((1,), (1,)), ((), ())), preferred_element_type=jnp.float32)
    count, rows = scores.shape
    share, half = count // X, docs // (YH * Z) // 2
    parts = lax.all_to_all(scores.reshape(X, share, rows), "x", 0, 0, tiled=True)
    placed = pl.pallas_call(
        place_kernel,
        out_shape=jax.ShapeDtypeStruct((YH * Z * half, 2 * share), jnp.float32),
        compiler_params=params(10),
        cost_estimate=cost(1 << 28, 1 << 20),
        name="place",
    )(parts, doc_ids.reshape(1, rows), owners.reshape(1, docs))
    blocks = lax.all_to_all(placed.reshape(YH * Z, half, 2 * share), ("yh", "z"), 0, 0, tiled=True)
    mine = pl.pallas_call(
        sum_kernel,
        out_shape=jax.ShapeDtypeStruct((half, 2 * share), jnp.float32),
        compiler_params=params(4),
        cost_estimate=cost(1 << 16, 1 << 18),
        name="sum",
    )(blocks)
    return scores, placed, mine


def assemble(at, mine):
    half, double = mine.shape
    parts = [mine] + [lax.ppermute(mine, "x", [(i, (i + s) % X) for i in range(X)]) for s in range(1, X)]
    return pl.pallas_call(
        assemble_kernel,
        grid_spec=pltpu.PrefetchScalarGridSpec(
            num_scalar_prefetch=1, grid=(1,),
            in_specs=[pl.BlockSpec((half, double), lambda g, at: (0, 0))] * X,
            out_specs=pl.BlockSpec((2 * half, X * double // 2), lambda g, at: (0, 0)),
        ),
        out_shape=jax.ShapeDtypeStruct((2 * half, X * double // 2), jnp.float32),
        compiler_params=params(2),
        cost_estimate=cost(0, 1 << 17),
        name="assemble",
    )(at, *parts)


def per_device(mantissas, exponents, queries, doc_ids, owners):
    mantissas = mantissas[:, 0, :]
    exponents = exponents[:, 0, :]
    total_rows = mantissas.shape[0] * YH * Z
    yh, z, x = lax.axis_index("yh"), lax.axis_index("z"), lax.axis_index("x")
    yl, core = lax.axis_index("yl"), lax.axis_index("core")
    far_block = (1 - yl) * Z + lax.rem(z + Z // 2, Z)
    at = jnp.stack([z, core, yl, far_block, yh, x]).astype(jnp.int32)
    stages = score_stages(mantissas, powers(exponents), queries[:, 0, :], doc_ids, owners)
    fisher = fisher_block(at, mantissas, exponents.T, total_rows, stages)
    return fisher[None], assemble(at, stages[-1])


def solution(mesh):
    fine = Mesh(mesh.devices.reshape(YH, Z, X, YL, CORE), ("yh", "z", "x", "yl", "core"))
    in_specs = (
        P(ROW_AXES, "x", None),
        P(ROW_AXES, "x", None),
        P(COL_AXES, "x", None),
        P(ROW_AXES),
        P(),
    )
    out_specs = (P("x", ROW_AXES, COL_AXES), P(ROW_AXES, COL_AXES))
    return jax.shard_map(per_device, mesh=fine, in_specs=in_specs, out_specs=out_specs, check_vma=False)
```

time: 143 us -> 118 us (0.83)
  local copies, waits for them, and re-layouts: 29.9 us -> 4.78 us
  waiting for transfers between devices: 25.8 us -> 43.3 us
  Pallas kernels: 30 us -> 20.3 us
  other arithmetic: 5.39 us -> 0.01 us
  matrix products: 6.07 us -> 3.07 us
  blocking collectives: 8.85 us -> 10.9 us
    unnamed x58 -> x26, local copies, waits for them, and re-layouts: 22 us -> 3.17 us
    ppermute x6 -> x9, waiting for transfers between devices: 0.02 us -> 17.7 us  [the longest x2 8.86 us: fisher_block(): lax.ppermute(add(g, s), 'yh', SWAP)]
    pallas_call x9 -> x11, Pallas kernels: 25.3 us -> 12.6 us  [the longest x2 7.93 us: gram(): pl.pallas_call(functools.partial(gram_kernel, sizes, kept), grid_spec=plt...]
    all_to_all x2 -> x1, waiting for transfers between devices: 0.01 us -> 8.58 us  [score_stages(): lax.all_to_all(placed.reshape(YH * Z, half, 2 * share), ('yh', 'z'), 0, 0...]
    ppermute x4, waiting for transfers between devices: 11.1 us -> 5.72 us  [fisher_block(): high = lax.ppermute(high, ('z', 'core'), RING)]
    all_to_all x2 -> x1, starting transfers between devices: 13.8 us -> 8.59 us  [score_stages(): lax.all_to_all(placed.reshape(YH * Z, half, 2 * share), ('yh', 'z'), 0, 0...]
    ppermute x1, waiting for transfers between devices: 0.01 us -> 5 us  [fisher_block(): far = lax.ppermute(far, 'z', [(i, (i + Z // 2) % Z) for i in range(Z)])]
    ppermute x6 -> x9, starting transfers between devices: 4.55 us -> 9.15 us  [the longest x3 4.26 us: assemble(): lax.ppermute(mine, 'x', [(i, (i + s) % X) for i in range(X)])]
  transfers between devices with their start and end apart: 19 -> 21, of which waited for: 6 -> 8; matrix products, arithmetic and copies ran while one was open for 14% -> 4% of each run, Pallas kernels for 18% -> 9%
where the time goes in v3:
time: 118 us; the launch traced here: 116 us
  waiting for transfers between devices  43.3 us (37%)
  starting transfers between devices  32.6 us (28%)
  Pallas kernels  20.3 us (17%)
  blocking collectives  10.9 us (9%)
  local copies, waits for them, and re-layouts  4.78 us (4%)
  matrix products  3.07 us (3%)
    all_to_all x1, blocking collectives, score_stages(): lax.all_to_all(scores.reshape(X, share, rows), 'x', 0, 0, tiled=True)  10.9 us
    ppermute x2, waiting for transfers between devices, fisher_block(): lax.ppermute(add(g, s), 'yh', SWAP)  8.86 us
    ppermute x3, waiting for transfers between devices, assemble(): lax.ppermute(mine, 'x', [(i, (i + s) % X) for i in range(X)])  8.81 us
    all_to_all x1, starting transfers between devices, score_stages(): lax.all_to_all(placed.reshape(YH * Z, half, 2 * share), ('yh', 'z'), 0, 0...  8.59 us
    all_to_all x1, waiting for transfers between devices, score_stages(): lax.all_to_all(placed.reshape(YH * Z, half, 2 * share), ('yh', 'z'), 0, 0...  8.58 us
    pallas_call x2, Pallas kernels, gram(): pl.pallas_call(functools.partial(gram_kernel, sizes, kept), grid_spec=plt...  7.93 us
    ppermute x4, waiting for transfers between devices, fisher_block(): low = lax.ppermute(low, ('z', 'core'), RING)  6.29 us
    ppermute x4, waiting for transfers between devices, fisher_block(): high = lax.ppermute(high, ('z', 'core'), RING)  5.72 us
  transfers between devices with their start and end apart: 21, of which 8 were waited for; matrix products, arithmetic and copies ran while one was open for 4% of the time, Pallas kernels for 9%

profile of v3, /device:TPU:2, one launch (start us, length us, event | category | flops | bytes accessed | tf_op | source)
XLA Modules:
  0.0 115.8 jit_solution(4339428244178044846)
XLA Ops:
  0.6 0.0 copy-start
  0.7 0.6 stack.27.at
  1.3 4.8 %dequant.1 = (bf16[256,1024]{1,0:T(8,128)(2,1)}, bf16[256,1024]{1,0:T(8,128)(2,1)}, bf16[128,256]{1,0:T(8,128)(2,1)}) custom-call(s32[6]{0:T(128)} %stack.27.at, s32[32,256]{1,0:T(8,128)} %bitcast.40, bf16[256,4096]{1,0:T(8,128)(2,1)} %bitcast.37, bf16[256,4096]{1,0:T(8,128)(2,1)} %bitcast.38), custom_call_target="tpu_custom_call" | custom-call | flops 33554432 | bytes 2097152 | tf_op jit(solution)/shard_map/dequant/pallas_call | solution.py:59
  6.1 2.0 %collective-permute-start = (bf16[256,1024]{1,0:T(8,128)(2,1)}, bf16[256,1024]{1,0:T(8,128)(2,1)S(1)}, u32[]{:S(2)}, u32[]{:S(2)}) collective-permute-start(bf16[256,1024]{1,0:T(8,128)(2,1)} %get-tuple-element.13.refs_0_.refs_10_), channel_id=1, source_target_pairs={{0,16},{16,32},{32,48},{48,64},{64,80},{80,96},{96,112},{112,0},{1... | collective-permute-start | bytes 1572872 | tf_op jit(solution)/shard_map/ppermute | solution.py:258
  8.1 1.9 %collective-permute-start.4 = (bf16[256,1024]{1,0:T(8,128)(2,1)}, bf16[256,1024]{1,0:T(8,128)(2,1)}, u32[]{:S(2)}, u32[]{:S(2)}) collective-permute-start(bf16[256,1024]{1,0:T(8,128)(2,1)} %get-tuple-element.14.refs_1_.refs_5_.refs_15_), channel_id=1, source_target_pairs={{0,16},{16,32},{32,48},{48,64},{64,80},{80,96},{96,112},{112,0},{1... | collective-permute-start | bytes 1572872 | tf_op jit(solution)/shard_map/ppermute | solution.py:259
  10.0 0.0 copy-start.9
  10.1 0.0 copy-start.10
  10.1 3.1 %fusion.1 = f32[256,256]{0,1:T(8,128)S(1)} fusion(bf16[256,1,4096]{2,0,1:T(8,128)(2,1)S(1)} %copy-done, s32[4096]{0:T(1024)S(1)} %add_select_fusion, s32[256,1,32]{0,2,1:T(8,128)S(1)} %copy-done.11, bf16[256,1,4096]{2,0,1:T(8,128)(2,1)} %param.5), kind=kOutput, calls=%fused_computation.2 | convolution fusion | flops 606232576 | bytes 4505600 | tf_op jit(solution)/shard_map/dot_general | solution.py:340
  13.1 6.3 %collective-permute-done.refs_0_ = bf16[256,1024]{1,0:T(8,128)(2,1)S(1)} collective-permute-done((bf16[256,1024]{1,0:T(8,128)(2,1)}, bf16[256,1024]{1,0:T(8,128)(2,1)S(1)}, u32[]{:S(2)}, u32[]{:S(2)}) %collective-permute-start) | collective-permute-done | bytes 524320 | tf_op jit(solution)/shard_map/ppermute | solution.py:258
  19.4 5.7 %collective-permute-done.4.refs_3_.refs_6_.refs_16_ = bf16[256,1024]{1,0:T(8,128)(2,1)} collective-permute-done((bf16[256,1024]{1,0:T(8,128)(2,1)}, bf16[256,1024]{1,0:T(8,128)(2,1)}, u32[]{:S(2)}, u32[]{:S(2)}) %collective-permute-start.4) | collective-permute-done | bytes 524320 | tf_op jit(solution)/shard_map/ppermute | solution.py:259
  25.2 10.9 %all_to_all.10.parts = f32[4,64,256]{2,1,0:T(8,128)S(1)} all-to-all(f32[4,64,256]{2,1,0:T(8,128)S(1)} %bitcast.34), channel_id=1, replica_groups=mesh['yh'=2,'z'=8,'x'=4,'yl'=2,'core'=2] {'x'}, dimensions={0} | all-to-all | bytes 524288 | tf_op jit(solution)/shard_map/all_to_all | solution.py:343
  36.1 1.6 %place.1.refs_1_ = f32[512,128]{1,0:T(8,128)} custom-call(f32[4,64,256]{2,1,0:T(8,128)S(1)} %all_to_all.10.parts, s32[1,256]{1,0:T(1,128)S(1)} %bitcast.36, s32[1,1024]{1,0:T(1,128)S(1)} %bitcast.35), custom_call_target="tpu_custom_call" | custom-call | flops 268435456 | bytes 1048576 | tf_op jit(solution)/shard_map/place/pallas_call | solution.py:344
  37.7 8.6 %all-to-all-start.1 = ((f32[16,32,128]{2,1,0:T(8,128)}), f32[16,32,128]{2,1,0:T(8,128)S(1)}, u32[]{:S(2)}, u32[]{:S(2)}) async-start(f32[16,32,128]{2,1,0:T(8,128)} %bitcast.14), calls=%async_computation.1 | async-start | bytes 524288 | tf_op jit(solution)/shard_map/all_to_all | solution.py:351
  46.3 2.0 %collective-permute-start.6 = (bf16[256,1024]{1,0:T(8,128)(2,1)}, bf16[256,1024]{1,0:T(8,128)(2,1)}, u32[]{:S(2)}, u32[]{:S(2)}) collective-permute-start(bf16[256,1024]{1,0:T(8,128)(2,1)} %collective-permute-done.5.refs_5_.refs_7_.refs_17_), channel_id=1, source_target_pairs={{0,16},{16,32},{32,48},{48,64},{64,80},{80,96},{96,112},{112,0},{1... | collective-permute-start | bytes 1572872 | tf_op jit(solution)/shard_map/ppermute | solution.py:259
  48.3 8.6 %all-to-all-done.1.parts = f32[16,32,128]{2,1,0:T(8,128)S(1)} async-done(((f32[16,32,128]{2,1,0:T(8,128)}), f32[16,32,128]{2,1,0:T(8,128)S(1)}, u32[]{:S(2)}, u32[]{:S(2)}) %all-to-all-start.1) | async-done | bytes 262176 | tf_op jit(solution)/shard_map/all_to_all | solution.py:351
  56.9 1.0 copy-done.2
  58.0 1.0 copy-done.4
  59.0 1.0 copy-done.6
  60.1 1.5 %pick.2 = bf16[640,256]{1,0:T(8,128)(2,1)S(1)} custom-call(s32[6]{0:T(128)S(1)} %copy-done.8, bf16[256,1024]{1,0:T(8,128)(2,1)S(1)} %copy-done.4, bf16[256,1024]{1,0:T(8,128)(2,1)S(1)} %copy-done.6, bf16[256,1024]{1,0:T(8,128)(2,1)S(1)} %copy-done.2, bf16[256,1024]{1,0:T(8,128)(2,1)} %collective-permute-done.4.refs_3_.refs_6_.refs_16_, ...), custom_call_target="tpu_custom_call" | custom-call | bytes 655360 | tf_op jit(solution)/shard_map/pick/pallas_call | solution.py:100
  61.6 0.0 copy-start.12
  61.6 0.0 copy-start.5
  61.6 0.8 collective-permute-start.8
  62.4 2.3 %collective-permute-start.3 = (bf16[128,1024]{1,0:T(8,128)(2,1)S(1)}, bf16[128,1024]{1,0:T(8,128)(2,1)S(1)}, u32[]{:S(2)}, u32[]{:S(2)}) collective-permute-start(bf16[128,1024]{1,0:T(8,128)(2,1)S(1)} %constant_dynamic-slice_fusion.1), channel_id=1, source_target_pairs={{0,16},{16,32},{32,48},{48,64},{64,80},{80,96},{96,112},{112,0},{1... | collective-permute-start | bytes 786440 | tf_op jit(solution)/shard_map/ppermute | solution.py:258
  64.7 1.0 constant_dynamic-slice_fusion
  65.7 1.2 %collective-permute-start.7 = (bf16[128,1024]{1,0:T(8,128)(2,1)S(1)}, bf16[128,1024]{1,0:T(8,128)(2,1)S(1)}, u32[]{:S(2)}, u32[]{:S(2)}) collective-permute-start(bf16[128,1024]{1,0:T(8,128)(2,1)S(1)} %constant_dynamic-slice_fusion), channel_id=1, source_target_pairs={{0,16},{16,32},{32,48},{48,64},{64,80},{80,96},{96,112},{112,0},{1... | collective-permute-start | bytes 786440 | tf_op jit(solution)/shard_map/ppermute | solution.py:259
  66.9 1.4 %pick.3 = bf16[256,256]{1,0:T(8,128)(2,1)S(1)} custom-call(s32[6]{0:T(128)S(1)} %copy-done.8, bf16[256,1024]{1,0:T(8,128)(2,1)S(1)} %tie.5.refs_0_.refs_3_.refs_13_, bf16[256,1024]{1,0:T(8,128)(2,1)} %collective-permute-done.6.refs_1_.refs_8_.refs_18_), custom_call_target="tpu_custom_call" | custom-call | bytes 262144 | tf_op jit(solution)/shard_map/pick/pallas_call | solution.py:100
  68.3 1.4 %collective-permute-start.9 = (bf16[256,256]{1,0:T(8,128)(2,1)S(1)}, bf16[256,256]{1,0:T(8,128)(2,1)S(1)}, u32[]{:S(2)}, u32[]{:S(2)}) collective-permute-start(bf16[256,256]{1,0:T(8,128)(2,1)S(1)} %pick.3), channel_id=1, source_target_pairs={{0,2},{2,0},{1,3},{3,1},{4,6},{6,4},{5,7},{7,5},{8,10},{10,8},{9,1... | collective-permute-start | bytes 393224 | tf_op jit(solution)/shard_map/ppermute | solution.py:266
  69.8 3.2 %collective-permute-start.10 = (bf16[128,256]{1,0:T(8,128)(2,1)S(1)}, bf16[128,256]{1,0:T(8,128)(2,1)S(1)}, u32[]{:S(2)}, u32[]{:S(2)}) collective-permute-start(bf16[128,256]{1,0:T(8,128)(2,1)S(1)} %copy-done.12), channel_id=1, source_target_pairs={{0,64},{16,80},{32,96},{48,112},{64,0},{80,16},{96,32},{112,48},{1... | collective-permute-start | bytes 196616 | tf_op jit(solution)/shard_map/ppermute | solution.py:261
  72.9 5.0 %collective-permute-done.10.refs_22_ = bf16[128,256]{1,0:T(8,128)(2,1)S(1)} collective-permute-done((bf16[128,256]{1,0:T(8,128)(2,1)S(1)}, bf16[128,256]{1,0:T(8,128)(2,1)S(1)}, u32[]{:S(2)}, u32[]{:S(2)}) %collective-permute-start.10) | collective-permute-done | bytes 65568 | tf_op jit(solution)/shard_map/ppermute | solution.py:261
  78.0 4.0 %gram.3 = (f32[256,512]{1,0:T(8,128)S(1)}, f32[256,512]{1,0:T(8,128)S(1)}, f32[256,512]{1,0:T(8,128)S(1)}, f32[256,512]{1,0:T(8,128)S(1)}) custom-call(s32[6]{0:T(128)S(1)} %copy-done.8, bf16[256,1024]{1,0:T(8,128)(2,1)S(1)} %copy-done.5, bf16[256,1024]{1,0:T(8,128)(2,1)S(1)} %copy-done.3, bf16[256,1024]{1,0:T(8,128)(2,1)S(1)} %tie.4.refs_4_.refs_2_.refs_12_, ...), custom_call_target="tpu_custom_call" | custom-call | flops 1073741824 | bytes 7340032 | tf_op jit(solution)/shard_map/gram/pallas_call | solution.py:174
  82.0 0.1 collective-permute-start.15
  82.1 0.5 collective-permute-start.13
  82.6 4.0 %gram.2 = (f32[256,512]{1,0:T(8,128)S(1)}, f32[256,512]{1,0:T(8,128)S(1)}, f32[256,512]{1,0:T(8,128)S(1)}, f32[256,512]{1,0:T(8,128)S(1)}) custom-call(s32[6]{0:T(128)S(1)} %copy-done.8, bf16[256,1024]{1,0:T(8,128)(2,1)S(1)} %copy-done.5, bf16[256,1024]{1,0:T(8,128)(2,1)S(1)} %copy-done.3, bf16[256,1024]{1,0:T(8,128)(2,1)S(1)} %tie.4.refs_4_.refs_2_.refs_12_, ...), custom_call_target="tpu_custom_call" | custom-call | flops 1073741824 | bytes 7340032 | tf_op jit(solution)/shard_map/gram/pallas_call | solution.py:174
  86.5 0.4 collective-permute-start.11
  87.0 0.2 collective-permute-start.12
  87.1 0.1 add.21
  87.2 1.7 %collective-permute-start.16 = (f32[256,512]{1,0:T(8,128)S(1)}, f32[256,512]{1,0:T(8,128)S(1)}, u32[]{:S(2)}, u32[]{:S(2)}) collective-permute-start(f32[256,512]{1,0:T(8,128)S(1)} %add.21), channel_id=1, source_target_pairs={{0,128},{128,0},{1,129},{129,1},{2,130},{130,2},{3,131},{131,3},{4... | collective-permute-start | bytes 1572872 | tf_op jit(solution)/shard_map/ppermute | solution.py:271
  89.0 0.1 add.20
  89.0 2.0 %collective-permute-start.14 = (f32[256,512]{1,0:T(8,128)S(1)}, f32[256,512]{1,0:T(8,128)S(1)}, u32[]{:S(2)}, u32[]{:S(2)}) collective-permute-start(f32[256,512]{1,0:T(8,128)S(1)} %add.20), channel_id=1, source_target_pairs={{0,128},{128,0},{1,129},{129,1},{2,130},{130,2},{3,131},{131,3},{4... | collective-permute-start | bytes 1572872 | tf_op jit(solution)/shard_map/ppermute | solution.py:271
  91.0 0.2 collective-permute-start.17
  91.2 3.6 %collective-permute-done.17.refs_1_ = f32[32,128]{1,0:T(8,128)S(1)} collective-permute-done((f32[32,128]{1,0:T(8,128)S(1)}, f32[32,128]{1,0:T(8,128)S(1)}, u32[]{:S(2)}, u32[]{:S(2)}) %collective-permute-start.17) | collective-permute-done | bytes 16416 | tf_op jit(solution)/shard_map/ppermute | solution.py:364
  94.8 1.4 %collective-permute-start.18 = (f32[32,128]{1,0:T(8,128)S(1)}, f32[32,128]{1,0:T(8,128)S(1)}, u32[]{:S(2)}, u32[]{:S(2)}) collective-permute-start(f32[32,128]{1,0:T(8,128)S(1)} %sum.1.refs_1_.refs_0_), channel_id=1, source_target_pairs={{0,8},{4,12},{8,0},{12,4},{1,9},{5,13},{9,1},{13,5},{2,10},{6,14},... | collective-permute-start | bytes 49160 | tf_op jit(solution)/shard_map/ppermute | solution.py:364
  96.2 3.8 %collective-permute-done.18.refs_2_ = f32[32,128]{1,0:T(8,128)S(1)} collective-permute-done((f32[32,128]{1,0:T(8,128)S(1)}, f32[32,128]{1,0:T(8,128)S(1)}, u32[]{:S(2)}, u32[]{:S(2)}) %collective-permute-start.18) | collective-permute-done | bytes 16416 | tf_op jit(solution)/shard_map/ppermute | solution.py:364
  100.0 2.6 %collective-permute-start.19 = (f32[32,128]{1,0:T(8,128)S(1)}, f32[32,128]{1,0:T(8,128)S(1)}, u32[]{:S(2)}, u32[]{:S(2)}) collective-permute-start(f32[32,128]{1,0:T(8,128)S(1)} %sum.1.refs_1_.refs_0_), channel_id=1, source_target_pairs={{0,12},{4,0},{8,4},{12,8},{1,13},{5,1},{9,5},{13,9},{2,14},{6,2},{... | collective-permute-start | bytes 49160 | tf_op jit(solution)/shard_map/ppermute | solution.py:364
  102.6 1.4 %collective-permute-done.19.refs_3_ = f32[32,128]{1,0:T(8,128)S(1)} collective-permute-done((f32[32,128]{1,0:T(8,128)S(1)}, f32[32,128]{1,0:T(8,128)S(1)}, u32[]{:S(2)}, u32[]{:S(2)}) %collective-permute-start.19) | collective-permute-done | bytes 16416 | tf_op jit(solution)/shard_map/ppermute | solution.py:364
  104.1 1.3 %assemble.1 = f32[64,256]{1,0:T(8,128)} custom-call(s32[6]{0:T(128)S(1)} %copy-done.8, f32[32,128]{1,0:T(8,128)S(1)} %sum.1.refs_1_.refs_0_, f32[32,128]{1,0:T(8,128)S(1)} %collective-permute-done.17.refs_1_, f32[32,128]{1,0:T(8,128)S(1)} %collective-permute-done.18.refs_2_, f32[32,128]{1,0:T(8,128)S(1)} %collective-permute-done.19.refs_3_), custom_call_target="tpu_custom_call" | custom-call | bytes 131072 | tf_op jit(solution)/shard_map/assemble/pallas_call | solution.py:365
  105.4 8.9 %collective-permute-done.14.low_got = f32[256,512]{1,0:T(8,128)S(1)} collective-permute-done((f32[256,512]{1,0:T(8,128)S(1)}, f32[256,512]{1,0:T(8,128)S(1)}, u32[]{:S(2)}, u32[]{:S(2)}) %collective-permute-start.14) | collective-permute-done | bytes 524320 | tf_op jit(solution)/shard_map/ppermute | solution.py:271
  114.2 1.6 %finish.1 = f32[256,1024]{1,0:T(8,128)} custom-call(f32[256,512]{1,0:T(8,128)S(1)} %get-tuple-element.16.low, f32[256,512]{1,0:T(8,128)S(1)} %get-tuple-element.17.high, f32[256,512]{1,0:T(8,128)S(1)} %collective-permute-done.11.low_core, f32[256,512]{1,0:T(8,128)S(1)} %collective-permute-done.12.high_core, f32[256,512]{1,0:T(8,128)S(1)} %collective-permute-done.14.low_got, ...), custom_call_target="tpu_custom_call" | custom-call | flops 1048576 | bytes 4194304 | tf_op jit(solution)/shard_map/finish/pallas_call | solution.py:218
  (40 shorter events, 0.1 us)
Async XLA Ops:
  0.6 9.4 %copy-start = (bf16[256,1,4096]{2,0,1:T(8,128)(2,1)S(1)}, bf16[256,1,4096]{2,0,1:T(8,128)(2,1)}, u32[]{:S(2)}) copy-start(bf16[256,1,4096]{2,0,1:T(8,128)(2,1)} %param.7) | copy-start | bytes 6291460
  1.3 8.8 %copy-start.11 = (s32[256,1,32]{0,2,1:T(8,128)S(1)}, s32[256,1,32]{0,2,1:T(8,128)}, u32[]{:S(2)}) copy-start(s32[256,1,32]{0,2,1:T(8,128)} %param.6) | copy-start | bytes 98308
  6.1 13.3 %collective-permute-start = (bf16[256,1024]{1,0:T(8,128)(2,1)}, bf16[256,1024]{1,0:T(8,128)(2,1)S(1)}, u32[]{:S(2)}, u32[]{:S(2)}) collective-permute-start(bf16[256,1024]{1,0:T(8,128)(2,1)} %get-tuple-element.13.refs_0_.refs_10_), channel_id=1, source_target_pairs={{0,16},{16,32},{32,48},{48,64},{64,80},{80,96},{96,112},{112,0},{1... | collective-permute-start | bytes 1572872 | tf_op jit(solution)/shard_map/ppermute | solution.py:258
  8.1 17.0 %collective-permute-start.4 = (bf16[256,1024]{1,0:T(8,128)(2,1)}, bf16[256,1024]{1,0:T(8,128)(2,1)}, u32[]{:S(2)}, u32[]{:S(2)}) collective-permute-start(bf16[256,1024]{1,0:T(8,128)(2,1)} %get-tuple-element.14.refs_1_.refs_5_.refs_15_), channel_id=1, source_target_pairs={{0,16},{16,32},{32,48},{48,64},{64,80},{80,96},{96,112},{112,0},{1... | collective-permute-start | bytes 1572872 | tf_op jit(solution)/shard_map/ppermute | solution.py:259
  10.0 26.0 %copy-start.9 = (s32[1024]{0:T(1024)S(1)}, s32[1024]{0:T(1024)}, u32[]{:S(2)}) copy-start(s32[1024]{0:T(1024)} %param.9) | copy-start | bytes 12292
  10.1 26.0 %copy-start.10 = (s32[256]{0:T(256)S(1)}, s32[256]{0:T(256)}, u32[]{:S(2)}) copy-start(s32[256]{0:T(256)} %param.8) | copy-start | bytes 3076
  19.4 18.3 %copy-start.1 = (bf16[256,1024]{1,0:T(8,128)(2,1)}, bf16[256,1024]{1,0:T(8,128)(2,1)S(1)}, u32[]{:S(2)}) copy-start(bf16[256,1024]{1,0:T(8,128)(2,1)S(1)} %tie.3.refs_2_.refs_1_.refs_11_) | copy-start | bytes 1572868
  19.4 37.5 %copy-start.8 = (s32[6]{0:T(128)S(1)}, s32[6]{0:T(128)}, u32[]{:S(2)}) copy-start(s32[6]{0:T(128)} %stack.27.at) | copy-start | bytes 76
  19.4 18.3 %collective-permute-start.1 = (bf16[256,1024]{1,0:T(8,128)(2,1)S(1)}, bf16[256,1024]{1,0:T(8,128)(2,1)S(1)}, u32[]{:S(2)}, u32[]{:S(2)}) collective-permute-start(bf16[256,1024]{1,0:T(8,128)(2,1)S(1)} %tie.3.refs_2_.refs_1_.refs_11_), channel_id=1, source_target_pairs={{0,16},{16,32},{32,48},{48,64},{64,80},{80,96},{96,112},{112,0},{1... | collective-permute-start | bytes 1572872 | tf_op jit(solution)/shard_map/ppermute | solution.py:258
  25.1 21.2 %collective-permute-start.5 = (bf16[256,1024]{1,0:T(8,128)(2,1)}, bf16[256,1024]{1,0:T(8,128)(2,1)}, u32[]{:S(2)}, u32[]{:S(2)}) collective-permute-start(bf16[256,1024]{1,0:T(8,128)(2,1)} %collective-permute-done.4.refs_3_.refs_6_.refs_16_), channel_id=1, source_target_pairs={{0,16},{16,32},{32,48},{48,64},{64,80},{80,96},{96,112},{112,0},{1... | collective-permute-start | bytes 1572872 | tf_op jit(solution)/shard_map/ppermute | solution.py:259
  37.7 24.7 %collective-permute-start.2 = (bf16[256,1024]{1,0:T(8,128)(2,1)S(1)}, bf16[256,1024]{1,0:T(8,128)(2,1)S(1)}, u32[]{:S(2)}, u32[]{:S(2)}) collective-permute-start(bf16[256,1024]{1,0:T(8,128)(2,1)S(1)} %tie.4.refs_4_.refs_2_.refs_12_), channel_id=1, source_target_pairs={{0,16},{16,32},{32,48},{48,64},{64,80},{80,96},{96,112},{112,0},{1... | collective-permute-start | bytes 1572872 | tf_op jit(solution)/shard_map/ppermute | solution.py:258
  37.7 19.2 %all-to-all-start.1 = ((f32[16,32,128]{2,1,0:T(8,128)}), f32[16,32,128]{2,1,0:T(8,128)S(1)}, u32[]{:S(2)}, u32[]{:S(2)}) async-start(f32[16,32,128]{2,1,0:T(8,128)} %bitcast.14), calls=%async_computation.1 | async-start | bytes 524288 | tf_op jit(solution)/shard_map/all_to_all | solution.py:351
  46.3 18.4 %collective-permute-start.6 = (bf16[256,1024]{1,0:T(8,128)(2,1)}, bf16[256,1024]{1,0:T(8,128)(2,1)}, u32[]{:S(2)}, u32[]{:S(2)}) collective-permute-start(bf16[256,1024]{1,0:T(8,128)(2,1)} %collective-permute-done.5.refs_5_.refs_7_.refs_17_), channel_id=1, source_target_pairs={{0,16},{16,32},{32,48},{48,64},{64,80},{80,96},{96,112},{112,0},{1... | collective-permute-start | bytes 1572872 | tf_op jit(solution)/shard_map/ppermute | solution.py:259
  56.9 1.0 copy-start.2
  58.0 1.0 copy-start.4
  59.0 1.0 copy-start.6
  61.6 8.2 %copy-start.12 = (bf16[128,256]{1,0:T(8,128)(2,1)S(1)}, bf16[128,256]{1,0:T(8,128)(2,1)}, u32[]{:S(2)}) copy-start(bf16[128,256]{1,0:T(8,128)(2,1)} %get-tuple-element.15) | copy-start | bytes 196612
  61.6 16.4 %copy-start.3 = (bf16[256,1024]{1,0:T(8,128)(2,1)S(1)}, bf16[256,1024]{1,0:T(8,128)(2,1)}, u32[]{:S(2)}) copy-start(bf16[256,1024]{1,0:T(8,128)(2,1)} %copy-done.1) | copy-start | bytes 1572868
  61.6 16.4 %copy-start.5 = (bf16[256,1024]{1,0:T(8,128)(2,1)S(1)}, bf16[256,1024]{1,0:T(8,128)(2,1)}, u32[]{:S(2)}) copy-start(bf16[256,1024]{1,0:T(8,128)(2,1)} %get-tuple-element.13.refs_0_.refs_10_) | copy-start | bytes 1572868
  61.6 16.4 %copy-start.7 = (bf16[256,1024]{1,0:T(8,128)(2,1)S(1)}, bf16[256,1024]{1,0:T(8,128)(2,1)}, u32[]{:S(2)}) copy-start(bf16[256,1024]{1,0:T(8,128)(2,1)} %get-tuple-element.14.refs_1_.refs_5_.refs_15_) | copy-start | bytes 1572868
  61.6 16.3 %collective-permute-start.8 = (bf16[640,256]{1,0:T(8,128)(2,1)S(1)}, bf16[640,256]{1,0:T(8,128)(2,1)S(1)}, u32[]{:S(2)}, u32[]{:S(2)}) collective-permute-start(bf16[640,256]{1,0:T(8,128)(2,1)S(1)} %pick.2), channel_id=1, source_target_pairs={{0,2},{2,0},{1,3},{3,1},{4,6},{6,4},{5,7},{7,5},{8,10},{10,8},{9,1... | collective-permute-start | bytes 983048 | tf_op jit(solution)/shard_map/ppermute | solution.py:265
  62.4 15.5 %collective-permute-start.3 = (bf16[128,1024]{1,0:T(8,128)(2,1)S(1)}, bf16[128,1024]{1,0:T(8,128)(2,1)S(1)}, u32[]{:S(2)}, u32[]{:S(2)}) collective-permute-start(bf16[128,1024]{1,0:T(8,128)(2,1)S(1)} %constant_dynamic-slice_fusion.1), channel_id=1, source_target_pairs={{0,16},{16,32},{32,48},{48,64},{64,80},{80,96},{96,112},{112,0},{1... | collective-permute-start | bytes 786440 | tf_op jit(solution)/shard_map/ppermute | solution.py:258
  65.7 12.2 %collective-permute-start.7 = (bf16[128,1024]{1,0:T(8,128)(2,1)S(1)}, bf16[128,1024]{1,0:T(8,128)(2,1)S(1)}, u32[]{:S(2)}, u32[]{:S(2)}) collective-permute-start(bf16[128,1024]{1,0:T(8,128)(2,1)S(1)} %constant_dynamic-slice_fusion), channel_id=1, source_target_pairs={{0,16},{16,32},{32,48},{48,64},{64,80},{80,96},{96,112},{112,0},{1... | collective-permute-start | bytes 786440 | tf_op jit(solution)/shard_map/ppermute | solution.py:259
  68.3 9.6 %collective-permute-start.9 = (bf16[256,256]{1,0:T(8,128)(2,1)S(1)}, bf16[256,256]{1,0:T(8,128)(2,1)S(1)}, u32[]{:S(2)}, u32[]{:S(2)}) collective-permute-start(bf16[256,256]{1,0:T(8,128)(2,1)S(1)} %pick.3), channel_id=1, source_target_pairs={{0,2},{2,0},{1,3},{3,1},{4,6},{6,4},{5,7},{7,5},{8,10},{10,8},{9,1... | collective-permute-start | bytes 393224 | tf_op jit(solution)/shard_map/ppermute | solution.py:266
  69.8 8.2 %collective-permute-start.10 = (bf16[128,256]{1,0:T(8,128)(2,1)S(1)}, bf16[128,256]{1,0:T(8,128)(2,1)S(1)}, u32[]{:S(2)}, u32[]{:S(2)}) collective-permute-start(bf16[128,256]{1,0:T(8,128)(2,1)S(1)} %copy-done.12), channel_id=1, source_target_pairs={{0,64},{16,80},{32,96},{48,112},{64,0},{80,16},{96,32},{112,48},{1... | collective-permute-start | bytes 196616 | tf_op jit(solution)/shard_map/ppermute | solution.py:261
  82.0 5.2 %collective-permute-start.15 = (f32[256,512]{1,0:T(8,128)S(1)}, f32[256,512]{1,0:T(8,128)S(1)}, u32[]{:S(2)}, u32[]{:S(2)}) collective-permute-start(f32[256,512]{1,0:T(8,128)S(1)} %get-tuple-element.23), channel_id=1, source_target_pairs={{0,1},{1,0},{2,3},{3,2},{4,5},{5,4},{6,7},{7,6},{8,9},{9,8},{10,11... | collective-permute-start | bytes 1572872 | tf_op jit(solution)/shard_map/ppermute | solution.py:270
  82.1 6.9 %collective-permute-start.13 = (f32[256,512]{1,0:T(8,128)S(1)}, f32[256,512]{1,0:T(8,128)S(1)}, u32[]{:S(2)}, u32[]{:S(2)}) collective-permute-start(f32[256,512]{1,0:T(8,128)S(1)} %get-tuple-element.21), channel_id=1, source_target_pairs={{0,1},{1,0},{2,3},{3,2},{4,5},{5,4},{6,7},{7,6},{8,9},{9,8},{10,11... | collective-permute-start | bytes 1572872 | tf_op jit(solution)/shard_map/ppermute | solution.py:270
  86.5 18.8 %collective-permute-start.11 = (f32[256,512]{1,0:T(8,128)S(1)}, f32[256,512]{1,0:T(8,128)S(1)}, u32[]{:S(2)}, u32[]{:S(2)}) collective-permute-start(f32[256,512]{1,0:T(8,128)S(1)} %get-tuple-element.18), channel_id=1, source_target_pairs={{0,1},{1,0},{2,3},{3,2},{4,5},{5,4},{6,7},{7,6},{8,9},{9,8},{10,11... | collective-permute-start | bytes 1572872 | tf_op jit(solution)/shard_map/ppermute | solution.py:273
  87.0 18.4 %collective-permute-start.12 = (f32[256,512]{1,0:T(8,128)S(1)}, f32[256,512]{1,0:T(8,128)S(1)}, u32[]{:S(2)}, u32[]{:S(2)}) collective-permute-start(f32[256,512]{1,0:T(8,128)S(1)} %get-tuple-element.19), channel_id=1, source_target_pairs={{0,1},{1,0},{2,3},{3,2},{4,5},{5,4},{6,7},{7,6},{8,9},{9,8},{10,11... | collective-permute-start | bytes 1572872 | tf_op jit(solution)/shard_map/ppermute | solution.py:273
  87.2 18.1 %collective-permute-start.16 = (f32[256,512]{1,0:T(8,128)S(1)}, f32[256,512]{1,0:T(8,128)S(1)}, u32[]{:S(2)}, u32[]{:S(2)}) collective-permute-start(f32[256,512]{1,0:T(8,128)S(1)} %add.21), channel_id=1, source_target_pairs={{0,128},{128,0},{1,129},{129,1},{2,130},{130,2},{3,131},{131,3},{4... | collective-permute-start | bytes 1572872 | tf_op jit(solution)/shard_map/ppermute | solution.py:271
  89.0 25.2 %collective-permute-start.14 = (f32[256,512]{1,0:T(8,128)S(1)}, f32[256,512]{1,0:T(8,128)S(1)}, u32[]{:S(2)}, u32[]{:S(2)}) collective-permute-start(f32[256,512]{1,0:T(8,128)S(1)} %add.20), channel_id=1, source_target_pairs={{0,128},{128,0},{1,129},{129,1},{2,130},{130,2},{3,131},{131,3},{4... | collective-permute-start | bytes 1572872 | tf_op jit(solution)/shard_map/ppermute | solution.py:271
  91.0 3.7 %collective-permute-start.17 = (f32[32,128]{1,0:T(8,128)S(1)}, f32[32,128]{1,0:T(8,128)S(1)}, u32[]{:S(2)}, u32[]{:S(2)}) collective-permute-start(f32[32,128]{1,0:T(8,128)S(1)} %sum.1.refs_1_.refs_0_), channel_id=1, source_target_pairs={{0,4},{4,8},{8,12},{12,0},{1,5},{5,9},{9,13},{13,1},{2,6},{6,10},{... | collective-permute-start | bytes 49160 | tf_op jit(solution)/shard_map/ppermute | solution.py:364
  94.8 5.2 %collective-permute-start.18 = (f32[32,128]{1,0:T(8,128)S(1)}, f32[32,128]{1,0:T(8,128)S(1)}, u32[]{:S(2)}, u32[]{:S(2)}) collective-permute-start(f32[32,128]{1,0:T(8,128)S(1)} %sum.1.refs_1_.refs_0_), channel_id=1, source_target_pairs={{0,8},{4,12},{8,0},{12,4},{1,9},{5,13},{9,1},{13,5},{2,10},{6,14},... | collective-permute-start | bytes 49160 | tf_op jit(solution)/shard_map/ppermute | solution.py:364
  100.0 4.1 %collective-permute-start.19 = (f32[32,128]{1,0:T(8,128)S(1)}, f32[32,128]{1,0:T(8,128)S(1)}, u32[]{:S(2)}, u32[]{:S(2)}) collective-permute-start(f32[32,128]{1,0:T(8,128)S(1)} %sum.1.refs_1_.refs_0_), channel_id=1, source_target_pairs={{0,12},{4,0},{8,4},{12,8},{1,13},{5,1},{9,5},{13,9},{2,14},{6,2},{... | collective-permute-start | bytes 49160 | tf_op jit(solution)/shard_map/ppermute | solution.py:364

commit v4 on v3

--- a/solution.py
+++ b/solution.py
@@ -27,7 +27,7 @@
     return pl.CostEstimate(flops=flops, bytes_accessed=moved, transcendentals=0)
 
 
-AT_Z, AT_CORE, AT_YL, AT_FAR, AT_YH, AT_X = 0, 1, 2, 3, 4, 5
+AT_Z, AT_CORE, AT_YL, AT_OWN, AT_FAR, AT_YH, AT_X = 0, 1, 2, 3, 4, 5, 6
 
 
 def wide_scale(turned, first_block, columns):
@@ -37,7 +37,7 @@
     return lax.dot_general(turned, pick, TURNED, preferred_element_type=jnp.float32)
 
 
-def dequant_kernel(at, exps, values, far_values, low, high, far):
+def dequant_kernel(at, exps, values, own_values, far_values, low, high, own, far):
     step = pl.program_id(0)
     turned = powers(exps[...])
     grads = values[...].astype(jnp.float32) * wide_scale(turned, at[AT_YL] * 16 + step * 4, 512)
@@ -48,9 +48,10 @@
     @pl.when(step == 0)
     def _():
         half = far.shape[0]
-        scale = wide_scale(turned, at[AT_FAR] * 2, 256)
-        scale = jnp.where(at[AT_CORE] == 0, scale[:half], scale[half:])
-        far[...] = (far_values[...].astype(jnp.float32) * scale).astype(jnp.bfloat16)
+        for block, source, result in ((AT_OWN, own_values, own), (AT_FAR, far_values, far)):
+            scale = wide_scale(turned, at[block] * 2, 256)
+            scale = jnp.where(at[AT_CORE] == 0, scale[:half], scale[half:])
+            result[...] = (source[...].astype(jnp.float32) * scale).astype(jnp.bfloat16)
 
 
 def dequant(at, exps, mantissas):
@@ -64,19 +65,21 @@
             in_specs=[
                 pl.BlockSpec(exps.shape, lambda g, at: (0, 0)),
                 pl.BlockSpec((rows, 512), lambda g, at: (0, at[AT_YL] * 4 + g)),
+                pl.BlockSpec((rows // 2, 256), lambda g, at: (at[AT_CORE], at[AT_OWN])),
                 pl.BlockSpec((rows // 2, 256), lambda g, at: (at[AT_CORE], at[AT_FAR])),
             ],
             out_specs=[
                 pl.BlockSpec((rows, 256), lambda g, at: (0, g)),
                 pl.BlockSpec((rows, 256), lambda g, at: (0, g)),
                 pl.BlockSpec((rows // 2, 256), lambda g, at: (0, 0)),
+                pl.BlockSpec((rows // 2, 256), lambda g, at: (0, 0)),
             ],
         ),
-        out_shape=[side, side, jax.ShapeDtypeStruct((rows // 2, 256), jnp.bfloat16)],
+        out_shape=[side, side] + [jax.ShapeDtypeStruct((rows // 2, 256), jnp.bfloat16)] * 2,
         compiler_params=params(58),
         cost_estimate=cost(1 << 25, 2 << 20),
         name="dequant",
-    )(at, exps, mantissas, mantissas)
+    )(at, exps, mantissas, mantissas, mantissas)
 
 
 def pick_kernel(count, at, *refs):
@@ -114,8 +117,8 @@
     count = len(sizes)
     lows, highs = refs[:count], refs[count : 2 * count]
     low_rights, high_rights = refs[2 * count : 3 * count], refs[3 * count : 4 * count]
-    near, third, far = refs[4 * count : 4 * count + 3]
-    low_other, high_other, low_own, high_own = refs[4 * count + 3 : 4 * count + 7]
+    own, near, third, far = refs[4 * count : 4 * count + 4]
+    low_other, high_other, low_own, high_own = refs[-5:-1]
     left = refs[-1]
     step = pl.program_id(0)
 
@@ -126,11 +129,11 @@
         row, start = 0, 0
         for i, rows in enumerate(sizes):
             mine = jnp.concatenate([lows[i][...], highs[i][...]], 1)
-            if i < count - 2:
+            if 0 < i < count - 2:
                 theirs = near[row : row + rows]
                 row += rows
             else:
-                theirs = third[...] if i == count - 2 else far[...]
+                theirs = (own if i == 0 else third if i == count - 2 else far)[...]
             left[start : start + rows] = jnp.where(use_mine, mine, theirs)
             start += rows
 
@@ -155,7 +158,7 @@
         high_own[...] = terms(high_rights)
 
 
-def gram(at, pieces, received, kept):
+def gram(at, pieces, received, kept, *after):
     sizes = tuple(n for n, _, _, _ in pieces)
     specs = [lanes_at_z(n, by_core) for n, by_core, _, _ in pieces] * 2
     for n, by_core, _, _ in pieces:
@@ -170,6 +173,7 @@
         )
     specs += specs[-len(pieces) :]
     specs += [pl.BlockSpec(r.shape, lambda g, at: (0, 0)) for r in received]
+    specs += [pl.BlockSpec(memory_space=pl.ANY)] * len(after)
     sides = [p[2] for p in pieces], [p[3] for p in pieces]
     return pl.pallas_call(
         functools.partial(gram_kernel, sizes, kept),
@@ -182,7 +186,7 @@
         compiler_params=params(20),
         cost_estimate=cost(2 * sum(sizes) * 256 * 2048, 7 << 20),
         name="gram",
-    )(at, *sides[0], *sides[1], *sides[0], *sides[1], *received)
+    )(at, *sides[0], *sides[1], *sides[0], *sides[1], *received, *after)
 
 
 def add_kernel(left, right, out):
@@ -244,10 +248,10 @@
     )(value, *earlier)
 
 
-def fisher_block(at, mantissas, exps, total_rows, stages):
+def fisher_terms(at, mantissas, exps, scores, placed):
     core = lax.axis_index("core")
     rows = mantissas.shape[0]
-    low, high, far = dequant(at, exps, mantissas)
+    low, high, own, far = dequant(at, exps, mantissas)
 
     half = rows // 2
     pieces = [(half, True, low, high)]
@@ -259,19 +263,22 @@
         high = lax.ppermute(high, ("z", "core"), RING)
         if step == 1:
             far = lax.ppermute(far, "z", [(i, (i + Z // 2) % Z) for i in range(Z)])
-        if step < Z // 2:
-            low = tie(low, stages[step - 1])
+            low = tie(low, far, scores)
+        if step == 3:
+            low = tie(low, placed)
         pieces.append((low.shape[0], False, low, high))
-    near = lax.ppermute(pick(at, pieces[:3]), "yl", SWAP)
-    third = lax.ppermute(pick(at, pieces[3:4]), "yl", SWAP)
-    received = (near, third, far)
+    near = lax.ppermute(pick(at, pieces[1:3]), "yl", SWAP)
+    third = pick(at, pieces[3:4])
+    mine = own_slots(tie(placed, third))
+    third = lax.ppermute(third, "yl", SWAP)
+    received = (own, near, third, far)
 
     *given_other, low_given, high_given = gram(at, pieces, received, False)
     swapped = [lax.ppermute(g, "core", SWAP) for g in given_other]
-    given = [lax.ppermute(add(g, s), "yh", SWAP) for g, s in zip((low_given, high_given), swapped)]
-    *kept_other, low_kept, high_kept = gram(at, pieces, received, True)
+    *kept_other, low_kept, high_kept = gram(at, pieces, received, True, mine)
+    given = [add(g, s) for g, s in zip((low_given, high_given), swapped)]
     kept = [lax.ppermute(k, "core", SWAP) for k in kept_other]
-    return finish(1.0 / total_rows, [low_kept, high_kept, *kept, *given])
+    return given, [low_kept, high_kept, *kept], mine
 
 
 def spread(scale):
@@ -282,9 +289,9 @@
     return wide.astype(jnp.bfloat16)
 
 
-def place_kernel(parts, ids, owners, out):
+def place_kernel(at, pair, got, ids, owners, out):
     docs, rows = owners.shape[1], ids.shape[1]
-    summed = (parts[0] + parts[1]) + (parts[2] + parts[3])
+    summed = jnp.where(at[AT_X] % 2 == 0, pair[0], pair[1]) + got[...]
     owner = jnp.broadcast_to(owners[...], (8, docs))
     digit = jnp.where(lax.broadcasted_iota(jnp.int32, (8, docs), 0) == 0, owner >> 5, owner & 31)
     doc = (lax.broadcasted_iota(jnp.int32, (docs, rows), 0) == ids[...]).astype(jnp.bfloat16)
@@ -320,60 +327,82 @@
     out[...] = total
 
 
-def assemble_kernel(at, *refs):
-    parts, out = refs[:-1], refs[-1]
-    half, double = parts[0].shape
-    share = double // 2
-    values = []
-    for source in range(X):
-        value = parts[0][...]
-        for shift in range(1, X):
-            value = jnp.where(lax.rem(source + shift, X) == at[AT_X], parts[shift][...], value)
-        values.append(value)
-    out[0:half] = jnp.concatenate([v[:, :share] for v in values], 1)
-    out[half:] = jnp.concatenate([v[:, share:] for v in values], 1)
-
-
-def score_stages(mantissas, scale, queries, doc_ids, owners):
+def flipped(bit):
+    return [(i, i ^ bit) for i in range(X)]
+
+
+def whole(shape):
+    return pl.BlockSpec(shape, lambda g, at: (0,) * len(shape))
+
+
+def placed_scores(at, mantissas, scale, queries, doc_ids, owners):
     docs = owners.shape[0]
+    x = lax.axis_index("x")
     grads = mantissas * spread(scale)
     scores = lax.dot_general(queries, grads, (((1,), (1,)), ((), ())), preferred_element_type=jnp.float32)
     count, rows = scores.shape
     share, half = count // X, docs // (YH * Z) // 2
-    parts = lax.all_to_all(scores.reshape(X, share, rows), "x", 0, 0, tiled=True)
+    upper = x // 2
+    got = lax.ppermute(lax.dynamic_slice_in_dim(scores, (1 - upper) * 2 * share, 2 * share, 0), "x", flipped(2))
+    pair = lax.dynamic_slice_in_dim(scores, upper * 2 * share, 2 * share, 0) + got
+    got = lax.ppermute(lax.dynamic_slice_in_dim(pair, (1 - x % 2) * share, share, 0), "x", flipped(1))
+    shapes = (X // 2, share, rows), (share, rows), (1, rows), (1, docs)
     placed = pl.pallas_call(
         place_kernel,
+        grid_spec=pltpu.PrefetchScalarGridSpec(
+            num_scalar_prefetch=1, grid=(1,), in_specs=[whole(shape) for shape in shapes],
+            out_specs=whole((YH * Z * half, 2 * share)),
+        ),
         out_shape=jax.ShapeDtypeStruct((YH * Z * half, 2 * share), jnp.float32),
         compiler_params=params(10),
         cost_estimate=cost(1 << 28, 1 << 20),
         name="place",
-    )(parts, doc_ids.reshape(1, rows), owners.reshape(1, docs))
-    blocks = lax.all_to_all(placed.reshape(YH * Z, half, 2 * share), ("yh", "z"), 0, 0, tiled=True)
-    mine = pl.pallas_call(
+    )(at, pair.reshape(shapes[0]), got, doc_ids.reshape(1, rows), owners.reshape(1, docs))
+    return scores, placed
+
+
+def assemble_kernel(at, pair, far_pair, out):
+    half, double = pair.shape[1:]
+    share = double // 2
+    values = []
+    for source in range(X):
+        near = (source // 2) == at[AT_X] // 2
+        first = (source % 2) == at[AT_X] % 2
+        own = jnp.where(first, pair[0], pair[1])
+        other = jnp.where(first, far_pair[0], far_pair[1])
+        values.append(jnp.where(near, own, other))
+    out[0:half] = jnp.concatenate([v[:, :share] for v in values], 1)
+    out[half:] = jnp.concatenate([v[:, share:] for v in values], 1)
+
+
+def own_slots(placed):
+    double = placed.shape[1]
+    half = placed.shape[0] // (YH * Z)
+    blocks = lax.all_to_all(placed.reshape(YH * Z, half, double), ("yh", "z"), 0, 0, tiled=True)
+    return pl.pallas_call(
         sum_kernel,
-        out_shape=jax.ShapeDtypeStruct((half, 2 * share), jnp.float32),
+        out_shape=jax.ShapeDtypeStruct((half, double), jnp.float32),
         compiler_params=params(4),
         cost_estimate=cost(1 << 16, 1 << 18),
         name="sum",
     )(blocks)
-    return scores, placed, mine
-
-
-def assemble(at, mine):
+
+
+def doc_block(at, mine):
     half, double = mine.shape
-    parts = [mine] + [lax.ppermute(mine, "x", [(i, (i + s) % X) for i in range(X)]) for s in range(1, X)]
+    pair = jnp.stack([mine, lax.ppermute(mine, "x", flipped(1))])
+    far_pair = lax.ppermute(pair, "x", flipped(2))
     return pl.pallas_call(
         assemble_kernel,
         grid_spec=pltpu.PrefetchScalarGridSpec(
-            num_scalar_prefetch=1, grid=(1,),
-            in_specs=[pl.BlockSpec((half, double), lambda g, at: (0, 0))] * X,
-            out_specs=pl.BlockSpec((2 * half, X * double // 2), lambda g, at: (0, 0)),
+            num_scalar_prefetch=1, grid=(1,), in_specs=[whole(pair.shape)] * 2,
+            out_specs=whole((2 * half, X * double // 2)),
         ),
         out_shape=jax.ShapeDtypeStruct((2 * half, X * double // 2), jnp.float32),
         compiler_params=params(2),
         cost_estimate=cost(0, 1 << 17),
         name="assemble",
-    )(at, *parts)
+    )(at, pair, far_pair)
 
 
 def per_device(mantissas, exponents, queries, doc_ids, owners):
@@ -382,11 +411,12 @@
     total_rows = mantissas.shape[0] * YH * Z
     yh, z, x = lax.axis_index("yh"), lax.axis_index("z"), lax.axis_index("x")
     yl, core = lax.axis_index("yl"), lax.axis_index("core")
-    far_block = (1 - yl) * Z + lax.rem(z + Z // 2, Z)
-    at = jnp.stack([z, core, yl, far_block, yh, x]).astype(jnp.int32)
-    stages = score_stages(mantissas, powers(exponents), queries[:, 0, :], doc_ids, owners)
-    fisher = fisher_block(at, mantissas, exponents.T, total_rows, stages)
-    return fisher[None], assemble(at, stages[-1])
+    other = (1 - yl) * Z
+    at = jnp.stack([z, core, yl, other + z, other + lax.rem(z + Z // 2, Z), yh, x]).astype(jnp.int32)
+    scores, placed = placed_scores(at, mantissas, powers(exponents), queries[:, 0, :], doc_ids, owners)
+    given, kept, mine = fisher_terms(at, mantissas, exponents.T, scores, placed)
+    got = [lax.ppermute(g, "yh", SWAP) for g in given]
+    return finish(1.0 / total_rows, kept + got)[None], doc_block(at, mine)
 
 
 def solution(mesh):

time: 118 us -> 117 us (level)
  blocking collectives: 10.9 us -> 0 us
  local copies, waits for them, and re-layouts: 4.78 us -> 11.7 us
  Pallas kernels: 20.3 us -> 26 us
  starting transfers between devices: 32.6 us -> 31.3 us
  waiting for transfers between devices: 43.3 us -> 42.1 us
    all_to_all x1 -> x0, blocking collectives: 10.9 us -> none  [score_stages(): lax.all_to_all(scores.reshape(X, share, rows), 'x', 0, 0, tiled=True)]
    all_to_all x1, waiting for transfers between devices: 8.58 us -> 1.09 us  [own_slots(): lax.all_to_all(placed.reshape(YH * Z, half, double), ('yh', 'z'), 0, 0, t...]
    ppermute x20 -> x21, waiting for transfers between devices: 34.7 us -> 41 us  [the longest x2 11.5 us: per_device(): got = [lax.ppermute(g, 'yh', SWAP) for g in given]]
    unnamed x26 -> x34, local copies, waits for them, and re-layouts: 3.17 us -> 8.06 us
    dynamic_slice x2 -> x4, local copies, waits for them, and re-layouts: 0.99 us -> 3.07 us  [the longest x1 1.67 us: fisher_terms(): high = lax.dynamic_slice_in_dim(high, core * half, half, 0)]
    pallas_call x2, Pallas kernels: 0.16 us -> 2.16 us  [add(): pl.pallas_call(add_kernel, grid=(2,), in_specs=[spec, spec], out_specs=sp...]
    pallas_call x2, Pallas kernels: 7.93 us -> 9.32 us  [gram(): pl.pallas_call(functools.partial(gram_kernel, sizes, kept), grid_spec=plt...]
    pallas_call x2, Pallas kernels: 2.91 us -> 4.28 us  [pick(): pl.pallas_call(functools.partial(pick_kernel, len(pieces)), grid_spec=plt...]
  transfers between devices with their start and end apart: 21 -> 22, of which waited for: 8 -> 10; matrix products, arithmetic and copies ran while one was open for 4% -> 6% of each run, Pallas kernels for 9% -> 17%
where the time goes in v4:
time: 117 us; the launch traced here: 116 us
  waiting for transfers between devices  42.1 us (36%)
  starting transfers between devices  31.3 us (27%)
  Pallas kernels  26 us (22%)
  local copies, waits for them, and re-layouts  11.7 us (10%)
  matrix products  3.06 us (3%)
    ppermute x2, waiting for transfers between devices, per_device(): got = [lax.ppermute(g, 'yh', SWAP) for g in given]  11.5 us
    ppermute x4, waiting for transfers between devices, fisher_terms(): high = lax.ppermute(high, ('z', 'core'), RING)  9.5 us
    pallas_call x2, Pallas kernels, gram(): pl.pallas_call(functools.partial(gram_kernel, sizes, kept), grid_spec=plt...  9.32 us
    all_to_all x1, starting transfers between devices, own_slots(): lax.all_to_all(placed.reshape(YH * Z, half, double), ('yh', 'z'), 0, 0, t...  8.67 us
    unnamed x34, local copies, waits for them, and re-layouts  8.06 us
    ppermute x1, starting transfers between devices, fisher_terms(): far = lax.ppermute(far, 'z', [(i, (i + Z // 2) % Z) for i in range(Z)])  6.29 us
    ppermute x1, waiting for transfers between devices, fisher_terms(): far = lax.ppermute(far, 'z', [(i, (i + Z // 2) % Z) for i in range(Z)])  5.52 us
    pallas_call x1, Pallas kernels, dequant(): pl.pallas_call(dequant_kernel, grid_spec=pltpu.PrefetchScalarGridSpec(num...  4.91 us
  transfers between devices with their start and end apart: 22, of which 10 were waited for; matrix products, arithmetic and copies ran while one was open for 6% of the time, Pallas kernels for 17%

profile of v4, /device:TPU:2, one launch (start us, length us, event | category | flops | bytes accessed | tf_op | source)
XLA Modules:
  0.0 116.0 jit_solution(15950834176396864918)
XLA Ops:
  0.7 0.6 stack.40.at
  1.3 4.9 %dequant.1 = (bf16[256,1024]{1,0:T(8,128)(2,1)}, bf16[256,1024]{1,0:T(8,128)(2,1)}, bf16[128,256]{1,0:T(8,128)(2,1)}, bf16[128,256]{1,0:T(8,128)(2,1)}) custom-call(s32[7]{0:T(128)} %stack.40.at, s32[32,256]{1,0:T(8,128)} %bitcast.49, bf16[256,4096]{1,0:T(8,128)(2,1)} %bitcast.45, bf16[256,4096]{1,0:T(8,128)(2,1)} %bitcast.46, bf16[256,4096]{1,0:T(8,128)(2,1)} %bitcast.47), custom_call_target="tpu_custom_call" | custom-call | flops 33554432 | bytes 2097152 | tf_op jit(solution)/shard_map/dequant/pallas_call | solution.py:60
  6.2 2.0 %collective-permute-start = (bf16[256,1024]{1,0:T(8,128)(2,1)}, bf16[256,1024]{1,0:T(8,128)(2,1)S(1)}, u32[]{:S(2)}, u32[]{:S(2)}) collective-permute-start(bf16[256,1024]{1,0:T(8,128)(2,1)} %get-tuple-element.14.refs_0_.refs_10_), channel_id=1, source_target_pairs={{0,16},{16,32},{32,48},{48,64},{64,80},{80,96},{96,112},{112,0},{1... | collective-permute-start | bytes 1572872 | tf_op jit(solution)/shard_map/ppermute | solution.py:262
  8.2 6.3 %collective-permute-start.1 = (bf16[128,256]{1,0:T(8,128)(2,1)}, bf16[128,256]{1,0:T(8,128)(2,1)S(1)}, u32[]{:S(2)}, u32[]{:S(2)}) collective-permute-start(bf16[128,256]{1,0:T(8,128)(2,1)} %get-tuple-element.15), channel_id=1, source_target_pairs={{0,64},{16,80},{32,96},{48,112},{64,0},{80,16},{96,32},{112,48},{1... | collective-permute-start | bytes 196616 | tf_op jit(solution)/shard_map/ppermute | solution.py:265
  14.5 1.0 collective-permute-start.7
  15.5 3.1 %fusion.1 = f32[256,256]{0,1:T(8,128)S(1)} fusion(bf16[256,1,4096]{2,0,1:T(8,128)(2,1)S(1)} %copy-done, s32[4096]{0:T(1024)S(1)} %add_select_fusion, s32[256,1,32]{0,2,1:T(8,128)S(1)} %copy-done.16, bf16[256,1,4096]{2,0,1:T(8,128)(2,1)} %param.5), kind=kOutput, calls=%fused_computation.2 | convolution fusion | flops 606232576 | bytes 4505600 | tf_op jit(solution)/shard_map/dot_general | solution.py:342
  18.6 5.5 %collective-permute-done.1.refs_1_.refs_23_ = bf16[128,256]{1,0:T(8,128)(2,1)S(1)} collective-permute-done((bf16[128,256]{1,0:T(8,128)(2,1)}, bf16[128,256]{1,0:T(8,128)(2,1)S(1)}, u32[]{:S(2)}, u32[]{:S(2)}) %collective-permute-start.1) | collective-permute-done | bytes 65568 | tf_op jit(solution)/shard_map/ppermute | solution.py:265
  24.1 3.9 %collective-permute-done.7.refs_1_.refs_6_.refs_16_ = bf16[256,1024]{1,0:T(8,128)(2,1)} collective-permute-done((bf16[256,1024]{1,0:T(8,128)(2,1)}, bf16[256,1024]{1,0:T(8,128)(2,1)}, u32[]{:S(2)}, u32[]{:S(2)}) %collective-permute-start.7) | collective-permute-done | bytes 524320 | tf_op jit(solution)/shard_map/ppermute | solution.py:263
  28.0 0.7 dynamic-slice_bitcast_fusion
  28.7 2.1 %collective-permute-start.4 = (f32[128,256]{1,0:T(8,128)}, f32[128,256]{1,0:T(8,128)}, u32[]{:S(2)}, u32[]{:S(2)}) collective-permute-start(f32[128,256]{1,0:T(8,128)} %dynamic-slice_bitcast_fusion), channel_id=1, source_target_pairs={{0,8},{4,12},{8,0},{12,4},{1,9},{5,13},{9,1},{13,5},{2,10},{6,14},... | collective-permute-start | bytes 393224 | tf_op jit(solution)/shard_map/ppermute | solution.py:346
  30.8 3.8 %collective-permute-done.2.refs_2_.refs_12_ = bf16[256,1024]{1,0:T(8,128)(2,1)} collective-permute-done((bf16[256,1024]{1,0:T(8,128)(2,1)S(1)}, bf16[256,1024]{1,0:T(8,128)(2,1)}, u32[]{:S(2)}, u32[]{:S(2)}) %collective-permute-start.2) | collective-permute-done | bytes 524320 | tf_op jit(solution)/shard_map/ppermute | solution.py:262
  34.6 5.6 %collective-permute-done.8.refs_3_.refs_7_.refs_17_ = bf16[256,1024]{1,0:T(8,128)(2,1)} collective-permute-done((bf16[256,1024]{1,0:T(8,128)(2,1)}, bf16[256,1024]{1,0:T(8,128)(2,1)}, u32[]{:S(2)}, u32[]{:S(2)}) %collective-permute-start.8) | collective-permute-done | bytes 524320 | tf_op jit(solution)/shard_map/ppermute | solution.py:263
  40.3 0.9 bitcast_add_fusion
  41.2 0.6 copy-done.10
  41.9 0.5 collective-permute-start.5
  42.4 4.1 %collective-permute-done.5.got = f32[64,256]{1,0:T(8,128)S(1)} collective-permute-done((f32[64,256]{1,0:T(8,128)S(1)}, f32[64,256]{1,0:T(8,128)S(1)}, u32[]{:S(2)}, u32[]{:S(2)}) %collective-permute-start.5) | collective-permute-done | bytes 65568 | tf_op jit(solution)/shard_map/ppermute | solution.py:348
  46.5 0.9 copy-done.11
  47.4 1.4 %place.1.refs_1_.refs_0_ = f32[512,128]{1,0:T(8,128)S(1)} custom-call(s32[7]{0:T(128)S(1)} %copy-done.13, f32[2,64,256]{2,1,0:T(8,128)S(1)} %bitcast.41, f32[64,256]{1,0:T(8,128)S(1)} %collective-permute-done.5.got, s32[1,256]{1,0:T(1,128)S(1)} %bitcast.44, s32[1,1024]{1,0:T(1,128)S(1)} %bitcast.43), custom_call_target="tpu_custom_call" | custom-call | flops 268435456 | bytes 1048576 | tf_op jit(solution)/shard_map/place/pallas_call | solution.py:350
  48.9 2.2 %pick.2 = bf16[512,256]{1,0:T(8,128)(2,1)} custom-call(s32[7]{0:T(128)S(1)} %copy-done.13, bf16[256,1024]{1,0:T(8,128)(2,1)S(1)} %tie.3.refs_0_.refs_1_.refs_11_, bf16[256,1024]{1,0:T(8,128)(2,1)} %collective-permute-done.7.refs_1_.refs_6_.refs_16_, bf16[256,1024]{1,0:T(8,128)(2,1)} %collective-permute-done.2.refs_2_.refs_12_, ...), custom_call_target="tpu_custom_call" | custom-call | bytes 524288 | tf_op jit(solution)/shard_map/pick/pallas_call | solution.py:103
  51.1 1.6 %collective-permute-start.11 = (bf16[512,256]{1,0:T(8,128)(2,1)}, bf16[512,256]{1,0:T(8,128)(2,1)}, u32[]{:S(2)}, u32[]{:S(2)}) collective-permute-start(bf16[512,256]{1,0:T(8,128)(2,1)} %pick.2), channel_id=1, source_target_pairs={{0,2},{2,0},{1,3},{3,1},{4,6},{6,4},{5,7},{7,5},{8,10},{10,8},{9,1... | collective-permute-start | bytes 786440 | tf_op jit(solution)/shard_map/ppermute | solution.py:270
  52.7 0.7 constant_dynamic-slice_fusion.1
  53.4 1.7 %constant_dynamic-slice_fusion = bf16[128,1024]{1,0:T(8,128)(2,1)} fusion(bf16[256,1024]{1,0:T(8,128)(2,1)} %collective-permute-done.9.refs_1_.refs_8_.refs_18_, s32[]{:T(128)S(6)} %select_n.39), kind=kLoop, calls=%fused_computation.21 | loop fusion | bytes 524292 | tf_op jit(solution)/shard_map/dynamic_slice | solution.py:261
  55.1 1.2 %collective-permute-start.10 = (bf16[128,1024]{1,0:T(8,128)(2,1)}, bf16[128,1024]{1,0:T(8,128)(2,1)}, u32[]{:S(2)}, u32[]{:S(2)}) collective-permute-start(bf16[128,1024]{1,0:T(8,128)(2,1)} %constant_dynamic-slice_fusion), channel_id=1, source_target_pairs={{0,16},{16,32},{32,48},{48,64},{64,80},{80,96},{96,112},{112,0},{1... | collective-permute-start | bytes 786440 | tf_op jit(solution)/shard_map/ppermute | solution.py:263
  56.2 2.1 %pick.3.refs_1_ = bf16[256,256]{1,0:T(8,128)(2,1)} custom-call(s32[7]{0:T(128)S(1)} %copy-done.13, bf16[256,1024]{1,0:T(8,128)(2,1)S(1)} %tie.4.refs_0_.refs_3_.refs_13_, bf16[256,1024]{1,0:T(8,128)(2,1)} %collective-permute-done.9.refs_1_.refs_8_.refs_18_), custom_call_target="tpu_custom_call" | custom-call | bytes 262144 | tf_op jit(solution)/shard_map/pick/pallas_call | solution.py:103
  58.8 0.7 copy-done.5
  59.5 8.7 %all-to-all-start = ((f32[16,32,128]{2,1,0:T(8,128)}), f32[16,32,128]{2,1,0:T(8,128)}, u32[]{:S(2)}, u32[]{:S(2)}) async-start(f32[16,32,128]{2,1,0:T(8,128)} %bitcast.39), calls=%async_computation | async-start | bytes 524288 | tf_op jit(solution)/shard_map/all_to_all | solution.py:381
  68.2 1.0 copy-done.1
  69.2 1.0 copy-done.3
  70.3 5.1 %gram.3 = (f32[256,512]{1,0:T(8,128)}, f32[256,512]{1,0:T(8,128)}, f32[256,512]{1,0:T(8,128)S(1)}, f32[256,512]{1,0:T(8,128)S(1)}) custom-call(s32[7]{0:T(128)S(1)} %copy-done.13, bf16[256,1024]{1,0:T(8,128)(2,1)S(1)} %copy-done.1, bf16[256,1024]{1,0:T(8,128)(2,1)S(1)} %tie.3.refs_0_.refs_1_.refs_11_, ...), custom_call_target="tpu_custom_call" | custom-call | flops 1073741824 | bytes 7340032 | tf_op jit(solution)/shard_map/gram/pallas_call | solution.py:178
  75.4 0.8 copy-done.6
  76.2 0.8 copy-done.8
  77.5 1.1 all-to-all-done.parts
  78.6 1.0 sum.1.refs_24_
  79.6 1.0 copy-done.2
  80.6 1.0 copy-done.4
  81.7 4.2 %gram.2 = (f32[256,512]{1,0:T(8,128)S(1)}, f32[256,512]{1,0:T(8,128)S(1)}, f32[256,512]{1,0:T(8,128)S(1)}, f32[256,512]{1,0:T(8,128)S(1)}) custom-call(s32[7]{0:T(128)S(1)} %copy-done.13, bf16[256,1024]{1,0:T(8,128)(2,1)S(1)} %copy-done.2, bf16[256,1024]{1,0:T(8,128)(2,1)S(1)} %tie.3.refs_0_.refs_1_.refs_11_, ...), custom_call_target="tpu_custom_call" | custom-call | flops 1073741824 | bytes 7340032 | tf_op jit(solution)/shard_map/gram/pallas_call | solution.py:178
  86.5 1.1 add.48
  87.6 2.4 %collective-permute-start.18 = (f32[256,512]{1,0:T(8,128)S(1)}, f32[256,512]{1,0:T(8,128)S(1)}, u32[]{:S(2)}, u32[]{:S(2)}) collective-permute-start(f32[256,512]{1,0:T(8,128)S(1)} %add.48), channel_id=1, source_target_pairs={{0,128},{128,0},{1,129},{129,1},{2,130},{130,2},{3,131},{131,3},{4... | collective-permute-start | bytes 1572872 | tf_op jit(solution)/shard_map/ppermute | solution.py:418
  90.0 1.1 add.47
  91.0 1.3 %collective-permute-start.16 = (f32[256,512]{1,0:T(8,128)S(1)}, f32[256,512]{1,0:T(8,128)S(1)}, u32[]{:S(2)}, u32[]{:S(2)}) collective-permute-start(f32[256,512]{1,0:T(8,128)S(1)} %add.47), channel_id=1, source_target_pairs={{0,128},{128,0},{1,129},{129,1},{2,130},{130,2},{3,131},{131,3},{4... | collective-permute-start | bytes 1572872 | tf_op jit(solution)/shard_map/ppermute | solution.py:418
  92.4 0.5 collective-permute-start.19
  92.9 3.2 %collective-permute-done.19 = f32[32,128]{1,0:T(8,128)S(1)} collective-permute-done((f32[32,128]{1,0:T(8,128)S(1)}, f32[32,128]{1,0:T(8,128)S(1)}, u32[]{:S(2)}, u32[]{:S(2)}) %collective-permute-start.19) | collective-permute-done | bytes 16416 | tf_op jit(solution)/shard_map/ppermute | solution.py:393
  96.1 2.1 %collective-permute-start.20 = (f32[2,32,128]{2,1,0:T(8,128)S(1)}, f32[2,32,128]{2,1,0:T(8,128)S(1)}, u32[]{:S(2)}, u32[]{:S(2)}) collective-permute-start(f32[2,32,128]{2,1,0:T(8,128)S(1)} %pad_maximum_fusion.pair), channel_id=1, source_target_pairs={{0,8},{4,12},{8,0},{12,4},{1,9},{5,13},{9,1},{13,5},{2,10},{6,14},... | collective-permute-start | bytes 98312 | tf_op jit(solution)/shard_map/ppermute | solution.py:394
  98.3 3.3 %collective-permute-done.20.far_pair = f32[2,32,128]{2,1,0:T(8,128)S(1)} collective-permute-done((f32[2,32,128]{2,1,0:T(8,128)S(1)}, f32[2,32,128]{2,1,0:T(8,128)S(1)}, u32[]{:S(2)}, u32[]{:S(2)}) %collective-permute-start.20) | collective-permute-done | bytes 32800 | tf_op jit(solution)/shard_map/ppermute | solution.py:394
  101.6 1.3 %assemble.1 = f32[64,256]{1,0:T(8,128)} custom-call(s32[7]{0:T(128)S(1)} %copy-done.13, f32[2,32,128]{2,1,0:T(8,128)S(1)} %pad_maximum_fusion.pair, f32[2,32,128]{2,1,0:T(8,128)S(1)} %collective-permute-done.20.far_pair), custom_call_target="tpu_custom_call" | custom-call | bytes 131072 | tf_op jit(solution)/shard_map/assemble/pallas_call | solution.py:395
  102.8 1.1 collective-permute-done.18.high_got
  104.0 10.4 %collective-permute-done.16.low_got = f32[256,512]{1,0:T(8,128)S(1)} collective-permute-done((f32[256,512]{1,0:T(8,128)S(1)}, f32[256,512]{1,0:T(8,128)S(1)}, u32[]{:S(2)}, u32[]{:S(2)}) %collective-permute-start.16) | collective-permute-done | bytes 524320 | tf_op jit(solution)/shard_map/ppermute | solution.py:418
  114.3 1.6 %finish.1 = f32[256,1024]{1,0:T(8,128)} custom-call(f32[256,512]{1,0:T(8,128)S(1)} %get-tuple-element.18.low, f32[256,512]{1,0:T(8,128)S(1)} %get-tuple-element.19.high, f32[256,512]{1,0:T(8,128)S(1)} %collective-permute-done.13.low_core, f32[256,512]{1,0:T(8,128)S(1)} %collective-permute-done.14.high_core, f32[256,512]{1,0:T(8,128)S(1)} %collective-permute-done.16.low_got, ...), custom_call_target="tpu_custom_call" | custom-call | flops 1048576 | bytes 4194304 | tf_op jit(solution)/shard_map/finish/pallas_call | solution.py:222
  (53 shorter events, 1.7 us)
Async XLA Ops:
  0.6 14.9 %copy-start = (bf16[256,1,4096]{2,0,1:T(8,128)(2,1)S(1)}, bf16[256,1,4096]{2,0,1:T(8,128)(2,1)}, u32[]{:S(2)}) copy-start(bf16[256,1,4096]{2,0,1:T(8,128)(2,1)} %param.7) | copy-start | bytes 6291460
  1.3 14.2 %copy-start.16 = (s32[256,1,32]{0,2,1:T(8,128)S(1)}, s32[256,1,32]{0,2,1:T(8,128)}, u32[]{:S(2)}) copy-start(s32[256,1,32]{0,2,1:T(8,128)} %param.6) | copy-start | bytes 98308
  6.2 17.9 %collective-permute-start = (bf16[256,1024]{1,0:T(8,128)(2,1)}, bf16[256,1024]{1,0:T(8,128)(2,1)S(1)}, u32[]{:S(2)}, u32[]{:S(2)}) collective-permute-start(bf16[256,1024]{1,0:T(8,128)(2,1)} %get-tuple-element.14.refs_0_.refs_10_), channel_id=1, source_target_pairs={{0,16},{16,32},{32,48},{48,64},{64,80},{80,96},{96,112},{112,0},{1... | collective-permute-start | bytes 1572872 | tf_op jit(solution)/shard_map/ppermute | solution.py:262
  8.2 16.0 %collective-permute-start.1 = (bf16[128,256]{1,0:T(8,128)(2,1)}, bf16[128,256]{1,0:T(8,128)(2,1)S(1)}, u32[]{:S(2)}, u32[]{:S(2)}) collective-permute-start(bf16[128,256]{1,0:T(8,128)(2,1)} %get-tuple-element.15), channel_id=1, source_target_pairs={{0,64},{16,80},{32,96},{48,112},{64,0},{80,16},{96,32},{112,48},{1... | collective-permute-start | bytes 196616 | tf_op jit(solution)/shard_map/ppermute | solution.py:265
  14.5 13.5 %collective-permute-start.7 = (bf16[256,1024]{1,0:T(8,128)(2,1)}, bf16[256,1024]{1,0:T(8,128)(2,1)}, u32[]{:S(2)}, u32[]{:S(2)}) collective-permute-start(bf16[256,1024]{1,0:T(8,128)(2,1)} %get-tuple-element.16.refs_5_.refs_15_), channel_id=1, source_target_pairs={{0,16},{16,32},{32,48},{48,64},{64,80},{80,96},{96,112},{112,0},{1... | collective-permute-start | bytes 1572872 | tf_op jit(solution)/shard_map/ppermute | solution.py:263
  18.6 27.9 %copy-start.13 = (s32[7]{0:T(128)S(1)}, s32[7]{0:T(128)}, u32[]{:S(2)}) copy-start(s32[7]{0:T(128)} %stack.40.at) | copy-start | bytes 88
  18.6 27.9 %copy-start.14 = (s32[1024]{0:T(1024)S(1)}, s32[1024]{0:T(1024)}, u32[]{:S(2)}) copy-start(s32[1024]{0:T(1024)} %param.9) | copy-start | bytes 12292
  18.6 27.9 %copy-start.15 = (s32[256]{0:T(256)S(1)}, s32[256]{0:T(256)}, u32[]{:S(2)}) copy-start(s32[256]{0:T(256)} %param.8) | copy-start | bytes 3076
  24.1 10.5 %collective-permute-start.2 = (bf16[256,1024]{1,0:T(8,128)(2,1)S(1)}, bf16[256,1024]{1,0:T(8,128)(2,1)}, u32[]{:S(2)}, u32[]{:S(2)}) collective-permute-start(bf16[256,1024]{1,0:T(8,128)(2,1)S(1)} %tie.3.refs_0_.refs_1_.refs_11_), channel_id=1, source_target_pairs={{0,16},{16,32},{32,48},{48,64},{64,80},{80,96},{96,112},{112,0},{1... | collective-permute-start | bytes 1572872 | tf_op jit(solution)/shard_map/ppermute | solution.py:262
  28.0 12.2 %collective-permute-start.8 = (bf16[256,1024]{1,0:T(8,128)(2,1)}, bf16[256,1024]{1,0:T(8,128)(2,1)}, u32[]{:S(2)}, u32[]{:S(2)}) collective-permute-start(bf16[256,1024]{1,0:T(8,128)(2,1)} %collective-permute-done.7.refs_1_.refs_6_.refs_16_), channel_id=1, source_target_pairs={{0,16},{16,32},{32,48},{48,64},{64,80},{80,96},{96,112},{112,0},{1... | collective-permute-start | bytes 1572872 | tf_op jit(solution)/shard_map/ppermute | solution.py:263
  28.7 11.6 %collective-permute-start.4 = (f32[128,256]{1,0:T(8,128)}, f32[128,256]{1,0:T(8,128)}, u32[]{:S(2)}, u32[]{:S(2)}) collective-permute-start(f32[128,256]{1,0:T(8,128)} %dynamic-slice_bitcast_fusion), channel_id=1, source_target_pairs={{0,8},{4,12},{8,0},{12,4},{1,9},{5,13},{9,1},{13,5},{2,10},{6,14},... | collective-permute-start | bytes 393224 | tf_op jit(solution)/shard_map/ppermute | solution.py:346
  34.6 18.0 %collective-permute-start.3 = (bf16[256,1024]{1,0:T(8,128)(2,1)}, bf16[256,1024]{1,0:T(8,128)(2,1)S(1)}, u32[]{:S(2)}, u32[]{:S(2)}) collective-permute-start(bf16[256,1024]{1,0:T(8,128)(2,1)} %collective-permute-done.2.refs_2_.refs_12_), channel_id=1, source_target_pairs={{0,16},{16,32},{32,48},{48,64},{64,80},{80,96},{96,112},{112,0},{1... | collective-permute-start | bytes 1572872 | tf_op jit(solution)/shard_map/ppermute | solution.py:262
  40.3 13.1 %collective-permute-start.9 = (bf16[256,1024]{1,0:T(8,128)(2,1)}, bf16[256,1024]{1,0:T(8,128)(2,1)}, u32[]{:S(2)}, u32[]{:S(2)}) collective-permute-start(bf16[256,1024]{1,0:T(8,128)(2,1)} %collective-permute-done.8.refs_3_.refs_7_.refs_17_), channel_id=1, source_target_pairs={{0,16},{16,32},{32,48},{48,64},{64,80},{80,96},{96,112},{112,0},{1... | collective-permute-start | bytes 1572872 | tf_op jit(solution)/shard_map/ppermute | solution.py:263
  41.2 0.7 copy-start.10
  41.9 4.6 %collective-permute-start.5 = (f32[64,256]{1,0:T(8,128)S(1)}, f32[64,256]{1,0:T(8,128)S(1)}, u32[]{:S(2)}, u32[]{:S(2)}) collective-permute-start(f32[64,256]{1,0:T(8,128)S(1)} %constant_dynamic-slice_fusion.2), channel_id=1, source_target_pairs={{0,4},{4,0},{8,12},{12,8},{1,5},{5,1},{9,13},{13,9},{2,6},{6,2},{1... | collective-permute-start | bytes 196616 | tf_op jit(solution)/shard_map/ppermute | solution.py:348
  46.5 0.9 copy-start.11
  51.1 17.1 %copy-start.12 = (bf16[128,256]{1,0:T(8,128)(2,1)S(1)}, bf16[128,256]{1,0:T(8,128)(2,1)}, u32[]{:S(2)}) copy-start(bf16[128,256]{1,0:T(8,128)(2,1)} %get-tuple-element.17.refs_20_) | copy-start | bytes 196612
  51.1 17.1 %collective-permute-start.11 = (bf16[512,256]{1,0:T(8,128)(2,1)}, bf16[512,256]{1,0:T(8,128)(2,1)}, u32[]{:S(2)}, u32[]{:S(2)}) collective-permute-start(bf16[512,256]{1,0:T(8,128)(2,1)} %pick.2), channel_id=1, source_target_pairs={{0,2},{2,0},{1,3},{3,1},{4,6},{6,4},{5,7},{7,5},{8,10},{10,8},{9,1... | collective-permute-start | bytes 786440 | tf_op jit(solution)/shard_map/ppermute | solution.py:270
  53.4 14.8 %collective-permute-start.6 = (bf16[128,1024]{1,0:T(8,128)(2,1)}, bf16[128,1024]{1,0:T(8,128)(2,1)S(1)}, u32[]{:S(2)}, u32[]{:S(2)}) collective-permute-start(bf16[128,1024]{1,0:T(8,128)(2,1)} %constant_dynamic-slice_fusion.1), channel_id=1, source_target_pairs={{0,16},{16,32},{32,48},{48,64},{64,80},{80,96},{96,112},{112,0},{1... | collective-permute-start | bytes 786440 | tf_op jit(solution)/shard_map/ppermute | solution.py:262
  55.1 13.1 %collective-permute-start.10 = (bf16[128,1024]{1,0:T(8,128)(2,1)}, bf16[128,1024]{1,0:T(8,128)(2,1)}, u32[]{:S(2)}, u32[]{:S(2)}) collective-permute-start(bf16[128,1024]{1,0:T(8,128)(2,1)} %constant_dynamic-slice_fusion), channel_id=1, source_target_pairs={{0,16},{16,32},{32,48},{48,64},{64,80},{80,96},{96,112},{112,0},{1... | collective-permute-start | bytes 786440 | tf_op jit(solution)/shard_map/ppermute | solution.py:263
  58.3 9.8 %collective-permute-start.12 = (bf16[256,256]{1,0:T(8,128)(2,1)}, bf16[256,256]{1,0:T(8,128)(2,1)}, u32[]{:S(2)}, u32[]{:S(2)}) collective-permute-start(bf16[256,256]{1,0:T(8,128)(2,1)} %pick.3.refs_1_), channel_id=1, source_target_pairs={{0,2},{2,0},{1,3},{3,1},{4,6},{6,4},{5,7},{7,5},{8,10},{10,8},{9,1... | collective-permute-start | bytes 393224 | tf_op jit(solution)/shard_map/ppermute | solution.py:273
  58.8 0.7 copy-start.5
  59.5 19.1 %all-to-all-start = ((f32[16,32,128]{2,1,0:T(8,128)}), f32[16,32,128]{2,1,0:T(8,128)}, u32[]{:S(2)}, u32[]{:S(2)}) async-start(f32[16,32,128]{2,1,0:T(8,128)} %bitcast.39), calls=%async_computation | async-start | bytes 524288 | tf_op jit(solution)/shard_map/all_to_all | solution.py:381
  68.2 1.0 copy-start.1
  69.2 1.0 copy-start.3
  75.4 0.8 copy-start.6
  76.2 0.8 copy-start.8
  77.0 9.5 %collective-permute-start.17 = (f32[256,512]{1,0:T(8,128)}, f32[256,512]{1,0:T(8,128)}, u32[]{:S(2)}, u32[]{:S(2)}) collective-permute-start(f32[256,512]{1,0:T(8,128)} %get-tuple-element.25), channel_id=1, source_target_pairs={{0,1},{1,0},{2,3},{3,2},{4,5},{5,4},{6,7},{7,6},{8,9},{9,8},{10,11... | collective-permute-start | bytes 1572872 | tf_op jit(solution)/shard_map/ppermute | solution.py:277
  77.0 13.0 %collective-permute-start.15 = (f32[256,512]{1,0:T(8,128)}, f32[256,512]{1,0:T(8,128)}, u32[]{:S(2)}, u32[]{:S(2)}) collective-permute-start(f32[256,512]{1,0:T(8,128)} %get-tuple-element.23), channel_id=1, source_target_pairs={{0,1},{1,0},{2,3},{3,2},{4,5},{5,4},{6,7},{7,6},{8,9},{9,8},{10,11... | collective-permute-start | bytes 1572872 | tf_op jit(solution)/shard_map/ppermute | solution.py:277
  79.6 1.0 copy-start.2
  80.6 1.0 copy-start.4
  81.7 4.8 %copy-start.9 = (f32[256,512]{1,0:T(8,128)S(1)}, f32[256,512]{1,0:T(8,128)}, u32[]{:S(2)}) copy-start(f32[256,512]{1,0:T(8,128)} %copy-done.8) | copy-start | bytes 1572868
  81.7 8.3 %copy-start.7 = (f32[256,512]{1,0:T(8,128)S(1)}, f32[256,512]{1,0:T(8,128)}, u32[]{:S(2)}) copy-start(f32[256,512]{1,0:T(8,128)} %copy-done.6) | copy-start | bytes 1572868
  85.9 16.9 %collective-permute-start.13 = (f32[256,512]{1,0:T(8,128)S(1)}, f32[256,512]{1,0:T(8,128)S(1)}, u32[]{:S(2)}, u32[]{:S(2)}) collective-permute-start(f32[256,512]{1,0:T(8,128)S(1)} %get-tuple-element.20), channel_id=1, source_target_pairs={{0,1},{1,0},{2,3},{3,2},{4,5},{5,4},{6,7},{7,6},{8,9},{9,8},{10,11... | collective-permute-start | bytes 1572872 | tf_op jit(solution)/shard_map/ppermute | solution.py:280
  86.0 16.8 %collective-permute-start.14 = (f32[256,512]{1,0:T(8,128)S(1)}, f32[256,512]{1,0:T(8,128)S(1)}, u32[]{:S(2)}, u32[]{:S(2)}) collective-permute-start(f32[256,512]{1,0:T(8,128)S(1)} %get-tuple-element.21), channel_id=1, source_target_pairs={{0,1},{1,0},{2,3},{3,2},{4,5},{5,4},{6,7},{7,6},{8,9},{9,8},{10,11... | collective-permute-start | bytes 1572872 | tf_op jit(solution)/shard_map/ppermute | solution.py:280
  87.6 16.4 %collective-permute-start.18 = (f32[256,512]{1,0:T(8,128)S(1)}, f32[256,512]{1,0:T(8,128)S(1)}, u32[]{:S(2)}, u32[]{:S(2)}) collective-permute-start(f32[256,512]{1,0:T(8,128)S(1)} %add.48), channel_id=1, source_target_pairs={{0,128},{128,0},{1,129},{129,1},{2,130},{130,2},{3,131},{131,3},{4... | collective-permute-start | bytes 1572872 | tf_op jit(solution)/shard_map/ppermute | solution.py:418
  91.0 23.3 %collective-permute-start.16 = (f32[256,512]{1,0:T(8,128)S(1)}, f32[256,512]{1,0:T(8,128)S(1)}, u32[]{:S(2)}, u32[]{:S(2)}) collective-permute-start(f32[256,512]{1,0:T(8,128)S(1)} %add.47), channel_id=1, source_target_pairs={{0,128},{128,0},{1,129},{129,1},{2,130},{130,2},{3,131},{131,3},{4... | collective-permute-start | bytes 1572872 | tf_op jit(solution)/shard_map/ppermute | solution.py:418
  92.4 3.7 %collective-permute-start.19 = (f32[32,128]{1,0:T(8,128)S(1)}, f32[32,128]{1,0:T(8,128)S(1)}, u32[]{:S(2)}, u32[]{:S(2)}) collective-permute-start(f32[32,128]{1,0:T(8,128)S(1)} %sum.1.refs_24_), channel_id=1, source_target_pairs={{0,4},{4,0},{8,12},{12,8},{1,5},{5,1},{9,13},{13,9},{2,6},{6,2},{1... | collective-permute-start | bytes 49160 | tf_op jit(solution)/shard_map/ppermute | solution.py:393
  96.1 5.4 %collective-permute-start.20 = (f32[2,32,128]{2,1,0:T(8,128)S(1)}, f32[2,32,128]{2,1,0:T(8,128)S(1)}, u32[]{:S(2)}, u32[]{:S(2)}) collective-permute-start(f32[2,32,128]{2,1,0:T(8,128)S(1)} %pad_maximum_fusion.pair), channel_id=1, source_target_pairs={{0,8},{4,12},{8,0},{12,4},{1,9},{5,13},{9,1},{13,5},{2,10},{6,14},... | collective-permute-start | bytes 98312 | tf_op jit(solution)/shard_map/ppermute | solution.py:394

commit v5 on v4

--- a/solution.py
+++ b/solution.py
@@ -76,14 +76,14 @@
             ],
         ),
         out_shape=[side, side] + [jax.ShapeDtypeStruct((rows // 2, 256), jnp.bfloat16)] * 2,
-        compiler_params=params(58),
+        compiler_params=params(61),
         cost_estimate=cost(1 << 25, 2 << 20),
         name="dequant",
     )(at, exps, mantissas, mantissas, mantissas)
 
 
 def pick_kernel(count, at, *refs):
-    sides, out = refs[:-1], refs[-1]
+    sides, out = refs[: 2 * count], refs[-1]
     row = 0
     for i in range(count):
         rows = sides[2 * i].shape[0]
@@ -97,9 +97,10 @@
     return pl.BlockSpec((rows, 128), lambda g, at: (0, at[AT_Z]))
 
 
-def pick(at, pieces):
+def pick(at, pieces, *after):
     rows = sum(n for n, _, _, _ in pieces)
     specs = [lanes_at_z(n, by_core) for n, by_core, _, _ in pieces for _ in range(2)]
+    specs += [pl.BlockSpec(memory_space=pl.ANY)] * len(after)
     return pl.pallas_call(
         functools.partial(pick_kernel, len(pieces)),
         grid_spec=pltpu.PrefetchScalarGridSpec(
@@ -110,7 +111,7 @@
         compiler_params=params(6),
         cost_estimate=cost(0, rows * 1024),
         name="pick",
-    )(at, *[side for _, _, low, high in pieces for side in (low, high)])
+    )(at, *[side for _, _, low, high in pieces for side in (low, high)], *after)
 
 
 def gram_kernel(sizes, kept, at, *refs):
@@ -248,7 +249,7 @@
     )(value, *earlier)
 
 
-def fisher_terms(at, mantissas, exps, scores, placed):
+def fisher_terms(at, mantissas, exps, pair, placed):
     core = lax.axis_index("core")
     rows = mantissas.shape[0]
     low, high, own, far = dequant(at, exps, mantissas)
@@ -262,20 +263,21 @@
         low = lax.ppermute(low, ("z", "core"), RING)
         high = lax.ppermute(high, ("z", "core"), RING)
         if step == 1:
-            far = lax.ppermute(far, "z", [(i, (i + Z // 2) % Z) for i in range(Z)])
-            low = tie(low, far, scores)
-        if step == 3:
+            far = lax.ppermute(tie(far, low), "z", [(i, (i + Z // 2) % Z) for i in range(Z)])
+            low = tie(low, pair)
+        if step == 2:
             low = tie(low, placed)
+            placed = tie(placed, high)
         pieces.append((low.shape[0], False, low, high))
     near = lax.ppermute(pick(at, pieces[1:3]), "yl", SWAP)
-    third = pick(at, pieces[3:4])
-    mine = own_slots(tie(placed, third))
+    mine = own_slots(placed)
+    third = pick(at, pieces[3:4], mine, far)
     third = lax.ppermute(third, "yl", SWAP)
     received = (own, near, third, far)
 
     *given_other, low_given, high_given = gram(at, pieces, received, False)
     swapped = [lax.ppermute(g, "core", SWAP) for g in given_other]
-    *kept_other, low_kept, high_kept = gram(at, pieces, received, True, mine)
+    *kept_other, low_kept, high_kept = gram(at, pieces, received, True)
     given = [add(g, s) for g, s in zip((low_given, high_given), swapped)]
     kept = [lax.ppermute(k, "core", SWAP) for k in kept_other]
     return given, [low_kept, high_kept, *kept], mine
@@ -358,7 +360,7 @@
         cost_estimate=cost(1 << 28, 1 << 20),
         name="place",
     )(at, pair.reshape(shapes[0]), got, doc_ids.reshape(1, rows), owners.reshape(1, docs))
-    return scores, placed
+    return pair, placed
 
 
 def assemble_kernel(at, pair, far_pair, out):
@@ -413,8 +415,8 @@
     yl, core = lax.axis_index("yl"), lax.axis_index("core")
     other = (1 - yl) * Z
     at = jnp.stack([z, core, yl, other + z, other + lax.rem(z + Z // 2, Z), yh, x]).astype(jnp.int32)
-    scores, placed = placed_scores(at, mantissas, powers(exponents), queries[:, 0, :], doc_ids, owners)
-    given, kept, mine = fisher_terms(at, mantissas, exponents.T, scores, placed)
+    pair, placed = placed_scores(at, mantissas, powers(exponents), queries[:, 0, :], doc_ids, owners)
+    given, kept, mine = fisher_terms(at, mantissas, exponents.T, pair, placed)
     got = [lax.ppermute(g, "yh", SWAP) for g in given]
     return finish(1.0 / total_rows, kept + got)[None], doc_block(at, mine)
 

time: 117 us -> 118 us (level)
  waiting for transfers between devices: 42.1 us -> 51.9 us
  local copies, waits for them, and re-layouts: 11.7 us -> 5.05 us
  Pallas kernels: 26 us -> 23.4 us
  starting transfers between devices: 31.3 us -> 32.9 us
    unnamed x34 -> x16, local copies, waits for them, and re-layouts: 8.06 us -> 1.08 us
    ppermute x4, waiting for transfers between devices: 3.81 us -> 8.87 us  [fisher_terms(): low = lax.ppermute(low, ('z', 'core'), RING)]
    ppermute x1, waiting for transfers between devices: 0.01 us -> 4.37 us  [placed_scores(): lax.ppermute(lax.dynamic_slice_in_dim(scores, (1 - upper) * 2 * share, 2...]
    ppermute x4, waiting for transfers between devices: 9.5 us -> 5.62 us  [fisher_terms(): high = lax.ppermute(high, ('z', 'core'), RING)]
    ppermute x1, waiting for transfers between devices: 0.01 us -> 3.62 us  [fisher_terms(): third = lax.ppermute(third, 'yl', SWAP)]
    ppermute x1, starting transfers between devices: 6.29 us -> 3.57 us  [fisher_terms(): lax.ppermute(tie(far, low), 'z', [(i, (i + Z // 2) % Z) for i in range(Z)])]
    pallas_call x2, Pallas kernels: 2.16 us -> 0.16 us  [add(): pl.pallas_call(add_kernel, grid=(2,), in_specs=[spec, spec], out_specs=sp...]
    ppermute x4, starting transfers between devices: 2 us -> 3.79 us  [fisher_terms(): low = lax.ppermute(low, ('z', 'core'), RING)]
  transfers between devices with their start and end apart: 22 -> 22, of which waited for: 10 -> 11; matrix products, arithmetic and copies ran while one was open for 6% -> 6% of each run, Pallas kernels for 17% -> 11%
where the time goes in v5:
time: 118 us; the launch traced here: 117 us
  waiting for transfers between devices  51.9 us (44%)
  starting transfers between devices  32.9 us (28%)
  Pallas kernels  23.4 us (20%)
  local copies, waits for them, and re-layouts  5.05 us (4%)
  matrix products  3.06 us (3%)
    ppermute x2, waiting for transfers between devices, per_device(): got = [lax.ppermute(g, 'yh', SWAP) for g in given]  12.7 us
    all_to_all x1, starting transfers between devices, own_slots(): lax.all_to_all(placed.reshape(YH * Z, half, double), ('yh', 'z'), 0, 0, t...  9.18 us
    ppermute x4, waiting for transfers between devices, fisher_terms(): low = lax.ppermute(low, ('z', 'core'), RING)  8.87 us
    pallas_call x2, Pallas kernels, gram(): pl.pallas_call(functools.partial(gram_kernel, sizes, kept), grid_spec=plt...  8.62 us
    ppermute x1, waiting for transfers between devices, fisher_terms(): lax.ppermute(tie(far, low), 'z', [(i, (i + Z // 2) % Z) for i in range(Z)])  6.26 us
    ppermute x4, waiting for transfers between devices, fisher_terms(): high = lax.ppermute(high, ('z', 'core'), RING)  5.62 us
    pallas_call x1, Pallas kernels, dequant(): pl.pallas_call(dequant_kernel, grid_spec=pltpu.PrefetchScalarGridSpec(num...  4.94 us
    ppermute x1, waiting for transfers between devices, placed_scores(): lax.ppermute(lax.dynamic_slice_in_dim(scores, (1 - upper) * 2 * share, 2...  4.37 us
  transfers between devices with their start and end apart: 22, of which 11 were waited for; matrix products, arithmetic and copies ran while one was open for 6% of the time, Pallas kernels for 11%

profile of v5, /device:TPU:2, one launch (start us, length us, event | category | flops | bytes accessed | tf_op | source)
XLA Modules:
  0.0 117.2 jit_solution(547303019239473129)
XLA Ops:
  0.6 0.0 copy-start
  0.7 0.6 stack.40.at
  1.3 4.9 %dequant.1 = (bf16[256,1024]{1,0:T(8,128)(2,1)}, bf16[256,1024]{1,0:T(8,128)(2,1)}, bf16[128,256]{1,0:T(8,128)(2,1)}, bf16[128,256]{1,0:T(8,128)(2,1)}) custom-call(s32[7]{0:T(128)} %stack.40.at, s32[32,256]{1,0:T(8,128)} %bitcast.46, bf16[256,4096]{1,0:T(8,128)(2,1)} %bitcast.42, bf16[256,4096]{1,0:T(8,128)(2,1)} %bitcast.43, bf16[256,4096]{1,0:T(8,128)(2,1)} %bitcast.44), custom_call_target="tpu_custom_call" | custom-call | flops 33554432 | bytes 2097152 | tf_op jit(solution)/shard_map/dequant/pallas_call | solution.py:60
  6.2 2.0 %collective-permute-start.6 = (bf16[256,1024]{1,0:T(8,128)(2,1)}, bf16[256,1024]{1,0:T(8,128)(2,1)}, u32[]{:S(2)}, u32[]{:S(2)}) collective-permute-start(bf16[256,1024]{1,0:T(8,128)(2,1)} %get-tuple-element.15.refs_5_.refs_15_), channel_id=1, source_target_pairs={{0,16},{16,32},{32,48},{48,64},{64,80},{80,96},{96,112},{112,0},{1... | collective-permute-start | bytes 1572872 | tf_op jit(solution)/shard_map/ppermute | solution.py:264
  8.2 1.9 %collective-permute-start = (bf16[256,1024]{1,0:T(8,128)(2,1)}, bf16[256,1024]{1,0:T(8,128)(2,1)S(1)}, u32[]{:S(2)}, u32[]{:S(2)}) collective-permute-start(bf16[256,1024]{1,0:T(8,128)(2,1)} %get-tuple-element.14.refs_0_.refs_10_), channel_id=1, source_target_pairs={{0,16},{16,32},{32,48},{48,64},{64,80},{80,96},{96,112},{112,0},{1... | collective-permute-start | bytes 1572872 | tf_op jit(solution)/shard_map/ppermute | solution.py:263
  10.1 3.1 %fusion.1 = f32[256,256]{0,1:T(8,128)S(1)} fusion(bf16[256,1,4096]{2,0,1:T(8,128)(2,1)S(1)} %copy-done, s32[4096]{0:T(1024)S(1)} %add_select_fusion, s32[256,1,32]{0,2,1:T(8,128)S(1)} %copy-done.7, bf16[256,1,4096]{2,0,1:T(8,128)(2,1)} %param.5), kind=kOutput, calls=%fused_computation.2 | convolution fusion | flops 606232576 | bytes 4505600 | tf_op jit(solution)/shard_map/dot_general | solution.py:344
  13.2 0.0 copy-start.5
  13.3 2.2 %collective-permute-start.1 = (f32[128,256]{1,0:T(8,128)S(1)}, f32[128,256]{1,0:T(8,128)S(1)}, u32[]{:S(2)}, u32[]{:S(2)}) collective-permute-start(f32[128,256]{1,0:T(8,128)S(1)} %dynamic-slice_bitcast_fusion), channel_id=1, source_target_pairs={{0,8},{4,12},{8,0},{12,4},{1,9},{5,13},{9,1},{13,5},{2,10},{6,14},... | collective-permute-start | bytes 393224 | tf_op jit(solution)/shard_map/ppermute | solution.py:348
  15.5 4.4 %collective-permute-done.1 = f32[128,256]{1,0:T(8,128)S(1)} collective-permute-done((f32[128,256]{1,0:T(8,128)S(1)}, f32[128,256]{1,0:T(8,128)S(1)}, u32[]{:S(2)}, u32[]{:S(2)}) %collective-permute-start.1) | collective-permute-done | bytes 131104 | tf_op jit(solution)/shard_map/ppermute | solution.py:348
  19.9 5.3 %collective-permute-done.refs_0_.refs_1_ = bf16[256,1024]{1,0:T(8,128)(2,1)S(1)} collective-permute-done((bf16[256,1024]{1,0:T(8,128)(2,1)}, bf16[256,1024]{1,0:T(8,128)(2,1)S(1)}, u32[]{:S(2)}, u32[]{:S(2)}) %collective-permute-start) | collective-permute-done | bytes 524320 | tf_op jit(solution)/shard_map/ppermute | solution.py:263
  25.2 0.1 collective-permute-start.7
  25.3 0.6 collective-permute-start.3
  25.9 4.0 %collective-permute-done.3.got = f32[64,256]{1,0:T(8,128)S(1)} collective-permute-done((f32[64,256]{1,0:T(8,128)S(1)}, f32[64,256]{1,0:T(8,128)S(1)}, u32[]{:S(2)}, u32[]{:S(2)}) %collective-permute-start.3) | collective-permute-done | bytes 65568 | tf_op jit(solution)/shard_map/ppermute | solution.py:350
  29.9 2.2 %place.1.refs_1_.refs_0_ = f32[512,128]{1,0:T(8,128)} custom-call(s32[7]{0:T(128)S(1)} %copy-done.4, f32[2,64,256]{2,1,0:T(8,128)S(1)} %bitcast.38, f32[64,256]{1,0:T(8,128)S(1)} %collective-permute-done.3.got, s32[1,256]{1,0:T(1,128)S(1)} %bitcast.41, s32[1,1024]{1,0:T(1,128)S(1)} %bitcast.40), custom_call_target="tpu_custom_call" | custom-call | flops 268435456 | bytes 1048576 | tf_op jit(solution)/shard_map/place/pallas_call | solution.py:352
  32.0 3.6 %collective-permute-done.2.refs_0_ = bf16[256,1024]{1,0:T(8,128)(2,1)} collective-permute-done((bf16[256,1024]{1,0:T(8,128)(2,1)S(1)}, bf16[256,1024]{1,0:T(8,128)(2,1)}, u32[]{:S(2)}, u32[]{:S(2)}) %collective-permute-start.2) | collective-permute-done | bytes 524320 | tf_op jit(solution)/shard_map/ppermute | solution.py:263
  35.6 5.6 %collective-permute-done.7.refs_3_.refs_1_.refs_7_.refs_17_ = bf16[256,1024]{1,0:T(8,128)(2,1)} collective-permute-done((bf16[256,1024]{1,0:T(8,128)(2,1)}, bf16[256,1024]{1,0:T(8,128)(2,1)}, u32[]{:S(2)}, u32[]{:S(2)}) %collective-permute-start.7) | collective-permute-done | bytes 524320 | tf_op jit(solution)/shard_map/ppermute | solution.py:264
  41.3 9.2 %all-to-all-start = ((f32[16,32,128]{2,1,0:T(8,128)}), f32[16,32,128]{2,1,0:T(8,128)}, u32[]{:S(2)}, u32[]{:S(2)}) async-start(f32[16,32,128]{2,1,0:T(8,128)} %bitcast.16), calls=%async_computation | async-start | bytes 524288 | tf_op jit(solution)/shard_map/all_to_all | solution.py:383
  50.5 2.2 %pick.2 = bf16[512,256]{1,0:T(8,128)(2,1)} custom-call(s32[7]{0:T(128)S(1)} %copy-done.4, bf16[256,1024]{1,0:T(8,128)(2,1)S(1)} %tie.4.refs_0_.refs_1_.refs_11_, bf16[256,1024]{1,0:T(8,128)(2,1)} %collective-permute-done.6.refs_1_.refs_6_.refs_16_, bf16[256,1024]{1,0:T(8,128)(2,1)} %tie.5.refs_2_.refs_12_, ...), custom_call_target="tpu_custom_call" | custom-call | bytes 524288 | tf_op jit(solution)/shard_map/pick/pallas_call | solution.py:104
  52.7 0.7 collective-permute-start.10
  53.4 1.7 %constant_dynamic-slice_fusion.1 = bf16[128,1024]{1,0:T(8,128)(2,1)} fusion(bf16[256,1024]{1,0:T(8,128)(2,1)} %collective-permute-done.4.refs_0_.refs_3_.refs_13_, s32[]{:T(128)S(6)} %select_n.39), kind=kLoop, calls=%fused_computation.22 | loop fusion | bytes 524292 | tf_op jit(solution)/shard_map/dynamic_slice | solution.py:261
  55.0 1.9 %collective-permute-start.5 = (bf16[128,1024]{1,0:T(8,128)(2,1)}, bf16[128,1024]{1,0:T(8,128)(2,1)S(1)}, u32[]{:S(2)}, u32[]{:S(2)}) collective-permute-start(bf16[128,1024]{1,0:T(8,128)(2,1)} %constant_dynamic-slice_fusion.1), channel_id=1, source_target_pairs={{0,16},{16,32},{32,48},{48,64},{64,80},{80,96},{96,112},{112,0},{1... | collective-permute-start | bytes 786440 | tf_op jit(solution)/shard_map/ppermute | solution.py:263
  56.9 1.7 %constant_dynamic-slice_fusion = bf16[128,1024]{1,0:T(8,128)(2,1)} fusion(bf16[256,1024]{1,0:T(8,128)(2,1)} %collective-permute-done.8.refs_1_.refs_8_.refs_18_, s32[]{:T(128)S(6)} %select_n.39), kind=kLoop, calls=%fused_computation.21 | loop fusion | bytes 524292 | tf_op jit(solution)/shard_map/dynamic_slice | solution.py:262
  58.6 1.5 %collective-permute-start.9 = (bf16[128,1024]{1,0:T(8,128)(2,1)}, bf16[128,1024]{1,0:T(8,128)(2,1)}, u32[]{:S(2)}, u32[]{:S(2)}) collective-permute-start(bf16[128,1024]{1,0:T(8,128)(2,1)} %constant_dynamic-slice_fusion), channel_id=1, source_target_pairs={{0,16},{16,32},{32,48},{48,64},{64,80},{80,96},{96,112},{112,0},{1... | collective-permute-start | bytes 786440 | tf_op jit(solution)/shard_map/ppermute | solution.py:264
  60.0 3.6 %collective-permute-start.11 = (bf16[128,256]{1,0:T(8,128)(2,1)}, bf16[128,256]{1,0:T(8,128)(2,1)S(1)}, u32[]{:S(2)}, u32[]{:S(2)}) collective-permute-start(bf16[128,256]{1,0:T(8,128)(2,1)} %tie.7), channel_id=1, source_target_pairs={{0,64},{16,80},{32,96},{48,112},{64,0},{80,16},{96,32},{112,48},{1... | collective-permute-start | bytes 196616 | tf_op jit(solution)/shard_map/ppermute | solution.py:266
  63.6 1.0 sum.1.refs_2_
  64.6 6.3 %collective-permute-done.11.refs_3_.refs_23_ = bf16[128,256]{1,0:T(8,128)(2,1)S(1)} collective-permute-done((bf16[128,256]{1,0:T(8,128)(2,1)}, bf16[128,256]{1,0:T(8,128)(2,1)S(1)}, u32[]{:S(2)}, u32[]{:S(2)}) %collective-permute-start.11) | collective-permute-done | bytes 65568 | tf_op jit(solution)/shard_map/ppermute | solution.py:266
  70.8 1.4 %pick.3 = bf16[256,256]{1,0:T(8,128)(2,1)S(1)} custom-call(s32[7]{0:T(128)S(1)} %copy-done.4, bf16[256,1024]{1,0:T(8,128)(2,1)} %collective-permute-done.4.refs_0_.refs_3_.refs_13_, bf16[256,1024]{1,0:T(8,128)(2,1)} %collective-permute-done.8.refs_1_.refs_8_.refs_18_, f32[32,128]{1,0:T(8,128)S(1)} %sum.1.refs_2_, ...), custom_call_target="tpu_custom_call" | custom-call | bytes 262144 | tf_op jit(solution)/shard_map/pick/pallas_call | solution.py:104
  72.3 1.6 %collective-permute-start.12 = (bf16[256,256]{1,0:T(8,128)(2,1)S(1)}, bf16[256,256]{1,0:T(8,128)(2,1)S(1)}, u32[]{:S(2)}, u32[]{:S(2)}) collective-permute-start(bf16[256,256]{1,0:T(8,128)(2,1)S(1)} %pick.3), channel_id=1, source_target_pairs={{0,2},{2,0},{1,3},{3,1},{4,6},{6,4},{5,7},{7,5},{8,10},{10,8},{9,1... | collective-permute-start | bytes 393224 | tf_op jit(solution)/shard_map/ppermute | solution.py:275
  73.9 3.6 %collective-permute-done.12.refs_22_ = bf16[256,256]{1,0:T(8,128)(2,1)S(1)} collective-permute-done((bf16[256,256]{1,0:T(8,128)(2,1)S(1)}, bf16[256,256]{1,0:T(8,128)(2,1)S(1)}, u32[]{:S(2)}, u32[]{:S(2)}) %collective-permute-start.12) | collective-permute-done | bytes 131104 | tf_op jit(solution)/shard_map/ppermute | solution.py:275
  77.5 1.0 copy-done.2
  78.6 4.3 %gram.3 = (f32[256,512]{1,0:T(8,128)S(1)}, f32[256,512]{1,0:T(8,128)S(1)}, f32[256,512]{1,0:T(8,128)S(1)}, f32[256,512]{1,0:T(8,128)S(1)}) custom-call(s32[7]{0:T(128)S(1)} %copy-done.4, bf16[256,1024]{1,0:T(8,128)(2,1)S(1)} %copy-done.1, bf16[256,1024]{1,0:T(8,128)(2,1)S(1)} %tie.4.refs_0_.refs_1_.refs_11_, bf16[256,1024]{1,0:T(8,128)(2,1)} %tie.5.refs_2_.refs_12_, ...), custom_call_target="tpu_custom_call" | custom-call | flops 1073741824 | bytes 7340032 | tf_op jit(solution)/shard_map/gram/pallas_call | solution.py:179
  82.9 0.1 collective-permute-start.17
  83.0 0.5 collective-permute-start.15
  83.5 4.3 %gram.2 = (f32[256,512]{1,0:T(8,128)S(1)}, f32[256,512]{1,0:T(8,128)S(1)}, f32[256,512]{1,0:T(8,128)S(1)}, f32[256,512]{1,0:T(8,128)S(1)}) custom-call(s32[7]{0:T(128)S(1)} %copy-done.4, bf16[256,1024]{1,0:T(8,128)(2,1)S(1)} %copy-done.1, bf16[256,1024]{1,0:T(8,128)(2,1)S(1)} %tie.4.refs_0_.refs_1_.refs_11_, bf16[256,1024]{1,0:T(8,128)(2,1)} %tie.5.refs_2_.refs_12_, ...), custom_call_target="tpu_custom_call" | custom-call | flops 1073741824 | bytes 7340032 | tf_op jit(solution)/shard_map/gram/pallas_call | solution.py:179
  87.8 0.2 collective-permute-start.13
  88.0 0.4 collective-permute-start.14
  88.4 0.1 add.48
  88.5 3.7 %collective-permute-start.18 = (f32[256,512]{1,0:T(8,128)S(1)}, f32[256,512]{1,0:T(8,128)S(1)}, u32[]{:S(2)}, u32[]{:S(2)}) collective-permute-start(f32[256,512]{1,0:T(8,128)S(1)} %add.48), channel_id=1, source_target_pairs={{0,128},{128,0},{1,129},{129,1},{2,130},{130,2},{3,131},{131,3},{4... | collective-permute-start | bytes 1572872 | tf_op jit(solution)/shard_map/ppermute | solution.py:420
  92.2 0.1 add.47
  92.3 0.1 collective-permute-start.16
  92.4 0.6 collective-permute-start.19
  93.0 3.2 %collective-permute-done.19 = f32[32,128]{1,0:T(8,128)S(1)} collective-permute-done((f32[32,128]{1,0:T(8,128)S(1)}, f32[32,128]{1,0:T(8,128)S(1)}, u32[]{:S(2)}, u32[]{:S(2)}) %collective-permute-start.19) | collective-permute-done | bytes 16416 | tf_op jit(solution)/shard_map/ppermute | solution.py:395
  96.2 2.1 %collective-permute-start.20 = (f32[2,32,128]{2,1,0:T(8,128)S(1)}, f32[2,32,128]{2,1,0:T(8,128)S(1)}, u32[]{:S(2)}, u32[]{:S(2)}) collective-permute-start(f32[2,32,128]{2,1,0:T(8,128)S(1)} %pad_maximum_fusion.pair), channel_id=1, source_target_pairs={{0,8},{4,12},{8,0},{12,4},{1,9},{5,13},{9,1},{13,5},{2,10},{6,14},... | collective-permute-start | bytes 98312 | tf_op jit(solution)/shard_map/ppermute | solution.py:396
  98.3 3.3 %collective-permute-done.20.far_pair = f32[2,32,128]{2,1,0:T(8,128)S(1)} collective-permute-done((f32[2,32,128]{2,1,0:T(8,128)S(1)}, f32[2,32,128]{2,1,0:T(8,128)S(1)}, u32[]{:S(2)}, u32[]{:S(2)}) %collective-permute-start.20) | collective-permute-done | bytes 32800 | tf_op jit(solution)/shard_map/ppermute | solution.py:396
  101.6 1.3 %assemble.1 = f32[64,256]{1,0:T(8,128)} custom-call(s32[7]{0:T(128)S(1)} %copy-done.4, f32[2,32,128]{2,1,0:T(8,128)S(1)} %pad_maximum_fusion.pair, f32[2,32,128]{2,1,0:T(8,128)S(1)} %collective-permute-done.20.far_pair), custom_call_target="tpu_custom_call" | custom-call | bytes 131072 | tf_op jit(solution)/shard_map/assemble/pallas_call | solution.py:397
  102.9 2.0 %collective-permute-done.18.high_got = f32[256,512]{1,0:T(8,128)S(1)} collective-permute-done((f32[256,512]{1,0:T(8,128)S(1)}, f32[256,512]{1,0:T(8,128)S(1)}, u32[]{:S(2)}, u32[]{:S(2)}) %collective-permute-start.18) | collective-permute-done | bytes 524320 | tf_op jit(solution)/shard_map/ppermute | solution.py:420
  104.9 10.7 %collective-permute-done.16.low_got = f32[256,512]{1,0:T(8,128)S(1)} collective-permute-done((f32[256,512]{1,0:T(8,128)S(1)}, f32[256,512]{1,0:T(8,128)S(1)}, u32[]{:S(2)}, u32[]{:S(2)}) %collective-permute-start.16) | collective-permute-done | bytes 524320 | tf_op jit(solution)/shard_map/ppermute | solution.py:420
  115.6 1.6 %finish.1 = f32[256,1024]{1,0:T(8,128)} custom-call(f32[256,512]{1,0:T(8,128)S(1)} %get-tuple-element.18.low, f32[256,512]{1,0:T(8,128)S(1)} %get-tuple-element.19.high, f32[256,512]{1,0:T(8,128)S(1)} %collective-permute-done.13.low_core, f32[256,512]{1,0:T(8,128)S(1)} %collective-permute-done.14.high_core, f32[256,512]{1,0:T(8,128)S(1)} %collective-permute-done.16.low_got, ...), custom_call_target="tpu_custom_call" | custom-call | flops 1048576 | bytes 4194304 | tf_op jit(solution)/shard_map/finish/pallas_call | solution.py:223
  (36 shorter events, 0.1 us)
Async XLA Ops:
  0.6 9.5 %copy-start = (bf16[256,1,4096]{2,0,1:T(8,128)(2,1)S(1)}, bf16[256,1,4096]{2,0,1:T(8,128)(2,1)}, u32[]{:S(2)}) copy-start(bf16[256,1,4096]{2,0,1:T(8,128)(2,1)} %param.7) | copy-start | bytes 6291460
  1.3 8.9 %copy-start.7 = (s32[256,1,32]{0,2,1:T(8,128)S(1)}, s32[256,1,32]{0,2,1:T(8,128)}, u32[]{:S(2)}) copy-start(s32[256,1,32]{0,2,1:T(8,128)} %param.6) | copy-start | bytes 98308
  6.2 18.9 %collective-permute-start.6 = (bf16[256,1024]{1,0:T(8,128)(2,1)}, bf16[256,1024]{1,0:T(8,128)(2,1)}, u32[]{:S(2)}, u32[]{:S(2)}) collective-permute-start(bf16[256,1024]{1,0:T(8,128)(2,1)} %get-tuple-element.15.refs_5_.refs_15_), channel_id=1, source_target_pairs={{0,16},{16,32},{32,48},{48,64},{64,80},{80,96},{96,112},{112,0},{1... | collective-permute-start | bytes 1572872 | tf_op jit(solution)/shard_map/ppermute | solution.py:264
  8.2 16.9 %collective-permute-start = (bf16[256,1024]{1,0:T(8,128)(2,1)}, bf16[256,1024]{1,0:T(8,128)(2,1)S(1)}, u32[]{:S(2)}, u32[]{:S(2)}) collective-permute-start(bf16[256,1024]{1,0:T(8,128)(2,1)} %get-tuple-element.14.refs_0_.refs_10_), channel_id=1, source_target_pairs={{0,16},{16,32},{32,48},{48,64},{64,80},{80,96},{96,112},{112,0},{1... | collective-permute-start | bytes 1572872 | tf_op jit(solution)/shard_map/ppermute | solution.py:263
  13.2 16.7 %copy-start.4 = (s32[7]{0:T(128)S(1)}, s32[7]{0:T(128)}, u32[]{:S(2)}) copy-start(s32[7]{0:T(128)} %stack.40.at) | copy-start | bytes 88
  13.2 16.7 %copy-start.5 = (s32[1024]{0:T(1024)S(1)}, s32[1024]{0:T(1024)}, u32[]{:S(2)}) copy-start(s32[1024]{0:T(1024)} %param.9) | copy-start | bytes 12292
  13.2 16.6 %copy-start.6 = (s32[256]{0:T(256)S(1)}, s32[256]{0:T(256)}, u32[]{:S(2)}) copy-start(s32[256]{0:T(256)} %param.8) | copy-start | bytes 3076
  13.3 6.6 %collective-permute-start.1 = (f32[128,256]{1,0:T(8,128)S(1)}, f32[128,256]{1,0:T(8,128)S(1)}, u32[]{:S(2)}, u32[]{:S(2)}) collective-permute-start(f32[128,256]{1,0:T(8,128)S(1)} %dynamic-slice_bitcast_fusion), channel_id=1, source_target_pairs={{0,8},{4,12},{8,0},{12,4},{1,9},{5,13},{9,1},{13,5},{2,10},{6,14},... | collective-permute-start | bytes 393224 | tf_op jit(solution)/shard_map/ppermute | solution.py:348
  25.1 10.5 %collective-permute-start.2 = (bf16[256,1024]{1,0:T(8,128)(2,1)S(1)}, bf16[256,1024]{1,0:T(8,128)(2,1)}, u32[]{:S(2)}, u32[]{:S(2)}) collective-permute-start(bf16[256,1024]{1,0:T(8,128)(2,1)S(1)} %tie.4.refs_0_.refs_1_.refs_11_), channel_id=1, source_target_pairs={{0,16},{16,32},{32,48},{48,64},{64,80},{80,96},{96,112},{112,0},{1... | collective-permute-start | bytes 1572872 | tf_op jit(solution)/shard_map/ppermute | solution.py:263
  25.2 16.1 %collective-permute-start.7 = (bf16[256,1024]{1,0:T(8,128)(2,1)}, bf16[256,1024]{1,0:T(8,128)(2,1)}, u32[]{:S(2)}, u32[]{:S(2)}) collective-permute-start(bf16[256,1024]{1,0:T(8,128)(2,1)} %collective-permute-done.6.refs_1_.refs_6_.refs_16_), channel_id=1, source_target_pairs={{0,16},{16,32},{32,48},{48,64},{64,80},{80,96},{96,112},{112,0},{1... | collective-permute-start | bytes 1572872 | tf_op jit(solution)/shard_map/ppermute | solution.py:264
  25.3 4.6 %collective-permute-start.3 = (f32[64,256]{1,0:T(8,128)S(1)}, f32[64,256]{1,0:T(8,128)S(1)}, u32[]{:S(2)}, u32[]{:S(2)}) collective-permute-start(f32[64,256]{1,0:T(8,128)S(1)} %constant_dynamic-slice_fusion.2), channel_id=1, source_target_pairs={{0,4},{4,0},{8,12},{12,8},{1,5},{5,1},{9,13},{13,9},{2,6},{6,2},{1... | collective-permute-start | bytes 196616 | tf_op jit(solution)/shard_map/ppermute | solution.py:350
  35.6 17.7 %collective-permute-start.4 = (bf16[256,1024]{1,0:T(8,128)(2,1)}, bf16[256,1024]{1,0:T(8,128)(2,1)}, u32[]{:S(2)}, u32[]{:S(2)}) collective-permute-start(bf16[256,1024]{1,0:T(8,128)(2,1)} %tie.5.refs_2_.refs_12_), channel_id=1, source_target_pairs={{0,16},{16,32},{32,48},{48,64},{64,80},{80,96},{96,112},{112,0},{1... | collective-permute-start | bytes 1572872 | tf_op jit(solution)/shard_map/ppermute | solution.py:263
  41.3 15.6 %collective-permute-start.8 = (bf16[256,1024]{1,0:T(8,128)(2,1)}, bf16[256,1024]{1,0:T(8,128)(2,1)}, u32[]{:S(2)}, u32[]{:S(2)}) collective-permute-start(bf16[256,1024]{1,0:T(8,128)(2,1)} %collective-permute-done.7.refs_3_.refs_1_.refs_7_.refs_17_), channel_id=1, source_target_pairs={{0,16},{16,32},{32,48},{48,64},{64,80},{80,96},{96,112},{112,0},{1... | collective-permute-start | bytes 1572872 | tf_op jit(solution)/shard_map/ppermute | solution.py:264
  41.3 22.3 %all-to-all-start = ((f32[16,32,128]{2,1,0:T(8,128)}), f32[16,32,128]{2,1,0:T(8,128)}, u32[]{:S(2)}, u32[]{:S(2)}) async-start(f32[16,32,128]{2,1,0:T(8,128)} %bitcast.16), calls=%async_computation | async-start | bytes 524288 | tf_op jit(solution)/shard_map/all_to_all | solution.py:383
  50.4 27.1 %copy-start.1 = (bf16[256,1024]{1,0:T(8,128)(2,1)S(1)}, bf16[256,1024]{1,0:T(8,128)(2,1)}, u32[]{:S(2)}) copy-start(bf16[256,1024]{1,0:T(8,128)(2,1)} %get-tuple-element.14.refs_0_.refs_10_) | copy-start | bytes 1572868
  50.5 27.1 %copy-start.3 = (bf16[128,256]{1,0:T(8,128)(2,1)S(1)}, bf16[128,256]{1,0:T(8,128)(2,1)}, u32[]{:S(2)}) copy-start(bf16[128,256]{1,0:T(8,128)(2,1)} %get-tuple-element.16.refs_20_) | copy-start | bytes 196612
  52.7 21.2 %collective-permute-start.10 = (bf16[512,256]{1,0:T(8,128)(2,1)}, bf16[512,256]{1,0:T(8,128)(2,1)}, u32[]{:S(2)}, u32[]{:S(2)}) collective-permute-start(bf16[512,256]{1,0:T(8,128)(2,1)} %pick.2), channel_id=1, source_target_pairs={{0,2},{2,0},{1,3},{3,1},{4,6},{6,4},{5,7},{7,5},{8,10},{10,8},{9,1... | collective-permute-start | bytes 786440 | tf_op jit(solution)/shard_map/ppermute | solution.py:272
  55.0 22.5 %collective-permute-start.5 = (bf16[128,1024]{1,0:T(8,128)(2,1)}, bf16[128,1024]{1,0:T(8,128)(2,1)S(1)}, u32[]{:S(2)}, u32[]{:S(2)}) collective-permute-start(bf16[128,1024]{1,0:T(8,128)(2,1)} %constant_dynamic-slice_fusion.1), channel_id=1, source_target_pairs={{0,16},{16,32},{32,48},{48,64},{64,80},{80,96},{96,112},{112,0},{1... | collective-permute-start | bytes 786440 | tf_op jit(solution)/shard_map/ppermute | solution.py:263
  58.6 18.9 %collective-permute-start.9 = (bf16[128,1024]{1,0:T(8,128)(2,1)}, bf16[128,1024]{1,0:T(8,128)(2,1)}, u32[]{:S(2)}, u32[]{:S(2)}) collective-permute-start(bf16[128,1024]{1,0:T(8,128)(2,1)} %constant_dynamic-slice_fusion), channel_id=1, source_target_pairs={{0,16},{16,32},{32,48},{48,64},{64,80},{80,96},{96,112},{112,0},{1... | collective-permute-start | bytes 786440 | tf_op jit(solution)/shard_map/ppermute | solution.py:264
  60.0 10.8 %collective-permute-start.11 = (bf16[128,256]{1,0:T(8,128)(2,1)}, bf16[128,256]{1,0:T(8,128)(2,1)S(1)}, u32[]{:S(2)}, u32[]{:S(2)}) collective-permute-start(bf16[128,256]{1,0:T(8,128)(2,1)} %tie.7), channel_id=1, source_target_pairs={{0,64},{16,80},{32,96},{48,112},{64,0},{80,16},{96,32},{112,48},{1... | collective-permute-start | bytes 196616 | tf_op jit(solution)/shard_map/ppermute | solution.py:266
  72.3 5.2 %collective-permute-start.12 = (bf16[256,256]{1,0:T(8,128)(2,1)S(1)}, bf16[256,256]{1,0:T(8,128)(2,1)S(1)}, u32[]{:S(2)}, u32[]{:S(2)}) collective-permute-start(bf16[256,256]{1,0:T(8,128)(2,1)S(1)} %pick.3), channel_id=1, source_target_pairs={{0,2},{2,0},{1,3},{3,1},{4,6},{6,4},{5,7},{7,5},{8,10},{10,8},{9,1... | collective-permute-start | bytes 393224 | tf_op jit(solution)/shard_map/ppermute | solution.py:275
  77.5 1.0 copy-start.2
  82.9 5.5 %collective-permute-start.17 = (f32[256,512]{1,0:T(8,128)S(1)}, f32[256,512]{1,0:T(8,128)S(1)}, u32[]{:S(2)}, u32[]{:S(2)}) collective-permute-start(f32[256,512]{1,0:T(8,128)S(1)} %get-tuple-element.25), channel_id=1, source_target_pairs={{0,1},{1,0},{2,3},{3,2},{4,5},{5,4},{6,7},{7,6},{8,9},{9,8},{10,11... | collective-permute-start | bytes 1572872 | tf_op jit(solution)/shard_map/ppermute | solution.py:279
  83.0 9.2 %collective-permute-start.15 = (f32[256,512]{1,0:T(8,128)S(1)}, f32[256,512]{1,0:T(8,128)S(1)}, u32[]{:S(2)}, u32[]{:S(2)}) collective-permute-start(f32[256,512]{1,0:T(8,128)S(1)} %get-tuple-element.23), channel_id=1, source_target_pairs={{0,1},{1,0},{2,3},{3,2},{4,5},{5,4},{6,7},{7,6},{8,9},{9,8},{10,11... | collective-permute-start | bytes 1572872 | tf_op jit(solution)/shard_map/ppermute | solution.py:279
  87.8 15.1 %collective-permute-start.13 = (f32[256,512]{1,0:T(8,128)S(1)}, f32[256,512]{1,0:T(8,128)S(1)}, u32[]{:S(2)}, u32[]{:S(2)}) collective-permute-start(f32[256,512]{1,0:T(8,128)S(1)} %get-tuple-element.20), channel_id=1, source_target_pairs={{0,1},{1,0},{2,3},{3,2},{4,5},{5,4},{6,7},{7,6},{8,9},{9,8},{10,11... | collective-permute-start | bytes 1572872 | tf_op jit(solution)/shard_map/ppermute | solution.py:282
  88.0 14.9 %collective-permute-start.14 = (f32[256,512]{1,0:T(8,128)S(1)}, f32[256,512]{1,0:T(8,128)S(1)}, u32[]{:S(2)}, u32[]{:S(2)}) collective-permute-start(f32[256,512]{1,0:T(8,128)S(1)} %get-tuple-element.21), channel_id=1, source_target_pairs={{0,1},{1,0},{2,3},{3,2},{4,5},{5,4},{6,7},{7,6},{8,9},{9,8},{10,11... | collective-permute-start | bytes 1572872 | tf_op jit(solution)/shard_map/ppermute | solution.py:282
  88.5 16.4 %collective-permute-start.18 = (f32[256,512]{1,0:T(8,128)S(1)}, f32[256,512]{1,0:T(8,128)S(1)}, u32[]{:S(2)}, u32[]{:S(2)}) collective-permute-start(f32[256,512]{1,0:T(8,128)S(1)} %add.48), channel_id=1, source_target_pairs={{0,128},{128,0},{1,129},{129,1},{2,130},{130,2},{3,131},{131,3},{4... | collective-permute-start | bytes 1572872 | tf_op jit(solution)/shard_map/ppermute | solution.py:420
  92.3 23.3 %collective-permute-start.16 = (f32[256,512]{1,0:T(8,128)S(1)}, f32[256,512]{1,0:T(8,128)S(1)}, u32[]{:S(2)}, u32[]{:S(2)}) collective-permute-start(f32[256,512]{1,0:T(8,128)S(1)} %add.47), channel_id=1, source_target_pairs={{0,128},{128,0},{1,129},{129,1},{2,130},{130,2},{3,131},{131,3},{4... | collective-permute-start | bytes 1572872 | tf_op jit(solution)/shard_map/ppermute | solution.py:420
  92.4 3.8 %collective-permute-start.19 = (f32[32,128]{1,0:T(8,128)S(1)}, f32[32,128]{1,0:T(8,128)S(1)}, u32[]{:S(2)}, u32[]{:S(2)}) collective-permute-start(f32[32,128]{1,0:T(8,128)S(1)} %sum.1.refs_2_), channel_id=1, source_target_pairs={{0,4},{4,0},{8,12},{12,8},{1,5},{5,1},{9,13},{13,9},{2,6},{6,2},{1... | collective-permute-start | bytes 49160 | tf_op jit(solution)/shard_map/ppermute | solution.py:395
  96.2 5.4 %collective-permute-start.20 = (f32[2,32,128]{2,1,0:T(8,128)S(1)}, f32[2,32,128]{2,1,0:T(8,128)S(1)}, u32[]{:S(2)}, u32[]{:S(2)}) collective-permute-start(f32[2,32,128]{2,1,0:T(8,128)S(1)} %pad_maximum_fusion.pair), channel_id=1, source_target_pairs={{0,8},{4,12},{8,0},{12,4},{1,9},{5,13},{9,1},{13,5},{2,10},{6,14},... | collective-permute-start | bytes 98312 | tf_op jit(solution)/shard_map/ppermute | solution.py:396

commit v6 on v5

--- a/solution.py
+++ b/solution.py
@@ -266,16 +266,16 @@
             far = lax.ppermute(tie(far, low), "z", [(i, (i + Z // 2) % Z) for i in range(Z)])
             low = tie(low, pair)
         if step == 2:
-            low = tie(low, placed)
+            low = tie(low, placed, far)
             placed = tie(placed, high)
         pieces.append((low.shape[0], False, low, high))
     near = lax.ppermute(pick(at, pieces[1:3]), "yl", SWAP)
     mine = own_slots(placed)
-    third = pick(at, pieces[3:4], mine, far)
+    third = pick(at, pieces[3:4])
     third = lax.ppermute(third, "yl", SWAP)
     received = (own, near, third, far)
 
-    *given_other, low_given, high_given = gram(at, pieces, received, False)
+    *given_other, low_given, high_given = gram(at, pieces, received, False, mine)
     swapped = [lax.ppermute(g, "core", SWAP) for g in given_other]
     *kept_other, low_kept, high_kept = gram(at, pieces, received, True)
     given = [add(g, s) for g, s in zip((low_given, high_given), swapped)]

time: 118 us -> 115 us (0.975)
  waiting for transfers between devices: 51.9 us -> 48.8 us
    ppermute x1, waiting for transfers between devices: 6.26 us -> 11.7 us  [fisher_terms(): lax.ppermute(tie(far, low), 'z', [(i, (i + Z // 2) % Z) for i in range(Z)])]
    ppermute x1, waiting for transfers between devices: 3.97 us -> 0.01 us  [placed_scores(): lax.ppermute(lax.dynamic_slice_in_dim(pair, (1 - x % 2) * share, share, 0...]
    ppermute x4, waiting for transfers between devices: 8.87 us -> 5.21 us  [fisher_terms(): low = lax.ppermute(low, ('z', 'core'), RING)]
    all_to_all x1, starting transfers between devices: 9.18 us -> 7.29 us  [own_slots(): lax.all_to_all(placed.reshape(YH * Z, half, double), ('yh', 'z'), 0, 0, t...]
    ppermute x1, starting transfers between devices: 3.57 us -> 5.16 us  [fisher_terms(): lax.ppermute(tie(far, low), 'z', [(i, (i + Z // 2) % Z) for i in range(Z)])]
  transfers between devices with their start and end apart: 22 -> 22, of which waited for: 11 -> 10; matrix products, arithmetic and copies ran while one was open for 6% -> 6% of each run, Pallas kernels for 11% -> 12%
where the time goes in v6:
time: 115 us; the launch traced here: 114 us
  waiting for transfers between devices  48.8 us (42%)
  starting transfers between devices  32.5 us (28%)
  Pallas kernels  24.1 us (21%)
  local copies, waits for them, and re-layouts  5.02 us (4%)
  matrix products  3.09 us (3%)
    ppermute x2, waiting for transfers between devices, per_device(): got = [lax.ppermute(g, 'yh', SWAP) for g in given]  12.5 us
    ppermute x1, waiting for transfers between devices, fisher_terms(): lax.ppermute(tie(far, low), 'z', [(i, (i + Z // 2) % Z) for i in range(Z)])  11.7 us
    pallas_call x2, Pallas kernels, gram(): pl.pallas_call(functools.partial(gram_kernel, sizes, kept), grid_spec=plt...  8.7 us
    all_to_all x1, starting transfers between devices, own_slots(): lax.all_to_all(placed.reshape(YH * Z, half, double), ('yh', 'z'), 0, 0, t...  7.29 us
    ppermute x4, waiting for transfers between devices, fisher_terms(): high = lax.ppermute(high, ('z', 'core'), RING)  5.82 us
    ppermute x4, waiting for transfers between devices, fisher_terms(): low = lax.ppermute(low, ('z', 'core'), RING)  5.21 us
    ppermute x1, starting transfers between devices, fisher_terms(): lax.ppermute(tie(far, low), 'z', [(i, (i + Z // 2) % Z) for i in range(Z)])  5.16 us
    pallas_call x1, Pallas kernels, dequant(): pl.pallas_call(dequant_kernel, grid_spec=pltpu.PrefetchScalarGridSpec(num...  4.93 us
  transfers between devices with their start and end apart: 22, of which 10 were waited for; matrix products, arithmetic and copies ran while one was open for 6% of the time, Pallas kernels for 12%

profile of v6, /device:TPU:2, one launch (start us, length us, event | category | flops | bytes accessed | tf_op | source)
XLA Modules:
  0.0 114.4 jit_solution(17120071145960322818)
XLA Ops:
  0.6 0.0 copy-start
  0.7 0.6 stack.40.at
  1.2 4.9 %dequant.1 = (bf16[256,1024]{1,0:T(8,128)(2,1)}, bf16[256,1024]{1,0:T(8,128)(2,1)}, bf16[128,256]{1,0:T(8,128)(2,1)}, bf16[128,256]{1,0:T(8,128)(2,1)}) custom-call(s32[7]{0:T(128)} %stack.40.at, s32[32,256]{1,0:T(8,128)} %bitcast.46, bf16[256,4096]{1,0:T(8,128)(2,1)} %bitcast.42, bf16[256,4096]{1,0:T(8,128)(2,1)} %bitcast.43, bf16[256,4096]{1,0:T(8,128)(2,1)} %bitcast.44), custom_call_target="tpu_custom_call" | custom-call | flops 33554432 | bytes 2097152 | tf_op jit(solution)/shard_map/dequant/pallas_call | solution.py:60
  6.2 2.0 %collective-permute-start.7 = (bf16[256,1024]{1,0:T(8,128)(2,1)}, bf16[256,1024]{1,0:T(8,128)(2,1)}, u32[]{:S(2)}, u32[]{:S(2)}) collective-permute-start(bf16[256,1024]{1,0:T(8,128)(2,1)} %get-tuple-element.16.refs_5_.refs_15_), channel_id=1, source_target_pairs={{0,16},{16,32},{32,48},{48,64},{64,80},{80,96},{96,112},{112,0},{1... | collective-permute-start | bytes 1572872 | tf_op jit(solution)/shard_map/ppermute | solution.py:264
  8.1 1.9 %collective-permute-start = (bf16[256,1024]{1,0:T(8,128)(2,1)}, bf16[256,1024]{1,0:T(8,128)(2,1)S(1)}, u32[]{:S(2)}, u32[]{:S(2)}) collective-permute-start(bf16[256,1024]{1,0:T(8,128)(2,1)} %get-tuple-element.14.refs_0_.refs_10_), channel_id=1, source_target_pairs={{0,16},{16,32},{32,48},{48,64},{64,80},{80,96},{96,112},{112,0},{1... | collective-permute-start | bytes 1572872 | tf_op jit(solution)/shard_map/ppermute | solution.py:263
  10.1 3.1 %fusion.1 = f32[256,256]{0,1:T(8,128)S(1)} fusion(bf16[256,1,4096]{2,0,1:T(8,128)(2,1)S(1)} %copy-done, s32[4096]{0:T(1024)S(1)} %add_select_fusion, s32[256,1,32]{0,2,1:T(8,128)S(1)} %copy-done.8, bf16[256,1,4096]{2,0,1:T(8,128)(2,1)} %param.5), kind=kOutput, calls=%fused_computation.2 | convolution fusion | flops 606232576 | bytes 4505600 | tf_op jit(solution)/shard_map/dot_general | solution.py:344
  13.2 0.0 copy-start.6
  13.2 0.0 copy-start.7
  13.3 2.2 %collective-permute-start.1 = (f32[128,256]{1,0:T(8,128)S(1)}, f32[128,256]{1,0:T(8,128)S(1)}, u32[]{:S(2)}, u32[]{:S(2)}) collective-permute-start(f32[128,256]{1,0:T(8,128)S(1)} %dynamic-slice_bitcast_fusion), channel_id=1, source_target_pairs={{0,8},{4,12},{8,0},{12,4},{1,9},{5,13},{9,1},{13,5},{2,10},{6,14},... | collective-permute-start | bytes 393224 | tf_op jit(solution)/shard_map/ppermute | solution.py:348
  15.5 4.4 %collective-permute-done.1 = f32[128,256]{1,0:T(8,128)S(1)} collective-permute-done((f32[128,256]{1,0:T(8,128)S(1)}, f32[128,256]{1,0:T(8,128)S(1)}, u32[]{:S(2)}, u32[]{:S(2)}) %collective-permute-start.1) | collective-permute-done | bytes 131104 | tf_op jit(solution)/shard_map/ppermute | solution.py:348
  19.9 5.2 %collective-permute-done.refs_0_.refs_1_ = bf16[256,1024]{1,0:T(8,128)(2,1)S(1)} collective-permute-done((bf16[256,1024]{1,0:T(8,128)(2,1)}, bf16[256,1024]{1,0:T(8,128)(2,1)S(1)}, u32[]{:S(2)}, u32[]{:S(2)}) %collective-permute-start) | collective-permute-done | bytes 524320 | tf_op jit(solution)/shard_map/ppermute | solution.py:263
  25.1 0.1 collective-permute-start.8
  25.2 0.6 collective-permute-start.3
  25.9 5.2 %collective-permute-start.4 = (bf16[128,256]{1,0:T(8,128)(2,1)S(1)}, bf16[128,256]{1,0:T(8,128)(2,1)S(1)}, u32[]{:S(2)}, u32[]{:S(2)}) collective-permute-start(bf16[128,256]{1,0:T(8,128)(2,1)S(1)} %tie.5), channel_id=1, source_target_pairs={{0,64},{16,80},{32,96},{48,112},{64,0},{80,16},{96,32},{112,48},{1... | collective-permute-start | bytes 196616 | tf_op jit(solution)/shard_map/ppermute | solution.py:266
  31.0 2.2 %place.1.refs_1_.refs_0_ = f32[512,128]{1,0:T(8,128)} custom-call(s32[7]{0:T(128)S(1)} %copy-done.5, f32[2,64,256]{2,1,0:T(8,128)S(1)} %bitcast.38, f32[64,256]{1,0:T(8,128)S(1)} %collective-permute-done.3.got, s32[1,256]{1,0:T(1,128)S(1)} %bitcast.41, s32[1,1024]{1,0:T(1,128)S(1)} %bitcast.40), custom_call_target="tpu_custom_call" | custom-call | flops 268435456 | bytes 1048576 | tf_op jit(solution)/shard_map/place/pallas_call | solution.py:352
  33.2 11.7 %collective-permute-done.4.refs_2_.refs_23_ = bf16[128,256]{1,0:T(8,128)(2,1)S(1)} collective-permute-done((bf16[128,256]{1,0:T(8,128)(2,1)S(1)}, bf16[128,256]{1,0:T(8,128)(2,1)S(1)}, u32[]{:S(2)}, u32[]{:S(2)}) %collective-permute-start.4) | collective-permute-done | bytes 65568 | tf_op jit(solution)/shard_map/ppermute | solution.py:266
  44.9 1.5 %collective-permute-start.9 = (bf16[256,1024]{1,0:T(8,128)(2,1)}, bf16[256,1024]{1,0:T(8,128)(2,1)}, u32[]{:S(2)}, u32[]{:S(2)}) collective-permute-start(bf16[256,1024]{1,0:T(8,128)(2,1)} %collective-permute-done.8.refs_3_.refs_7_.refs_17_.refs_1_), channel_id=1, source_target_pairs={{0,16},{16,32},{32,48},{48,64},{64,80},{80,96},{96,112},{112,0},{1... | collective-permute-start | bytes 1572872 | tf_op jit(solution)/shard_map/ppermute | solution.py:264
  46.4 7.3 %all-to-all-start = ((f32[16,32,128]{2,1,0:T(8,128)}), f32[16,32,128]{2,1,0:T(8,128)}, u32[]{:S(2)}, u32[]{:S(2)}) async-start(f32[16,32,128]{2,1,0:T(8,128)} %bitcast.16), calls=%async_computation | async-start | bytes 524288 | tf_op jit(solution)/shard_map/all_to_all | solution.py:383
  53.7 2.2 %pick.2 = bf16[512,256]{1,0:T(8,128)(2,1)} custom-call(s32[7]{0:T(128)S(1)} %copy-done.5, bf16[256,1024]{1,0:T(8,128)(2,1)S(1)} %tie.4.refs_0_.refs_1_.refs_11_, bf16[256,1024]{1,0:T(8,128)(2,1)} %collective-permute-done.7.refs_1_.refs_6_.refs_16_, bf16[256,1024]{1,0:T(8,128)(2,1)} %tie.6.refs_2_.refs_12_, ...), custom_call_target="tpu_custom_call" | custom-call | bytes 524288 | tf_op jit(solution)/shard_map/pick/pallas_call | solution.py:104
  55.9 0.7 collective-permute-start.11
  56.6 1.7 %constant_dynamic-slice_fusion.1 = bf16[128,1024]{1,0:T(8,128)(2,1)} fusion(bf16[256,1024]{1,0:T(8,128)(2,1)} %collective-permute-done.5.refs_0_.refs_3_.refs_13_, s32[]{:T(128)S(6)} %select_n.39), kind=kLoop, calls=%fused_computation.22 | loop fusion | bytes 524292 | tf_op jit(solution)/shard_map/dynamic_slice | solution.py:261
  58.3 1.9 %collective-permute-start.6 = (bf16[128,1024]{1,0:T(8,128)(2,1)}, bf16[128,1024]{1,0:T(8,128)(2,1)S(1)}, u32[]{:S(2)}, u32[]{:S(2)}) collective-permute-start(bf16[128,1024]{1,0:T(8,128)(2,1)} %constant_dynamic-slice_fusion.1), channel_id=1, source_target_pairs={{0,16},{16,32},{32,48},{48,64},{64,80},{80,96},{96,112},{112,0},{1... | collective-permute-start | bytes 786440 | tf_op jit(solution)/shard_map/ppermute | solution.py:263
  60.1 5.3 %collective-permute-done.9.refs_1_.refs_8_.refs_18_ = bf16[256,1024]{1,0:T(8,128)(2,1)} collective-permute-done((bf16[256,1024]{1,0:T(8,128)(2,1)}, bf16[256,1024]{1,0:T(8,128)(2,1)}, u32[]{:S(2)}, u32[]{:S(2)}) %collective-permute-start.9) | collective-permute-done | bytes 524320 | tf_op jit(solution)/shard_map/ppermute | solution.py:264
  65.4 1.7 %constant_dynamic-slice_fusion = bf16[128,1024]{1,0:T(8,128)(2,1)} fusion(bf16[256,1024]{1,0:T(8,128)(2,1)} %collective-permute-done.9.refs_1_.refs_8_.refs_18_, s32[]{:T(128)S(6)} %select_n.39), kind=kLoop, calls=%fused_computation.21 | loop fusion | bytes 524292 | tf_op jit(solution)/shard_map/dynamic_slice | solution.py:262
  67.1 2.1 %pick.3 = bf16[256,256]{1,0:T(8,128)(2,1)} custom-call(s32[7]{0:T(128)S(1)} %copy-done.5, bf16[256,1024]{1,0:T(8,128)(2,1)} %collective-permute-done.5.refs_0_.refs_3_.refs_13_, bf16[256,1024]{1,0:T(8,128)(2,1)} %collective-permute-done.9.refs_1_.refs_8_.refs_18_), custom_call_target="tpu_custom_call" | custom-call | bytes 262144 | tf_op jit(solution)/shard_map/pick/pallas_call | solution.py:104
  69.2 1.6 %collective-permute-start.12 = (bf16[256,256]{1,0:T(8,128)(2,1)}, bf16[256,256]{1,0:T(8,128)(2,1)}, u32[]{:S(2)}, u32[]{:S(2)}) collective-permute-start(bf16[256,256]{1,0:T(8,128)(2,1)} %pick.3), channel_id=1, source_target_pairs={{0,2},{2,0},{1,3},{3,1},{4,6},{6,4},{5,7},{7,5},{8,10},{10,8},{9,1... | collective-permute-start | bytes 393224 | tf_op jit(solution)/shard_map/ppermute | solution.py:275
  70.8 1.0 sum.1.refs_24_
  71.8 2.7 %collective-permute-done.12.refs_22_ = bf16[256,256]{1,0:T(8,128)(2,1)} collective-permute-done((bf16[256,256]{1,0:T(8,128)(2,1)}, bf16[256,256]{1,0:T(8,128)(2,1)}, u32[]{:S(2)}, u32[]{:S(2)}) %collective-permute-start.12) | collective-permute-done | bytes 131104 | tf_op jit(solution)/shard_map/ppermute | solution.py:275
  74.5 0.5 collective-permute-done.10.refs_9_.refs_19_
  75.0 1.0 copy-done.2
  76.0 4.4 %gram.3 = (f32[256,512]{1,0:T(8,128)S(1)}, f32[256,512]{1,0:T(8,128)S(1)}, f32[256,512]{1,0:T(8,128)S(1)}, f32[256,512]{1,0:T(8,128)S(1)}) custom-call(s32[7]{0:T(128)S(1)} %copy-done.5, bf16[256,1024]{1,0:T(8,128)(2,1)S(1)} %copy-done.1, bf16[256,1024]{1,0:T(8,128)(2,1)S(1)} %tie.4.refs_0_.refs_1_.refs_11_, bf16[256,1024]{1,0:T(8,128)(2,1)} %tie.6.refs_2_.refs_12_, ...), custom_call_target="tpu_custom_call" | custom-call | flops 1073741824 | bytes 7340032 | tf_op jit(solution)/shard_map/gram/pallas_call | solution.py:179
  80.4 0.1 collective-permute-start.17
  80.5 0.5 collective-permute-start.15
  81.0 4.3 %gram.2 = (f32[256,512]{1,0:T(8,128)S(1)}, f32[256,512]{1,0:T(8,128)S(1)}, f32[256,512]{1,0:T(8,128)S(1)}, f32[256,512]{1,0:T(8,128)S(1)}) custom-call(s32[7]{0:T(128)S(1)} %copy-done.5, bf16[256,1024]{1,0:T(8,128)(2,1)S(1)} %copy-done.1, bf16[256,1024]{1,0:T(8,128)(2,1)S(1)} %tie.4.refs_0_.refs_1_.refs_11_, bf16[256,1024]{1,0:T(8,128)(2,1)} %tie.6.refs_2_.refs_12_, ...), custom_call_target="tpu_custom_call" | custom-call | flops 1073741824 | bytes 7340032 | tf_op jit(solution)/shard_map/gram/pallas_call | solution.py:179
  85.4 0.2 collective-permute-start.13
  85.5 0.4 collective-permute-start.14
  86.0 0.1 add.48
  86.0 3.3 %collective-permute-start.18 = (f32[256,512]{1,0:T(8,128)S(1)}, f32[256,512]{1,0:T(8,128)S(1)}, u32[]{:S(2)}, u32[]{:S(2)}) collective-permute-start(f32[256,512]{1,0:T(8,128)S(1)} %add.48), channel_id=1, source_target_pairs={{0,128},{128,0},{1,129},{129,1},{2,130},{130,2},{3,131},{131,3},{4... | collective-permute-start | bytes 1572872 | tf_op jit(solution)/shard_map/ppermute | solution.py:420
  89.3 0.1 add.47
  89.4 0.4 collective-permute-start.16
  89.8 0.5 collective-permute-start.19
  90.4 3.2 %collective-permute-done.19 = f32[32,128]{1,0:T(8,128)S(1)} collective-permute-done((f32[32,128]{1,0:T(8,128)S(1)}, f32[32,128]{1,0:T(8,128)S(1)}, u32[]{:S(2)}, u32[]{:S(2)}) %collective-permute-start.19) | collective-permute-done | bytes 16416 | tf_op jit(solution)/shard_map/ppermute | solution.py:395
  93.6 2.1 %collective-permute-start.20 = (f32[2,32,128]{2,1,0:T(8,128)S(1)}, f32[2,32,128]{2,1,0:T(8,128)S(1)}, u32[]{:S(2)}, u32[]{:S(2)}) collective-permute-start(f32[2,32,128]{2,1,0:T(8,128)S(1)} %pad_maximum_fusion.pair), channel_id=1, source_target_pairs={{0,8},{4,12},{8,0},{12,4},{1,9},{5,13},{9,1},{13,5},{2,10},{6,14},... | collective-permute-start | bytes 98312 | tf_op jit(solution)/shard_map/ppermute | solution.py:396
  95.7 3.3 %collective-permute-done.20.far_pair = f32[2,32,128]{2,1,0:T(8,128)S(1)} collective-permute-done((f32[2,32,128]{2,1,0:T(8,128)S(1)}, f32[2,32,128]{2,1,0:T(8,128)S(1)}, u32[]{:S(2)}, u32[]{:S(2)}) %collective-permute-start.20) | collective-permute-done | bytes 32800 | tf_op jit(solution)/shard_map/ppermute | solution.py:396
  99.0 1.3 %assemble.1 = f32[64,256]{1,0:T(8,128)} custom-call(s32[7]{0:T(128)S(1)} %copy-done.5, f32[2,32,128]{2,1,0:T(8,128)S(1)} %pad_maximum_fusion.pair, f32[2,32,128]{2,1,0:T(8,128)S(1)} %collective-permute-done.20.far_pair), custom_call_target="tpu_custom_call" | custom-call | bytes 131072 | tf_op jit(solution)/shard_map/assemble/pallas_call | solution.py:397
  100.3 2.1 %collective-permute-done.18.high_got = f32[256,512]{1,0:T(8,128)S(1)} collective-permute-done((f32[256,512]{1,0:T(8,128)S(1)}, f32[256,512]{1,0:T(8,128)S(1)}, u32[]{:S(2)}, u32[]{:S(2)}) %collective-permute-start.18) | collective-permute-done | bytes 524320 | tf_op jit(solution)/shard_map/ppermute | solution.py:420
  102.4 10.4 %collective-permute-done.16.low_got = f32[256,512]{1,0:T(8,128)S(1)} collective-permute-done((f32[256,512]{1,0:T(8,128)S(1)}, f32[256,512]{1,0:T(8,128)S(1)}, u32[]{:S(2)}, u32[]{:S(2)}) %collective-permute-start.16) | collective-permute-done | bytes 524320 | tf_op jit(solution)/shard_map/ppermute | solution.py:420
  112.8 1.6 %finish.1 = f32[256,1024]{1,0:T(8,128)} custom-call(f32[256,512]{1,0:T(8,128)S(1)} %get-tuple-element.18.low, f32[256,512]{1,0:T(8,128)S(1)} %get-tuple-element.19.high, f32[256,512]{1,0:T(8,128)S(1)} %collective-permute-done.13.low_core, f32[256,512]{1,0:T(8,128)S(1)} %collective-permute-done.14.high_core, f32[256,512]{1,0:T(8,128)S(1)} %collective-permute-done.16.low_got, ...), custom_call_target="tpu_custom_call" | custom-call | flops 1048576 | bytes 4194304 | tf_op jit(solution)/shard_map/finish/pallas_call | solution.py:223
  (38 shorter events, 0.1 us)
Async XLA Ops:
  0.6 9.4 %copy-start = (bf16[256,1,4096]{2,0,1:T(8,128)(2,1)S(1)}, bf16[256,1,4096]{2,0,1:T(8,128)(2,1)}, u32[]{:S(2)}) copy-start(bf16[256,1,4096]{2,0,1:T(8,128)(2,1)} %param.7) | copy-start | bytes 6291460
  1.2 8.9 %copy-start.8 = (s32[256,1,32]{0,2,1:T(8,128)S(1)}, s32[256,1,32]{0,2,1:T(8,128)}, u32[]{:S(2)}) copy-start(s32[256,1,32]{0,2,1:T(8,128)} %param.6) | copy-start | bytes 98308
  6.2 18.9 %collective-permute-start.7 = (bf16[256,1024]{1,0:T(8,128)(2,1)}, bf16[256,1024]{1,0:T(8,128)(2,1)}, u32[]{:S(2)}, u32[]{:S(2)}) collective-permute-start(bf16[256,1024]{1,0:T(8,128)(2,1)} %get-tuple-element.16.refs_5_.refs_15_), channel_id=1, source_target_pairs={{0,16},{16,32},{32,48},{48,64},{64,80},{80,96},{96,112},{112,0},{1... | collective-permute-start | bytes 1572872 | tf_op jit(solution)/shard_map/ppermute | solution.py:264
  8.1 16.9 %collective-permute-start = (bf16[256,1024]{1,0:T(8,128)(2,1)}, bf16[256,1024]{1,0:T(8,128)(2,1)S(1)}, u32[]{:S(2)}, u32[]{:S(2)}) collective-permute-start(bf16[256,1024]{1,0:T(8,128)(2,1)} %get-tuple-element.14.refs_0_.refs_10_), channel_id=1, source_target_pairs={{0,16},{16,32},{32,48},{48,64},{64,80},{80,96},{96,112},{112,0},{1... | collective-permute-start | bytes 1572872 | tf_op jit(solution)/shard_map/ppermute | solution.py:263
  10.1 15.0 %copy-start.4 = (bf16[128,256]{1,0:T(8,128)(2,1)S(1)}, bf16[128,256]{1,0:T(8,128)(2,1)}, u32[]{:S(2)}) copy-start(bf16[128,256]{1,0:T(8,128)(2,1)} %get-tuple-element.15.refs_0_) | copy-start | bytes 196612
  13.2 17.8 %copy-start.5 = (s32[7]{0:T(128)S(1)}, s32[7]{0:T(128)}, u32[]{:S(2)}) copy-start(s32[7]{0:T(128)} %stack.40.at) | copy-start | bytes 88
  13.2 17.8 %copy-start.6 = (s32[1024]{0:T(1024)S(1)}, s32[1024]{0:T(1024)}, u32[]{:S(2)}) copy-start(s32[1024]{0:T(1024)} %param.9) | copy-start | bytes 12292
  13.2 17.8 %copy-start.7 = (s32[256]{0:T(256)S(1)}, s32[256]{0:T(256)}, u32[]{:S(2)}) copy-start(s32[256]{0:T(256)} %param.8) | copy-start | bytes 3076
  13.3 6.6 %collective-permute-start.1 = (f32[128,256]{1,0:T(8,128)S(1)}, f32[128,256]{1,0:T(8,128)S(1)}, u32[]{:S(2)}, u32[]{:S(2)}) collective-permute-start(f32[128,256]{1,0:T(8,128)S(1)} %dynamic-slice_bitcast_fusion), channel_id=1, source_target_pairs={{0,8},{4,12},{8,0},{12,4},{1,9},{5,13},{9,1},{13,5},{2,10},{6,14},... | collective-permute-start | bytes 393224 | tf_op jit(solution)/shard_map/ppermute | solution.py:348
  25.1 19.8 %collective-permute-start.2 = (bf16[256,1024]{1,0:T(8,128)(2,1)S(1)}, bf16[256,1024]{1,0:T(8,128)(2,1)}, u32[]{:S(2)}, u32[]{:S(2)}) collective-permute-start(bf16[256,1024]{1,0:T(8,128)(2,1)S(1)} %tie.4.refs_0_.refs_1_.refs_11_), channel_id=1, source_target_pairs={{0,16},{16,32},{32,48},{48,64},{64,80},{80,96},{96,112},{112,0},{1... | collective-permute-start | bytes 1572872 | tf_op jit(solution)/shard_map/ppermute | solution.py:263
  25.1 19.8 %collective-permute-start.8 = (bf16[256,1024]{1,0:T(8,128)(2,1)}, bf16[256,1024]{1,0:T(8,128)(2,1)}, u32[]{:S(2)}, u32[]{:S(2)}) collective-permute-start(bf16[256,1024]{1,0:T(8,128)(2,1)} %collective-permute-done.7.refs_1_.refs_6_.refs_16_), channel_id=1, source_target_pairs={{0,16},{16,32},{32,48},{48,64},{64,80},{80,96},{96,112},{112,0},{1... | collective-permute-start | bytes 1572872 | tf_op jit(solution)/shard_map/ppermute | solution.py:264
  25.2 5.8 %collective-permute-start.3 = (f32[64,256]{1,0:T(8,128)S(1)}, f32[64,256]{1,0:T(8,128)S(1)}, u32[]{:S(2)}, u32[]{:S(2)}) collective-permute-start(f32[64,256]{1,0:T(8,128)S(1)} %constant_dynamic-slice_fusion.2), channel_id=1, source_target_pairs={{0,4},{4,0},{8,12},{12,8},{1,5},{5,1},{9,13},{13,9},{2,6},{6,2},{1... | collective-permute-start | bytes 196616 | tf_op jit(solution)/shard_map/ppermute | solution.py:350
  25.9 19.0 %collective-permute-start.4 = (bf16[128,256]{1,0:T(8,128)(2,1)S(1)}, bf16[128,256]{1,0:T(8,128)(2,1)S(1)}, u32[]{:S(2)}, u32[]{:S(2)}) collective-permute-start(bf16[128,256]{1,0:T(8,128)(2,1)S(1)} %tie.5), channel_id=1, source_target_pairs={{0,64},{16,80},{32,96},{48,112},{64,0},{80,16},{96,32},{112,48},{1... | collective-permute-start | bytes 196616 | tf_op jit(solution)/shard_map/ppermute | solution.py:266
  44.9 11.7 %collective-permute-start.5 = (bf16[256,1024]{1,0:T(8,128)(2,1)}, bf16[256,1024]{1,0:T(8,128)(2,1)}, u32[]{:S(2)}, u32[]{:S(2)}) collective-permute-start(bf16[256,1024]{1,0:T(8,128)(2,1)} %tie.6.refs_2_.refs_12_), channel_id=1, source_target_pairs={{0,16},{16,32},{32,48},{48,64},{64,80},{80,96},{96,112},{112,0},{1... | collective-permute-start | bytes 1572872 | tf_op jit(solution)/shard_map/ppermute | solution.py:263
  44.9 20.5 %collective-permute-start.9 = (bf16[256,1024]{1,0:T(8,128)(2,1)}, bf16[256,1024]{1,0:T(8,128)(2,1)}, u32[]{:S(2)}, u32[]{:S(2)}) collective-permute-start(bf16[256,1024]{1,0:T(8,128)(2,1)} %collective-permute-done.8.refs_3_.refs_7_.refs_17_.refs_1_), channel_id=1, source_target_pairs={{0,16},{16,32},{32,48},{48,64},{64,80},{80,96},{96,112},{112,0},{1... | collective-permute-start | bytes 1572872 | tf_op jit(solution)/shard_map/ppermute | solution.py:264
  46.4 24.4 %all-to-all-start = ((f32[16,32,128]{2,1,0:T(8,128)}), f32[16,32,128]{2,1,0:T(8,128)}, u32[]{:S(2)}, u32[]{:S(2)}) async-start(f32[16,32,128]{2,1,0:T(8,128)} %bitcast.16), calls=%async_computation | async-start | bytes 524288 | tf_op jit(solution)/shard_map/all_to_all | solution.py:383
  53.7 21.3 %copy-start.1 = (bf16[256,1024]{1,0:T(8,128)(2,1)S(1)}, bf16[256,1024]{1,0:T(8,128)(2,1)}, u32[]{:S(2)}) copy-start(bf16[256,1024]{1,0:T(8,128)(2,1)} %get-tuple-element.14.refs_0_.refs_10_) | copy-start | bytes 1572868
  53.7 21.3 %copy-start.3 = (bf16[128,256]{1,0:T(8,128)(2,1)S(1)}, bf16[128,256]{1,0:T(8,128)(2,1)}, u32[]{:S(2)}) copy-start(bf16[128,256]{1,0:T(8,128)(2,1)} %get-tuple-element.17.refs_20_) | copy-start | bytes 196612
  55.9 15.9 %collective-permute-start.11 = (bf16[512,256]{1,0:T(8,128)(2,1)}, bf16[512,256]{1,0:T(8,128)(2,1)}, u32[]{:S(2)}, u32[]{:S(2)}) collective-permute-start(bf16[512,256]{1,0:T(8,128)(2,1)} %pick.2), channel_id=1, source_target_pairs={{0,2},{2,0},{1,3},{3,1},{4,6},{6,4},{5,7},{7,5},{8,10},{10,8},{9,1... | collective-permute-start | bytes 786440 | tf_op jit(solution)/shard_map/ppermute | solution.py:272
  58.3 16.2 %collective-permute-start.6 = (bf16[128,1024]{1,0:T(8,128)(2,1)}, bf16[128,1024]{1,0:T(8,128)(2,1)S(1)}, u32[]{:S(2)}, u32[]{:S(2)}) collective-permute-start(bf16[128,1024]{1,0:T(8,128)(2,1)} %constant_dynamic-slice_fusion.1), channel_id=1, source_target_pairs={{0,16},{16,32},{32,48},{48,64},{64,80},{80,96},{96,112},{112,0},{1... | collective-permute-start | bytes 786440 | tf_op jit(solution)/shard_map/ppermute | solution.py:263
  67.1 7.9 %collective-permute-start.10 = (bf16[128,1024]{1,0:T(8,128)(2,1)}, bf16[128,1024]{1,0:T(8,128)(2,1)}, u32[]{:S(2)}, u32[]{:S(2)}) collective-permute-start(bf16[128,1024]{1,0:T(8,128)(2,1)} %constant_dynamic-slice_fusion), channel_id=1, source_target_pairs={{0,16},{16,32},{32,48},{48,64},{64,80},{80,96},{96,112},{112,0},{1... | collective-permute-start | bytes 786440 | tf_op jit(solution)/shard_map/ppermute | solution.py:264
  69.2 5.3 %collective-permute-start.12 = (bf16[256,256]{1,0:T(8,128)(2,1)}, bf16[256,256]{1,0:T(8,128)(2,1)}, u32[]{:S(2)}, u32[]{:S(2)}) collective-permute-start(bf16[256,256]{1,0:T(8,128)(2,1)} %pick.3), channel_id=1, source_target_pairs={{0,2},{2,0},{1,3},{3,1},{4,6},{6,4},{5,7},{7,5},{8,10},{10,8},{9,1... | collective-permute-start | bytes 393224 | tf_op jit(solution)/shard_map/ppermute | solution.py:275
  75.0 1.0 copy-start.2
  80.4 5.5 %collective-permute-start.17 = (f32[256,512]{1,0:T(8,128)S(1)}, f32[256,512]{1,0:T(8,128)S(1)}, u32[]{:S(2)}, u32[]{:S(2)}) collective-permute-start(f32[256,512]{1,0:T(8,128)S(1)} %get-tuple-element.25), channel_id=1, source_target_pairs={{0,1},{1,0},{2,3},{3,2},{4,5},{5,4},{6,7},{7,6},{8,9},{9,8},{10,11... | collective-permute-start | bytes 1572872 | tf_op jit(solution)/shard_map/ppermute | solution.py:279
  80.5 8.8 %collective-permute-start.15 = (f32[256,512]{1,0:T(8,128)S(1)}, f32[256,512]{1,0:T(8,128)S(1)}, u32[]{:S(2)}, u32[]{:S(2)}) collective-permute-start(f32[256,512]{1,0:T(8,128)S(1)} %get-tuple-element.23), channel_id=1, source_target_pairs={{0,1},{1,0},{2,3},{3,2},{4,5},{5,4},{6,7},{7,6},{8,9},{9,8},{10,11... | collective-permute-start | bytes 1572872 | tf_op jit(solution)/shard_map/ppermute | solution.py:279
  85.4 14.9 %collective-permute-start.13 = (f32[256,512]{1,0:T(8,128)S(1)}, f32[256,512]{1,0:T(8,128)S(1)}, u32[]{:S(2)}, u32[]{:S(2)}) collective-permute-start(f32[256,512]{1,0:T(8,128)S(1)} %get-tuple-element.20), channel_id=1, source_target_pairs={{0,1},{1,0},{2,3},{3,2},{4,5},{5,4},{6,7},{7,6},{8,9},{9,8},{10,11... | collective-permute-start | bytes 1572872 | tf_op jit(solution)/shard_map/ppermute | solution.py:282
  85.5 14.7 %collective-permute-start.14 = (f32[256,512]{1,0:T(8,128)S(1)}, f32[256,512]{1,0:T(8,128)S(1)}, u32[]{:S(2)}, u32[]{:S(2)}) collective-permute-start(f32[256,512]{1,0:T(8,128)S(1)} %get-tuple-element.21), channel_id=1, source_target_pairs={{0,1},{1,0},{2,3},{3,2},{4,5},{5,4},{6,7},{7,6},{8,9},{9,8},{10,11... | collective-permute-start | bytes 1572872 | tf_op jit(solution)/shard_map/ppermute | solution.py:282
  86.0 16.4 %collective-permute-start.18 = (f32[256,512]{1,0:T(8,128)S(1)}, f32[256,512]{1,0:T(8,128)S(1)}, u32[]{:S(2)}, u32[]{:S(2)}) collective-permute-start(f32[256,512]{1,0:T(8,128)S(1)} %add.48), channel_id=1, source_target_pairs={{0,128},{128,0},{1,129},{129,1},{2,130},{130,2},{3,131},{131,3},{4... | collective-permute-start | bytes 1572872 | tf_op jit(solution)/shard_map/ppermute | solution.py:420
  89.4 23.4 %collective-permute-start.16 = (f32[256,512]{1,0:T(8,128)S(1)}, f32[256,512]{1,0:T(8,128)S(1)}, u32[]{:S(2)}, u32[]{:S(2)}) collective-permute-start(f32[256,512]{1,0:T(8,128)S(1)} %add.47), channel_id=1, source_target_pairs={{0,128},{128,0},{1,129},{129,1},{2,130},{130,2},{3,131},{131,3},{4... | collective-permute-start | bytes 1572872 | tf_op jit(solution)/shard_map/ppermute | solution.py:420
  89.8 3.7 %collective-permute-start.19 = (f32[32,128]{1,0:T(8,128)S(1)}, f32[32,128]{1,0:T(8,128)S(1)}, u32[]{:S(2)}, u32[]{:S(2)}) collective-permute-start(f32[32,128]{1,0:T(8,128)S(1)} %sum.1.refs_24_), channel_id=1, source_target_pairs={{0,4},{4,0},{8,12},{12,8},{1,5},{5,1},{9,13},{13,9},{2,6},{6,2},{1... | collective-permute-start | bytes 49160 | tf_op jit(solution)/shard_map/ppermute | solution.py:395
  93.6 5.4 %collective-permute-start.20 = (f32[2,32,128]{2,1,0:T(8,128)S(1)}, f32[2,32,128]{2,1,0:T(8,128)S(1)}, u32[]{:S(2)}, u32[]{:S(2)}) collective-permute-start(f32[2,32,128]{2,1,0:T(8,128)S(1)} %pad_maximum_fusion.pair), channel_id=1, source_target_pairs={{0,8},{4,12},{8,0},{12,4},{1,9},{5,13},{9,1},{13,5},{2,10},{6,14},... | collective-permute-start | bytes 98312 | tf_op jit(solution)/shard_map/ppermute | solution.py:396

commit v7 on v6

--- a/solution.py
+++ b/solution.py
@@ -37,26 +37,32 @@
     return lax.dot_general(turned, pick, TURNED, preferred_element_type=jnp.float32)
 
 
-def dequant_kernel(at, exps, values, own_values, far_values, low, high, own, far):
+FAR = 32
+
+
+def dequant_kernel(at, exps, values, own_values, far_values, low, high, own, far_scale):
     step = pl.program_id(0)
+    rows, half = values.shape[0], own.shape[0]
     turned = powers(exps[...])
+
+    @pl.when(step == 0)
+    def _():
+        far_scale[...] = wide_scale(turned, at[AT_FAR] * 2, 256)
+        scale = wide_scale(turned, at[AT_OWN] * 2, 256)
+        scale = jnp.where(at[AT_CORE] == 0, scale[:half], scale[half:])
+        own[...] = (own_values[...].astype(jnp.float32) * scale).astype(jnp.bfloat16)
+
     grads = values[...].astype(jnp.float32) * wide_scale(turned, at[AT_YL] * 16 + step * 4, 512)
     grads = grads.astype(jnp.bfloat16)
-    low[...] = jnp.concatenate([grads[:, 0:128], grads[:, 256:384]], 1)
+    low[0:rows] = jnp.concatenate([grads[:, 0:128], grads[:, 256:384]], 1)
     high[...] = jnp.concatenate([grads[:, 128:256], grads[:, 384:512]], 1)
-
-    @pl.when(step == 0)
-    def _():
-        half = far.shape[0]
-        for block, source, result in ((AT_OWN, own_values, own), (AT_FAR, far_values, far)):
-            scale = wide_scale(turned, at[block] * 2, 256)
-            scale = jnp.where(at[AT_CORE] == 0, scale[:half], scale[half:])
-            result[...] = (source[...].astype(jnp.float32) * scale).astype(jnp.bfloat16)
+    scale = far_scale[pl.ds(pl.multiple_of(at[AT_CORE] * half + step * FAR, FAR), FAR)]
+    low[rows : rows + FAR] = (far_values[...].astype(jnp.float32) * scale).astype(jnp.bfloat16)
 
 
 def dequant(at, exps, mantissas):
     rows, width = mantissas.shape
-    side = jax.ShapeDtypeStruct((rows, width // 4), jnp.bfloat16)
+    half = rows // 2
     return pl.pallas_call(
         dequant_kernel,
         grid_spec=pltpu.PrefetchScalarGridSpec(
@@ -65,21 +71,67 @@
             in_specs=[
                 pl.BlockSpec(exps.shape, lambda g, at: (0, 0)),
                 pl.BlockSpec((rows, 512), lambda g, at: (0, at[AT_YL] * 4 + g)),
-                pl.BlockSpec((rows // 2, 256), lambda g, at: (at[AT_CORE], at[AT_OWN])),
-                pl.BlockSpec((rows // 2, 256), lambda g, at: (at[AT_CORE], at[AT_FAR])),
+                pl.BlockSpec((half, 256), lambda g, at: (at[AT_CORE], at[AT_OWN])),
+                pl.BlockSpec((FAR, 256), lambda g, at: (at[AT_CORE] * 4 + g, at[AT_FAR])),
             ],
             out_specs=[
+                pl.BlockSpec((rows + FAR, 256), lambda g, at: (0, g)),
                 pl.BlockSpec((rows, 256), lambda g, at: (0, g)),
-                pl.BlockSpec((rows, 256), lambda g, at: (0, g)),
-                pl.BlockSpec((rows // 2, 256), lambda g, at: (0, 0)),
-                pl.BlockSpec((rows // 2, 256), lambda g, at: (0, 0)),
+                pl.BlockSpec((half, 256), lambda g, at: (0, 0)),
             ],
-        ),
-        out_shape=[side, side] + [jax.ShapeDtypeStruct((rows // 2, 256), jnp.bfloat16)] * 2,
-        compiler_params=params(61),
+            scratch_shapes=[pltpu.VMEM((rows, 256), jnp.float32)],
+        ),
+        out_shape=[
+            jax.ShapeDtypeStruct((rows + FAR, width // 4), jnp.bfloat16),
+            jax.ShapeDtypeStruct((rows, width // 4), jnp.bfloat16),
+            jax.ShapeDtypeStruct((half, 256), jnp.bfloat16),
+        ],
+        compiler_params=params(62),
         cost_estimate=cost(1 << 25, 2 << 20),
         name="dequant",
     )(at, exps, mantissas, mantissas, mantissas)
+
+
+def halve_kernel(at, low, far, high, low_lanes, high_lanes, after, low_half, high_half, third):
+    del after
+    half = low.shape[0]
+    low_half[0:half] = low[...]
+    low_half[half : half + FAR] = far[...]
+    high_half[...] = high[...]
+    third[...] = jnp.concatenate([low_lanes[...], high_lanes[...]], 1)
+
+
+def halve(at, low, high, after):
+    rows, width = high.shape
+    half = rows // 2
+    return pl.pallas_call(
+        halve_kernel,
+        grid_spec=pltpu.PrefetchScalarGridSpec(
+            num_scalar_prefetch=1,
+            grid=(1,),
+            in_specs=[
+                pl.BlockSpec((half, width), lambda g, at: (at[AT_CORE], 0)),
+                pl.BlockSpec((FAR, width), lambda g, at: (rows // FAR, 0)),
+                pl.BlockSpec((half, width), lambda g, at: (at[AT_CORE], 0)),
+                lanes_at_z(rows, False),
+                lanes_at_z(rows, False),
+                pl.BlockSpec(memory_space=pl.ANY),
+            ],
+            out_specs=[
+                pl.BlockSpec((half + FAR, width), lambda g, at: (0, 0)),
+                pl.BlockSpec((half, width), lambda g, at: (0, 0)),
+                pl.BlockSpec((rows, 256), lambda g, at: (0, 0)),
+            ],
+        ),
+        out_shape=[
+            jax.ShapeDtypeStruct((half + FAR, width), jnp.bfloat16),
+            jax.ShapeDtypeStruct((half, width), jnp.bfloat16),
+            jax.ShapeDtypeStruct((rows, 256), jnp.bfloat16),
+        ],
+        compiler_params=params(8),
+        cost_estimate=cost(0, 2 << 20),
+        name="halve",
+    )(at, low, low, high, low, high, after)
 
 
 def pick_kernel(count, at, *refs):
@@ -134,7 +186,9 @@
                 theirs = near[row : row + rows]
                 row += rows
             else:
-                theirs = (own if i == 0 else third if i == count - 2 else far)[...]
+                theirs = (own if i == 0 else third)[...] if i < count - 1 else jnp.concatenate(
+                    [far[:, lane : lane + 256] for lane in range(0, 1024, 256)], 0
+                )
             left[start : start + rows] = jnp.where(use_mine, mine, theirs)
             start += rows
 
@@ -174,6 +228,8 @@
         )
     specs += specs[-len(pieces) :]
     specs += [pl.BlockSpec(r.shape, lambda g, at: (0, 0)) for r in received]
+    last = pieces[-1][2]
+    specs.append(pl.BlockSpec((FAR, last.shape[1]), lambda g, at: (last.shape[0] // FAR - 1, 0)))
     specs += [pl.BlockSpec(memory_space=pl.ANY)] * len(after)
     sides = [p[2] for p in pieces], [p[3] for p in pieces]
     return pl.pallas_call(
@@ -187,7 +243,7 @@
         compiler_params=params(20),
         cost_estimate=cost(2 * sum(sizes) * 256 * 2048, 7 << 20),
         name="gram",
-    )(at, *sides[0], *sides[1], *sides[0], *sides[1], *received, *after)
+    )(at, *sides[0], *sides[1], *sides[0], *sides[1], *received, last, *after)
 
 
 def add_kernel(left, right, out):
@@ -250,30 +306,27 @@
 
 
 def fisher_terms(at, mantissas, exps, pair, placed):
-    core = lax.axis_index("core")
     rows = mantissas.shape[0]
-    low, high, own, far = dequant(at, exps, mantissas)
+    low, high, own = dequant(at, exps, mantissas)
 
     half = rows // 2
     pieces = [(half, True, low, high)]
     for step in range(1, Z // 2 + 1):
         if step == Z // 2:
-            low = lax.dynamic_slice_in_dim(low, core * half, half, 0)
-            high = lax.dynamic_slice_in_dim(high, core * half, half, 0)
+            low, high, third = halve(at, low, high, near)
         low = lax.ppermute(low, ("z", "core"), RING)
         high = lax.ppermute(high, ("z", "core"), RING)
         if step == 1:
-            far = lax.ppermute(tie(far, low), "z", [(i, (i + Z // 2) % Z) for i in range(Z)])
             low = tie(low, pair)
         if step == 2:
-            low = tie(low, placed, far)
-            placed = tie(placed, high)
-        pieces.append((low.shape[0], False, low, high))
-    near = lax.ppermute(pick(at, pieces[1:3]), "yl", SWAP)
+            low = tie(low, placed)
+        pieces.append((rows if step < Z // 2 else half, False, low, high))
+        if step == 2:
+            near = pick(at, pieces[1:3])
+            placed = tie(placed, near)
+            near = lax.ppermute(near, "yl", SWAP)
     mine = own_slots(placed)
-    third = pick(at, pieces[3:4])
-    third = lax.ppermute(third, "yl", SWAP)
-    received = (own, near, third, far)
+    received = (own, near, lax.ppermute(third, "yl", SWAP))
 
     *given_other, low_given, high_given = gram(at, pieces, received, False, mine)
     swapped = [lax.ppermute(g, "core", SWAP) for g in given_other]

time: 115 us -> 106 us (0.922)
  waiting for transfers between devices: 48.8 us -> 38.3 us
  starting transfers between devices: 32.5 us -> 37.2 us
  Pallas kernels: 24.1 us -> 21.6 us
  local copies, waits for them, and re-layouts: 5.02 us -> 3.51 us
    ppermute x3 -> x2, waiting for transfers between devices: 14.4 us -> 0.66 us  [the longest x1 0.66 us: fisher_terms(): received = (own, near, lax.ppermute(third, 'yl', SWAP))]
    ppermute x4, waiting for transfers between devices: 5.21 us -> 0.32 us  [fisher_terms(): low = lax.ppermute(low, ('z', 'core'), RING)]
    ppermute x4, starting transfers between devices: 3.8 us -> 8.06 us  [fisher_terms(): low = lax.ppermute(low, ('z', 'core'), RING)]
    ppermute x1, waiting for transfers between devices: 0.01 us -> 3.91 us  [placed_scores(): lax.ppermute(lax.dynamic_slice_in_dim(pair, (1 - x % 2) * share, share, 0...]
    dynamic_slice x2 -> x0, local copies, waits for them, and re-layouts: 3.33 us -> none  [the longest x1 1.67 us: fisher_terms(): low = lax.dynamic_slice_in_dim(low, core * half, half, 0)]
    pallas_call x2 -> x1, Pallas kernels: 4.3 us -> 1.34 us  [pick(): pl.pallas_call(functools.partial(pick_kernel, len(pieces)), grid_spec=plt...]
    ppermute x4, waiting for transfers between devices: 5.82 us -> 8.39 us  [fisher_terms(): high = lax.ppermute(high, ('z', 'core'), RING)]
    ppermute x3 -> x2, starting transfers between devices: 7.43 us -> 5.56 us  [the longest x1 3.98 us: fisher_terms(): received = (own, near, lax.ppermute(third, 'yl', SWAP))]
  transfers between devices with their start and end apart: 22 -> 21, of which waited for: 10 -> 12; matrix products, arithmetic and copies ran while one was open for 6% -> 4% of each run, Pallas kernels for 12% -> 10%
where the time goes in v7:
time: 106 us; the launch traced here: 105 us
  waiting for transfers between devices  38.3 us (36%)
  starting transfers between devices  37.2 us (35%)
  Pallas kernels  21.6 us (20%)
  matrix products  3.69 us (3%)
  local copies, waits for them, and re-layouts  3.51 us (3%)
    ppermute x2, waiting for transfers between devices, per_device(): got = [lax.ppermute(g, 'yh', SWAP) for g in given]  12.6 us
    ppermute x4, waiting for transfers between devices, fisher_terms(): high = lax.ppermute(high, ('z', 'core'), RING)  8.39 us
    pallas_call x2, Pallas kernels, gram(): pl.pallas_call(functools.partial(gram_kernel, sizes, kept), grid_spec=plt...  8.31 us
    all_to_all x1, starting transfers between devices, own_slots(): lax.all_to_all(placed.reshape(YH * Z, half, double), ('yh', 'z'), 0, 0, t...  8.09 us
    ppermute x4, starting transfers between devices, fisher_terms(): low = lax.ppermute(low, ('z', 'core'), RING)  8.06 us
    ppermute x4, starting transfers between devices, fisher_terms(): high = lax.ppermute(high, ('z', 'core'), RING)  5.08 us
    pallas_call x1, Pallas kernels, dequant(): pl.pallas_call(dequant_kernel, grid_spec=pltpu.PrefetchScalarGridSpec(num...  4.96 us
    ppermute x1, waiting for transfers between devices, placed_scores(): lax.ppermute(lax.dynamic_slice_in_dim(scores, (1 - upper) * 2 * share, 2...  4.4 us
  transfers between devices with their start and end apart: 21, of which 12 were waited for; matrix products, arithmetic and copies ran while one was open for 4% of the time, Pallas kernels for 10%

profile of v7, /device:TPU:2, one launch (start us, length us, event | category | flops | bytes accessed | tf_op | source)
XLA Modules:
  0.0 105.1 jit_solution(17184569209429452897)
XLA Ops:
  0.6 0.7 stack.40.at
  1.3 5.0 %dequant.1 = (bf16[288,1024]{1,0:T(8,128)(2,1)}, bf16[256,1024]{1,0:T(8,128)(2,1)}, bf16[128,256]{1,0:T(8,128)(2,1)}) custom-call(s32[7]{0:T(128)} %stack.40.at, s32[32,256]{1,0:T(8,128)} %bitcast.47, bf16[256,4096]{1,0:T(8,128)(2,1)} %bitcast.43, bf16[256,4096]{1,0:T(8,128)(2,1)} %bitcast.44, bf16[256,4096]{1,0:T(8,128)(2,1)} %bitcast.45), custom_call_target="tpu_custom_call" | custom-call | flops 33554432 | bytes 2097152 | tf_op jit(solution)/shard_map/dequant/pallas_call | solution.py:66
  6.3 1.9 %collective-permute-start = (bf16[288,1024]{1,0:T(8,128)(2,1)}, bf16[288,1024]{1,0:T(8,128)(2,1)S(1)}, u32[]{:S(2)}, u32[]{:S(2)}) collective-permute-start(bf16[288,1024]{1,0:T(8,128)(2,1)} %get-tuple-element.16.refs_0_.refs_10_), channel_id=1, source_target_pairs={{0,16},{16,32},{32,48},{48,64},{64,80},{80,96},{96,112},{112,0},{1... | collective-permute-start | bytes 1769480 | tf_op jit(solution)/shard_map/ppermute | solution.py:317
  8.2 1.9 %collective-permute-start.5 = (bf16[256,1024]{1,0:T(8,128)(2,1)}, bf16[256,1024]{1,0:T(8,128)(2,1)S(1)}, u32[]{:S(2)}, u32[]{:S(2)}) collective-permute-start(bf16[256,1024]{1,0:T(8,128)(2,1)} %get-tuple-element.17.refs_5_.refs_15_), channel_id=1, source_target_pairs={{0,16},{16,32},{32,48},{48,64},{64,80},{80,96},{96,112},{112,0},{1... | collective-permute-start | bytes 1572872 | tf_op jit(solution)/shard_map/ppermute | solution.py:318
  10.1 3.7 %fusion.1 = f32[256,256]{0,1:T(8,128)S(1)} fusion(bf16[256,1,4096]{2,0,1:T(8,128)(2,1)} %param.7, s32[4096]{0:T(1024)S(1)} %add_select_fusion, s32[256,1,32]{0,2,1:T(8,128)S(1)} %copy-done.7, bf16[256,1,4096]{2,0,1:T(8,128)(2,1)} %param.5), kind=kOutput, calls=%fused_computation.2 | convolution fusion | flops 606232576 | bytes 4505600 | tf_op jit(solution)/shard_map/dot_general | solution.py:397
  13.9 2.2 %collective-permute-start.1 = (f32[128,256]{1,0:T(8,128)S(1)}, f32[128,256]{1,0:T(8,128)S(1)}, u32[]{:S(2)}, u32[]{:S(2)}) collective-permute-start(f32[128,256]{1,0:T(8,128)S(1)} %dynamic-slice_bitcast_fusion), channel_id=1, source_target_pairs={{0,8},{4,12},{8,0},{12,4},{1,9},{5,13},{9,1},{13,5},{2,10},{6,14},... | collective-permute-start | bytes 393224 | tf_op jit(solution)/shard_map/ppermute | solution.py:401
  16.1 4.4 %collective-permute-done.1 = f32[128,256]{1,0:T(8,128)S(1)} collective-permute-done((f32[128,256]{1,0:T(8,128)S(1)}, f32[128,256]{1,0:T(8,128)S(1)}, u32[]{:S(2)}, u32[]{:S(2)}) %collective-permute-start.1) | collective-permute-done | bytes 131104 | tf_op jit(solution)/shard_map/ppermute | solution.py:401
  20.5 3.0 %collective-permute-start.2 = (bf16[288,1024]{1,0:T(8,128)(2,1)S(1)}, bf16[288,1024]{1,0:T(8,128)(2,1)S(1)}, u32[]{:S(2)}, u32[]{:S(2)}) collective-permute-start(bf16[288,1024]{1,0:T(8,128)(2,1)S(1)} %tie.3.refs_0_.refs_1_.refs_11_), channel_id=1, source_target_pairs={{0,16},{16,32},{32,48},{48,64},{64,80},{80,96},{96,112},{112,0},{1... | collective-permute-start | bytes 1769480 | tf_op jit(solution)/shard_map/ppermute | solution.py:317
  23.5 2.3 %collective-permute-done.5.refs_1_.refs_6_.refs_16_ = bf16[256,1024]{1,0:T(8,128)(2,1)S(1)} collective-permute-done((bf16[256,1024]{1,0:T(8,128)(2,1)}, bf16[256,1024]{1,0:T(8,128)(2,1)S(1)}, u32[]{:S(2)}, u32[]{:S(2)}) %collective-permute-start.5) | collective-permute-done | bytes 524320 | tf_op jit(solution)/shard_map/ppermute | solution.py:318
  25.8 0.6 collective-permute-start.3
  26.4 3.9 %collective-permute-done.3.got = f32[64,256]{1,0:T(8,128)S(1)} collective-permute-done((f32[64,256]{1,0:T(8,128)S(1)}, f32[64,256]{1,0:T(8,128)S(1)}, u32[]{:S(2)}, u32[]{:S(2)}) %collective-permute-start.3) | collective-permute-done | bytes 65568 | tf_op jit(solution)/shard_map/ppermute | solution.py:403
  30.4 1.4 %place.1.refs_1_.refs_0_ = f32[512,128]{1,0:T(8,128)S(1)} custom-call(s32[7]{0:T(128)S(1)} %copy-done.4, f32[2,64,256]{2,1,0:T(8,128)S(1)} %bitcast.39, f32[64,256]{1,0:T(8,128)S(1)} %collective-permute-done.3.got, s32[1,256]{1,0:T(1,128)S(1)} %bitcast.42, s32[1,1024]{1,0:T(1,128)S(1)} %bitcast.41), custom_call_target="tpu_custom_call" | custom-call | flops 268435456 | bytes 1048576 | tf_op jit(solution)/shard_map/place/pallas_call | solution.py:405
  31.8 0.3 collective-permute-done.2.refs_0_
  32.1 1.3 %collective-permute-start.4 = (bf16[288,1024]{1,0:T(8,128)(2,1)S(1)}, bf16[288,1024]{1,0:T(8,128)(2,1)S(1)}, u32[]{:S(2)}, u32[]{:S(2)}) collective-permute-start(bf16[288,1024]{1,0:T(8,128)(2,1)S(1)} %tie.4.refs_2_.refs_12_), channel_id=1, source_target_pairs={{0,16},{16,32},{32,48},{48,64},{64,80},{80,96},{96,112},{112,0},{1... | collective-permute-start | bytes 1769480 | tf_op jit(solution)/shard_map/ppermute | solution.py:317
  33.4 4.3 %collective-permute-done.6.refs_3_.refs_7_.refs_17_ = bf16[256,1024]{1,0:T(8,128)(2,1)S(1)} collective-permute-done((bf16[256,1024]{1,0:T(8,128)(2,1)S(1)}, bf16[256,1024]{1,0:T(8,128)(2,1)S(1)}, u32[]{:S(2)}, u32[]{:S(2)}) %collective-permute-start.6) | collective-permute-done | bytes 524320 | tf_op jit(solution)/shard_map/ppermute | solution.py:318
  37.7 1.3 %collective-permute-start.7 = (bf16[256,1024]{1,0:T(8,128)(2,1)S(1)}, bf16[256,1024]{1,0:T(8,128)(2,1)S(1)}, u32[]{:S(2)}, u32[]{:S(2)}) collective-permute-start(bf16[256,1024]{1,0:T(8,128)(2,1)S(1)} %collective-permute-done.6.refs_3_.refs_7_.refs_17_), channel_id=1, source_target_pairs={{0,16},{16,32},{32,48},{48,64},{64,80},{80,96},{96,112},{112,0},{1... | collective-permute-start | bytes 1572872 | tf_op jit(solution)/shard_map/ppermute | solution.py:318
  39.0 1.3 %pick.1.refs_1_ = bf16[512,256]{1,0:T(8,128)(2,1)} custom-call(s32[7]{0:T(128)S(1)} %copy-done.4, bf16[288,1024]{1,0:T(8,128)(2,1)S(1)} %tie.3.refs_0_.refs_1_.refs_11_, bf16[256,1024]{1,0:T(8,128)(2,1)S(1)} %collective-permute-done.5.refs_1_.refs_6_.refs_16_, bf16[288,1024]{1,0:T(8,128)(2,1)S(1)} %tie.4.refs_2_.refs_12_, ...), custom_call_target="tpu_custom_call" | custom-call | bytes 524288 | tf_op jit(solution)/shard_map/pick/pallas_call | solution.py:156
  40.4 1.6 %collective-permute-start.8 = (bf16[512,256]{1,0:T(8,128)(2,1)}, bf16[512,256]{1,0:T(8,128)(2,1)}, u32[]{:S(2)}, u32[]{:S(2)}) collective-permute-start(bf16[512,256]{1,0:T(8,128)(2,1)} %pick.1.refs_1_), channel_id=1, source_target_pairs={{0,2},{2,0},{1,3},{3,1},{4,6},{6,4},{5,7},{7,5},{8,10},{10,8},{9,1... | collective-permute-start | bytes 786440 | tf_op jit(solution)/shard_map/ppermute | solution.py:327
  42.0 0.7 copy-done.2
  42.7 8.1 %all-to-all-start = ((f32[16,32,128]{2,1,0:T(8,128)}), f32[16,32,128]{2,1,0:T(8,128)}, u32[]{:S(2)}, u32[]{:S(2)}) async-start(f32[16,32,128]{2,1,0:T(8,128)} %bitcast.38), calls=%async_computation | async-start | bytes 524288 | tf_op jit(solution)/shard_map/all_to_all | solution.py:436
  50.8 1.4 %halve.1 = (bf16[160,1024]{1,0:T(8,128)(2,1)}, bf16[128,1024]{1,0:T(8,128)(2,1)}, bf16[256,256]{1,0:T(8,128)(2,1)}) custom-call(s32[7]{0:T(128)S(1)} %copy-done.4, bf16[288,1024]{1,0:T(8,128)(2,1)S(1)} %collective-permute-done.4.low.far.low_lanes.refs_3_.refs_13_, bf16[288,1024]{1,0:T(8,128)(2,1)S(1)} %collective-permute-done.4.low.far.low_lanes.refs_3_.refs_13_, ...), custom_call_target="tpu_custom_call" | custom-call | bytes 2097152 | tf_op jit(solution)/shard_map/halve/pallas_call | solution.py:107
  52.2 1.9 %collective-permute-start.9 = (bf16[160,1024]{1,0:T(8,128)(2,1)}, bf16[160,1024]{1,0:T(8,128)(2,1)}, u32[]{:S(2)}, u32[]{:S(2)}) collective-permute-start(bf16[160,1024]{1,0:T(8,128)(2,1)} %get-tuple-element.18), channel_id=1, source_target_pairs={{0,16},{16,32},{32,48},{48,64},{64,80},{80,96},{96,112},{112,0},{1... | collective-permute-start | bytes 983048 | tf_op jit(solution)/shard_map/ppermute | solution.py:317
  54.1 1.9 %collective-permute-start.10 = (bf16[128,1024]{1,0:T(8,128)(2,1)}, bf16[128,1024]{1,0:T(8,128)(2,1)}, u32[]{:S(2)}, u32[]{:S(2)}) collective-permute-start(bf16[128,1024]{1,0:T(8,128)(2,1)} %get-tuple-element.19), channel_id=1, source_target_pairs={{0,16},{16,32},{32,48},{48,64},{64,80},{80,96},{96,112},{112,0},{1... | collective-permute-start | bytes 786440 | tf_op jit(solution)/shard_map/ppermute | solution.py:318
  56.0 4.0 %collective-permute-start.11 = (bf16[256,256]{1,0:T(8,128)(2,1)}, bf16[256,256]{1,0:T(8,128)(2,1)S(1)}, u32[]{:S(2)}, u32[]{:S(2)}) collective-permute-start(bf16[256,256]{1,0:T(8,128)(2,1)} %get-tuple-element.21), channel_id=1, source_target_pairs={{0,2},{2,0},{1,3},{3,1},{4,6},{6,4},{5,7},{7,5},{8,10},{10,8},{9,1... | collective-permute-start | bytes 393224 | tf_op jit(solution)/shard_map/ppermute | solution.py:329
  59.9 1.5 %all-to-all-done.parts = f32[16,32,128]{2,1,0:T(8,128)} async-done(((f32[16,32,128]{2,1,0:T(8,128)}), f32[16,32,128]{2,1,0:T(8,128)}, u32[]{:S(2)}, u32[]{:S(2)}) %all-to-all-start) | async-done | bytes 262176 | tf_op jit(solution)/shard_map/all_to_all | solution.py:436
  61.5 1.0 sum.1.refs_24_
  62.4 0.7 collective-permute-done.11.refs_22_
  63.1 1.8 %collective-permute-done.10.refs_9_.refs_19_ = bf16[128,1024]{1,0:T(8,128)(2,1)} collective-permute-done((bf16[128,1024]{1,0:T(8,128)(2,1)}, bf16[128,1024]{1,0:T(8,128)(2,1)}, u32[]{:S(2)}, u32[]{:S(2)}) %collective-permute-start.10) | collective-permute-done | bytes 262176 | tf_op jit(solution)/shard_map/ppermute | solution.py:318
  64.9 1.1 %copy-done = bf16[288,1024]{1,0:T(8,128)(2,1)S(1)} copy-done((bf16[288,1024]{1,0:T(8,128)(2,1)S(1)}, bf16[288,1024]{1,0:T(8,128)(2,1)}, u32[]{:S(2)}) %copy-start) | copy-done | bytes 589848
  66.0 1.0 copy-done.1
  67.0 4.1 %gram.3 = (f32[256,512]{1,0:T(8,128)S(1)}, f32[256,512]{1,0:T(8,128)S(1)}, f32[256,512]{1,0:T(8,128)S(1)}, f32[256,512]{1,0:T(8,128)S(1)}) custom-call(s32[7]{0:T(128)S(1)} %copy-done.4, bf16[288,1024]{1,0:T(8,128)(2,1)S(1)} %copy-done, bf16[288,1024]{1,0:T(8,128)(2,1)S(1)} %tie.3.refs_0_.refs_1_.refs_11_, bf16[288,1024]{1,0:T(8,128)(2,1)S(1)} %tie.4.refs_2_.refs_12_, ...), custom_call_target="tpu_custom_call" | custom-call | flops 1073741824 | bytes 7340032 | tf_op jit(solution)/shard_map/gram/pallas_call | solution.py:235
  71.1 0.1 collective-permute-start.16
  71.2 0.5 collective-permute-start.14
  71.7 4.2 %gram.2 = (f32[256,512]{1,0:T(8,128)S(1)}, f32[256,512]{1,0:T(8,128)S(1)}, f32[256,512]{1,0:T(8,128)S(1)}, f32[256,512]{1,0:T(8,128)S(1)}) custom-call(s32[7]{0:T(128)S(1)} %copy-done.4, bf16[288,1024]{1,0:T(8,128)(2,1)S(1)} %copy-done, bf16[288,1024]{1,0:T(8,128)(2,1)S(1)} %tie.3.refs_0_.refs_1_.refs_11_, bf16[288,1024]{1,0:T(8,128)(2,1)S(1)} %tie.4.refs_2_.refs_12_, ...), custom_call_target="tpu_custom_call" | custom-call | flops 1073741824 | bytes 7340032 | tf_op jit(solution)/shard_map/gram/pallas_call | solution.py:235
  75.9 0.2 collective-permute-start.12
  76.1 0.4 collective-permute-start.13
  76.5 0.1 add.43
  76.6 3.4 %collective-permute-start.17 = (f32[256,512]{1,0:T(8,128)S(1)}, f32[256,512]{1,0:T(8,128)S(1)}, u32[]{:S(2)}, u32[]{:S(2)}) collective-permute-start(f32[256,512]{1,0:T(8,128)S(1)} %add.43), channel_id=1, source_target_pairs={{0,128},{128,0},{1,129},{129,1},{2,130},{130,2},{3,131},{131,3},{4... | collective-permute-start | bytes 1572872 | tf_op jit(solution)/shard_map/ppermute | solution.py:473
  80.0 0.1 add.42
  80.1 0.3 collective-permute-start.15
  80.4 0.5 collective-permute-start.18
  80.9 3.2 %collective-permute-done.18 = f32[32,128]{1,0:T(8,128)S(1)} collective-permute-done((f32[32,128]{1,0:T(8,128)S(1)}, f32[32,128]{1,0:T(8,128)S(1)}, u32[]{:S(2)}, u32[]{:S(2)}) %collective-permute-start.18) | collective-permute-done | bytes 16416 | tf_op jit(solution)/shard_map/ppermute | solution.py:448
  84.1 2.1 %collective-permute-start.19 = (f32[2,32,128]{2,1,0:T(8,128)S(1)}, f32[2,32,128]{2,1,0:T(8,128)S(1)}, u32[]{:S(2)}, u32[]{:S(2)}) collective-permute-start(f32[2,32,128]{2,1,0:T(8,128)S(1)} %pad_maximum_fusion.pair), channel_id=1, source_target_pairs={{0,8},{4,12},{8,0},{12,4},{1,9},{5,13},{9,1},{13,5},{2,10},{6,14},... | collective-permute-start | bytes 98312 | tf_op jit(solution)/shard_map/ppermute | solution.py:449
  86.3 3.3 %collective-permute-done.19.far_pair = f32[2,32,128]{2,1,0:T(8,128)S(1)} collective-permute-done((f32[2,32,128]{2,1,0:T(8,128)S(1)}, f32[2,32,128]{2,1,0:T(8,128)S(1)}, u32[]{:S(2)}, u32[]{:S(2)}) %collective-permute-start.19) | collective-permute-done | bytes 32800 | tf_op jit(solution)/shard_map/ppermute | solution.py:449
  89.6 1.3 %assemble.1 = f32[64,256]{1,0:T(8,128)} custom-call(s32[7]{0:T(128)S(1)} %copy-done.4, f32[2,32,128]{2,1,0:T(8,128)S(1)} %pad_maximum_fusion.pair, f32[2,32,128]{2,1,0:T(8,128)S(1)} %collective-permute-done.19.far_pair), custom_call_target="tpu_custom_call" | custom-call | bytes 131072 | tf_op jit(solution)/shard_map/assemble/pallas_call | solution.py:450
  90.8 2.1 %collective-permute-done.17.high_got = f32[256,512]{1,0:T(8,128)S(1)} collective-permute-done((f32[256,512]{1,0:T(8,128)S(1)}, f32[256,512]{1,0:T(8,128)S(1)}, u32[]{:S(2)}, u32[]{:S(2)}) %collective-permute-start.17) | collective-permute-done | bytes 524320 | tf_op jit(solution)/shard_map/ppermute | solution.py:473
  93.0 10.4 %collective-permute-done.15.low_got = f32[256,512]{1,0:T(8,128)S(1)} collective-permute-done((f32[256,512]{1,0:T(8,128)S(1)}, f32[256,512]{1,0:T(8,128)S(1)}, u32[]{:S(2)}, u32[]{:S(2)}) %collective-permute-start.15) | collective-permute-done | bytes 524320 | tf_op jit(solution)/shard_map/ppermute | solution.py:473
  103.4 1.6 %finish.1 = f32[256,1024]{1,0:T(8,128)} custom-call(f32[256,512]{1,0:T(8,128)S(1)} %get-tuple-element.22.low, f32[256,512]{1,0:T(8,128)S(1)} %get-tuple-element.23.high, f32[256,512]{1,0:T(8,128)S(1)} %collective-permute-done.12.low_core, f32[256,512]{1,0:T(8,128)S(1)} %collective-permute-done.13.high_core, f32[256,512]{1,0:T(8,128)S(1)} %collective-permute-done.15.low_got, ...), custom_call_target="tpu_custom_call" | custom-call | flops 1048576 | bytes 4194304 | tf_op jit(solution)/shard_map/finish/pallas_call | solution.py:279
  (31 shorter events, 0.1 us)
Async XLA Ops:
  1.3 8.8 %copy-start.7 = (s32[256,1,32]{0,2,1:T(8,128)S(1)}, s32[256,1,32]{0,2,1:T(8,128)}, u32[]{:S(2)}) copy-start(s32[256,1,32]{0,2,1:T(8,128)} %param.6) | copy-start | bytes 98308
  6.3 14.2 %collective-permute-start = (bf16[288,1024]{1,0:T(8,128)(2,1)}, bf16[288,1024]{1,0:T(8,128)(2,1)S(1)}, u32[]{:S(2)}, u32[]{:S(2)}) collective-permute-start(bf16[288,1024]{1,0:T(8,128)(2,1)} %get-tuple-element.16.refs_0_.refs_10_), channel_id=1, source_target_pairs={{0,16},{16,32},{32,48},{48,64},{64,80},{80,96},{96,112},{112,0},{1... | collective-permute-start | bytes 1769480 | tf_op jit(solution)/shard_map/ppermute | solution.py:317
  8.2 17.6 %collective-permute-start.5 = (bf16[256,1024]{1,0:T(8,128)(2,1)}, bf16[256,1024]{1,0:T(8,128)(2,1)S(1)}, u32[]{:S(2)}, u32[]{:S(2)}) collective-permute-start(bf16[256,1024]{1,0:T(8,128)(2,1)} %get-tuple-element.17.refs_5_.refs_15_), channel_id=1, source_target_pairs={{0,16},{16,32},{32,48},{48,64},{64,80},{80,96},{96,112},{112,0},{1... | collective-permute-start | bytes 1572872 | tf_op jit(solution)/shard_map/ppermute | solution.py:318
  13.8 16.5 %copy-start.4 = (s32[7]{0:T(128)S(1)}, s32[7]{0:T(128)}, u32[]{:S(2)}) copy-start(s32[7]{0:T(128)} %stack.40.at) | copy-start | bytes 88
  13.8 16.5 %copy-start.5 = (s32[1024]{0:T(1024)S(1)}, s32[1024]{0:T(1024)}, u32[]{:S(2)}) copy-start(s32[1024]{0:T(1024)} %param.9) | copy-start | bytes 12292
  13.8 16.5 %copy-start.6 = (s32[256]{0:T(256)S(1)}, s32[256]{0:T(256)}, u32[]{:S(2)}) copy-start(s32[256]{0:T(256)} %param.8) | copy-start | bytes 3076
  13.9 6.6 %collective-permute-start.1 = (f32[128,256]{1,0:T(8,128)S(1)}, f32[128,256]{1,0:T(8,128)S(1)}, u32[]{:S(2)}, u32[]{:S(2)}) collective-permute-start(f32[128,256]{1,0:T(8,128)S(1)} %dynamic-slice_bitcast_fusion), channel_id=1, source_target_pairs={{0,8},{4,12},{8,0},{12,4},{1,9},{5,13},{9,1},{13,5},{2,10},{6,14},... | collective-permute-start | bytes 393224 | tf_op jit(solution)/shard_map/ppermute | solution.py:401
  20.5 11.6 %collective-permute-start.2 = (bf16[288,1024]{1,0:T(8,128)(2,1)S(1)}, bf16[288,1024]{1,0:T(8,128)(2,1)S(1)}, u32[]{:S(2)}, u32[]{:S(2)}) collective-permute-start(bf16[288,1024]{1,0:T(8,128)(2,1)S(1)} %tie.3.refs_0_.refs_1_.refs_11_), channel_id=1, source_target_pairs={{0,16},{16,32},{32,48},{48,64},{64,80},{80,96},{96,112},{112,0},{1... | collective-permute-start | bytes 1769480 | tf_op jit(solution)/shard_map/ppermute | solution.py:317
  25.8 11.9 %collective-permute-start.6 = (bf16[256,1024]{1,0:T(8,128)(2,1)S(1)}, bf16[256,1024]{1,0:T(8,128)(2,1)S(1)}, u32[]{:S(2)}, u32[]{:S(2)}) collective-permute-start(bf16[256,1024]{1,0:T(8,128)(2,1)S(1)} %collective-permute-done.5.refs_1_.refs_6_.refs_16_), channel_id=1, source_target_pairs={{0,16},{16,32},{32,48},{48,64},{64,80},{80,96},{96,112},{112,0},{1... | collective-permute-start | bytes 1572872 | tf_op jit(solution)/shard_map/ppermute | solution.py:318
  25.8 4.5 %collective-permute-start.3 = (f32[64,256]{1,0:T(8,128)S(1)}, f32[64,256]{1,0:T(8,128)S(1)}, u32[]{:S(2)}, u32[]{:S(2)}) collective-permute-start(f32[64,256]{1,0:T(8,128)S(1)} %constant_dynamic-slice_fusion), channel_id=1, source_target_pairs={{0,4},{4,0},{8,12},{12,8},{1,5},{5,1},{9,13},{13,9},{2,6},{6,2},{1... | collective-permute-start | bytes 196616 | tf_op jit(solution)/shard_map/ppermute | solution.py:403
  32.1 18.6 %collective-permute-start.4 = (bf16[288,1024]{1,0:T(8,128)(2,1)S(1)}, bf16[288,1024]{1,0:T(8,128)(2,1)S(1)}, u32[]{:S(2)}, u32[]{:S(2)}) collective-permute-start(bf16[288,1024]{1,0:T(8,128)(2,1)S(1)} %tie.4.refs_2_.refs_12_), channel_id=1, source_target_pairs={{0,16},{16,32},{32,48},{48,64},{64,80},{80,96},{96,112},{112,0},{1... | collective-permute-start | bytes 1769480 | tf_op jit(solution)/shard_map/ppermute | solution.py:317
  37.7 13.0 %collective-permute-start.7 = (bf16[256,1024]{1,0:T(8,128)(2,1)S(1)}, bf16[256,1024]{1,0:T(8,128)(2,1)S(1)}, u32[]{:S(2)}, u32[]{:S(2)}) collective-permute-start(bf16[256,1024]{1,0:T(8,128)(2,1)S(1)} %collective-permute-done.6.refs_3_.refs_7_.refs_17_), channel_id=1, source_target_pairs={{0,16},{16,32},{32,48},{48,64},{64,80},{80,96},{96,112},{112,0},{1... | collective-permute-start | bytes 1572872 | tf_op jit(solution)/shard_map/ppermute | solution.py:318
  40.4 10.4 %collective-permute-start.8 = (bf16[512,256]{1,0:T(8,128)(2,1)}, bf16[512,256]{1,0:T(8,128)(2,1)}, u32[]{:S(2)}, u32[]{:S(2)}) collective-permute-start(bf16[512,256]{1,0:T(8,128)(2,1)} %pick.1.refs_1_), channel_id=1, source_target_pairs={{0,2},{2,0},{1,3},{3,1},{4,6},{6,4},{5,7},{7,5},{8,10},{10,8},{9,1... | collective-permute-start | bytes 786440 | tf_op jit(solution)/shard_map/ppermute | solution.py:327
  42.0 0.7 copy-start.2
  42.7 22.2 %copy-start.3 = (bf16[128,256]{1,0:T(8,128)(2,1)S(1)}, bf16[128,256]{1,0:T(8,128)(2,1)}, u32[]{:S(2)}) copy-start(bf16[128,256]{1,0:T(8,128)(2,1)} %get-tuple-element.20.refs_20_) | copy-start | bytes 196612
  42.7 18.8 %all-to-all-start = ((f32[16,32,128]{2,1,0:T(8,128)}), f32[16,32,128]{2,1,0:T(8,128)}, u32[]{:S(2)}, u32[]{:S(2)}) async-start(f32[16,32,128]{2,1,0:T(8,128)} %bitcast.38), calls=%async_computation | async-start | bytes 524288 | tf_op jit(solution)/shard_map/all_to_all | solution.py:436
  52.2 12.6 %collective-permute-start.9 = (bf16[160,1024]{1,0:T(8,128)(2,1)}, bf16[160,1024]{1,0:T(8,128)(2,1)}, u32[]{:S(2)}, u32[]{:S(2)}) collective-permute-start(bf16[160,1024]{1,0:T(8,128)(2,1)} %get-tuple-element.18), channel_id=1, source_target_pairs={{0,16},{16,32},{32,48},{48,64},{64,80},{80,96},{96,112},{112,0},{1... | collective-permute-start | bytes 983048 | tf_op jit(solution)/shard_map/ppermute | solution.py:317
  54.1 10.8 %collective-permute-start.10 = (bf16[128,1024]{1,0:T(8,128)(2,1)}, bf16[128,1024]{1,0:T(8,128)(2,1)}, u32[]{:S(2)}, u32[]{:S(2)}) collective-permute-start(bf16[128,1024]{1,0:T(8,128)(2,1)} %get-tuple-element.19), channel_id=1, source_target_pairs={{0,16},{16,32},{32,48},{48,64},{64,80},{80,96},{96,112},{112,0},{1... | collective-permute-start | bytes 786440 | tf_op jit(solution)/shard_map/ppermute | solution.py:318
  56.0 7.1 %collective-permute-start.11 = (bf16[256,256]{1,0:T(8,128)(2,1)}, bf16[256,256]{1,0:T(8,128)(2,1)S(1)}, u32[]{:S(2)}, u32[]{:S(2)}) collective-permute-start(bf16[256,256]{1,0:T(8,128)(2,1)} %get-tuple-element.21), channel_id=1, source_target_pairs={{0,2},{2,0},{1,3},{3,1},{4,6},{6,4},{5,7},{7,5},{8,10},{10,8},{9,1... | collective-permute-start | bytes 393224 | tf_op jit(solution)/shard_map/ppermute | solution.py:329
  64.9 1.1 %copy-start = (bf16[288,1024]{1,0:T(8,128)(2,1)S(1)}, bf16[288,1024]{1,0:T(8,128)(2,1)}, u32[]{:S(2)}) copy-start(bf16[288,1024]{1,0:T(8,128)(2,1)} %get-tuple-element.16.refs_0_.refs_10_) | copy-start | bytes 1769476
  65.9 1.0 copy-start.1
  71.1 5.4 %collective-permute-start.16 = (f32[256,512]{1,0:T(8,128)S(1)}, f32[256,512]{1,0:T(8,128)S(1)}, u32[]{:S(2)}, u32[]{:S(2)}) collective-permute-start(f32[256,512]{1,0:T(8,128)S(1)} %get-tuple-element.29), channel_id=1, source_target_pairs={{0,1},{1,0},{2,3},{3,2},{4,5},{5,4},{6,7},{7,6},{8,9},{9,8},{10,11... | collective-permute-start | bytes 1572872 | tf_op jit(solution)/shard_map/ppermute | solution.py:332
  71.2 8.7 %collective-permute-start.14 = (f32[256,512]{1,0:T(8,128)S(1)}, f32[256,512]{1,0:T(8,128)S(1)}, u32[]{:S(2)}, u32[]{:S(2)}) collective-permute-start(f32[256,512]{1,0:T(8,128)S(1)} %get-tuple-element.27), channel_id=1, source_target_pairs={{0,1},{1,0},{2,3},{3,2},{4,5},{5,4},{6,7},{7,6},{8,9},{9,8},{10,11... | collective-permute-start | bytes 1572872 | tf_op jit(solution)/shard_map/ppermute | solution.py:332
  75.9 14.9 %collective-permute-start.12 = (f32[256,512]{1,0:T(8,128)S(1)}, f32[256,512]{1,0:T(8,128)S(1)}, u32[]{:S(2)}, u32[]{:S(2)}) collective-permute-start(f32[256,512]{1,0:T(8,128)S(1)} %get-tuple-element.24), channel_id=1, source_target_pairs={{0,1},{1,0},{2,3},{3,2},{4,5},{5,4},{6,7},{7,6},{8,9},{9,8},{10,11... | collective-permute-start | bytes 1572872 | tf_op jit(solution)/shard_map/ppermute | solution.py:335
  76.1 14.7 %collective-permute-start.13 = (f32[256,512]{1,0:T(8,128)S(1)}, f32[256,512]{1,0:T(8,128)S(1)}, u32[]{:S(2)}, u32[]{:S(2)}) collective-permute-start(f32[256,512]{1,0:T(8,128)S(1)} %get-tuple-element.25), channel_id=1, source_target_pairs={{0,1},{1,0},{2,3},{3,2},{4,5},{5,4},{6,7},{7,6},{8,9},{9,8},{10,11... | collective-permute-start | bytes 1572872 | tf_op jit(solution)/shard_map/ppermute | solution.py:335
  76.6 16.4 %collective-permute-start.17 = (f32[256,512]{1,0:T(8,128)S(1)}, f32[256,512]{1,0:T(8,128)S(1)}, u32[]{:S(2)}, u32[]{:S(2)}) collective-permute-start(f32[256,512]{1,0:T(8,128)S(1)} %add.43), channel_id=1, source_target_pairs={{0,128},{128,0},{1,129},{129,1},{2,130},{130,2},{3,131},{131,3},{4... | collective-permute-start | bytes 1572872 | tf_op jit(solution)/shard_map/ppermute | solution.py:473
  80.1 23.3 %collective-permute-start.15 = (f32[256,512]{1,0:T(8,128)S(1)}, f32[256,512]{1,0:T(8,128)S(1)}, u32[]{:S(2)}, u32[]{:S(2)}) collective-permute-start(f32[256,512]{1,0:T(8,128)S(1)} %add.42), channel_id=1, source_target_pairs={{0,128},{128,0},{1,129},{129,1},{2,130},{130,2},{3,131},{131,3},{4... | collective-permute-start | bytes 1572872 | tf_op jit(solution)/shard_map/ppermute | solution.py:473
  80.4 3.7 %collective-permute-start.18 = (f32[32,128]{1,0:T(8,128)S(1)}, f32[32,128]{1,0:T(8,128)S(1)}, u32[]{:S(2)}, u32[]{:S(2)}) collective-permute-start(f32[32,128]{1,0:T(8,128)S(1)} %sum.1.refs_24_), channel_id=1, source_target_pairs={{0,4},{4,0},{8,12},{12,8},{1,5},{5,1},{9,13},{13,9},{2,6},{6,2},{1... | collective-permute-start | bytes 49160 | tf_op jit(solution)/shard_map/ppermute | solution.py:448
  84.1 5.4 %collective-permute-start.19 = (f32[2,32,128]{2,1,0:T(8,128)S(1)}, f32[2,32,128]{2,1,0:T(8,128)S(1)}, u32[]{:S(2)}, u32[]{:S(2)}) collective-permute-start(f32[2,32,128]{2,1,0:T(8,128)S(1)} %pad_maximum_fusion.pair), channel_id=1, source_target_pairs={{0,8},{4,12},{8,0},{12,4},{1,9},{5,13},{9,1},{13,5},{2,10},{6,14},... | collective-permute-start | bytes 98312 | tf_op jit(solution)/shard_map/ppermute | solution.py:449

commit v8 on v7

--- a/solution.py
+++ b/solution.py
@@ -166,12 +166,12 @@
     )(at, *[side for _, _, low, high in pieces for side in (low, high)], *after)
 
 
-def gram_kernel(sizes, kept, at, *refs):
+def gram_kernel(sizes, kept, parts, at, *refs):
     count = len(sizes)
     lows, highs = refs[:count], refs[count : 2 * count]
     low_rights, high_rights = refs[2 * count : 3 * count], refs[3 * count : 4 * count]
     own, near, third, far = refs[4 * count : 4 * count + 4]
-    low_other, high_other, low_own, high_own = refs[-5:-1]
+    outs = refs[-1 - 2 * parts : -1]
     left = refs[-1]
     step = pl.program_id(0)
 
@@ -202,18 +202,16 @@
             start += rows
         return total
 
-    @pl.when(step == 0)
-    def _():
-        low_other[...] = terms(low_rights)
-        high_other[...] = terms(high_rights)
-
-    @pl.when(step == 1)
-    def _():
-        low_own[...] = terms(low_rights)
-        high_own[...] = terms(high_rights)
-
-
-def gram(at, pieces, received, kept, *after):
+    for part in range(parts):
+
+        @pl.when(step == part)
+        def _(part=part):
+            outs[2 * part][...] = terms(low_rights)
+            outs[2 * part + 1][...] = terms(high_rights)
+
+
+def gram(at, pieces, received, kept, parts, *after):
+    first = parts[0]
     sizes = tuple(n for n, _, _, _ in pieces)
     specs = [lanes_at_z(n, by_core) for n, by_core, _, _ in pieces] * 2
     for n, by_core, _, _ in pieces:
@@ -222,7 +220,7 @@
                 (n, 512),
                 lambda g, at, by_core=by_core: (
                     at[AT_CORE] if by_core else 0,
-                    (1 - g) * (1 - at[AT_CORE]) + g * at[AT_CORE],
+                    (1 - first - g) * (1 - at[AT_CORE]) + (first + g) * at[AT_CORE],
                 ),
             )
         )
@@ -233,43 +231,44 @@
     specs += [pl.BlockSpec(memory_space=pl.ANY)] * len(after)
     sides = [p[2] for p in pieces], [p[3] for p in pieces]
     return pl.pallas_call(
-        functools.partial(gram_kernel, sizes, kept),
-        grid_spec=pltpu.PrefetchScalarGridSpec(
-            num_scalar_prefetch=1, grid=(2,), in_specs=specs,
-            out_specs=[pl.BlockSpec((256, 512), lambda g, at: (0, 0))] * 4,
+        functools.partial(gram_kernel, sizes, kept, len(parts)),
+        grid_spec=pltpu.PrefetchScalarGridSpec(
+            num_scalar_prefetch=1, grid=(len(parts),), in_specs=specs,
+            out_specs=[pl.BlockSpec((256, 512), lambda g, at: (0, 0))] * (2 * len(parts)),
             scratch_shapes=[pltpu.VMEM((sum(sizes), 256), jnp.bfloat16)],
         ),
-        out_shape=[jax.ShapeDtypeStruct((256, 512), jnp.float32)] * 4,
+        out_shape=[jax.ShapeDtypeStruct((256, 512), jnp.float32)] * (2 * len(parts)),
         compiler_params=params(20),
-        cost_estimate=cost(2 * sum(sizes) * 256 * 2048, 7 << 20),
+        cost_estimate=cost(0, 0),
         name="gram",
     )(at, *sides[0], *sides[1], *sides[0], *sides[1], *received, last, *after)
 
 
-def add_kernel(left, right, out):
-    out[...] = left[...] + right[...]
-
-
-def add(left, right):
-    rows, columns = left.shape
-    spec = pl.BlockSpec((rows // 2, columns), lambda g: (g, 0))
+def add_kernel(low, high, low_got, high_got, out):
+    columns = low.shape[1]
+    out[:, 0:columns] = low[...] + low_got[...]
+    out[:, columns:] = high[...] + high_got[...]
+
+
+def add(terms):
+    rows, columns = terms[0].shape
     return pl.pallas_call(
         add_kernel,
         grid=(2,),
-        in_specs=[spec, spec],
-        out_specs=spec,
-        out_shape=jax.ShapeDtypeStruct(left.shape, left.dtype),
+        in_specs=[pl.BlockSpec((rows // 2, columns), lambda g: (g, 0))] * 4,
+        out_specs=pl.BlockSpec((rows // 2, 2 * columns), lambda g: (g, 0)),
+        out_shape=jax.ShapeDtypeStruct((rows, 2 * columns), jnp.float32),
         compiler_params=params(6),
-        cost_estimate=cost(1 << 18, 3 << 19),
+        cost_estimate=cost(0, 0),
         name="add",
-    )(left, right)
-
-
-def finish_kernel(factor, low, high, low_core, high_core, low_got, high_got, out):
+    )(*terms)
+
+
+def finish_kernel(factor, low, high, low_core, high_core, got, out):
     for i in range(4):
         lanes = slice(i * 128, i * 128 + 128)
-        first = (low[:, lanes] + low_core[:, lanes]) + low_got[:, lanes]
-        second = (high[:, lanes] + high_core[:, lanes]) + high_got[:, lanes]
+        first = (low[:, lanes] + low_core[:, lanes]) + got[:, lanes]
+        second = (high[:, lanes] + high_core[:, lanes]) + got[:, 512 + i * 128 : 640 + i * 128]
         out[:, i * 256 : i * 256 + 128] = first * factor
         out[:, i * 256 + 128 : i * 256 + 256] = second * factor
 
@@ -279,7 +278,8 @@
     return pl.pallas_call(
         functools.partial(finish_kernel, factor),
         grid=(4,),
-        in_specs=[pl.BlockSpec((rows // 4, columns), lambda g: (g, 0))] * 6,
+        in_specs=[pl.BlockSpec((rows // 4, columns), lambda g: (g, 0))] * 4
+        + [pl.BlockSpec((rows // 4, 2 * columns), lambda g: (g, 0))],
         out_specs=pl.BlockSpec((rows // 4, 2 * columns), lambda g: (g, 0)),
         out_shape=jax.ShapeDtypeStruct((rows, 2 * columns), jnp.float32),
         compiler_params=params(8),
@@ -328,10 +328,11 @@
     mine = own_slots(placed)
     received = (own, near, lax.ppermute(third, "yl", SWAP))
 
-    *given_other, low_given, high_given = gram(at, pieces, received, False, mine)
+    given_other = gram(at, pieces, received, False, (0,), mine)
     swapped = [lax.ppermute(g, "core", SWAP) for g in given_other]
-    *kept_other, low_kept, high_kept = gram(at, pieces, received, True)
-    given = [add(g, s) for g, s in zip((low_given, high_given), swapped)]
+    given_own = gram(at, pieces, received, False, (1,), *given_other)
+    given = add([*given_own, *swapped])
+    *kept_other, low_kept, high_kept = gram(at, pieces, received, True, (0, 1), given)
     kept = [lax.ppermute(k, "core", SWAP) for k in kept_other]
     return given, [low_kept, high_kept, *kept], mine
 
@@ -470,8 +471,8 @@
     at = jnp.stack([z, core, yl, other + z, other + lax.rem(z + Z // 2, Z), yh, x]).astype(jnp.int32)
     pair, placed = placed_scores(at, mantissas, powers(exponents), queries[:, 0, :], doc_ids, owners)
     given, kept, mine = fisher_terms(at, mantissas, exponents.T, pair, placed)
-    got = [lax.ppermute(g, "yh", SWAP) for g in given]
-    return finish(1.0 / total_rows, kept + got)[None], doc_block(at, mine)
+    got = lax.ppermute(given, "yh", SWAP)
+    return finish(1.0 / total_rows, kept + [got])[None], doc_block(at, mine)
 
 
 def solution(mesh):

time: 106 us -> 104 us (0.981)
  waiting for transfers between devices: 38.3 us -> 33.4 us
  Pallas kernels: 21.6 us -> 23.2 us
    ppermute x2 -> x1, waiting for transfers between devices: 12.6 us -> 8.49 us  [per_device(): got = lax.ppermute(given, 'yh', SWAP)]
    ppermute x4, starting transfers between devices: 5.08 us -> 6.62 us  [fisher_terms(): high = lax.ppermute(high, ('z', 'core'), RING)]
    ppermute x1, starting transfers between devices: 3.98 us -> 2.54 us  [fisher_terms(): received = (own, near, lax.ppermute(third, 'yl', SWAP))]
    unnamed x16 -> x20, local copies, waits for them, and re-layouts: 2.83 us -> 3.93 us
    ppermute x2 -> x1, starting transfers between devices: 3.7 us -> 3.29 us  [per_device(): got = lax.ppermute(given, 'yh', SWAP)]
  transfers between devices with their start and end apart: 21 -> 20, of which waited for: 12 -> 10; matrix products, arithmetic and copies ran while one was open for 4% -> 4% of each run, Pallas kernels for 10% -> 13%
where the time goes in v8:
time: 104 us; the launch traced here: 103 us
  starting transfers between devices  37 us (36%)
  waiting for transfers between devices  33.4 us (32%)
  Pallas kernels  23.2 us (22%)
  local copies, waits for them, and re-layouts  4.52 us (4%)
  matrix products  3.69 us (4%)
    pallas_call x3, Pallas kernels, gram(): pl.pallas_call(functools.partial(gram_kernel, sizes, kept, len(parts)), g...  9.18 us
    ppermute x1, waiting for transfers between devices, per_device(): got = lax.ppermute(given, 'yh', SWAP)  8.49 us
    ppermute x4, starting transfers between devices, fisher_terms(): low = lax.ppermute(low, ('z', 'core'), RING)  8.08 us
    all_to_all x1, starting transfers between devices, own_slots(): lax.all_to_all(placed.reshape(YH * Z, half, double), ('yh', 'z'), 0, 0, t...  7.95 us
    ppermute x4, waiting for transfers between devices, fisher_terms(): high = lax.ppermute(high, ('z', 'core'), RING)  7.88 us
    ppermute x4, starting transfers between devices, fisher_terms(): high = lax.ppermute(high, ('z', 'core'), RING)  6.62 us
    pallas_call x1, Pallas kernels, dequant(): pl.pallas_call(dequant_kernel, grid_spec=pltpu.PrefetchScalarGridSpec(num...  4.94 us
    ppermute x1, waiting for transfers between devices, placed_scores(): lax.ppermute(lax.dynamic_slice_in_dim(scores, (1 - upper) * 2 * share, 2...  4.38 us
  transfers between devices with their start and end apart: 20, of which 10 were waited for; matrix products, arithmetic and copies ran while one was open for 4% of the time, Pallas kernels for 13%

profile of v8, /device:TPU:2, one launch (start us, length us, event | category | flops | bytes accessed | tf_op | source)
XLA Modules:
  0.0 102.7 jit_solution(13182601607925749029)
XLA Ops:
  0.6 0.6 stack.40.at
  1.2 4.9 %dequant.1 = (bf16[288,1024]{1,0:T(8,128)(2,1)}, bf16[256,1024]{1,0:T(8,128)(2,1)}, bf16[128,256]{1,0:T(8,128)(2,1)}) custom-call(s32[7]{0:T(128)} %stack.40.at, s32[32,256]{1,0:T(8,128)} %bitcast.46, bf16[256,4096]{1,0:T(8,128)(2,1)} %bitcast.42, bf16[256,4096]{1,0:T(8,128)(2,1)} %bitcast.43, bf16[256,4096]{1,0:T(8,128)(2,1)} %bitcast.44), custom_call_target="tpu_custom_call" | custom-call | flops 33554432 | bytes 2097152 | tf_op jit(solution)/shard_map/dequant/pallas_call | solution.py:66
  6.2 1.9 %collective-permute-start = (bf16[288,1024]{1,0:T(8,128)(2,1)}, bf16[288,1024]{1,0:T(8,128)(2,1)S(1)}, u32[]{:S(2)}, u32[]{:S(2)}) collective-permute-start(bf16[288,1024]{1,0:T(8,128)(2,1)} %get-tuple-element.16.refs_0_.refs_10_), channel_id=1, source_target_pairs={{0,16},{16,32},{32,48},{48,64},{64,80},{80,96},{96,112},{112,0},{1... | collective-permute-start | bytes 1769480 | tf_op jit(solution)/shard_map/ppermute | solution.py:317
  8.1 1.9 %collective-permute-start.5 = (bf16[256,1024]{1,0:T(8,128)(2,1)}, bf16[256,1024]{1,0:T(8,128)(2,1)S(1)}, u32[]{:S(2)}, u32[]{:S(2)}) collective-permute-start(bf16[256,1024]{1,0:T(8,128)(2,1)} %get-tuple-element.17.refs_5_.refs_15_), channel_id=1, source_target_pairs={{0,16},{16,32},{32,48},{48,64},{64,80},{80,96},{96,112},{112,0},{1... | collective-permute-start | bytes 1572872 | tf_op jit(solution)/shard_map/ppermute | solution.py:318
  10.0 3.7 %fusion.1 = f32[256,256]{0,1:T(8,128)S(1)} fusion(bf16[256,1,4096]{2,0,1:T(8,128)(2,1)} %param.7, s32[4096]{0:T(1024)S(1)} %add_select_fusion, s32[256,1,32]{0,2,1:T(8,128)S(1)} %copy-done.9, bf16[256,1,4096]{2,0,1:T(8,128)(2,1)} %param.5), kind=kOutput, calls=%fused_computation.2 | convolution fusion | flops 606232576 | bytes 4505600 | tf_op jit(solution)/shard_map/dot_general | solution.py:398
  13.7 0.0 copy-start.7
  13.7 0.0 copy-start.8
  13.8 2.2 %collective-permute-start.1 = (f32[128,256]{1,0:T(8,128)S(1)}, f32[128,256]{1,0:T(8,128)S(1)}, u32[]{:S(2)}, u32[]{:S(2)}) collective-permute-start(f32[128,256]{1,0:T(8,128)S(1)} %dynamic-slice_bitcast_fusion), channel_id=1, source_target_pairs={{0,8},{4,12},{8,0},{12,4},{1,9},{5,13},{9,1},{13,5},{2,10},{6,14},... | collective-permute-start | bytes 393224 | tf_op jit(solution)/shard_map/ppermute | solution.py:402
  16.0 4.4 %collective-permute-done.1 = f32[128,256]{1,0:T(8,128)S(1)} collective-permute-done((f32[128,256]{1,0:T(8,128)S(1)}, f32[128,256]{1,0:T(8,128)S(1)}, u32[]{:S(2)}, u32[]{:S(2)}) %collective-permute-start.1) | collective-permute-done | bytes 131104 | tf_op jit(solution)/shard_map/ppermute | solution.py:402
  20.4 3.0 %collective-permute-start.2 = (bf16[288,1024]{1,0:T(8,128)(2,1)S(1)}, bf16[288,1024]{1,0:T(8,128)(2,1)S(1)}, u32[]{:S(2)}, u32[]{:S(2)}) collective-permute-start(bf16[288,1024]{1,0:T(8,128)(2,1)S(1)} %tie.3.refs_0_.refs_1_.refs_11_), channel_id=1, source_target_pairs={{0,16},{16,32},{32,48},{48,64},{64,80},{80,96},{96,112},{112,0},{1... | collective-permute-start | bytes 1769480 | tf_op jit(solution)/shard_map/ppermute | solution.py:317
  23.4 2.3 %collective-permute-done.5.refs_1_.refs_6_.refs_16_ = bf16[256,1024]{1,0:T(8,128)(2,1)S(1)} collective-permute-done((bf16[256,1024]{1,0:T(8,128)(2,1)}, bf16[256,1024]{1,0:T(8,128)(2,1)S(1)}, u32[]{:S(2)}, u32[]{:S(2)}) %collective-permute-start.5) | collective-permute-done | bytes 524320 | tf_op jit(solution)/shard_map/ppermute | solution.py:318
  25.7 0.6 collective-permute-start.3
  26.3 3.9 %collective-permute-done.3.got = f32[64,256]{1,0:T(8,128)S(1)} collective-permute-done((f32[64,256]{1,0:T(8,128)S(1)}, f32[64,256]{1,0:T(8,128)S(1)}, u32[]{:S(2)}, u32[]{:S(2)}) %collective-permute-start.3) | collective-permute-done | bytes 65568 | tf_op jit(solution)/shard_map/ppermute | solution.py:404
  30.3 2.2 %place.1.refs_1_.refs_0_ = f32[512,128]{1,0:T(8,128)} custom-call(s32[7]{0:T(128)S(1)} %copy-done.6, f32[2,64,256]{2,1,0:T(8,128)S(1)} %bitcast.38, f32[64,256]{1,0:T(8,128)S(1)} %collective-permute-done.3.got, s32[1,256]{1,0:T(1,128)S(1)} %bitcast.41, s32[1,1024]{1,0:T(1,128)S(1)} %bitcast.40), custom_call_target="tpu_custom_call" | custom-call | flops 268435456 | bytes 1048576 | tf_op jit(solution)/shard_map/place/pallas_call | solution.py:406
  32.4 0.9 collective-permute-start.4
  33.3 4.4 %collective-permute-done.6.refs_3_.refs_7_.refs_17_ = bf16[256,1024]{1,0:T(8,128)(2,1)} collective-permute-done((bf16[256,1024]{1,0:T(8,128)(2,1)S(1)}, bf16[256,1024]{1,0:T(8,128)(2,1)}, u32[]{:S(2)}, u32[]{:S(2)}) %collective-permute-start.6) | collective-permute-done | bytes 524320 | tf_op jit(solution)/shard_map/ppermute | solution.py:318
  37.7 1.3 %collective-permute-start.7 = (bf16[256,1024]{1,0:T(8,128)(2,1)}, bf16[256,1024]{1,0:T(8,128)(2,1)S(1)}, u32[]{:S(2)}, u32[]{:S(2)}) collective-permute-start(bf16[256,1024]{1,0:T(8,128)(2,1)} %collective-permute-done.6.refs_3_.refs_7_.refs_17_), channel_id=1, source_target_pairs={{0,16},{16,32},{32,48},{48,64},{64,80},{80,96},{96,112},{112,0},{1... | collective-permute-start | bytes 1572872 | tf_op jit(solution)/shard_map/ppermute | solution.py:318
  39.0 1.5 %pick.1.refs_1_ = bf16[512,256]{1,0:T(8,128)(2,1)S(1)} custom-call(s32[7]{0:T(128)S(1)} %copy-done.6, bf16[288,1024]{1,0:T(8,128)(2,1)S(1)} %tie.3.refs_0_.refs_1_.refs_11_, bf16[256,1024]{1,0:T(8,128)(2,1)S(1)} %collective-permute-done.5.refs_1_.refs_6_.refs_16_, bf16[288,1024]{1,0:T(8,128)(2,1)S(1)} %tie.4.refs_2_.refs_12_, ...), custom_call_target="tpu_custom_call" | custom-call | bytes 524288 | tf_op jit(solution)/shard_map/pick/pallas_call | solution.py:156
  40.5 1.7 %collective-permute-start.8 = (bf16[512,256]{1,0:T(8,128)(2,1)S(1)}, bf16[512,256]{1,0:T(8,128)(2,1)S(1)}, u32[]{:S(2)}, u32[]{:S(2)}) collective-permute-start(bf16[512,256]{1,0:T(8,128)(2,1)S(1)} %pick.1.refs_1_), channel_id=1, source_target_pairs={{0,2},{2,0},{1,3},{3,1},{4,6},{6,4},{5,7},{7,5},{8,10},{10,8},{9,1... | collective-permute-start | bytes 786440 | tf_op jit(solution)/shard_map/ppermute | solution.py:327
  42.2 8.0 %all-to-all-start = ((f32[16,32,128]{2,1,0:T(8,128)}), f32[16,32,128]{2,1,0:T(8,128)}, u32[]{:S(2)}, u32[]{:S(2)}) async-start(f32[16,32,128]{2,1,0:T(8,128)} %bitcast.16), calls=%async_computation | async-start | bytes 524288 | tf_op jit(solution)/shard_map/all_to_all | solution.py:437
  50.2 1.4 %halve.1 = (bf16[160,1024]{1,0:T(8,128)(2,1)}, bf16[128,1024]{1,0:T(8,128)(2,1)}, bf16[256,256]{1,0:T(8,128)(2,1)}) custom-call(s32[7]{0:T(128)S(1)} %copy-done.6, bf16[288,1024]{1,0:T(8,128)(2,1)S(1)} %collective-permute-done.4.low.far.low_lanes.refs_3_.refs_13_, bf16[288,1024]{1,0:T(8,128)(2,1)S(1)} %collective-permute-done.4.low.far.low_lanes.refs_3_.refs_13_, ...), custom_call_target="tpu_custom_call" | custom-call | bytes 2097152 | tf_op jit(solution)/shard_map/halve/pallas_call | solution.py:107
  51.6 2.3 %collective-permute-start.9 = (bf16[160,1024]{1,0:T(8,128)(2,1)}, bf16[160,1024]{1,0:T(8,128)(2,1)S(1)}, u32[]{:S(2)}, u32[]{:S(2)}) collective-permute-start(bf16[160,1024]{1,0:T(8,128)(2,1)} %get-tuple-element.18), channel_id=1, source_target_pairs={{0,16},{16,32},{32,48},{48,64},{64,80},{80,96},{96,112},{112,0},{1... | collective-permute-start | bytes 983048 | tf_op jit(solution)/shard_map/ppermute | solution.py:317
  53.9 3.4 %collective-permute-start.10 = (bf16[128,1024]{1,0:T(8,128)(2,1)}, bf16[128,1024]{1,0:T(8,128)(2,1)S(1)}, u32[]{:S(2)}, u32[]{:S(2)}) collective-permute-start(bf16[128,1024]{1,0:T(8,128)(2,1)} %get-tuple-element.19), channel_id=1, source_target_pairs={{0,16},{16,32},{32,48},{48,64},{64,80},{80,96},{96,112},{112,0},{1... | collective-permute-start | bytes 786440 | tf_op jit(solution)/shard_map/ppermute | solution.py:318
  57.3 2.5 %collective-permute-start.11 = (bf16[256,256]{1,0:T(8,128)(2,1)}, bf16[256,256]{1,0:T(8,128)(2,1)S(1)}, u32[]{:S(2)}, u32[]{:S(2)}) collective-permute-start(bf16[256,256]{1,0:T(8,128)(2,1)} %get-tuple-element.21), channel_id=1, source_target_pairs={{0,2},{2,0},{1,3},{3,1},{4,6},{6,4},{5,7},{7,5},{8,10},{10,8},{9,1... | collective-permute-start | bytes 393224 | tf_op jit(solution)/shard_map/ppermute | solution.py:329
  59.8 0.9 all-to-all-done.parts
  60.7 1.0 sum.1.refs_24_
  61.7 1.3 %collective-permute-done.11.refs_22_ = bf16[256,256]{1,0:T(8,128)(2,1)S(1)} collective-permute-done((bf16[256,256]{1,0:T(8,128)(2,1)}, bf16[256,256]{1,0:T(8,128)(2,1)S(1)}, u32[]{:S(2)}, u32[]{:S(2)}) %collective-permute-start.11) | collective-permute-done | bytes 131104 | tf_op jit(solution)/shard_map/ppermute | solution.py:329
  63.0 1.2 %collective-permute-done.10.refs_9_.refs_19_ = bf16[128,1024]{1,0:T(8,128)(2,1)S(1)} collective-permute-done((bf16[128,1024]{1,0:T(8,128)(2,1)}, bf16[128,1024]{1,0:T(8,128)(2,1)S(1)}, u32[]{:S(2)}, u32[]{:S(2)}) %collective-permute-start.10) | collective-permute-done | bytes 262176 | tf_op jit(solution)/shard_map/ppermute | solution.py:318
  64.2 1.1 %copy-done = bf16[288,1024]{1,0:T(8,128)(2,1)S(1)} copy-done((bf16[288,1024]{1,0:T(8,128)(2,1)S(1)}, bf16[288,1024]{1,0:T(8,128)(2,1)}, u32[]{:S(2)}) %copy-start) | copy-done | bytes 589848
  65.2 1.0 %copy-done.1 = bf16[256,1024]{1,0:T(8,128)(2,1)S(1)} copy-done((bf16[256,1024]{1,0:T(8,128)(2,1)S(1)}, bf16[256,1024]{1,0:T(8,128)(2,1)}, u32[]{:S(2)}) %copy-start.1) | copy-done | bytes 524312
  66.3 0.9 copy-done.3
  67.2 0.8 copy-done.4
  68.1 2.6 %gram.3 = (f32[256,512]{1,0:T(8,128)S(1)}, f32[256,512]{1,0:T(8,128)S(1)}) custom-call(s32[7]{0:T(128)S(1)} %copy-done.6, bf16[288,1024]{1,0:T(8,128)(2,1)S(1)} %copy-done, bf16[288,1024]{1,0:T(8,128)(2,1)S(1)} %tie.3.refs_0_.refs_1_.refs_11_, bf16[288,1024]{1,0:T(8,128)(2,1)S(1)} %tie.4.refs_2_.refs_12_, ...), custom_call_target="tpu_custom_call" | custom-call | tf_op jit(solution)/shard_map/gram/pallas_call | solution.py:233
  70.7 0.3 collective-permute-start.12
  71.0 0.5 collective-permute-start.13
  71.5 2.6 %gram.4 = (f32[256,512]{1,0:T(8,128)S(1)}, f32[256,512]{1,0:T(8,128)S(1)}) custom-call(s32[7]{0:T(128)S(1)} %copy-done.6, bf16[288,1024]{1,0:T(8,128)(2,1)S(1)} %copy-done, bf16[288,1024]{1,0:T(8,128)(2,1)S(1)} %tie.3.refs_0_.refs_1_.refs_11_, bf16[288,1024]{1,0:T(8,128)(2,1)S(1)} %tie.4.refs_2_.refs_12_, ...), custom_call_target="tpu_custom_call" | custom-call | tf_op jit(solution)/shard_map/gram/pallas_call | solution.py:233
  74.1 0.2 add.41.refs_24_
  74.3 3.3 %collective-permute-start.16 = (f32[256,1024]{1,0:T(8,128)S(1)}, f32[256,1024]{1,0:T(8,128)S(1)}, u32[]{:S(2)}, u32[]{:S(2)}) collective-permute-start(f32[256,1024]{1,0:T(8,128)S(1)} %add.41.refs_24_), channel_id=1, source_target_pairs={{0,128},{128,0},{1,129},{129,1},{2,130},{130,2},{3,131},{131,3},{4... | collective-permute-start | bytes 3145736 | tf_op jit(solution)/shard_map/ppermute | solution.py:474
  77.6 3.9 %gram.5 = (f32[256,512]{1,0:T(8,128)S(1)}, f32[256,512]{1,0:T(8,128)S(1)}, f32[256,512]{1,0:T(8,128)S(1)}, f32[256,512]{1,0:T(8,128)S(1)}) custom-call(s32[7]{0:T(128)S(1)} %copy-done.6, bf16[288,1024]{1,0:T(8,128)(2,1)S(1)} %copy-done, bf16[288,1024]{1,0:T(8,128)(2,1)S(1)} %tie.3.refs_0_.refs_1_.refs_11_, bf16[288,1024]{1,0:T(8,128)(2,1)S(1)} %tie.4.refs_2_.refs_12_, ...), custom_call_target="tpu_custom_call" | custom-call | tf_op jit(solution)/shard_map/gram/pallas_call | solution.py:233
  81.5 0.1 collective-permute-start.14
  81.6 0.5 collective-permute-start.15
  82.1 0.5 collective-permute-start.17
  82.7 3.2 %collective-permute-done.17 = f32[32,128]{1,0:T(8,128)S(1)} collective-permute-done((f32[32,128]{1,0:T(8,128)S(1)}, f32[32,128]{1,0:T(8,128)S(1)}, u32[]{:S(2)}, u32[]{:S(2)}) %collective-permute-start.17) | collective-permute-done | bytes 16416 | tf_op jit(solution)/shard_map/ppermute | solution.py:449
  85.9 2.1 %collective-permute-start.18 = (f32[2,32,128]{2,1,0:T(8,128)S(1)}, f32[2,32,128]{2,1,0:T(8,128)S(1)}, u32[]{:S(2)}, u32[]{:S(2)}) collective-permute-start(f32[2,32,128]{2,1,0:T(8,128)S(1)} %pad_maximum_fusion.pair), channel_id=1, source_target_pairs={{0,8},{4,12},{8,0},{12,4},{1,9},{5,13},{9,1},{13,5},{2,10},{6,14},... | collective-permute-start | bytes 98312 | tf_op jit(solution)/shard_map/ppermute | solution.py:450
  88.0 3.3 %collective-permute-done.18.far_pair = f32[2,32,128]{2,1,0:T(8,128)S(1)} collective-permute-done((f32[2,32,128]{2,1,0:T(8,128)S(1)}, f32[2,32,128]{2,1,0:T(8,128)S(1)}, u32[]{:S(2)}, u32[]{:S(2)}) %collective-permute-start.18) | collective-permute-done | bytes 32800 | tf_op jit(solution)/shard_map/ppermute | solution.py:450
  91.3 1.3 %assemble.1 = f32[64,256]{1,0:T(8,128)} custom-call(s32[7]{0:T(128)S(1)} %copy-done.6, f32[2,32,128]{2,1,0:T(8,128)S(1)} %pad_maximum_fusion.pair, f32[2,32,128]{2,1,0:T(8,128)S(1)} %collective-permute-done.18.far_pair), custom_call_target="tpu_custom_call" | custom-call | bytes 131072 | tf_op jit(solution)/shard_map/assemble/pallas_call | solution.py:451
  92.6 8.5 %collective-permute-done.16.got = f32[256,1024]{1,0:T(8,128)S(1)} collective-permute-done((f32[256,1024]{1,0:T(8,128)S(1)}, f32[256,1024]{1,0:T(8,128)S(1)}, u32[]{:S(2)}, u32[]{:S(2)}) %collective-permute-start.16) | collective-permute-done | bytes 1048608 | tf_op jit(solution)/shard_map/ppermute | solution.py:474
  101.1 1.6 %finish.1 = f32[256,1024]{1,0:T(8,128)} custom-call(f32[256,512]{1,0:T(8,128)S(1)} %get-tuple-element.26.low, f32[256,512]{1,0:T(8,128)S(1)} %get-tuple-element.27.high, f32[256,512]{1,0:T(8,128)S(1)} %collective-permute-done.14.low_core, f32[256,512]{1,0:T(8,128)S(1)} %collective-permute-done.15.high_core, f32[256,1024]{1,0:T(8,128)S(1)} %collective-permute-done.16.got), custom_call_target="tpu_custom_call" | custom-call | flops 1048576 | bytes 4194304 | tf_op jit(solution)/shard_map/finish/pallas_call | solution.py:278
  (33 shorter events, 0.1 us)
Async XLA Ops:
  1.2 8.8 %copy-start.9 = (s32[256,1,32]{0,2,1:T(8,128)S(1)}, s32[256,1,32]{0,2,1:T(8,128)}, u32[]{:S(2)}) copy-start(s32[256,1,32]{0,2,1:T(8,128)} %param.6) | copy-start | bytes 98308
  6.2 14.2 %collective-permute-start = (bf16[288,1024]{1,0:T(8,128)(2,1)}, bf16[288,1024]{1,0:T(8,128)(2,1)S(1)}, u32[]{:S(2)}, u32[]{:S(2)}) collective-permute-start(bf16[288,1024]{1,0:T(8,128)(2,1)} %get-tuple-element.16.refs_0_.refs_10_), channel_id=1, source_target_pairs={{0,16},{16,32},{32,48},{48,64},{64,80},{80,96},{96,112},{112,0},{1... | collective-permute-start | bytes 1769480 | tf_op jit(solution)/shard_map/ppermute | solution.py:317
  8.1 17.6 %collective-permute-start.5 = (bf16[256,1024]{1,0:T(8,128)(2,1)}, bf16[256,1024]{1,0:T(8,128)(2,1)S(1)}, u32[]{:S(2)}, u32[]{:S(2)}) collective-permute-start(bf16[256,1024]{1,0:T(8,128)(2,1)} %get-tuple-element.17.refs_5_.refs_15_), channel_id=1, source_target_pairs={{0,16},{16,32},{32,48},{48,64},{64,80},{80,96},{96,112},{112,0},{1... | collective-permute-start | bytes 1572872 | tf_op jit(solution)/shard_map/ppermute | solution.py:318
  13.7 16.5 %copy-start.6 = (s32[7]{0:T(128)S(1)}, s32[7]{0:T(128)}, u32[]{:S(2)}) copy-start(s32[7]{0:T(128)} %stack.40.at) | copy-start | bytes 88
  13.7 16.5 %copy-start.7 = (s32[1024]{0:T(1024)S(1)}, s32[1024]{0:T(1024)}, u32[]{:S(2)}) copy-start(s32[1024]{0:T(1024)} %param.9) | copy-start | bytes 12292
  13.7 16.5 %copy-start.8 = (s32[256]{0:T(256)S(1)}, s32[256]{0:T(256)}, u32[]{:S(2)}) copy-start(s32[256]{0:T(256)} %param.8) | copy-start | bytes 3076
  13.8 6.6 %collective-permute-start.1 = (f32[128,256]{1,0:T(8,128)S(1)}, f32[128,256]{1,0:T(8,128)S(1)}, u32[]{:S(2)}, u32[]{:S(2)}) collective-permute-start(f32[128,256]{1,0:T(8,128)S(1)} %dynamic-slice_bitcast_fusion), channel_id=1, source_target_pairs={{0,8},{4,12},{8,0},{12,4},{1,9},{5,13},{9,1},{13,5},{2,10},{6,14},... | collective-permute-start | bytes 393224 | tf_op jit(solution)/shard_map/ppermute | solution.py:402
  20.4 12.0 %collective-permute-start.2 = (bf16[288,1024]{1,0:T(8,128)(2,1)S(1)}, bf16[288,1024]{1,0:T(8,128)(2,1)S(1)}, u32[]{:S(2)}, u32[]{:S(2)}) collective-permute-start(bf16[288,1024]{1,0:T(8,128)(2,1)S(1)} %tie.3.refs_0_.refs_1_.refs_11_), channel_id=1, source_target_pairs={{0,16},{16,32},{32,48},{48,64},{64,80},{80,96},{96,112},{112,0},{1... | collective-permute-start | bytes 1769480 | tf_op jit(solution)/shard_map/ppermute | solution.py:317
  25.7 12.0 %collective-permute-start.6 = (bf16[256,1024]{1,0:T(8,128)(2,1)S(1)}, bf16[256,1024]{1,0:T(8,128)(2,1)}, u32[]{:S(2)}, u32[]{:S(2)}) collective-permute-start(bf16[256,1024]{1,0:T(8,128)(2,1)S(1)} %collective-permute-done.5.refs_1_.refs_6_.refs_16_), channel_id=1, source_target_pairs={{0,16},{16,32},{32,48},{48,64},{64,80},{80,96},{96,112},{112,0},{1... | collective-permute-start | bytes 1572872 | tf_op jit(solution)/shard_map/ppermute | solution.py:318
  25.7 4.5 %collective-permute-start.3 = (f32[64,256]{1,0:T(8,128)S(1)}, f32[64,256]{1,0:T(8,128)S(1)}, u32[]{:S(2)}, u32[]{:S(2)}) collective-permute-start(f32[64,256]{1,0:T(8,128)S(1)} %constant_dynamic-slice_fusion), channel_id=1, source_target_pairs={{0,4},{4,0},{8,12},{12,8},{1,5},{5,1},{9,13},{13,9},{2,6},{6,2},{1... | collective-permute-start | bytes 196616 | tf_op jit(solution)/shard_map/ppermute | solution.py:404
  32.4 17.8 %collective-permute-start.4 = (bf16[288,1024]{1,0:T(8,128)(2,1)S(1)}, bf16[288,1024]{1,0:T(8,128)(2,1)S(1)}, u32[]{:S(2)}, u32[]{:S(2)}) collective-permute-start(bf16[288,1024]{1,0:T(8,128)(2,1)S(1)} %tie.4.refs_2_.refs_12_), channel_id=1, source_target_pairs={{0,16},{16,32},{32,48},{48,64},{64,80},{80,96},{96,112},{112,0},{1... | collective-permute-start | bytes 1769480 | tf_op jit(solution)/shard_map/ppermute | solution.py:317
  37.7 12.4 %collective-permute-start.7 = (bf16[256,1024]{1,0:T(8,128)(2,1)}, bf16[256,1024]{1,0:T(8,128)(2,1)S(1)}, u32[]{:S(2)}, u32[]{:S(2)}) collective-permute-start(bf16[256,1024]{1,0:T(8,128)(2,1)} %collective-permute-done.6.refs_3_.refs_7_.refs_17_), channel_id=1, source_target_pairs={{0,16},{16,32},{32,48},{48,64},{64,80},{80,96},{96,112},{112,0},{1... | collective-permute-start | bytes 1572872 | tf_op jit(solution)/shard_map/ppermute | solution.py:318
  40.5 9.6 %collective-permute-start.8 = (bf16[512,256]{1,0:T(8,128)(2,1)S(1)}, bf16[512,256]{1,0:T(8,128)(2,1)S(1)}, u32[]{:S(2)}, u32[]{:S(2)}) collective-permute-start(bf16[512,256]{1,0:T(8,128)(2,1)S(1)} %pick.1.refs_1_), channel_id=1, source_target_pairs={{0,2},{2,0},{1,3},{3,1},{4,6},{6,4},{5,7},{7,5},{8,10},{10,8},{9,1... | collective-permute-start | bytes 786440 | tf_op jit(solution)/shard_map/ppermute | solution.py:327
  42.2 18.5 %all-to-all-start = ((f32[16,32,128]{2,1,0:T(8,128)}), f32[16,32,128]{2,1,0:T(8,128)}, u32[]{:S(2)}, u32[]{:S(2)}) async-start(f32[16,32,128]{2,1,0:T(8,128)} %bitcast.16), calls=%async_computation | async-start | bytes 524288 | tf_op jit(solution)/shard_map/all_to_all | solution.py:437
  50.1 1.5 %copy-start.2 = (bf16[512,256]{1,0:T(8,128)(2,1)}, bf16[512,256]{1,0:T(8,128)(2,1)S(1)}, u32[]{:S(2)}) copy-start(bf16[512,256]{1,0:T(8,128)(2,1)S(1)} %collective-permute-done.8.after.refs_21_) | copy-start | bytes 786436
  51.6 12.5 %collective-permute-start.9 = (bf16[160,1024]{1,0:T(8,128)(2,1)}, bf16[160,1024]{1,0:T(8,128)(2,1)S(1)}, u32[]{:S(2)}, u32[]{:S(2)}) collective-permute-start(bf16[160,1024]{1,0:T(8,128)(2,1)} %get-tuple-element.18), channel_id=1, source_target_pairs={{0,16},{16,32},{32,48},{48,64},{64,80},{80,96},{96,112},{112,0},{1... | collective-permute-start | bytes 983048 | tf_op jit(solution)/shard_map/ppermute | solution.py:317
  53.9 10.3 %collective-permute-start.10 = (bf16[128,1024]{1,0:T(8,128)(2,1)}, bf16[128,1024]{1,0:T(8,128)(2,1)S(1)}, u32[]{:S(2)}, u32[]{:S(2)}) collective-permute-start(bf16[128,1024]{1,0:T(8,128)(2,1)} %get-tuple-element.19), channel_id=1, source_target_pairs={{0,16},{16,32},{32,48},{48,64},{64,80},{80,96},{96,112},{112,0},{1... | collective-permute-start | bytes 786440 | tf_op jit(solution)/shard_map/ppermute | solution.py:318
  57.3 5.7 %collective-permute-start.11 = (bf16[256,256]{1,0:T(8,128)(2,1)}, bf16[256,256]{1,0:T(8,128)(2,1)S(1)}, u32[]{:S(2)}, u32[]{:S(2)}) collective-permute-start(bf16[256,256]{1,0:T(8,128)(2,1)} %get-tuple-element.21), channel_id=1, source_target_pairs={{0,2},{2,0},{1,3},{3,1},{4,6},{6,4},{5,7},{7,5},{8,10},{10,8},{9,1... | collective-permute-start | bytes 393224 | tf_op jit(solution)/shard_map/ppermute | solution.py:329
  64.2 1.1 %copy-start = (bf16[288,1024]{1,0:T(8,128)(2,1)S(1)}, bf16[288,1024]{1,0:T(8,128)(2,1)}, u32[]{:S(2)}) copy-start(bf16[288,1024]{1,0:T(8,128)(2,1)} %get-tuple-element.16.refs_0_.refs_10_) | copy-start | bytes 1769476
  65.2 1.0 %copy-start.1 = (bf16[256,1024]{1,0:T(8,128)(2,1)S(1)}, bf16[256,1024]{1,0:T(8,128)(2,1)}, u32[]{:S(2)}) copy-start(bf16[256,1024]{1,0:T(8,128)(2,1)} %get-tuple-element.17.refs_5_.refs_15_) | copy-start | bytes 1572868
  66.3 0.9 copy-start.3
  67.2 0.8 copy-start.4
  70.7 3.4 %collective-permute-start.12 = (f32[256,512]{1,0:T(8,128)S(1)}, f32[256,512]{1,0:T(8,128)S(1)}, u32[]{:S(2)}, u32[]{:S(2)}) collective-permute-start(f32[256,512]{1,0:T(8,128)S(1)} %get-tuple-element.22.refs_24_), channel_id=1, source_target_pairs={{0,1},{1,0},{2,3},{3,2},{4,5},{5,4},{6,7},{7,6},{8,9},{9,8},{10,11... | collective-permute-start | bytes 1572872 | tf_op jit(solution)/shard_map/ppermute | solution.py:332
  71.0 3.2 %collective-permute-start.13 = (f32[256,512]{1,0:T(8,128)S(1)}, f32[256,512]{1,0:T(8,128)S(1)}, u32[]{:S(2)}, u32[]{:S(2)}) collective-permute-start(f32[256,512]{1,0:T(8,128)S(1)} %get-tuple-element.23.refs_25_), channel_id=1, source_target_pairs={{0,1},{1,0},{2,3},{3,2},{4,5},{5,4},{6,7},{7,6},{8,9},{9,8},{10,11... | collective-permute-start | bytes 1572872 | tf_op jit(solution)/shard_map/ppermute | solution.py:332
  74.1 3.5 %copy-start.5 = (bf16[128,256]{1,0:T(8,128)(2,1)S(1)}, bf16[128,256]{1,0:T(8,128)(2,1)}, u32[]{:S(2)}) copy-start(bf16[128,256]{1,0:T(8,128)(2,1)} %get-tuple-element.20.refs_20_) | copy-start | bytes 196612
  74.3 26.8 %collective-permute-start.16 = (f32[256,1024]{1,0:T(8,128)S(1)}, f32[256,1024]{1,0:T(8,128)S(1)}, u32[]{:S(2)}, u32[]{:S(2)}) collective-permute-start(f32[256,1024]{1,0:T(8,128)S(1)} %add.41.refs_24_), channel_id=1, source_target_pairs={{0,128},{128,0},{1,129},{129,1},{2,130},{130,2},{3,131},{131,3},{4... | collective-permute-start | bytes 3145736 | tf_op jit(solution)/shard_map/ppermute | solution.py:474
  81.5 11.0 %collective-permute-start.14 = (f32[256,512]{1,0:T(8,128)S(1)}, f32[256,512]{1,0:T(8,128)S(1)}, u32[]{:S(2)}, u32[]{:S(2)}) collective-permute-start(f32[256,512]{1,0:T(8,128)S(1)} %get-tuple-element.28), channel_id=1, source_target_pairs={{0,1},{1,0},{2,3},{3,2},{4,5},{5,4},{6,7},{7,6},{8,9},{9,8},{10,11... | collective-permute-start | bytes 1572872 | tf_op jit(solution)/shard_map/ppermute | solution.py:336
  81.6 10.9 %collective-permute-start.15 = (f32[256,512]{1,0:T(8,128)S(1)}, f32[256,512]{1,0:T(8,128)S(1)}, u32[]{:S(2)}, u32[]{:S(2)}) collective-permute-start(f32[256,512]{1,0:T(8,128)S(1)} %get-tuple-element.29), channel_id=1, source_target_pairs={{0,1},{1,0},{2,3},{3,2},{4,5},{5,4},{6,7},{7,6},{8,9},{9,8},{10,11... | collective-permute-start | bytes 1572872 | tf_op jit(solution)/shard_map/ppermute | solution.py:336
  82.1 3.7 %collective-permute-start.17 = (f32[32,128]{1,0:T(8,128)S(1)}, f32[32,128]{1,0:T(8,128)S(1)}, u32[]{:S(2)}, u32[]{:S(2)}) collective-permute-start(f32[32,128]{1,0:T(8,128)S(1)} %sum.1.refs_24_), channel_id=1, source_target_pairs={{0,4},{4,0},{8,12},{12,8},{1,5},{5,1},{9,13},{13,9},{2,6},{6,2},{1... | collective-permute-start | bytes 49160 | tf_op jit(solution)/shard_map/ppermute | solution.py:449
  85.9 5.4 %collective-permute-start.18 = (f32[2,32,128]{2,1,0:T(8,128)S(1)}, f32[2,32,128]{2,1,0:T(8,128)S(1)}, u32[]{:S(2)}, u32[]{:S(2)}) collective-permute-start(f32[2,32,128]{2,1,0:T(8,128)S(1)} %pad_maximum_fusion.pair), channel_id=1, source_target_pairs={{0,8},{4,12},{8,0},{12,4},{1,9},{5,13},{9,1},{13,5},{2,10},{6,14},... | collective-permute-start | bytes 98312 | tf_op jit(solution)/shard_map/ppermute | solution.py:450

commit v9 on v8

--- a/solution.py
+++ b/solution.py
@@ -40,7 +40,7 @@
 FAR = 32
 
 
-def dequant_kernel(at, exps, values, own_values, far_values, low, high, own, far_scale):
+def dequant_kernel(at, exps, values, own_values, far_values, low, high, low_half, high_half, own, far_scale):
     step = pl.program_id(0)
     rows, half = values.shape[0], own.shape[0]
     turned = powers(exps[...])
@@ -54,8 +54,11 @@
 
     grads = values[...].astype(jnp.float32) * wide_scale(turned, at[AT_YL] * 16 + step * 4, 512)
     grads = grads.astype(jnp.bfloat16)
-    low[0:rows] = jnp.concatenate([grads[:, 0:128], grads[:, 256:384]], 1)
-    high[...] = jnp.concatenate([grads[:, 128:256], grads[:, 384:512]], 1)
+    lows = jnp.concatenate([grads[:, 0:128], grads[:, 256:384]], 1)
+    highs = jnp.concatenate([grads[:, 128:256], grads[:, 384:512]], 1)
+    low[0:rows], high[...] = lows, highs
+    low_half[...] = jnp.where(at[AT_CORE] == 0, lows[:half], lows[half:])
+    high_half[...] = jnp.where(at[AT_CORE] == 0, highs[:half], highs[half:])
     scale = far_scale[pl.ds(pl.multiple_of(at[AT_CORE] * half + step * FAR, FAR), FAR)]
     low[rows : rows + FAR] = (far_values[...].astype(jnp.float32) * scale).astype(jnp.bfloat16)
 
@@ -77,6 +80,8 @@
             out_specs=[
                 pl.BlockSpec((rows + FAR, 256), lambda g, at: (0, g)),
                 pl.BlockSpec((rows, 256), lambda g, at: (0, g)),
+                pl.BlockSpec((half, 256), lambda g, at: (0, g)),
+                pl.BlockSpec((half, 256), lambda g, at: (0, g)),
                 pl.BlockSpec((half, 256), lambda g, at: (0, 0)),
             ],
             scratch_shapes=[pltpu.VMEM((rows, 256), jnp.float32)],
@@ -84,6 +89,8 @@
         out_shape=[
             jax.ShapeDtypeStruct((rows + FAR, width // 4), jnp.bfloat16),
             jax.ShapeDtypeStruct((rows, width // 4), jnp.bfloat16),
+            jax.ShapeDtypeStruct((half, width // 4), jnp.bfloat16),
+            jax.ShapeDtypeStruct((half, width // 4), jnp.bfloat16),
             jax.ShapeDtypeStruct((half, 256), jnp.bfloat16),
         ],
         compiler_params=params(62),
@@ -307,10 +314,10 @@
 
 def fisher_terms(at, mantissas, exps, pair, placed):
     rows = mantissas.shape[0]
-    low, high, own = dequant(at, exps, mantissas)
+    low, high, low_half, high_half, own = dequant(at, exps, mantissas)
 
     half = rows // 2
-    pieces = [(half, True, low, high)]
+    pieces = [(half, False, low_half, high_half)]
     for step in range(1, Z // 2 + 1):
         if step == Z // 2:
             low, high, third = halve(at, low, high, near)
@@ -328,11 +335,11 @@
     mine = own_slots(placed)
     received = (own, near, lax.ppermute(third, "yl", SWAP))
 
-    given_other = gram(at, pieces, received, False, (0,), mine)
+    given_other = gram(at, pieces, received, False, (0,))
     swapped = [lax.ppermute(g, "core", SWAP) for g in given_other]
     given_own = gram(at, pieces, received, False, (1,), *given_other)
     given = add([*given_own, *swapped])
-    *kept_other, low_kept, high_kept = gram(at, pieces, received, True, (0, 1), given)
+    *kept_other, low_kept, high_kept = gram(at, pieces, received, True, (0, 1), given, mine)
     kept = [lax.ppermute(k, "core", SWAP) for k in kept_other]
     return given, [low_kept, high_kept, *kept], mine
 

time: 104 us -> 117 us (1.12)
  blocking collectives: 0 us -> 26.3 us
  starting transfers between devices: 37 us -> 17.6 us
  waiting for transfers between devices: 33.4 us -> 50.2 us
  Pallas kernels: 23.2 us -> 17.3 us
  local copies, waits for them, and re-layouts: 4.52 us -> 0.69 us
    all_to_all x0 -> x1, blocking collectives: none -> 26.3 us  [own_slots(): lax.all_to_all(placed.reshape(YH * Z, half, double), ('yh', 'z'), 0, 0, t...]
    ppermute x4, waiting for transfers between devices: 0.01 us -> 10.3 us  [fisher_terms(): low = lax.ppermute(low, ('z', 'core'), RING)]
    ppermute x1, waiting for transfers between devices: 8.49 us -> 0.01 us  [per_device(): got = lax.ppermute(given, 'yh', SWAP)]
    all_to_all x1 -> x0, starting transfers between devices: 7.95 us -> none  [own_slots(): lax.all_to_all(placed.reshape(YH * Z, half, double), ('yh', 'z'), 0, 0, t...]
    ppermute x1, waiting for transfers between devices: 0.01 us -> 7.11 us  [fisher_terms(): near = lax.ppermute(near, 'yl', SWAP)]
    ppermute x4, starting transfers between devices: 8.08 us -> 1.99 us  [fisher_terms(): low = lax.ppermute(low, ('z', 'core'), RING)]
    ppermute x4, waiting for transfers between devices: 7.88 us -> 13.2 us  [fisher_terms(): high = lax.ppermute(high, ('z', 'core'), RING)]
    ppermute x4, starting transfers between devices: 6.62 us -> 2.14 us  [fisher_terms(): high = lax.ppermute(high, ('z', 'core'), RING)]
  transfers between devices with their start and end apart: 20 -> 19, of which waited for: 10 -> 12; matrix products, arithmetic and copies ran while one was open for 4% -> 3% of each run, Pallas kernels for 13% -> 7%
where the time goes in v9:
time: 117 us
  waiting for transfers between devices  50.2 us (43%)
  blocking collectives  26.3 us (22%)
  starting transfers between devices  17.6 us (15%)
  Pallas kernels  17.3 us (15%)
  matrix products  3.7 us (3%)
    all_to_all x1, blocking collectives, own_slots(): lax.all_to_all(placed.reshape(YH * Z, half, double), ('yh', 'z'), 0, 0, t...  26.3 us
    ppermute x4, waiting for transfers between devices, fisher_terms(): high = lax.ppermute(high, ('z', 'core'), RING)  13.2 us
    ppermute x4, waiting for transfers between devices, fisher_terms(): low = lax.ppermute(low, ('z', 'core'), RING)  10.3 us
    ppermute x1, waiting for transfers between devices, fisher_terms(): near = lax.ppermute(near, 'yl', SWAP)  7.11 us
    pallas_call x3, Pallas kernels, gram(): pl.pallas_call(functools.partial(gram_kernel, sizes, kept, len(parts)), g...  6.5 us
    pallas_call x1, Pallas kernels, dequant(): pl.pallas_call(dequant_kernel, grid_spec=pltpu.PrefetchScalarGridSpec(num...  5.03 us
    ppermute x1, waiting for transfers between devices, placed_scores(): lax.ppermute(lax.dynamic_slice_in_dim(scores, (1 - upper) * 2 * share, 2...  4.36 us
    ppermute x1, waiting for transfers between devices, fisher_terms(): received = (own, near, lax.ppermute(third, 'yl', SWAP))  4.17 us
  transfers between devices with their start and end apart: 19, of which 12 were waited for; matrix products, arithmetic and copies ran while one was open for 3% of the time, Pallas kernels for 7%

profile of v9, /device:TPU:2, one launch (start us, length us, event | category | flops | bytes accessed | tf_op | source)
XLA Modules:
  0.0 116.7 jit_solution(12420256370817700548)
XLA Ops:
  0.6 0.6 stack.40.at
  1.3 5.0 %dequant.1 = (bf16[288,1024]{1,0:T(8,128)(2,1)}, bf16[256,1024]{1,0:T(8,128)(2,1)}, bf16[128,1024]{1,0:T(8,128)(2,1)}, bf16[128,1024]{1,0:T(8,128)(2,1)}, bf16[128,256]{1,0:T(8,128)(2,1)}) custom-call(s32[7]{0:T(128)} %stack.40.at, s32[32,256]{1,0:T(8,128)} %bitcast.47, bf16[256,4096]{1,0:T(8,128)(2,1)} %bitcast.43, bf16[256,4096]{1,0:T(8,128)(2,1)} %bitcast.44, ...), custom_call_target="tpu_custom_call" | custom-call | flops 33554432 | bytes 2097152 | tf_op jit(solution)/shard_map/dequant/pallas_call | solution.py:69
  6.3 2.0 %collective-permute-start.5 = (bf16[256,1024]{1,0:T(8,128)(2,1)}, bf16[256,1024]{1,0:T(8,128)(2,1)S(1)}, u32[]{:S(2)}, u32[]{:S(2)}) collective-permute-start(bf16[256,1024]{1,0:T(8,128)(2,1)} %get-tuple-element.20), channel_id=1, source_target_pairs={{0,16},{16,32},{32,48},{48,64},{64,80},{80,96},{96,112},{112,0},{1... | collective-permute-start | bytes 1572872 | tf_op jit(solution)/shard_map/ppermute | solution.py:325
  8.3 1.9 %collective-permute-start = (bf16[288,1024]{1,0:T(8,128)(2,1)}, bf16[288,1024]{1,0:T(8,128)(2,1)S(1)}, u32[]{:S(2)}, u32[]{:S(2)}) collective-permute-start(bf16[288,1024]{1,0:T(8,128)(2,1)} %get-tuple-element.19), channel_id=1, source_target_pairs={{0,16},{16,32},{32,48},{48,64},{64,80},{80,96},{96,112},{112,0},{1... | collective-permute-start | bytes 1769480 | tf_op jit(solution)/shard_map/ppermute | solution.py:324
  10.2 3.7 %fusion.1 = f32[256,256]{0,1:T(8,128)S(1)} fusion(bf16[256,1,4096]{2,0,1:T(8,128)(2,1)} %param.7, s32[4096]{0:T(1024)S(1)} %add_select_fusion, s32[256,1,32]{0,2,1:T(8,128)S(1)} %copy-done.6, bf16[256,1,4096]{2,0,1:T(8,128)(2,1)} %param.5), kind=kOutput, calls=%fused_computation.2 | convolution fusion | flops 606232576 | bytes 4505600 | tf_op jit(solution)/shard_map/dot_general | solution.py:405
  13.9 0.0 copy-start.4
  13.9 0.0 copy-start.5
  14.0 2.2 %collective-permute-start.1 = (f32[128,256]{1,0:T(8,128)S(1)}, f32[128,256]{1,0:T(8,128)S(1)}, u32[]{:S(2)}, u32[]{:S(2)}) collective-permute-start(f32[128,256]{1,0:T(8,128)S(1)} %dynamic-slice_bitcast_fusion), channel_id=1, source_target_pairs={{0,8},{4,12},{8,0},{12,4},{1,9},{5,13},{9,1},{13,5},{2,10},{6,14},... | collective-permute-start | bytes 393224 | tf_op jit(solution)/shard_map/ppermute | solution.py:409
  16.2 4.4 %collective-permute-done.1 = f32[128,256]{1,0:T(8,128)S(1)} collective-permute-done((f32[128,256]{1,0:T(8,128)S(1)}, f32[128,256]{1,0:T(8,128)S(1)}, u32[]{:S(2)}, u32[]{:S(2)}) %collective-permute-start.1) | collective-permute-done | bytes 131104 | tf_op jit(solution)/shard_map/ppermute | solution.py:409
  20.6 5.3 %collective-permute-done.refs_0_ = bf16[288,1024]{1,0:T(8,128)(2,1)S(1)} collective-permute-done((bf16[288,1024]{1,0:T(8,128)(2,1)}, bf16[288,1024]{1,0:T(8,128)(2,1)S(1)}, u32[]{:S(2)}, u32[]{:S(2)}) %collective-permute-start) | collective-permute-done | bytes 589856 | tf_op jit(solution)/shard_map/ppermute | solution.py:324
  25.9 0.0 collective-permute-start.2
  25.9 0.1 collective-permute-start.6
  26.0 0.6 collective-permute-start.3
  26.7 4.0 %collective-permute-done.3.got = f32[64,256]{1,0:T(8,128)S(1)} collective-permute-done((f32[64,256]{1,0:T(8,128)S(1)}, f32[64,256]{1,0:T(8,128)S(1)}, u32[]{:S(2)}, u32[]{:S(2)}) %collective-permute-start.3) | collective-permute-done | bytes 65568 | tf_op jit(solution)/shard_map/ppermute | solution.py:411
  30.6 1.4 %place.1.refs_1_.refs_0_ = f32[512,128]{1,0:T(8,128)S(1)} custom-call(s32[7]{0:T(128)S(1)} %copy-done.3, f32[2,64,256]{2,1,0:T(8,128)S(1)} %bitcast.39, f32[64,256]{1,0:T(8,128)S(1)} %collective-permute-done.3.got, s32[1,256]{1,0:T(1,128)S(1)} %bitcast.42, s32[1,1024]{1,0:T(1,128)S(1)} %bitcast.41), custom_call_target="tpu_custom_call" | custom-call | flops 268435456 | bytes 1048576 | tf_op jit(solution)/shard_map/place/pallas_call | solution.py:413
  32.1 4.9 %collective-permute-done.2.refs_0_ = bf16[288,1024]{1,0:T(8,128)(2,1)S(1)} collective-permute-done((bf16[288,1024]{1,0:T(8,128)(2,1)S(1)}, bf16[288,1024]{1,0:T(8,128)(2,1)S(1)}, u32[]{:S(2)}, u32[]{:S(2)}) %collective-permute-start.2) | collective-permute-done | bytes 589856 | tf_op jit(solution)/shard_map/ppermute | solution.py:324
  37.0 0.0 collective-permute-start.4
  37.0 5.6 %collective-permute-done.6.refs_3_.refs_7_.refs_17_ = bf16[256,1024]{1,0:T(8,128)(2,1)S(1)} collective-permute-done((bf16[256,1024]{1,0:T(8,128)(2,1)S(1)}, bf16[256,1024]{1,0:T(8,128)(2,1)S(1)}, u32[]{:S(2)}, u32[]{:S(2)}) %collective-permute-start.6) | collective-permute-done | bytes 524320 | tf_op jit(solution)/shard_map/ppermute | solution.py:325
  42.6 0.0 collective-permute-start.7
  42.6 0.6 pick.1.refs_1_
  43.3 0.0 copy-start.2
  43.3 1.7 %collective-permute-start.8 = (bf16[512,256]{1,0:T(8,128)(2,1)S(1)}, bf16[512,256]{1,0:T(8,128)(2,1)S(1)}, u32[]{:S(2)}, u32[]{:S(2)}) collective-permute-start(bf16[512,256]{1,0:T(8,128)(2,1)S(1)} %pick.1.refs_1_), channel_id=1, source_target_pairs={{0,2},{2,0},{1,3},{3,1},{4,6},{6,4},{5,7},{7,5},{8,10},{10,8},{9,1... | collective-permute-start | bytes 786440 | tf_op jit(solution)/shard_map/ppermute | solution.py:334
  45.0 7.1 %collective-permute-done.8.after.refs_21_ = bf16[512,256]{1,0:T(8,128)(2,1)S(1)} collective-permute-done((bf16[512,256]{1,0:T(8,128)(2,1)S(1)}, bf16[512,256]{1,0:T(8,128)(2,1)S(1)}, u32[]{:S(2)}, u32[]{:S(2)}) %collective-permute-start.8) | collective-permute-done | bytes 262176 | tf_op jit(solution)/shard_map/ppermute | solution.py:334
  52.1 2.5 %collective-permute-done.7.high.high_lanes.refs_8_.refs_18_ = bf16[256,1024]{1,0:T(8,128)(2,1)S(1)} collective-permute-done((bf16[256,1024]{1,0:T(8,128)(2,1)S(1)}, bf16[256,1024]{1,0:T(8,128)(2,1)S(1)}, u32[]{:S(2)}, u32[]{:S(2)}) %collective-permute-start.7) | collective-permute-done | bytes 524320 | tf_op jit(solution)/shard_map/ppermute | solution.py:325
  54.6 0.6 halve.1
  55.2 0.1 collective-permute-start.9
  55.3 0.1 collective-permute-start.10
  55.4 1.7 %collective-permute-start.11 = (bf16[256,256]{1,0:T(8,128)(2,1)S(1)}, bf16[256,256]{1,0:T(8,128)(2,1)S(1)}, u32[]{:S(2)}, u32[]{:S(2)}) collective-permute-start(bf16[256,256]{1,0:T(8,128)(2,1)S(1)} %get-tuple-element.25), channel_id=1, source_target_pairs={{0,2},{2,0},{1,3},{3,1},{4,6},{6,4},{5,7},{7,5},{8,10},{10,8},{9,1... | collective-permute-start | bytes 393224 | tf_op jit(solution)/shard_map/ppermute | solution.py:336
  57.1 4.2 %collective-permute-done.11.refs_22_ = bf16[256,256]{1,0:T(8,128)(2,1)S(1)} collective-permute-done((bf16[256,256]{1,0:T(8,128)(2,1)S(1)}, bf16[256,256]{1,0:T(8,128)(2,1)S(1)}, u32[]{:S(2)}, u32[]{:S(2)}) %collective-permute-start.11) | collective-permute-done | bytes 131104 | tf_op jit(solution)/shard_map/ppermute | solution.py:336
  61.2 5.1 %collective-permute-done.10.refs_9_.refs_19_ = bf16[128,1024]{1,0:T(8,128)(2,1)S(1)} collective-permute-done((bf16[128,1024]{1,0:T(8,128)(2,1)S(1)}, bf16[128,1024]{1,0:T(8,128)(2,1)S(1)}, u32[]{:S(2)}, u32[]{:S(2)}) %collective-permute-start.10) | collective-permute-done | bytes 262176 | tf_op jit(solution)/shard_map/ppermute | solution.py:325
  66.4 1.5 %gram.3 = (f32[256,512]{1,0:T(8,128)S(1)}, f32[256,512]{1,0:T(8,128)S(1)}) custom-call(s32[7]{0:T(128)S(1)} %copy-done.3, bf16[128,1024]{1,0:T(8,128)(2,1)S(1)} %copy-done, bf16[288,1024]{1,0:T(8,128)(2,1)S(1)} %tie.3.refs_0_.refs_1_.refs_11_, bf16[288,1024]{1,0:T(8,128)(2,1)S(1)} %tie.4.refs_2_.refs_12_, ...), custom_call_target="tpu_custom_call" | custom-call | tf_op jit(solution)/shard_map/gram/pallas_call | solution.py:240
  67.9 0.3 collective-permute-start.12
  68.2 0.5 collective-permute-start.13
  68.7 1.5 %gram.4 = (f32[256,512]{1,0:T(8,128)S(1)}, f32[256,512]{1,0:T(8,128)S(1)}) custom-call(s32[7]{0:T(128)S(1)} %copy-done.3, bf16[128,1024]{1,0:T(8,128)(2,1)S(1)} %copy-done, bf16[288,1024]{1,0:T(8,128)(2,1)S(1)} %tie.3.refs_0_.refs_1_.refs_11_, bf16[288,1024]{1,0:T(8,128)(2,1)S(1)} %tie.4.refs_2_.refs_12_, ...), custom_call_target="tpu_custom_call" | custom-call | tf_op jit(solution)/shard_map/gram/pallas_call | solution.py:240
  70.3 0.6 collective-permute-done.13.high_got
  70.9 0.1 add.41.refs_24_
  71.0 3.3 %collective-permute-start.16 = (f32[256,1024]{1,0:T(8,128)S(1)}, f32[256,1024]{1,0:T(8,128)S(1)}, u32[]{:S(2)}, u32[]{:S(2)}) collective-permute-start(f32[256,1024]{1,0:T(8,128)S(1)} %add.41.refs_24_), channel_id=1, source_target_pairs={{0,128},{128,0},{1,129},{129,1},{2,130},{130,2},{3,131},{131,3},{4... | collective-permute-start | bytes 3145736 | tf_op jit(solution)/shard_map/ppermute | solution.py:481
  74.3 26.3 %all_to_all.5.parts = f32[16,32,128]{2,1,0:T(8,128)S(1)} all-to-all(f32[16,32,128]{2,1,0:T(8,128)S(1)} %bitcast.38), channel_id=1, replica_groups=mesh['yh'=2,'z'=8,'x'=4,'yl'=2,'core'=2] {'yh','z'}, dimensions={0} | all-to-all | bytes 524288 | tf_op jit(solution)/shard_map/all_to_all | solution.py:444
  100.6 3.4 %gram.5 = (f32[256,512]{1,0:T(8,128)S(1)}, f32[256,512]{1,0:T(8,128)S(1)}, f32[256,512]{1,0:T(8,128)S(1)}, f32[256,512]{1,0:T(8,128)S(1)}) custom-call(s32[7]{0:T(128)S(1)} %copy-done.3, bf16[128,1024]{1,0:T(8,128)(2,1)S(1)} %copy-done, bf16[288,1024]{1,0:T(8,128)(2,1)S(1)} %tie.3.refs_0_.refs_1_.refs_11_, bf16[288,1024]{1,0:T(8,128)(2,1)S(1)} %tie.4.refs_2_.refs_12_, ...), custom_call_target="tpu_custom_call" | custom-call | tf_op jit(solution)/shard_map/gram/pallas_call | solution.py:240
  104.1 0.1 collective-permute-start.14
  104.2 0.5 collective-permute-start.15
  104.7 0.5 collective-permute-start.17
  105.2 3.2 %collective-permute-done.17 = f32[32,128]{1,0:T(8,128)S(1)} collective-permute-done((f32[32,128]{1,0:T(8,128)S(1)}, f32[32,128]{1,0:T(8,128)S(1)}, u32[]{:S(2)}, u32[]{:S(2)}) %collective-permute-start.17) | collective-permute-done | bytes 16416 | tf_op jit(solution)/shard_map/ppermute | solution.py:456
  108.4 2.1 %collective-permute-start.18 = (f32[2,32,128]{2,1,0:T(8,128)S(1)}, f32[2,32,128]{2,1,0:T(8,128)S(1)}, u32[]{:S(2)}, u32[]{:S(2)}) collective-permute-start(f32[2,32,128]{2,1,0:T(8,128)S(1)} %pad_maximum_fusion.pair), channel_id=1, source_target_pairs={{0,8},{4,12},{8,0},{12,4},{1,9},{5,13},{9,1},{13,5},{2,10},{6,14},... | collective-permute-start | bytes 98312 | tf_op jit(solution)/shard_map/ppermute | solution.py:457
  110.5 3.3 %collective-permute-done.18.far_pair = f32[2,32,128]{2,1,0:T(8,128)S(1)} collective-permute-done((f32[2,32,128]{2,1,0:T(8,128)S(1)}, f32[2,32,128]{2,1,0:T(8,128)S(1)}, u32[]{:S(2)}, u32[]{:S(2)}) %collective-permute-start.18) | collective-permute-done | bytes 32800 | tf_op jit(solution)/shard_map/ppermute | solution.py:457
  113.8 1.3 %assemble.1 = f32[64,256]{1,0:T(8,128)} custom-call(s32[7]{0:T(128)S(1)} %copy-done.3, f32[2,32,128]{2,1,0:T(8,128)S(1)} %pad_maximum_fusion.pair, f32[2,32,128]{2,1,0:T(8,128)S(1)} %collective-permute-done.18.far_pair), custom_call_target="tpu_custom_call" | custom-call | bytes 131072 | tf_op jit(solution)/shard_map/assemble/pallas_call | solution.py:458
  115.1 0.0 collective-permute-done.14.low_core
  115.1 1.6 %finish.1 = f32[256,1024]{1,0:T(8,128)} custom-call(f32[256,512]{1,0:T(8,128)S(1)} %get-tuple-element.30.low, f32[256,512]{1,0:T(8,128)S(1)} %get-tuple-element.31.high, f32[256,512]{1,0:T(8,128)S(1)} %collective-permute-done.14.low_core, f32[256,512]{1,0:T(8,128)S(1)} %collective-permute-done.15.high_core, f32[256,1024]{1,0:T(8,128)S(1)} %collective-permute-done.16.got), custom_call_target="tpu_custom_call" | custom-call | flops 1048576 | bytes 4194304 | tf_op jit(solution)/shard_map/finish/pallas_call | solution.py:285
  (26 shorter events, 0.1 us)
Async XLA Ops:
  1.3 8.9 %copy-start.6 = (s32[256,1,32]{0,2,1:T(8,128)S(1)}, s32[256,1,32]{0,2,1:T(8,128)}, u32[]{:S(2)}) copy-start(s32[256,1,32]{0,2,1:T(8,128)} %param.6) | copy-start | bytes 98308
  6.3 19.6 %collective-permute-start.5 = (bf16[256,1024]{1,0:T(8,128)(2,1)}, bf16[256,1024]{1,0:T(8,128)(2,1)S(1)}, u32[]{:S(2)}, u32[]{:S(2)}) collective-permute-start(bf16[256,1024]{1,0:T(8,128)(2,1)} %get-tuple-element.20), channel_id=1, source_target_pairs={{0,16},{16,32},{32,48},{48,64},{64,80},{80,96},{96,112},{112,0},{1... | collective-permute-start | bytes 1572872 | tf_op jit(solution)/shard_map/ppermute | solution.py:325
  8.3 17.6 %collective-permute-start = (bf16[288,1024]{1,0:T(8,128)(2,1)}, bf16[288,1024]{1,0:T(8,128)(2,1)S(1)}, u32[]{:S(2)}, u32[]{:S(2)}) collective-permute-start(bf16[288,1024]{1,0:T(8,128)(2,1)} %get-tuple-element.19), channel_id=1, source_target_pairs={{0,16},{16,32},{32,48},{48,64},{64,80},{80,96},{96,112},{112,0},{1... | collective-permute-start | bytes 1769480 | tf_op jit(solution)/shard_map/ppermute | solution.py:324
  13.9 16.7 %copy-start.3 = (s32[7]{0:T(128)S(1)}, s32[7]{0:T(128)}, u32[]{:S(2)}) copy-start(s32[7]{0:T(128)} %stack.40.at) | copy-start | bytes 88
  13.9 16.7 %copy-start.4 = (s32[1024]{0:T(1024)S(1)}, s32[1024]{0:T(1024)}, u32[]{:S(2)}) copy-start(s32[1024]{0:T(1024)} %param.9) | copy-start | bytes 12292
  13.9 16.7 %copy-start.5 = (s32[256]{0:T(256)S(1)}, s32[256]{0:T(256)}, u32[]{:S(2)}) copy-start(s32[256]{0:T(256)} %param.8) | copy-start | bytes 3076
  14.0 6.6 %collective-permute-start.1 = (f32[128,256]{1,0:T(8,128)S(1)}, f32[128,256]{1,0:T(8,128)S(1)}, u32[]{:S(2)}, u32[]{:S(2)}) collective-permute-start(f32[128,256]{1,0:T(8,128)S(1)} %dynamic-slice_bitcast_fusion), channel_id=1, source_target_pairs={{0,8},{4,12},{8,0},{12,4},{1,9},{5,13},{9,1},{13,5},{2,10},{6,14},... | collective-permute-start | bytes 393224 | tf_op jit(solution)/shard_map/ppermute | solution.py:409
  25.9 11.1 %collective-permute-start.2 = (bf16[288,1024]{1,0:T(8,128)(2,1)S(1)}, bf16[288,1024]{1,0:T(8,128)(2,1)S(1)}, u32[]{:S(2)}, u32[]{:S(2)}) collective-permute-start(bf16[288,1024]{1,0:T(8,128)(2,1)S(1)} %tie.3.refs_0_.refs_1_.refs_11_), channel_id=1, source_target_pairs={{0,16},{16,32},{32,48},{48,64},{64,80},{80,96},{96,112},{112,0},{1... | collective-permute-start | bytes 1769480 | tf_op jit(solution)/shard_map/ppermute | solution.py:324
  25.9 16.7 %collective-permute-start.6 = (bf16[256,1024]{1,0:T(8,128)(2,1)S(1)}, bf16[256,1024]{1,0:T(8,128)(2,1)S(1)}, u32[]{:S(2)}, u32[]{:S(2)}) collective-permute-start(bf16[256,1024]{1,0:T(8,128)(2,1)S(1)} %collective-permute-done.5.refs_1_.refs_6_.refs_16_), channel_id=1, source_target_pairs={{0,16},{16,32},{32,48},{48,64},{64,80},{80,96},{96,112},{112,0},{1... | collective-permute-start | bytes 1572872 | tf_op jit(solution)/shard_map/ppermute | solution.py:325
  26.0 4.6 %collective-permute-start.3 = (f32[64,256]{1,0:T(8,128)S(1)}, f32[64,256]{1,0:T(8,128)S(1)}, u32[]{:S(2)}, u32[]{:S(2)}) collective-permute-start(f32[64,256]{1,0:T(8,128)S(1)} %constant_dynamic-slice_fusion), channel_id=1, source_target_pairs={{0,4},{4,0},{8,12},{12,8},{1,5},{5,1},{9,13},{13,9},{2,6},{6,2},{1... | collective-permute-start | bytes 196616 | tf_op jit(solution)/shard_map/ppermute | solution.py:411
  37.0 17.6 %collective-permute-start.4 = (bf16[288,1024]{1,0:T(8,128)(2,1)S(1)}, bf16[288,1024]{1,0:T(8,128)(2,1)S(1)}, u32[]{:S(2)}, u32[]{:S(2)}) collective-permute-start(bf16[288,1024]{1,0:T(8,128)(2,1)S(1)} %tie.4.refs_2_.refs_12_), channel_id=1, source_target_pairs={{0,16},{16,32},{32,48},{48,64},{64,80},{80,96},{96,112},{112,0},{1... | collective-permute-start | bytes 1769480 | tf_op jit(solution)/shard_map/ppermute | solution.py:324
  42.6 11.9 %collective-permute-start.7 = (bf16[256,1024]{1,0:T(8,128)(2,1)S(1)}, bf16[256,1024]{1,0:T(8,128)(2,1)S(1)}, u32[]{:S(2)}, u32[]{:S(2)}) collective-permute-start(bf16[256,1024]{1,0:T(8,128)(2,1)S(1)} %collective-permute-done.6.refs_3_.refs_7_.refs_17_), channel_id=1, source_target_pairs={{0,16},{16,32},{32,48},{48,64},{64,80},{80,96},{96,112},{112,0},{1... | collective-permute-start | bytes 1572872 | tf_op jit(solution)/shard_map/ppermute | solution.py:325
  43.3 23.1 %copy-start = (bf16[128,1024]{1,0:T(8,128)(2,1)S(1)}, bf16[128,1024]{1,0:T(8,128)(2,1)}, u32[]{:S(2)}) copy-start(bf16[128,1024]{1,0:T(8,128)(2,1)} %get-tuple-element.18.refs_0_.refs_10_) | copy-start | bytes 786436
  43.3 23.1 %copy-start.1 = (bf16[128,1024]{1,0:T(8,128)(2,1)S(1)}, bf16[128,1024]{1,0:T(8,128)(2,1)}, u32[]{:S(2)}) copy-start(bf16[128,1024]{1,0:T(8,128)(2,1)} %get-tuple-element.22.refs_5_.refs_15_) | copy-start | bytes 786436
  43.3 23.1 %copy-start.2 = (bf16[128,256]{1,0:T(8,128)(2,1)S(1)}, bf16[128,256]{1,0:T(8,128)(2,1)}, u32[]{:S(2)}) copy-start(bf16[128,256]{1,0:T(8,128)(2,1)} %get-tuple-element.24.refs_20_) | copy-start | bytes 196612
  43.3 8.8 %collective-permute-start.8 = (bf16[512,256]{1,0:T(8,128)(2,1)S(1)}, bf16[512,256]{1,0:T(8,128)(2,1)S(1)}, u32[]{:S(2)}, u32[]{:S(2)}) collective-permute-start(bf16[512,256]{1,0:T(8,128)(2,1)S(1)} %pick.1.refs_1_), channel_id=1, source_target_pairs={{0,2},{2,0},{1,3},{3,1},{4,6},{6,4},{5,7},{7,5},{8,10},{10,8},{9,1... | collective-permute-start | bytes 786440 | tf_op jit(solution)/shard_map/ppermute | solution.py:334
  55.2 11.2 %collective-permute-start.9 = (bf16[160,1024]{1,0:T(8,128)(2,1)S(1)}, bf16[160,1024]{1,0:T(8,128)(2,1)S(1)}, u32[]{:S(2)}, u32[]{:S(2)}) collective-permute-start(bf16[160,1024]{1,0:T(8,128)(2,1)S(1)} %get-tuple-element.21), channel_id=1, source_target_pairs={{0,16},{16,32},{32,48},{48,64},{64,80},{80,96},{96,112},{112,0},{1... | collective-permute-start | bytes 983048 | tf_op jit(solution)/shard_map/ppermute | solution.py:324
  55.3 11.1 %collective-permute-start.10 = (bf16[128,1024]{1,0:T(8,128)(2,1)S(1)}, bf16[128,1024]{1,0:T(8,128)(2,1)S(1)}, u32[]{:S(2)}, u32[]{:S(2)}) collective-permute-start(bf16[128,1024]{1,0:T(8,128)(2,1)S(1)} %get-tuple-element.23), channel_id=1, source_target_pairs={{0,16},{16,32},{32,48},{48,64},{64,80},{80,96},{96,112},{112,0},{1... | collective-permute-start | bytes 786440 | tf_op jit(solution)/shard_map/ppermute | solution.py:325
  55.4 5.9 %collective-permute-start.11 = (bf16[256,256]{1,0:T(8,128)(2,1)S(1)}, bf16[256,256]{1,0:T(8,128)(2,1)S(1)}, u32[]{:S(2)}, u32[]{:S(2)}) collective-permute-start(bf16[256,256]{1,0:T(8,128)(2,1)S(1)} %get-tuple-element.25), channel_id=1, source_target_pairs={{0,2},{2,0},{1,3},{3,1},{4,6},{6,4},{5,7},{7,5},{8,10},{10,8},{9,1... | collective-permute-start | bytes 393224 | tf_op jit(solution)/shard_map/ppermute | solution.py:336
  67.9 2.3 %collective-permute-start.12 = (f32[256,512]{1,0:T(8,128)S(1)}, f32[256,512]{1,0:T(8,128)S(1)}, u32[]{:S(2)}, u32[]{:S(2)}) collective-permute-start(f32[256,512]{1,0:T(8,128)S(1)} %get-tuple-element.26.refs_24_), channel_id=1, source_target_pairs={{0,1},{1,0},{2,3},{3,2},{4,5},{5,4},{6,7},{7,6},{8,9},{9,8},{10,11... | collective-permute-start | bytes 1572872 | tf_op jit(solution)/shard_map/ppermute | solution.py:339
  68.2 2.6 %collective-permute-start.13 = (f32[256,512]{1,0:T(8,128)S(1)}, f32[256,512]{1,0:T(8,128)S(1)}, u32[]{:S(2)}, u32[]{:S(2)}) collective-permute-start(f32[256,512]{1,0:T(8,128)S(1)} %get-tuple-element.27.refs_25_), channel_id=1, source_target_pairs={{0,1},{1,0},{2,3},{3,2},{4,5},{5,4},{6,7},{7,6},{8,9},{9,8},{10,11... | collective-permute-start | bytes 1572872 | tf_op jit(solution)/shard_map/ppermute | solution.py:339
  71.0 44.1 %collective-permute-start.16 = (f32[256,1024]{1,0:T(8,128)S(1)}, f32[256,1024]{1,0:T(8,128)S(1)}, u32[]{:S(2)}, u32[]{:S(2)}) collective-permute-start(f32[256,1024]{1,0:T(8,128)S(1)} %add.41.refs_24_), channel_id=1, source_target_pairs={{0,128},{128,0},{1,129},{129,1},{2,130},{130,2},{3,131},{131,3},{4... | collective-permute-start | bytes 3145736 | tf_op jit(solution)/shard_map/ppermute | solution.py:481
  104.1 11.0 %collective-permute-start.14 = (f32[256,512]{1,0:T(8,128)S(1)}, f32[256,512]{1,0:T(8,128)S(1)}, u32[]{:S(2)}, u32[]{:S(2)}) collective-permute-start(f32[256,512]{1,0:T(8,128)S(1)} %get-tuple-element.32), channel_id=1, source_target_pairs={{0,1},{1,0},{2,3},{3,2},{4,5},{5,4},{6,7},{7,6},{8,9},{9,8},{10,11... | collective-permute-start | bytes 1572872 | tf_op jit(solution)/shard_map/ppermute | solution.py:343
  104.2 10.9 %collective-permute-start.15 = (f32[256,512]{1,0:T(8,128)S(1)}, f32[256,512]{1,0:T(8,128)S(1)}, u32[]{:S(2)}, u32[]{:S(2)}) collective-permute-start(f32[256,512]{1,0:T(8,128)S(1)} %get-tuple-element.33), channel_id=1, source_target_pairs={{0,1},{1,0},{2,3},{3,2},{4,5},{5,4},{6,7},{7,6},{8,9},{9,8},{10,11... | collective-permute-start | bytes 1572872 | tf_op jit(solution)/shard_map/ppermute | solution.py:343
  104.7 3.7 %collective-permute-start.17 = (f32[32,128]{1,0:T(8,128)S(1)}, f32[32,128]{1,0:T(8,128)S(1)}, u32[]{:S(2)}, u32[]{:S(2)}) collective-permute-start(f32[32,128]{1,0:T(8,128)S(1)} %sum.1.refs_25_), channel_id=1, source_target_pairs={{0,4},{4,0},{8,12},{12,8},{1,5},{5,1},{9,13},{13,9},{2,6},{6,2},{1... | collective-permute-start | bytes 49160 | tf_op jit(solution)/shard_map/ppermute | solution.py:456
  108.4 5.4 %collective-permute-start.18 = (f32[2,32,128]{2,1,0:T(8,128)S(1)}, f32[2,32,128]{2,1,0:T(8,128)S(1)}, u32[]{:S(2)}, u32[]{:S(2)}) collective-permute-start(f32[2,32,128]{2,1,0:T(8,128)S(1)} %pad_maximum_fusion.pair), channel_id=1, source_target_pairs={{0,8},{4,12},{8,0},{12,4},{1,9},{5,13},{9,1},{13,5},{2,10},{6,14},... | collective-permute-start | bytes 98312 | tf_op jit(solution)/shard_map/ppermute | solution.py:457

commit v10 on v9

--- a/solution.py
+++ b/solution.py
@@ -99,46 +99,66 @@
     )(at, exps, mantissas, mantissas, mantissas)
 
 
-def halve_kernel(at, low, far, high, low_lanes, high_lanes, after, low_half, high_half, third):
-    del after
+def halve_low_kernel(at, low, far, low_half):
     half = low.shape[0]
     low_half[0:half] = low[...]
     low_half[half : half + FAR] = far[...]
-    high_half[...] = high[...]
-    third[...] = jnp.concatenate([low_lanes[...], high_lanes[...]], 1)
-
-
-def halve(at, low, high, after):
-    rows, width = high.shape
+
+
+def halve_low(at, low):
+    rows, width = low.shape[0] - FAR, low.shape[1]
     half = rows // 2
     return pl.pallas_call(
-        halve_kernel,
+        halve_low_kernel,
         grid_spec=pltpu.PrefetchScalarGridSpec(
             num_scalar_prefetch=1,
             grid=(1,),
             in_specs=[
                 pl.BlockSpec((half, width), lambda g, at: (at[AT_CORE], 0)),
                 pl.BlockSpec((FAR, width), lambda g, at: (rows // FAR, 0)),
+            ],
+            out_specs=pl.BlockSpec((half + FAR, width), lambda g, at: (0, 0)),
+        ),
+        out_shape=jax.ShapeDtypeStruct((half + FAR, width), jnp.bfloat16),
+        compiler_params=params(8),
+        cost_estimate=cost(0, 1 << 19),
+        name="halve_low",
+    )(at, low, low)
+
+
+def halve_high_kernel(at, high, low_lanes, high_lanes, after, high_half, third):
+    del after
+    high_half[...] = high[...]
+    third[...] = jnp.concatenate([low_lanes[...], high_lanes[...]], 1)
+
+
+def halve_high(at, low, high, after):
+    rows, width = high.shape
+    half = rows // 2
+    return pl.pallas_call(
+        halve_high_kernel,
+        grid_spec=pltpu.PrefetchScalarGridSpec(
+            num_scalar_prefetch=1,
+            grid=(1,),
+            in_specs=[
                 pl.BlockSpec((half, width), lambda g, at: (at[AT_CORE], 0)),
                 lanes_at_z(rows, False),
                 lanes_at_z(rows, False),
                 pl.BlockSpec(memory_space=pl.ANY),
             ],
             out_specs=[
-                pl.BlockSpec((half + FAR, width), lambda g, at: (0, 0)),
                 pl.BlockSpec((half, width), lambda g, at: (0, 0)),
                 pl.BlockSpec((rows, 256), lambda g, at: (0, 0)),
             ],
         ),
         out_shape=[
-            jax.ShapeDtypeStruct((half + FAR, width), jnp.bfloat16),
             jax.ShapeDtypeStruct((half, width), jnp.bfloat16),
             jax.ShapeDtypeStruct((rows, 256), jnp.bfloat16),
         ],
         compiler_params=params(8),
-        cost_estimate=cost(0, 2 << 20),
-        name="halve",
-    )(at, low, low, high, low, high, after)
+        cost_estimate=cost(0, 1 << 20),
+        name="halve_high",
+    )(at, high, low, high, after)
 
 
 def pick_kernel(count, at, *refs):
@@ -320,7 +340,8 @@
     pieces = [(half, False, low_half, high_half)]
     for step in range(1, Z // 2 + 1):
         if step == Z // 2:
-            low, high, third = halve(at, low, high, near)
+            high, third = halve_high(at, low, high, near)
+            low = halve_low(at, low)
         low = lax.ppermute(low, ("z", "core"), RING)
         high = lax.ppermute(high, ("z", "core"), RING)
         if step == 1:
@@ -335,11 +356,11 @@
     mine = own_slots(placed)
     received = (own, near, lax.ppermute(third, "yl", SWAP))
 
-    given_other = gram(at, pieces, received, False, (0,))
+    given_other = gram(at, pieces, received, False, (0,), mine)
     swapped = [lax.ppermute(g, "core", SWAP) for g in given_other]
     given_own = gram(at, pieces, received, False, (1,), *given_other)
     given = add([*given_own, *swapped])
-    *kept_other, low_kept, high_kept = gram(at, pieces, received, True, (0, 1), given, mine)
+    *kept_other, low_kept, high_kept = gram(at, pieces, received, True, (0, 1), given)
     kept = [lax.ppermute(k, "core", SWAP) for k in kept_other]
     return given, [low_kept, high_kept, *kept], mine
 

time: 117 us -> 104 us (0.89); the launches traced: 117 us -> 102 us
  blocking collectives: 26.3 us -> 0 us
  starting transfers between devices: 17.6 us -> 31.7 us
  waiting for transfers between devices: 50.2 us -> 37.6 us
  Pallas kernels: 17.3 us -> 25.5 us
  local copies, waits for them, and re-layouts: 0.69 us -> 2.51 us
    all_to_all x1 -> x0, blocking collectives: 26.3 us -> none  [own_slots(): lax.all_to_all(placed.reshape(YH * Z, half, double), ('yh', 'z'), 0, 0, t...]
    all_to_all x0 -> x1, starting transfers between devices: none -> 9.57 us  [own_slots(): lax.all_to_all(placed.reshape(YH * Z, half, double), ('yh', 'z'), 0, 0, t...]
    ppermute x4, waiting for transfers between devices: 10.3 us -> 1.58 us  [fisher_terms(): low = lax.ppermute(low, ('z', 'core'), RING)]
    ppermute x1, waiting for transfers between devices: 0.01 us -> 8.44 us  [per_device(): got = lax.ppermute(given, 'yh', SWAP)]
    ppermute x1, waiting for transfers between devices: 7.11 us -> 0.01 us  [fisher_terms(): near = lax.ppermute(near, 'yl', SWAP)]
    all_to_all x0 -> x1, waiting for transfers between devices: none -> 4.36 us  [own_slots(): lax.all_to_all(placed.reshape(YH * Z, half, double), ('yh', 'z'), 0, 0, t...]
    ppermute x1, waiting for transfers between devices: 4.17 us -> 0.01 us  [fisher_terms(): received = (own, near, lax.ppermute(third, 'yl', SWAP))]
    ppermute x4, starting transfers between devices: 1.99 us -> 6.09 us  [fisher_terms(): low = lax.ppermute(low, ('z', 'core'), RING)]
  transfers between devices with their start and end apart: 19 -> 20, of which waited for: 12 -> 10; matrix products, arithmetic and copies ran while one was open for 3% -> 4% of each run, Pallas kernels for 7% -> 16%
where the time goes in v10:
time: 104 us; the launch traced here: 102 us
  waiting for transfers between devices  37.6 us (36%)
  starting transfers between devices  31.7 us (30%)
  Pallas kernels  25.5 us (25%)
  matrix products  3.75 us (4%)
  local copies, waits for them, and re-layouts  2.51 us (2%)
    ppermute x4, waiting for transfers between devices, fisher_terms(): high = lax.ppermute(high, ('z', 'core'), RING)  11.3 us
    all_to_all x1, starting transfers between devices, own_slots(): lax.all_to_all(placed.reshape(YH * Z, half, double), ('yh', 'z'), 0, 0, t...  9.57 us
    pallas_call x3, Pallas kernels, gram(): pl.pallas_call(functools.partial(gram_kernel, sizes, kept, len(parts)), g...  9.5 us
    ppermute x1, waiting for transfers between devices, per_device(): got = lax.ppermute(given, 'yh', SWAP)  8.44 us
    ppermute x4, starting transfers between devices, fisher_terms(): low = lax.ppermute(low, ('z', 'core'), RING)  6.09 us
    pallas_call x1, Pallas kernels, dequant(): pl.pallas_call(dequant_kernel, grid_spec=pltpu.PrefetchScalarGridSpec(num...  5.02 us
    all_to_all x1, waiting for transfers between devices, own_slots(): lax.all_to_all(placed.reshape(YH * Z, half, double), ('yh', 'z'), 0, 0, t...  4.36 us
    dot_general x1, matrix products, placed_scores(): lax.dot_general(queries, grads, (((1,), (1,)), ((), ())), preferred_eleme...  3.75 us
  transfers between devices with their start and end apart: 20, of which 10 were waited for; matrix products, arithmetic and copies ran while one was open for 4% of the time, Pallas kernels for 16%

profile of v10, /device:TPU:2, one launch (start us, length us, event | category | flops | bytes accessed | tf_op | source)
XLA Modules:
  0.0 101.9 jit_solution(15573803310581093236)
XLA Ops:
  0.6 0.7 stack.40.at
  1.3 5.0 %dequant.1 = (bf16[288,1024]{1,0:T(8,128)(2,1)}, bf16[256,1024]{1,0:T(8,128)(2,1)}, bf16[128,1024]{1,0:T(8,128)(2,1)}, bf16[128,1024]{1,0:T(8,128)(2,1)}, bf16[128,256]{1,0:T(8,128)(2,1)}) custom-call(s32[7]{0:T(128)} %stack.40.at, s32[32,256]{1,0:T(8,128)} %bitcast.46, bf16[256,4096]{1,0:T(8,128)(2,1)} %bitcast.42, bf16[256,4096]{1,0:T(8,128)(2,1)} %bitcast.43, ...), custom_call_target="tpu_custom_call" | custom-call | flops 33554432 | bytes 2097152 | tf_op jit(solution)/shard_map/dequant/pallas_call | solution.py:69
  6.3 2.0 %collective-permute-start = (bf16[288,1024]{1,0:T(8,128)(2,1)}, bf16[288,1024]{1,0:T(8,128)(2,1)S(1)}, u32[]{:S(2)}, u32[]{:S(2)}) collective-permute-start(bf16[288,1024]{1,0:T(8,128)(2,1)} %get-tuple-element.18), channel_id=1, source_target_pairs={{0,16},{16,32},{32,48},{48,64},{64,80},{80,96},{96,112},{112,0},{1... | collective-permute-start | bytes 1769480 | tf_op jit(solution)/shard_map/ppermute | solution.py:345
  8.3 3.8 %fusion.1 = f32[256,256]{0,1:T(8,128)S(1)} fusion(bf16[256,1,4096]{2,0,1:T(8,128)(2,1)} %param.7, s32[4096]{0:T(1024)S(1)} %add_select_fusion, s32[256,1,32]{0,2,1:T(8,128)S(1)} %copy-done.7, bf16[256,1,4096]{2,0,1:T(8,128)(2,1)} %param.5), kind=kOutput, calls=%fused_computation.2 | convolution fusion | flops 606232576 | bytes 4505600 | tf_op jit(solution)/shard_map/dot_general | solution.py:426
  12.1 0.0 copy-start.5
  12.1 0.0 copy-start.6
  12.2 2.2 %collective-permute-start.1 = (f32[128,256]{1,0:T(8,128)S(1)}, f32[128,256]{1,0:T(8,128)S(1)}, u32[]{:S(2)}, u32[]{:S(2)}) collective-permute-start(f32[128,256]{1,0:T(8,128)S(1)} %dynamic-slice_bitcast_fusion), channel_id=1, source_target_pairs={{0,8},{4,12},{8,0},{12,4},{1,9},{5,13},{9,1},{13,5},{2,10},{6,14},... | collective-permute-start | bytes 393224 | tf_op jit(solution)/shard_map/ppermute | solution.py:430
  14.4 1.9 %collective-permute-start.6 = (bf16[256,1024]{1,0:T(8,128)(2,1)S(1)}, bf16[256,1024]{1,0:T(8,128)(2,1)S(1)}, u32[]{:S(2)}, u32[]{:S(2)}) collective-permute-start(bf16[256,1024]{1,0:T(8,128)(2,1)S(1)} %copy-done.8), channel_id=1, source_target_pairs={{0,16},{16,32},{32,48},{48,64},{64,80},{80,96},{96,112},{112,0},{1... | collective-permute-start | bytes 1572872 | tf_op jit(solution)/shard_map/ppermute | solution.py:346
  16.3 2.4 %collective-permute-done.1 = f32[128,256]{1,0:T(8,128)S(1)} collective-permute-done((f32[128,256]{1,0:T(8,128)S(1)}, f32[128,256]{1,0:T(8,128)S(1)}, u32[]{:S(2)}, u32[]{:S(2)}) %collective-permute-start.1) | collective-permute-done | bytes 131104 | tf_op jit(solution)/shard_map/ppermute | solution.py:430
  18.7 1.6 %collective-permute-done.refs_0_ = bf16[288,1024]{1,0:T(8,128)(2,1)S(1)} collective-permute-done((bf16[288,1024]{1,0:T(8,128)(2,1)}, bf16[288,1024]{1,0:T(8,128)(2,1)S(1)}, u32[]{:S(2)}, u32[]{:S(2)}) %collective-permute-start) | collective-permute-done | bytes 589856 | tf_op jit(solution)/shard_map/ppermute | solution.py:345
  20.3 0.4 collective-permute-start.2
  20.7 5.2 %collective-permute-done.6.refs_1_.refs_6_.refs_16_ = bf16[256,1024]{1,0:T(8,128)(2,1)S(1)} collective-permute-done((bf16[256,1024]{1,0:T(8,128)(2,1)S(1)}, bf16[256,1024]{1,0:T(8,128)(2,1)S(1)}, u32[]{:S(2)}, u32[]{:S(2)}) %collective-permute-start.6) | collective-permute-done | bytes 524320 | tf_op jit(solution)/shard_map/ppermute | solution.py:346
  25.9 0.0 collective-permute-start.7
  25.9 1.1 %collective-permute-start.3 = (f32[64,256]{1,0:T(8,128)S(1)}, f32[64,256]{1,0:T(8,128)S(1)}, u32[]{:S(2)}, u32[]{:S(2)}) collective-permute-start(f32[64,256]{1,0:T(8,128)S(1)} %constant_dynamic-slice_fusion), channel_id=1, source_target_pairs={{0,4},{4,0},{8,12},{12,8},{1,5},{5,1},{9,13},{13,9},{2,6},{6,2},{1... | collective-permute-start | bytes 196616 | tf_op jit(solution)/shard_map/ppermute | solution.py:432
  27.0 3.5 %collective-permute-done.3.got = f32[64,256]{1,0:T(8,128)S(1)} collective-permute-done((f32[64,256]{1,0:T(8,128)S(1)}, f32[64,256]{1,0:T(8,128)S(1)}, u32[]{:S(2)}, u32[]{:S(2)}) %collective-permute-start.3) | collective-permute-done | bytes 65568 | tf_op jit(solution)/shard_map/ppermute | solution.py:432
  30.5 2.2 %place.1.refs_1_.refs_0_ = f32[512,128]{1,0:T(8,128)} custom-call(s32[7]{0:T(128)S(1)} %copy-done.4, f32[2,64,256]{2,1,0:T(8,128)S(1)} %bitcast.38, f32[64,256]{1,0:T(8,128)S(1)} %collective-permute-done.3.got, s32[1,256]{1,0:T(1,128)S(1)} %bitcast.41, s32[1,1024]{1,0:T(1,128)S(1)} %bitcast.40), custom_call_target="tpu_custom_call" | custom-call | flops 268435456 | bytes 1048576 | tf_op jit(solution)/shard_map/place/pallas_call | solution.py:434
  32.6 0.0 collective-permute-done.2.refs_0_
  32.7 1.8 %collective-permute-start.4 = (bf16[288,1024]{1,0:T(8,128)(2,1)S(1)}, bf16[288,1024]{1,0:T(8,128)(2,1)S(1)}, u32[]{:S(2)}, u32[]{:S(2)}) collective-permute-start(bf16[288,1024]{1,0:T(8,128)(2,1)S(1)} %tie.4.refs_2_.refs_12_), channel_id=1, source_target_pairs={{0,16},{16,32},{32,48},{48,64},{64,80},{80,96},{96,112},{112,0},{1... | collective-permute-start | bytes 1769480 | tf_op jit(solution)/shard_map/ppermute | solution.py:345
  34.5 3.5 %collective-permute-done.7.refs_3_.refs_7_.refs_17_ = bf16[256,1024]{1,0:T(8,128)(2,1)} collective-permute-done((bf16[256,1024]{1,0:T(8,128)(2,1)S(1)}, bf16[256,1024]{1,0:T(8,128)(2,1)}, u32[]{:S(2)}, u32[]{:S(2)}) %collective-permute-start.7) | collective-permute-done | bytes 524320 | tf_op jit(solution)/shard_map/ppermute | solution.py:346
  38.0 2.2 %pick.1.refs_1_ = bf16[512,256]{1,0:T(8,128)(2,1)} custom-call(s32[7]{0:T(128)S(1)} %copy-done.4, bf16[288,1024]{1,0:T(8,128)(2,1)S(1)} %tie.3.refs_0_.refs_1_.refs_11_, bf16[256,1024]{1,0:T(8,128)(2,1)S(1)} %collective-permute-done.6.refs_1_.refs_6_.refs_16_, bf16[288,1024]{1,0:T(8,128)(2,1)S(1)} %tie.4.refs_2_.refs_12_, ...), custom_call_target="tpu_custom_call" | custom-call | bytes 524288 | tf_op jit(solution)/shard_map/pick/pallas_call | solution.py:183
  40.1 1.6 %collective-permute-start.9 = (bf16[512,256]{1,0:T(8,128)(2,1)}, bf16[512,256]{1,0:T(8,128)(2,1)}, u32[]{:S(2)}, u32[]{:S(2)}) collective-permute-start(bf16[512,256]{1,0:T(8,128)(2,1)} %pick.1.refs_1_), channel_id=1, source_target_pairs={{0,2},{2,0},{1,3},{3,1},{4,6},{6,4},{5,7},{7,5},{8,10},{10,8},{9,1... | collective-permute-start | bytes 786440 | tf_op jit(solution)/shard_map/ppermute | solution.py:355
  41.7 9.6 %all-to-all-start = ((f32[16,32,128]{2,1,0:T(8,128)}), f32[16,32,128]{2,1,0:T(8,128)}, u32[]{:S(2)}, u32[]{:S(2)}) async-start(f32[16,32,128]{2,1,0:T(8,128)} %bitcast.16), calls=%async_computation | async-start | bytes 524288 | tf_op jit(solution)/shard_map/all_to_all | solution.py:465
  51.3 1.3 %halve_low.1 = bf16[160,1024]{1,0:T(8,128)(2,1)} custom-call(s32[7]{0:T(128)S(1)} %copy-done.4, bf16[288,1024]{1,0:T(8,128)(2,1)S(1)} %collective-permute-done.4.low.far.low_lanes.refs_3_.refs_13_, bf16[288,1024]{1,0:T(8,128)(2,1)S(1)} %collective-permute-done.4.low.far.low_lanes.refs_3_.refs_13_), custom_call_target="tpu_custom_call" | custom-call | bytes 524288 | tf_op jit(solution)/shard_map/halve_low/pallas_call | solution.py:111
  52.6 1.9 %collective-permute-start.5 = (bf16[160,1024]{1,0:T(8,128)(2,1)}, bf16[160,1024]{1,0:T(8,128)(2,1)S(1)}, u32[]{:S(2)}, u32[]{:S(2)}) collective-permute-start(bf16[160,1024]{1,0:T(8,128)(2,1)} %halve_low.1), channel_id=1, source_target_pairs={{0,16},{16,32},{32,48},{48,64},{64,80},{80,96},{96,112},{112,0},{1... | collective-permute-start | bytes 983048 | tf_op jit(solution)/shard_map/ppermute | solution.py:345
  54.5 1.4 %halve_high.1 = (bf16[128,1024]{1,0:T(8,128)(2,1)}, bf16[256,256]{1,0:T(8,128)(2,1)}) custom-call(s32[7]{0:T(128)S(1)} %copy-done.4, bf16[256,1024]{1,0:T(8,128)(2,1)S(1)} %collective-permute-done.8.high.high_lanes.refs_8_.refs_18_, bf16[288,1024]{1,0:T(8,128)(2,1)S(1)} %collective-permute-done.4.low.far.low_lanes.refs_3_.refs_13_, ...), custom_call_target="tpu_custom_call" | custom-call | bytes 1048576 | tf_op jit(solution)/shard_map/halve_high/pallas_call | solution.py:138
  55.8 1.5 %collective-permute-start.10 = (bf16[128,1024]{1,0:T(8,128)(2,1)}, bf16[128,1024]{1,0:T(8,128)(2,1)}, u32[]{:S(2)}, u32[]{:S(2)}) collective-permute-start(bf16[128,1024]{1,0:T(8,128)(2,1)} %get-tuple-element.21), channel_id=1, source_target_pairs={{0,16},{16,32},{32,48},{48,64},{64,80},{80,96},{96,112},{112,0},{1... | collective-permute-start | bytes 786440 | tf_op jit(solution)/shard_map/ppermute | solution.py:346
  57.3 0.2 collective-permute-start.11
  57.4 4.4 %all-to-all-done.parts = f32[16,32,128]{2,1,0:T(8,128)} async-done(((f32[16,32,128]{2,1,0:T(8,128)}), f32[16,32,128]{2,1,0:T(8,128)}, u32[]{:S(2)}, u32[]{:S(2)}) %all-to-all-start) | async-done | bytes 262176 | tf_op jit(solution)/shard_map/all_to_all | solution.py:465
  61.8 1.0 sum.1.refs_24_
  62.8 2.6 %collective-permute-done.10.refs_9_.refs_19_ = bf16[128,1024]{1,0:T(8,128)(2,1)} collective-permute-done((bf16[128,1024]{1,0:T(8,128)(2,1)}, bf16[128,1024]{1,0:T(8,128)(2,1)}, u32[]{:S(2)}, u32[]{:S(2)}) %collective-permute-start.10) | collective-permute-done | bytes 262176 | tf_op jit(solution)/shard_map/ppermute | solution.py:346
  65.4 0.9 copy-done.1
  66.3 0.8 copy-done.2
  67.2 2.7 %gram.3 = (f32[256,512]{1,0:T(8,128)S(1)}, f32[256,512]{1,0:T(8,128)S(1)}) custom-call(s32[7]{0:T(128)S(1)} %copy-done.4, bf16[128,1024]{1,0:T(8,128)(2,1)S(1)} %copy-done, bf16[288,1024]{1,0:T(8,128)(2,1)S(1)} %tie.3.refs_0_.refs_1_.refs_11_, bf16[288,1024]{1,0:T(8,128)(2,1)S(1)} %tie.4.refs_2_.refs_12_, ...), custom_call_target="tpu_custom_call" | custom-call | tf_op jit(solution)/shard_map/gram/pallas_call | solution.py:260
  69.9 0.3 collective-permute-start.12
  70.1 0.5 collective-permute-start.13
  70.6 2.7 %gram.4 = (f32[256,512]{1,0:T(8,128)S(1)}, f32[256,512]{1,0:T(8,128)S(1)}) custom-call(s32[7]{0:T(128)S(1)} %copy-done.4, bf16[128,1024]{1,0:T(8,128)(2,1)S(1)} %copy-done, bf16[288,1024]{1,0:T(8,128)(2,1)S(1)} %tie.3.refs_0_.refs_1_.refs_11_, bf16[288,1024]{1,0:T(8,128)(2,1)S(1)} %tie.4.refs_2_.refs_12_, ...), custom_call_target="tpu_custom_call" | custom-call | tf_op jit(solution)/shard_map/gram/pallas_call | solution.py:260
  73.4 0.2 add.41.refs_24_
  73.5 3.2 %collective-permute-start.16 = (f32[256,1024]{1,0:T(8,128)S(1)}, f32[256,1024]{1,0:T(8,128)S(1)}, u32[]{:S(2)}, u32[]{:S(2)}) collective-permute-start(f32[256,1024]{1,0:T(8,128)S(1)} %add.41.refs_24_), channel_id=1, source_target_pairs={{0,128},{128,0},{1,129},{129,1},{2,130},{130,2},{3,131},{131,3},{4... | collective-permute-start | bytes 3145736 | tf_op jit(solution)/shard_map/ppermute | solution.py:502
  76.7 4.1 %gram.5 = (f32[256,512]{1,0:T(8,128)S(1)}, f32[256,512]{1,0:T(8,128)S(1)}, f32[256,512]{1,0:T(8,128)S(1)}, f32[256,512]{1,0:T(8,128)S(1)}) custom-call(s32[7]{0:T(128)S(1)} %copy-done.4, bf16[128,1024]{1,0:T(8,128)(2,1)S(1)} %copy-done, bf16[288,1024]{1,0:T(8,128)(2,1)S(1)} %tie.3.refs_0_.refs_1_.refs_11_, bf16[288,1024]{1,0:T(8,128)(2,1)S(1)} %tie.4.refs_2_.refs_12_, ...), custom_call_target="tpu_custom_call" | custom-call | tf_op jit(solution)/shard_map/gram/pallas_call | solution.py:260
  80.8 0.1 collective-permute-start.14
  80.9 0.5 collective-permute-start.15
  81.4 1.4 %collective-permute-start.17 = (f32[32,128]{1,0:T(8,128)S(1)}, f32[32,128]{1,0:T(8,128)S(1)}, u32[]{:S(2)}, u32[]{:S(2)}) collective-permute-start(f32[32,128]{1,0:T(8,128)S(1)} %sum.1.refs_24_), channel_id=1, source_target_pairs={{0,4},{4,0},{8,12},{12,8},{1,5},{5,1},{9,13},{13,9},{2,6},{6,2},{1... | collective-permute-start | bytes 49160 | tf_op jit(solution)/shard_map/ppermute | solution.py:477
  82.8 2.3 %collective-permute-done.17 = f32[32,128]{1,0:T(8,128)S(1)} collective-permute-done((f32[32,128]{1,0:T(8,128)S(1)}, f32[32,128]{1,0:T(8,128)S(1)}, u32[]{:S(2)}, u32[]{:S(2)}) %collective-permute-start.17) | collective-permute-done | bytes 16416 | tf_op jit(solution)/shard_map/ppermute | solution.py:477
  85.2 1.7 %collective-permute-start.18 = (f32[2,32,128]{2,1,0:T(8,128)S(1)}, f32[2,32,128]{2,1,0:T(8,128)S(1)}, u32[]{:S(2)}, u32[]{:S(2)}) collective-permute-start(f32[2,32,128]{2,1,0:T(8,128)S(1)} %pad_maximum_fusion.pair), channel_id=1, source_target_pairs={{0,8},{4,12},{8,0},{12,4},{1,9},{5,13},{9,1},{13,5},{2,10},{6,14},... | collective-permute-start | bytes 98312 | tf_op jit(solution)/shard_map/ppermute | solution.py:478
  86.8 3.7 %collective-permute-done.18.far_pair = f32[2,32,128]{2,1,0:T(8,128)S(1)} collective-permute-done((f32[2,32,128]{2,1,0:T(8,128)S(1)}, f32[2,32,128]{2,1,0:T(8,128)S(1)}, u32[]{:S(2)}, u32[]{:S(2)}) %collective-permute-start.18) | collective-permute-done | bytes 32800 | tf_op jit(solution)/shard_map/ppermute | solution.py:478
  90.6 1.3 %assemble.1 = f32[64,256]{1,0:T(8,128)} custom-call(s32[7]{0:T(128)S(1)} %copy-done.4, f32[2,32,128]{2,1,0:T(8,128)S(1)} %pad_maximum_fusion.pair, f32[2,32,128]{2,1,0:T(8,128)S(1)} %collective-permute-done.18.far_pair), custom_call_target="tpu_custom_call" | custom-call | bytes 131072 | tf_op jit(solution)/shard_map/assemble/pallas_call | solution.py:479
  91.8 8.4 %collective-permute-done.16.got = f32[256,1024]{1,0:T(8,128)S(1)} collective-permute-done((f32[256,1024]{1,0:T(8,128)S(1)}, f32[256,1024]{1,0:T(8,128)S(1)}, u32[]{:S(2)}, u32[]{:S(2)}) %collective-permute-start.16) | collective-permute-done | bytes 1048608 | tf_op jit(solution)/shard_map/ppermute | solution.py:502
  100.3 1.6 %finish.1 = f32[256,1024]{1,0:T(8,128)} custom-call(f32[256,512]{1,0:T(8,128)S(1)} %get-tuple-element.28.low, f32[256,512]{1,0:T(8,128)S(1)} %get-tuple-element.29.high, f32[256,512]{1,0:T(8,128)S(1)} %collective-permute-done.14.low_core, f32[256,512]{1,0:T(8,128)S(1)} %collective-permute-done.15.high_core, f32[256,1024]{1,0:T(8,128)S(1)} %collective-permute-done.16.got), custom_call_target="tpu_custom_call" | custom-call | flops 1048576 | bytes 4194304 | tf_op jit(solution)/shard_map/finish/pallas_call | solution.py:305
  (32 shorter events, 0.1 us)
Async XLA Ops:
  1.3 7.0 %copy-start.7 = (s32[256,1,32]{0,2,1:T(8,128)S(1)}, s32[256,1,32]{0,2,1:T(8,128)}, u32[]{:S(2)}) copy-start(s32[256,1,32]{0,2,1:T(8,128)} %param.6) | copy-start | bytes 98308
  6.3 14.0 %collective-permute-start = (bf16[288,1024]{1,0:T(8,128)(2,1)}, bf16[288,1024]{1,0:T(8,128)(2,1)S(1)}, u32[]{:S(2)}, u32[]{:S(2)}) collective-permute-start(bf16[288,1024]{1,0:T(8,128)(2,1)} %get-tuple-element.18), channel_id=1, source_target_pairs={{0,16},{16,32},{32,48},{48,64},{64,80},{80,96},{96,112},{112,0},{1... | collective-permute-start | bytes 1769480 | tf_op jit(solution)/shard_map/ppermute | solution.py:345
  8.3 6.0 %copy-start.8 = (bf16[256,1024]{1,0:T(8,128)(2,1)S(1)}, bf16[256,1024]{1,0:T(8,128)(2,1)}, u32[]{:S(2)}) copy-start(bf16[256,1024]{1,0:T(8,128)(2,1)} %get-tuple-element.20) | copy-start | bytes 1572868
  12.1 18.4 %copy-start.4 = (s32[7]{0:T(128)S(1)}, s32[7]{0:T(128)}, u32[]{:S(2)}) copy-start(s32[7]{0:T(128)} %stack.40.at) | copy-start | bytes 88
  12.1 18.4 %copy-start.5 = (s32[1024]{0:T(1024)S(1)}, s32[1024]{0:T(1024)}, u32[]{:S(2)}) copy-start(s32[1024]{0:T(1024)} %param.9) | copy-start | bytes 12292
  12.1 18.4 %copy-start.6 = (s32[256]{0:T(256)S(1)}, s32[256]{0:T(256)}, u32[]{:S(2)}) copy-start(s32[256]{0:T(256)} %param.8) | copy-start | bytes 3076
  12.2 6.6 %collective-permute-start.1 = (f32[128,256]{1,0:T(8,128)S(1)}, f32[128,256]{1,0:T(8,128)S(1)}, u32[]{:S(2)}, u32[]{:S(2)}) collective-permute-start(f32[128,256]{1,0:T(8,128)S(1)} %dynamic-slice_bitcast_fusion), channel_id=1, source_target_pairs={{0,8},{4,12},{8,0},{12,4},{1,9},{5,13},{9,1},{13,5},{2,10},{6,14},... | collective-permute-start | bytes 393224 | tf_op jit(solution)/shard_map/ppermute | solution.py:430
  14.4 11.6 %collective-permute-start.6 = (bf16[256,1024]{1,0:T(8,128)(2,1)S(1)}, bf16[256,1024]{1,0:T(8,128)(2,1)S(1)}, u32[]{:S(2)}, u32[]{:S(2)}) collective-permute-start(bf16[256,1024]{1,0:T(8,128)(2,1)S(1)} %copy-done.8), channel_id=1, source_target_pairs={{0,16},{16,32},{32,48},{48,64},{64,80},{80,96},{96,112},{112,0},{1... | collective-permute-start | bytes 1572872 | tf_op jit(solution)/shard_map/ppermute | solution.py:346
  20.3 12.3 %collective-permute-start.2 = (bf16[288,1024]{1,0:T(8,128)(2,1)S(1)}, bf16[288,1024]{1,0:T(8,128)(2,1)S(1)}, u32[]{:S(2)}, u32[]{:S(2)}) collective-permute-start(bf16[288,1024]{1,0:T(8,128)(2,1)S(1)} %tie.3.refs_0_.refs_1_.refs_11_), channel_id=1, source_target_pairs={{0,16},{16,32},{32,48},{48,64},{64,80},{80,96},{96,112},{112,0},{1... | collective-permute-start | bytes 1769480 | tf_op jit(solution)/shard_map/ppermute | solution.py:345
  25.9 12.0 %collective-permute-start.7 = (bf16[256,1024]{1,0:T(8,128)(2,1)S(1)}, bf16[256,1024]{1,0:T(8,128)(2,1)}, u32[]{:S(2)}, u32[]{:S(2)}) collective-permute-start(bf16[256,1024]{1,0:T(8,128)(2,1)S(1)} %collective-permute-done.6.refs_1_.refs_6_.refs_16_), channel_id=1, source_target_pairs={{0,16},{16,32},{32,48},{48,64},{64,80},{80,96},{96,112},{112,0},{1... | collective-permute-start | bytes 1572872 | tf_op jit(solution)/shard_map/ppermute | solution.py:346
  25.9 4.5 %collective-permute-start.3 = (f32[64,256]{1,0:T(8,128)S(1)}, f32[64,256]{1,0:T(8,128)S(1)}, u32[]{:S(2)}, u32[]{:S(2)}) collective-permute-start(f32[64,256]{1,0:T(8,128)S(1)} %constant_dynamic-slice_fusion), channel_id=1, source_target_pairs={{0,4},{4,0},{8,12},{12,8},{1,5},{5,1},{9,13},{13,9},{2,6},{6,2},{1... | collective-permute-start | bytes 196616 | tf_op jit(solution)/shard_map/ppermute | solution.py:432
  32.7 18.6 %collective-permute-start.4 = (bf16[288,1024]{1,0:T(8,128)(2,1)S(1)}, bf16[288,1024]{1,0:T(8,128)(2,1)S(1)}, u32[]{:S(2)}, u32[]{:S(2)}) collective-permute-start(bf16[288,1024]{1,0:T(8,128)(2,1)S(1)} %tie.4.refs_2_.refs_12_), channel_id=1, source_target_pairs={{0,16},{16,32},{32,48},{48,64},{64,80},{80,96},{96,112},{112,0},{1... | collective-permute-start | bytes 1769480 | tf_op jit(solution)/shard_map/ppermute | solution.py:345
  38.0 16.5 %collective-permute-start.8 = (bf16[256,1024]{1,0:T(8,128)(2,1)}, bf16[256,1024]{1,0:T(8,128)(2,1)S(1)}, u32[]{:S(2)}, u32[]{:S(2)}) collective-permute-start(bf16[256,1024]{1,0:T(8,128)(2,1)} %collective-permute-done.7.refs_3_.refs_7_.refs_17_), channel_id=1, source_target_pairs={{0,16},{16,32},{32,48},{48,64},{64,80},{80,96},{96,112},{112,0},{1... | collective-permute-start | bytes 1572872 | tf_op jit(solution)/shard_map/ppermute | solution.py:346
  40.1 14.3 %collective-permute-start.9 = (bf16[512,256]{1,0:T(8,128)(2,1)}, bf16[512,256]{1,0:T(8,128)(2,1)}, u32[]{:S(2)}, u32[]{:S(2)}) collective-permute-start(bf16[512,256]{1,0:T(8,128)(2,1)} %pick.1.refs_1_), channel_id=1, source_target_pairs={{0,2},{2,0},{1,3},{3,1},{4,6},{6,4},{5,7},{7,5},{8,10},{10,8},{9,1... | collective-permute-start | bytes 786440 | tf_op jit(solution)/shard_map/ppermute | solution.py:355
  41.7 23.7 %copy-start = (bf16[128,1024]{1,0:T(8,128)(2,1)S(1)}, bf16[128,1024]{1,0:T(8,128)(2,1)}, u32[]{:S(2)}) copy-start(bf16[128,1024]{1,0:T(8,128)(2,1)} %get-tuple-element.17.refs_0_.refs_10_) | copy-start | bytes 786436
  41.7 20.1 %all-to-all-start = ((f32[16,32,128]{2,1,0:T(8,128)}), f32[16,32,128]{2,1,0:T(8,128)}, u32[]{:S(2)}, u32[]{:S(2)}) async-start(f32[16,32,128]{2,1,0:T(8,128)} %bitcast.16), calls=%async_computation | async-start | bytes 524288 | tf_op jit(solution)/shard_map/all_to_all | solution.py:465
  52.6 12.8 %collective-permute-start.5 = (bf16[160,1024]{1,0:T(8,128)(2,1)}, bf16[160,1024]{1,0:T(8,128)(2,1)S(1)}, u32[]{:S(2)}, u32[]{:S(2)}) collective-permute-start(bf16[160,1024]{1,0:T(8,128)(2,1)} %halve_low.1), channel_id=1, source_target_pairs={{0,16},{16,32},{32,48},{48,64},{64,80},{80,96},{96,112},{112,0},{1... | collective-permute-start | bytes 983048 | tf_op jit(solution)/shard_map/ppermute | solution.py:345
  55.8 9.5 %collective-permute-start.10 = (bf16[128,1024]{1,0:T(8,128)(2,1)}, bf16[128,1024]{1,0:T(8,128)(2,1)}, u32[]{:S(2)}, u32[]{:S(2)}) collective-permute-start(bf16[128,1024]{1,0:T(8,128)(2,1)} %get-tuple-element.21), channel_id=1, source_target_pairs={{0,16},{16,32},{32,48},{48,64},{64,80},{80,96},{96,112},{112,0},{1... | collective-permute-start | bytes 786440 | tf_op jit(solution)/shard_map/ppermute | solution.py:346
  57.3 5.5 %collective-permute-start.11 = (bf16[256,256]{1,0:T(8,128)(2,1)}, bf16[256,256]{1,0:T(8,128)(2,1)S(1)}, u32[]{:S(2)}, u32[]{:S(2)}) collective-permute-start(bf16[256,256]{1,0:T(8,128)(2,1)} %get-tuple-element.23), channel_id=1, source_target_pairs={{0,2},{2,0},{1,3},{3,1},{4,6},{6,4},{5,7},{7,5},{8,10},{10,8},{9,1... | collective-permute-start | bytes 393224 | tf_op jit(solution)/shard_map/ppermute | solution.py:357
  65.4 1.0 copy-start.1
  66.3 0.8 copy-start.2
  67.2 3.5 %copy-start.3 = (bf16[128,256]{1,0:T(8,128)(2,1)S(1)}, bf16[128,256]{1,0:T(8,128)(2,1)}, u32[]{:S(2)}) copy-start(bf16[128,256]{1,0:T(8,128)(2,1)} %get-tuple-element.22.refs_20_) | copy-start | bytes 196612
  69.9 3.5 %collective-permute-start.12 = (f32[256,512]{1,0:T(8,128)S(1)}, f32[256,512]{1,0:T(8,128)S(1)}, u32[]{:S(2)}, u32[]{:S(2)}) collective-permute-start(f32[256,512]{1,0:T(8,128)S(1)} %get-tuple-element.24.refs_24_), channel_id=1, source_target_pairs={{0,1},{1,0},{2,3},{3,2},{4,5},{5,4},{6,7},{7,6},{8,9},{9,8},{10,11... | collective-permute-start | bytes 1572872 | tf_op jit(solution)/shard_map/ppermute | solution.py:360
  70.1 3.2 %collective-permute-start.13 = (f32[256,512]{1,0:T(8,128)S(1)}, f32[256,512]{1,0:T(8,128)S(1)}, u32[]{:S(2)}, u32[]{:S(2)}) collective-permute-start(f32[256,512]{1,0:T(8,128)S(1)} %get-tuple-element.25.refs_25_), channel_id=1, source_target_pairs={{0,1},{1,0},{2,3},{3,2},{4,5},{5,4},{6,7},{7,6},{8,9},{9,8},{10,11... | collective-permute-start | bytes 1572872 | tf_op jit(solution)/shard_map/ppermute | solution.py:360
  73.5 26.8 %collective-permute-start.16 = (f32[256,1024]{1,0:T(8,128)S(1)}, f32[256,1024]{1,0:T(8,128)S(1)}, u32[]{:S(2)}, u32[]{:S(2)}) collective-permute-start(f32[256,1024]{1,0:T(8,128)S(1)} %add.41.refs_24_), channel_id=1, source_target_pairs={{0,128},{128,0},{1,129},{129,1},{2,130},{130,2},{3,131},{131,3},{4... | collective-permute-start | bytes 3145736 | tf_op jit(solution)/shard_map/ppermute | solution.py:502
  80.8 11.0 %collective-permute-start.14 = (f32[256,512]{1,0:T(8,128)S(1)}, f32[256,512]{1,0:T(8,128)S(1)}, u32[]{:S(2)}, u32[]{:S(2)}) collective-permute-start(f32[256,512]{1,0:T(8,128)S(1)} %get-tuple-element.30), channel_id=1, source_target_pairs={{0,1},{1,0},{2,3},{3,2},{4,5},{5,4},{6,7},{7,6},{8,9},{9,8},{10,11... | collective-permute-start | bytes 1572872 | tf_op jit(solution)/shard_map/ppermute | solution.py:364
  80.9 10.9 %collective-permute-start.15 = (f32[256,512]{1,0:T(8,128)S(1)}, f32[256,512]{1,0:T(8,128)S(1)}, u32[]{:S(2)}, u32[]{:S(2)}) collective-permute-start(f32[256,512]{1,0:T(8,128)S(1)} %get-tuple-element.31), channel_id=1, source_target_pairs={{0,1},{1,0},{2,3},{3,2},{4,5},{5,4},{6,7},{7,6},{8,9},{9,8},{10,11... | collective-permute-start | bytes 1572872 | tf_op jit(solution)/shard_map/ppermute | solution.py:364
  81.4 3.7 %collective-permute-start.17 = (f32[32,128]{1,0:T(8,128)S(1)}, f32[32,128]{1,0:T(8,128)S(1)}, u32[]{:S(2)}, u32[]{:S(2)}) collective-permute-start(f32[32,128]{1,0:T(8,128)S(1)} %sum.1.refs_24_), channel_id=1, source_target_pairs={{0,4},{4,0},{8,12},{12,8},{1,5},{5,1},{9,13},{13,9},{2,6},{6,2},{1... | collective-permute-start | bytes 49160 | tf_op jit(solution)/shard_map/ppermute | solution.py:477
  85.2 5.4 %collective-permute-start.18 = (f32[2,32,128]{2,1,0:T(8,128)S(1)}, f32[2,32,128]{2,1,0:T(8,128)S(1)}, u32[]{:S(2)}, u32[]{:S(2)}) collective-permute-start(f32[2,32,128]{2,1,0:T(8,128)S(1)} %pad_maximum_fusion.pair), channel_id=1, source_target_pairs={{0,8},{4,12},{8,0},{12,4},{1,9},{5,13},{9,1},{13,5},{2,10},{6,14},... | collective-permute-start | bytes 98312 | tf_op jit(solution)/shard_map/ppermute | solution.py:478

commit v11 on v10

--- a/solution.py
+++ b/solution.py
@@ -52,8 +52,7 @@
         scale = jnp.where(at[AT_CORE] == 0, scale[:half], scale[half:])
         own[...] = (own_values[...].astype(jnp.float32) * scale).astype(jnp.bfloat16)
 
-    grads = values[...].astype(jnp.float32) * wide_scale(turned, at[AT_YL] * 16 + step * 4, 512)
-    grads = grads.astype(jnp.bfloat16)
+    grads = values[...] * wide_scale(turned, at[AT_YL] * 16 + step * 4, 512).astype(jnp.bfloat16)
     lows = jnp.concatenate([grads[:, 0:128], grads[:, 256:384]], 1)
     highs = jnp.concatenate([grads[:, 128:256], grads[:, 384:512]], 1)
     low[0:rows], high[...] = lows, highs

time: 104 us -> 104 us (level)
  no operation moved by 1% of the time
where the time goes in v11:
time: 104 us; the launch traced here: 102 us
  waiting for transfers between devices  37.6 us (36%)
  starting transfers between devices  31.7 us (30%)
  Pallas kernels  25.5 us (25%)
  matrix products  3.75 us (4%)
  local copies, waits for them, and re-layouts  2.51 us (2%)
    ppermute x4, waiting for transfers between devices, fisher_terms(): high = lax.ppermute(high, ('z', 'core'), RING)  11.3 us
    all_to_all x1, starting transfers between devices, own_slots(): lax.all_to_all(placed.reshape(YH * Z, half, double), ('yh', 'z'), 0, 0, t...  9.57 us
    pallas_call x3, Pallas kernels, gram(): pl.pallas_call(functools.partial(gram_kernel, sizes, kept, len(parts)), g...  9.5 us
    ppermute x1, waiting for transfers between devices, per_device(): got = lax.ppermute(given, 'yh', SWAP)  8.44 us
    ppermute x4, starting transfers between devices, fisher_terms(): low = lax.ppermute(low, ('z', 'core'), RING)  6.09 us
    pallas_call x1, Pallas kernels, dequant(): pl.pallas_call(dequant_kernel, grid_spec=pltpu.PrefetchScalarGridSpec(num...  5.02 us
    all_to_all x1, waiting for transfers between devices, own_slots(): lax.all_to_all(placed.reshape(YH * Z, half, double), ('yh', 'z'), 0, 0, t...  4.36 us
    dot_general x1, matrix products, placed_scores(): lax.dot_general(queries, grads, (((1,), (1,)), ((), ())), preferred_eleme...  3.75 us
  transfers between devices with their start and end apart: 20, of which 10 were waited for; matrix products, arithmetic and copies ran while one was open for 4% of the time, Pallas kernels for 16%

profile of v11, /device:TPU:2, one launch (start us, length us, event | category | flops | bytes accessed | tf_op | source)
XLA Modules:
  0.0 101.9 jit_solution(11977264344766316896)
XLA Ops:
  0.6 0.7 stack.40.at
  1.3 5.0 %dequant.1 = (bf16[288,1024]{1,0:T(8,128)(2,1)}, bf16[256,1024]{1,0:T(8,128)(2,1)}, bf16[128,1024]{1,0:T(8,128)(2,1)}, bf16[128,1024]{1,0:T(8,128)(2,1)}, bf16[128,256]{1,0:T(8,128)(2,1)}) custom-call(s32[7]{0:T(128)} %stack.40.at, s32[32,256]{1,0:T(8,128)} %bitcast.46, bf16[256,4096]{1,0:T(8,128)(2,1)} %bitcast.42, bf16[256,4096]{1,0:T(8,128)(2,1)} %bitcast.43, ...), custom_call_target="tpu_custom_call" | custom-call | flops 33554432 | bytes 2097152 | tf_op jit(solution)/shard_map/dequant/pallas_call | solution.py:68
  6.3 2.0 %collective-permute-start = (bf16[288,1024]{1,0:T(8,128)(2,1)}, bf16[288,1024]{1,0:T(8,128)(2,1)S(1)}, u32[]{:S(2)}, u32[]{:S(2)}) collective-permute-start(bf16[288,1024]{1,0:T(8,128)(2,1)} %get-tuple-element.18), channel_id=1, source_target_pairs={{0,16},{16,32},{32,48},{48,64},{64,80},{80,96},{96,112},{112,0},{1... | collective-permute-start | bytes 1769480 | tf_op jit(solution)/shard_map/ppermute | solution.py:344
  8.3 3.8 %fusion.1 = f32[256,256]{0,1:T(8,128)S(1)} fusion(bf16[256,1,4096]{2,0,1:T(8,128)(2,1)} %param.7, s32[4096]{0:T(1024)S(1)} %add_select_fusion, s32[256,1,32]{0,2,1:T(8,128)S(1)} %copy-done.7, bf16[256,1,4096]{2,0,1:T(8,128)(2,1)} %param.5), kind=kOutput, calls=%fused_computation.2 | convolution fusion | flops 606232576 | bytes 4505600 | tf_op jit(solution)/shard_map/dot_general | solution.py:425
  12.1 0.0 copy-start.5
  12.1 0.0 copy-start.6
  12.2 2.2 %collective-permute-start.1 = (f32[128,256]{1,0:T(8,128)S(1)}, f32[128,256]{1,0:T(8,128)S(1)}, u32[]{:S(2)}, u32[]{:S(2)}) collective-permute-start(f32[128,256]{1,0:T(8,128)S(1)} %dynamic-slice_bitcast_fusion), channel_id=1, source_target_pairs={{0,8},{4,12},{8,0},{12,4},{1,9},{5,13},{9,1},{13,5},{2,10},{6,14},... | collective-permute-start | bytes 393224 | tf_op jit(solution)/shard_map/ppermute | solution.py:429
  14.4 1.9 %collective-permute-start.6 = (bf16[256,1024]{1,0:T(8,128)(2,1)S(1)}, bf16[256,1024]{1,0:T(8,128)(2,1)S(1)}, u32[]{:S(2)}, u32[]{:S(2)}) collective-permute-start(bf16[256,1024]{1,0:T(8,128)(2,1)S(1)} %copy-done.8), channel_id=1, source_target_pairs={{0,16},{16,32},{32,48},{48,64},{64,80},{80,96},{96,112},{112,0},{1... | collective-permute-start | bytes 1572872 | tf_op jit(solution)/shard_map/ppermute | solution.py:345
  16.3 2.4 %collective-permute-done.1 = f32[128,256]{1,0:T(8,128)S(1)} collective-permute-done((f32[128,256]{1,0:T(8,128)S(1)}, f32[128,256]{1,0:T(8,128)S(1)}, u32[]{:S(2)}, u32[]{:S(2)}) %collective-permute-start.1) | collective-permute-done | bytes 131104 | tf_op jit(solution)/shard_map/ppermute | solution.py:429
  18.7 1.6 %collective-permute-done.refs_0_ = bf16[288,1024]{1,0:T(8,128)(2,1)S(1)} collective-permute-done((bf16[288,1024]{1,0:T(8,128)(2,1)}, bf16[288,1024]{1,0:T(8,128)(2,1)S(1)}, u32[]{:S(2)}, u32[]{:S(2)}) %collective-permute-start) | collective-permute-done | bytes 589856 | tf_op jit(solution)/shard_map/ppermute | solution.py:344
  20.3 0.4 collective-permute-start.2
  20.7 5.2 %collective-permute-done.6.refs_1_.refs_6_.refs_16_ = bf16[256,1024]{1,0:T(8,128)(2,1)S(1)} collective-permute-done((bf16[256,1024]{1,0:T(8,128)(2,1)S(1)}, bf16[256,1024]{1,0:T(8,128)(2,1)S(1)}, u32[]{:S(2)}, u32[]{:S(2)}) %collective-permute-start.6) | collective-permute-done | bytes 524320 | tf_op jit(solution)/shard_map/ppermute | solution.py:345
  25.9 0.0 collective-permute-start.7
  25.9 1.1 %collective-permute-start.3 = (f32[64,256]{1,0:T(8,128)S(1)}, f32[64,256]{1,0:T(8,128)S(1)}, u32[]{:S(2)}, u32[]{:S(2)}) collective-permute-start(f32[64,256]{1,0:T(8,128)S(1)} %constant_dynamic-slice_fusion), channel_id=1, source_target_pairs={{0,4},{4,0},{8,12},{12,8},{1,5},{5,1},{9,13},{13,9},{2,6},{6,2},{1... | collective-permute-start | bytes 196616 | tf_op jit(solution)/shard_map/ppermute | solution.py:431
  27.0 3.4 %collective-permute-done.3.got = f32[64,256]{1,0:T(8,128)S(1)} collective-permute-done((f32[64,256]{1,0:T(8,128)S(1)}, f32[64,256]{1,0:T(8,128)S(1)}, u32[]{:S(2)}, u32[]{:S(2)}) %collective-permute-start.3) | collective-permute-done | bytes 65568 | tf_op jit(solution)/shard_map/ppermute | solution.py:431
  30.5 2.2 %place.1.refs_1_.refs_0_ = f32[512,128]{1,0:T(8,128)} custom-call(s32[7]{0:T(128)S(1)} %copy-done.4, f32[2,64,256]{2,1,0:T(8,128)S(1)} %bitcast.38, f32[64,256]{1,0:T(8,128)S(1)} %collective-permute-done.3.got, s32[1,256]{1,0:T(1,128)S(1)} %bitcast.41, s32[1,1024]{1,0:T(1,128)S(1)} %bitcast.40), custom_call_target="tpu_custom_call" | custom-call | flops 268435456 | bytes 1048576 | tf_op jit(solution)/shard_map/place/pallas_call | solution.py:433
  32.7 1.8 %collective-permute-start.4 = (bf16[288,1024]{1,0:T(8,128)(2,1)S(1)}, bf16[288,1024]{1,0:T(8,128)(2,1)S(1)}, u32[]{:S(2)}, u32[]{:S(2)}) collective-permute-start(bf16[288,1024]{1,0:T(8,128)(2,1)S(1)} %tie.4.refs_2_.refs_12_), channel_id=1, source_target_pairs={{0,16},{16,32},{32,48},{48,64},{64,80},{80,96},{96,112},{112,0},{1... | collective-permute-start | bytes 1769480 | tf_op jit(solution)/shard_map/ppermute | solution.py:344
  34.5 3.5 %collective-permute-done.7.refs_3_.refs_7_.refs_17_ = bf16[256,1024]{1,0:T(8,128)(2,1)} collective-permute-done((bf16[256,1024]{1,0:T(8,128)(2,1)S(1)}, bf16[256,1024]{1,0:T(8,128)(2,1)}, u32[]{:S(2)}, u32[]{:S(2)}) %collective-permute-start.7) | collective-permute-done | bytes 524320 | tf_op jit(solution)/shard_map/ppermute | solution.py:345
  38.0 2.2 %pick.1.refs_1_ = bf16[512,256]{1,0:T(8,128)(2,1)} custom-call(s32[7]{0:T(128)S(1)} %copy-done.4, bf16[288,1024]{1,0:T(8,128)(2,1)S(1)} %tie.3.refs_0_.refs_1_.refs_11_, bf16[256,1024]{1,0:T(8,128)(2,1)S(1)} %collective-permute-done.6.refs_1_.refs_6_.refs_16_, bf16[288,1024]{1,0:T(8,128)(2,1)S(1)} %tie.4.refs_2_.refs_12_, ...), custom_call_target="tpu_custom_call" | custom-call | bytes 524288 | tf_op jit(solution)/shard_map/pick/pallas_call | solution.py:182
  40.1 1.6 %collective-permute-start.9 = (bf16[512,256]{1,0:T(8,128)(2,1)}, bf16[512,256]{1,0:T(8,128)(2,1)}, u32[]{:S(2)}, u32[]{:S(2)}) collective-permute-start(bf16[512,256]{1,0:T(8,128)(2,1)} %pick.1.refs_1_), channel_id=1, source_target_pairs={{0,2},{2,0},{1,3},{3,1},{4,6},{6,4},{5,7},{7,5},{8,10},{10,8},{9,1... | collective-permute-start | bytes 786440 | tf_op jit(solution)/shard_map/ppermute | solution.py:354
  41.7 9.6 %all-to-all-start = ((f32[16,32,128]{2,1,0:T(8,128)}), f32[16,32,128]{2,1,0:T(8,128)}, u32[]{:S(2)}, u32[]{:S(2)}) async-start(f32[16,32,128]{2,1,0:T(8,128)} %bitcast.16), calls=%async_computation | async-start | bytes 524288 | tf_op jit(solution)/shard_map/all_to_all | solution.py:464
  51.3 0.0 collective-permute-done.4.low.far.low_lanes.refs_3_.refs_13_
  51.3 1.3 %halve_low.1 = bf16[160,1024]{1,0:T(8,128)(2,1)} custom-call(s32[7]{0:T(128)S(1)} %copy-done.4, bf16[288,1024]{1,0:T(8,128)(2,1)S(1)} %collective-permute-done.4.low.far.low_lanes.refs_3_.refs_13_, bf16[288,1024]{1,0:T(8,128)(2,1)S(1)} %collective-permute-done.4.low.far.low_lanes.refs_3_.refs_13_), custom_call_target="tpu_custom_call" | custom-call | bytes 524288 | tf_op jit(solution)/shard_map/halve_low/pallas_call | solution.py:110
  52.6 1.9 %collective-permute-start.5 = (bf16[160,1024]{1,0:T(8,128)(2,1)}, bf16[160,1024]{1,0:T(8,128)(2,1)S(1)}, u32[]{:S(2)}, u32[]{:S(2)}) collective-permute-start(bf16[160,1024]{1,0:T(8,128)(2,1)} %halve_low.1), channel_id=1, source_target_pairs={{0,16},{16,32},{32,48},{48,64},{64,80},{80,96},{96,112},{112,0},{1... | collective-permute-start | bytes 983048 | tf_op jit(solution)/shard_map/ppermute | solution.py:344
  54.5 1.4 %halve_high.1 = (bf16[128,1024]{1,0:T(8,128)(2,1)}, bf16[256,256]{1,0:T(8,128)(2,1)}) custom-call(s32[7]{0:T(128)S(1)} %copy-done.4, bf16[256,1024]{1,0:T(8,128)(2,1)S(1)} %collective-permute-done.8.high.high_lanes.refs_8_.refs_18_, bf16[288,1024]{1,0:T(8,128)(2,1)S(1)} %collective-permute-done.4.low.far.low_lanes.refs_3_.refs_13_, ...), custom_call_target="tpu_custom_call" | custom-call | bytes 1048576 | tf_op jit(solution)/shard_map/halve_high/pallas_call | solution.py:137
  55.8 1.5 %collective-permute-start.10 = (bf16[128,1024]{1,0:T(8,128)(2,1)}, bf16[128,1024]{1,0:T(8,128)(2,1)}, u32[]{:S(2)}, u32[]{:S(2)}) collective-permute-start(bf16[128,1024]{1,0:T(8,128)(2,1)} %get-tuple-element.21), channel_id=1, source_target_pairs={{0,16},{16,32},{32,48},{48,64},{64,80},{80,96},{96,112},{112,0},{1... | collective-permute-start | bytes 786440 | tf_op jit(solution)/shard_map/ppermute | solution.py:345
  57.3 0.1 collective-permute-start.11
  57.4 4.4 %all-to-all-done.parts = f32[16,32,128]{2,1,0:T(8,128)} async-done(((f32[16,32,128]{2,1,0:T(8,128)}), f32[16,32,128]{2,1,0:T(8,128)}, u32[]{:S(2)}, u32[]{:S(2)}) %all-to-all-start) | async-done | bytes 262176 | tf_op jit(solution)/shard_map/all_to_all | solution.py:464
  61.8 1.0 sum.1.refs_24_
  62.8 2.6 %collective-permute-done.10.refs_9_.refs_19_ = bf16[128,1024]{1,0:T(8,128)(2,1)} collective-permute-done((bf16[128,1024]{1,0:T(8,128)(2,1)}, bf16[128,1024]{1,0:T(8,128)(2,1)}, u32[]{:S(2)}, u32[]{:S(2)}) %collective-permute-start.10) | collective-permute-done | bytes 262176 | tf_op jit(solution)/shard_map/ppermute | solution.py:345
  65.4 0.9 copy-done.1
  66.3 0.8 copy-done.2
  67.2 2.7 %gram.3 = (f32[256,512]{1,0:T(8,128)S(1)}, f32[256,512]{1,0:T(8,128)S(1)}) custom-call(s32[7]{0:T(128)S(1)} %copy-done.4, bf16[128,1024]{1,0:T(8,128)(2,1)S(1)} %copy-done, bf16[288,1024]{1,0:T(8,128)(2,1)S(1)} %tie.3.refs_0_.refs_1_.refs_11_, bf16[288,1024]{1,0:T(8,128)(2,1)S(1)} %tie.4.refs_2_.refs_12_, ...), custom_call_target="tpu_custom_call" | custom-call | tf_op jit(solution)/shard_map/gram/pallas_call | solution.py:259
  69.9 0.3 collective-permute-start.12
  70.1 0.5 collective-permute-start.13
  70.6 2.7 %gram.4 = (f32[256,512]{1,0:T(8,128)S(1)}, f32[256,512]{1,0:T(8,128)S(1)}) custom-call(s32[7]{0:T(128)S(1)} %copy-done.4, bf16[128,1024]{1,0:T(8,128)(2,1)S(1)} %copy-done, bf16[288,1024]{1,0:T(8,128)(2,1)S(1)} %tie.3.refs_0_.refs_1_.refs_11_, bf16[288,1024]{1,0:T(8,128)(2,1)S(1)} %tie.4.refs_2_.refs_12_, ...), custom_call_target="tpu_custom_call" | custom-call | tf_op jit(solution)/shard_map/gram/pallas_call | solution.py:259
  73.4 0.2 add.41.refs_24_
  73.5 3.2 %collective-permute-start.16 = (f32[256,1024]{1,0:T(8,128)S(1)}, f32[256,1024]{1,0:T(8,128)S(1)}, u32[]{:S(2)}, u32[]{:S(2)}) collective-permute-start(f32[256,1024]{1,0:T(8,128)S(1)} %add.41.refs_24_), channel_id=1, source_target_pairs={{0,128},{128,0},{1,129},{129,1},{2,130},{130,2},{3,131},{131,3},{4... | collective-permute-start | bytes 3145736 | tf_op jit(solution)/shard_map/ppermute | solution.py:501
  76.7 4.1 %gram.5 = (f32[256,512]{1,0:T(8,128)S(1)}, f32[256,512]{1,0:T(8,128)S(1)}, f32[256,512]{1,0:T(8,128)S(1)}, f32[256,512]{1,0:T(8,128)S(1)}) custom-call(s32[7]{0:T(128)S(1)} %copy-done.4, bf16[128,1024]{1,0:T(8,128)(2,1)S(1)} %copy-done, bf16[288,1024]{1,0:T(8,128)(2,1)S(1)} %tie.3.refs_0_.refs_1_.refs_11_, bf16[288,1024]{1,0:T(8,128)(2,1)S(1)} %tie.4.refs_2_.refs_12_, ...), custom_call_target="tpu_custom_call" | custom-call | tf_op jit(solution)/shard_map/gram/pallas_call | solution.py:259
  80.8 0.1 collective-permute-start.14
  80.9 0.5 collective-permute-start.15
  81.4 1.4 %collective-permute-start.17 = (f32[32,128]{1,0:T(8,128)S(1)}, f32[32,128]{1,0:T(8,128)S(1)}, u32[]{:S(2)}, u32[]{:S(2)}) collective-permute-start(f32[32,128]{1,0:T(8,128)S(1)} %sum.1.refs_24_), channel_id=1, source_target_pairs={{0,4},{4,0},{8,12},{12,8},{1,5},{5,1},{9,13},{13,9},{2,6},{6,2},{1... | collective-permute-start | bytes 49160 | tf_op jit(solution)/shard_map/ppermute | solution.py:476
  82.8 2.3 %collective-permute-done.17 = f32[32,128]{1,0:T(8,128)S(1)} collective-permute-done((f32[32,128]{1,0:T(8,128)S(1)}, f32[32,128]{1,0:T(8,128)S(1)}, u32[]{:S(2)}, u32[]{:S(2)}) %collective-permute-start.17) | collective-permute-done | bytes 16416 | tf_op jit(solution)/shard_map/ppermute | solution.py:476
  85.1 1.7 %collective-permute-start.18 = (f32[2,32,128]{2,1,0:T(8,128)S(1)}, f32[2,32,128]{2,1,0:T(8,128)S(1)}, u32[]{:S(2)}, u32[]{:S(2)}) collective-permute-start(f32[2,32,128]{2,1,0:T(8,128)S(1)} %pad_maximum_fusion.pair), channel_id=1, source_target_pairs={{0,8},{4,12},{8,0},{12,4},{1,9},{5,13},{9,1},{13,5},{2,10},{6,14},... | collective-permute-start | bytes 98312 | tf_op jit(solution)/shard_map/ppermute | solution.py:477
  86.8 3.7 %collective-permute-done.18.far_pair = f32[2,32,128]{2,1,0:T(8,128)S(1)} collective-permute-done((f32[2,32,128]{2,1,0:T(8,128)S(1)}, f32[2,32,128]{2,1,0:T(8,128)S(1)}, u32[]{:S(2)}, u32[]{:S(2)}) %collective-permute-start.18) | collective-permute-done | bytes 32800 | tf_op jit(solution)/shard_map/ppermute | solution.py:477
  90.6 1.3 %assemble.1 = f32[64,256]{1,0:T(8,128)} custom-call(s32[7]{0:T(128)S(1)} %copy-done.4, f32[2,32,128]{2,1,0:T(8,128)S(1)} %pad_maximum_fusion.pair, f32[2,32,128]{2,1,0:T(8,128)S(1)} %collective-permute-done.18.far_pair), custom_call_target="tpu_custom_call" | custom-call | bytes 131072 | tf_op jit(solution)/shard_map/assemble/pallas_call | solution.py:478
  91.8 8.4 %collective-permute-done.16.got = f32[256,1024]{1,0:T(8,128)S(1)} collective-permute-done((f32[256,1024]{1,0:T(8,128)S(1)}, f32[256,1024]{1,0:T(8,128)S(1)}, u32[]{:S(2)}, u32[]{:S(2)}) %collective-permute-start.16) | collective-permute-done | bytes 1048608 | tf_op jit(solution)/shard_map/ppermute | solution.py:501
  100.3 1.6 %finish.1 = f32[256,1024]{1,0:T(8,128)} custom-call(f32[256,512]{1,0:T(8,128)S(1)} %get-tuple-element.28.low, f32[256,512]{1,0:T(8,128)S(1)} %get-tuple-element.29.high, f32[256,512]{1,0:T(8,128)S(1)} %collective-permute-done.14.low_core, f32[256,512]{1,0:T(8,128)S(1)} %collective-permute-done.15.high_core, f32[256,1024]{1,0:T(8,128)S(1)} %collective-permute-done.16.got), custom_call_target="tpu_custom_call" | custom-call | flops 1048576 | bytes 4194304 | tf_op jit(solution)/shard_map/finish/pallas_call | solution.py:304
  (32 shorter events, 0.1 us)
Async XLA Ops:
  1.3 7.0 %copy-start.7 = (s32[256,1,32]{0,2,1:T(8,128)S(1)}, s32[256,1,32]{0,2,1:T(8,128)}, u32[]{:S(2)}) copy-start(s32[256,1,32]{0,2,1:T(8,128)} %param.6) | copy-start | bytes 98308
  6.3 14.0 %collective-permute-start = (bf16[288,1024]{1,0:T(8,128)(2,1)}, bf16[288,1024]{1,0:T(8,128)(2,1)S(1)}, u32[]{:S(2)}, u32[]{:S(2)}) collective-permute-start(bf16[288,1024]{1,0:T(8,128)(2,1)} %get-tuple-element.18), channel_id=1, source_target_pairs={{0,16},{16,32},{32,48},{48,64},{64,80},{80,96},{96,112},{112,0},{1... | collective-permute-start | bytes 1769480 | tf_op jit(solution)/shard_map/ppermute | solution.py:344
  8.3 6.0 %copy-start.8 = (bf16[256,1024]{1,0:T(8,128)(2,1)S(1)}, bf16[256,1024]{1,0:T(8,128)(2,1)}, u32[]{:S(2)}) copy-start(bf16[256,1024]{1,0:T(8,128)(2,1)} %get-tuple-element.20) | copy-start | bytes 1572868
  12.1 18.4 %copy-start.4 = (s32[7]{0:T(128)S(1)}, s32[7]{0:T(128)}, u32[]{:S(2)}) copy-start(s32[7]{0:T(128)} %stack.40.at) | copy-start | bytes 88
  12.1 18.4 %copy-start.5 = (s32[1024]{0:T(1024)S(1)}, s32[1024]{0:T(1024)}, u32[]{:S(2)}) copy-start(s32[1024]{0:T(1024)} %param.9) | copy-start | bytes 12292
  12.1 18.4 %copy-start.6 = (s32[256]{0:T(256)S(1)}, s32[256]{0:T(256)}, u32[]{:S(2)}) copy-start(s32[256]{0:T(256)} %param.8) | copy-start | bytes 3076
  12.2 6.6 %collective-permute-start.1 = (f32[128,256]{1,0:T(8,128)S(1)}, f32[128,256]{1,0:T(8,128)S(1)}, u32[]{:S(2)}, u32[]{:S(2)}) collective-permute-start(f32[128,256]{1,0:T(8,128)S(1)} %dynamic-slice_bitcast_fusion), channel_id=1, source_target_pairs={{0,8},{4,12},{8,0},{12,4},{1,9},{5,13},{9,1},{13,5},{2,10},{6,14},... | collective-permute-start | bytes 393224 | tf_op jit(solution)/shard_map/ppermute | solution.py:429
  14.4 11.6 %collective-permute-start.6 = (bf16[256,1024]{1,0:T(8,128)(2,1)S(1)}, bf16[256,1024]{1,0:T(8,128)(2,1)S(1)}, u32[]{:S(2)}, u32[]{:S(2)}) collective-permute-start(bf16[256,1024]{1,0:T(8,128)(2,1)S(1)} %copy-done.8), channel_id=1, source_target_pairs={{0,16},{16,32},{32,48},{48,64},{64,80},{80,96},{96,112},{112,0},{1... | collective-permute-start | bytes 1572872 | tf_op jit(solution)/shard_map/ppermute | solution.py:345
  20.3 12.3 %collective-permute-start.2 = (bf16[288,1024]{1,0:T(8,128)(2,1)S(1)}, bf16[288,1024]{1,0:T(8,128)(2,1)S(1)}, u32[]{:S(2)}, u32[]{:S(2)}) collective-permute-start(bf16[288,1024]{1,0:T(8,128)(2,1)S(1)} %tie.3.refs_0_.refs_1_.refs_11_), channel_id=1, source_target_pairs={{0,16},{16,32},{32,48},{48,64},{64,80},{80,96},{96,112},{112,0},{1... | collective-permute-start | bytes 1769480 | tf_op jit(solution)/shard_map/ppermute | solution.py:344
  25.9 12.0 %collective-permute-start.7 = (bf16[256,1024]{1,0:T(8,128)(2,1)S(1)}, bf16[256,1024]{1,0:T(8,128)(2,1)}, u32[]{:S(2)}, u32[]{:S(2)}) collective-permute-start(bf16[256,1024]{1,0:T(8,128)(2,1)S(1)} %collective-permute-done.6.refs_1_.refs_6_.refs_16_), channel_id=1, source_target_pairs={{0,16},{16,32},{32,48},{48,64},{64,80},{80,96},{96,112},{112,0},{1... | collective-permute-start | bytes 1572872 | tf_op jit(solution)/shard_map/ppermute | solution.py:345
  25.9 4.5 %collective-permute-start.3 = (f32[64,256]{1,0:T(8,128)S(1)}, f32[64,256]{1,0:T(8,128)S(1)}, u32[]{:S(2)}, u32[]{:S(2)}) collective-permute-start(f32[64,256]{1,0:T(8,128)S(1)} %constant_dynamic-slice_fusion), channel_id=1, source_target_pairs={{0,4},{4,0},{8,12},{12,8},{1,5},{5,1},{9,13},{13,9},{2,6},{6,2},{1... | collective-permute-start | bytes 196616 | tf_op jit(solution)/shard_map/ppermute | solution.py:431
  32.7 18.6 %collective-permute-start.4 = (bf16[288,1024]{1,0:T(8,128)(2,1)S(1)}, bf16[288,1024]{1,0:T(8,128)(2,1)S(1)}, u32[]{:S(2)}, u32[]{:S(2)}) collective-permute-start(bf16[288,1024]{1,0:T(8,128)(2,1)S(1)} %tie.4.refs_2_.refs_12_), channel_id=1, source_target_pairs={{0,16},{16,32},{32,48},{48,64},{64,80},{80,96},{96,112},{112,0},{1... | collective-permute-start | bytes 1769480 | tf_op jit(solution)/shard_map/ppermute | solution.py:344
  38.0 16.5 %collective-permute-start.8 = (bf16[256,1024]{1,0:T(8,128)(2,1)}, bf16[256,1024]{1,0:T(8,128)(2,1)S(1)}, u32[]{:S(2)}, u32[]{:S(2)}) collective-permute-start(bf16[256,1024]{1,0:T(8,128)(2,1)} %collective-permute-done.7.refs_3_.refs_7_.refs_17_), channel_id=1, source_target_pairs={{0,16},{16,32},{32,48},{48,64},{64,80},{80,96},{96,112},{112,0},{1... | collective-permute-start | bytes 1572872 | tf_op jit(solution)/shard_map/ppermute | solution.py:345
  40.1 14.3 %collective-permute-start.9 = (bf16[512,256]{1,0:T(8,128)(2,1)}, bf16[512,256]{1,0:T(8,128)(2,1)}, u32[]{:S(2)}, u32[]{:S(2)}) collective-permute-start(bf16[512,256]{1,0:T(8,128)(2,1)} %pick.1.refs_1_), channel_id=1, source_target_pairs={{0,2},{2,0},{1,3},{3,1},{4,6},{6,4},{5,7},{7,5},{8,10},{10,8},{9,1... | collective-permute-start | bytes 786440 | tf_op jit(solution)/shard_map/ppermute | solution.py:354
  41.7 23.7 %copy-start = (bf16[128,1024]{1,0:T(8,128)(2,1)S(1)}, bf16[128,1024]{1,0:T(8,128)(2,1)}, u32[]{:S(2)}) copy-start(bf16[128,1024]{1,0:T(8,128)(2,1)} %get-tuple-element.17.refs_0_.refs_10_) | copy-start | bytes 786436
  41.7 20.1 %all-to-all-start = ((f32[16,32,128]{2,1,0:T(8,128)}), f32[16,32,128]{2,1,0:T(8,128)}, u32[]{:S(2)}, u32[]{:S(2)}) async-start(f32[16,32,128]{2,1,0:T(8,128)} %bitcast.16), calls=%async_computation | async-start | bytes 524288 | tf_op jit(solution)/shard_map/all_to_all | solution.py:464
  52.6 12.8 %collective-permute-start.5 = (bf16[160,1024]{1,0:T(8,128)(2,1)}, bf16[160,1024]{1,0:T(8,128)(2,1)S(1)}, u32[]{:S(2)}, u32[]{:S(2)}) collective-permute-start(bf16[160,1024]{1,0:T(8,128)(2,1)} %halve_low.1), channel_id=1, source_target_pairs={{0,16},{16,32},{32,48},{48,64},{64,80},{80,96},{96,112},{112,0},{1... | collective-permute-start | bytes 983048 | tf_op jit(solution)/shard_map/ppermute | solution.py:344
  55.8 9.5 %collective-permute-start.10 = (bf16[128,1024]{1,0:T(8,128)(2,1)}, bf16[128,1024]{1,0:T(8,128)(2,1)}, u32[]{:S(2)}, u32[]{:S(2)}) collective-permute-start(bf16[128,1024]{1,0:T(8,128)(2,1)} %get-tuple-element.21), channel_id=1, source_target_pairs={{0,16},{16,32},{32,48},{48,64},{64,80},{80,96},{96,112},{112,0},{1... | collective-permute-start | bytes 786440 | tf_op jit(solution)/shard_map/ppermute | solution.py:345
  57.3 5.5 %collective-permute-start.11 = (bf16[256,256]{1,0:T(8,128)(2,1)}, bf16[256,256]{1,0:T(8,128)(2,1)S(1)}, u32[]{:S(2)}, u32[]{:S(2)}) collective-permute-start(bf16[256,256]{1,0:T(8,128)(2,1)} %get-tuple-element.23), channel_id=1, source_target_pairs={{0,2},{2,0},{1,3},{3,1},{4,6},{6,4},{5,7},{7,5},{8,10},{10,8},{9,1... | collective-permute-start | bytes 393224 | tf_op jit(solution)/shard_map/ppermute | solution.py:356
  65.4 1.0 copy-start.1
  66.3 0.8 copy-start.2
  67.2 3.5 %copy-start.3 = (bf16[128,256]{1,0:T(8,128)(2,1)S(1)}, bf16[128,256]{1,0:T(8,128)(2,1)}, u32[]{:S(2)}) copy-start(bf16[128,256]{1,0:T(8,128)(2,1)} %get-tuple-element.22.refs_20_) | copy-start | bytes 196612
  69.9 3.5 %collective-permute-start.12 = (f32[256,512]{1,0:T(8,128)S(1)}, f32[256,512]{1,0:T(8,128)S(1)}, u32[]{:S(2)}, u32[]{:S(2)}) collective-permute-start(f32[256,512]{1,0:T(8,128)S(1)} %get-tuple-element.24.refs_24_), channel_id=1, source_target_pairs={{0,1},{1,0},{2,3},{3,2},{4,5},{5,4},{6,7},{7,6},{8,9},{9,8},{10,11... | collective-permute-start | bytes 1572872 | tf_op jit(solution)/shard_map/ppermute | solution.py:359
  70.1 3.2 %collective-permute-start.13 = (f32[256,512]{1,0:T(8,128)S(1)}, f32[256,512]{1,0:T(8,128)S(1)}, u32[]{:S(2)}, u32[]{:S(2)}) collective-permute-start(f32[256,512]{1,0:T(8,128)S(1)} %get-tuple-element.25.refs_25_), channel_id=1, source_target_pairs={{0,1},{1,0},{2,3},{3,2},{4,5},{5,4},{6,7},{7,6},{8,9},{9,8},{10,11... | collective-permute-start | bytes 1572872 | tf_op jit(solution)/shard_map/ppermute | solution.py:359
  73.5 26.8 %collective-permute-start.16 = (f32[256,1024]{1,0:T(8,128)S(1)}, f32[256,1024]{1,0:T(8,128)S(1)}, u32[]{:S(2)}, u32[]{:S(2)}) collective-permute-start(f32[256,1024]{1,0:T(8,128)S(1)} %add.41.refs_24_), channel_id=1, source_target_pairs={{0,128},{128,0},{1,129},{129,1},{2,130},{130,2},{3,131},{131,3},{4... | collective-permute-start | bytes 3145736 | tf_op jit(solution)/shard_map/ppermute | solution.py:501
  80.8 11.0 %collective-permute-start.14 = (f32[256,512]{1,0:T(8,128)S(1)}, f32[256,512]{1,0:T(8,128)S(1)}, u32[]{:S(2)}, u32[]{:S(2)}) collective-permute-start(f32[256,512]{1,0:T(8,128)S(1)} %get-tuple-element.30), channel_id=1, source_target_pairs={{0,1},{1,0},{2,3},{3,2},{4,5},{5,4},{6,7},{7,6},{8,9},{9,8},{10,11... | collective-permute-start | bytes 1572872 | tf_op jit(solution)/shard_map/ppermute | solution.py:363
  80.9 10.9 %collective-permute-start.15 = (f32[256,512]{1,0:T(8,128)S(1)}, f32[256,512]{1,0:T(8,128)S(1)}, u32[]{:S(2)}, u32[]{:S(2)}) collective-permute-start(f32[256,512]{1,0:T(8,128)S(1)} %get-tuple-element.31), channel_id=1, source_target_pairs={{0,1},{1,0},{2,3},{3,2},{4,5},{5,4},{6,7},{7,6},{8,9},{9,8},{10,11... | collective-permute-start | bytes 1572872 | tf_op jit(solution)/shard_map/ppermute | solution.py:363
  81.4 3.7 %collective-permute-start.17 = (f32[32,128]{1,0:T(8,128)S(1)}, f32[32,128]{1,0:T(8,128)S(1)}, u32[]{:S(2)}, u32[]{:S(2)}) collective-permute-start(f32[32,128]{1,0:T(8,128)S(1)} %sum.1.refs_24_), channel_id=1, source_target_pairs={{0,4},{4,0},{8,12},{12,8},{1,5},{5,1},{9,13},{13,9},{2,6},{6,2},{1... | collective-permute-start | bytes 49160 | tf_op jit(solution)/shard_map/ppermute | solution.py:476
  85.1 5.4 %collective-permute-start.18 = (f32[2,32,128]{2,1,0:T(8,128)S(1)}, f32[2,32,128]{2,1,0:T(8,128)S(1)}, u32[]{:S(2)}, u32[]{:S(2)}) collective-permute-start(f32[2,32,128]{2,1,0:T(8,128)S(1)} %pad_maximum_fusion.pair), channel_id=1, source_target_pairs={{0,8},{4,12},{8,0},{12,4},{1,9},{5,13},{9,1},{13,5},{2,10},{6,14},... | collective-permute-start | bytes 98312 | tf_op jit(solution)/shard_map/ppermute | solution.py:477
